TPU v7x, 32 devices: a whole 2x2x4 slice. The times are simulated.
32 devices in a mesh: dp: 16 (over z, x, core), tensor: 2 (over y).
Axes of the slice: x: 2, y: 2, z: 4, core: 2. Of those that a mesh axis runs over, the one named last changes fastest.
Arguments:
- tokens: bfloat16 [8192, 2048], P('dp'), may hold values from -6 to 6
- positions: int32 [8192], P('dp'), may hold values from 0 to 2046, as said below
- attn_gain: bfloat16 [2048], P('dp'), may hold values from 0.099609375 to 1.8984375
- w_query: bfloat16 [2048, 2048], P('dp', 'tensor'), may hold values from -0.125 to 0.125
- w_key: bfloat16 [2048, 2048], P('dp', 'tensor'), may hold values from -0.125 to 0.125
- w_value: bfloat16 [2048, 2048], P('dp', 'tensor'), may hold values from -0.125 to 0.125
- w_out: bfloat16 [2048, 2048], P('tensor', 'dp'), may hold values from -1 to 1
- ffn_gain: bfloat16 [2048], P('dp'), may hold values from 0.099609375 to 1.8984375
- w_gate: bfloat16 [2048, 5504], P('dp', 'tensor'), may hold values from -0.125 to 0.125
- w_up: bfloat16 [2048, 5504], P('dp', 'tensor'), may hold values from -0.125 to 0.125
- w_down: bfloat16 [5504, 2048], P('tensor', 'dp'), may hold values from -0.078125 to 0.078125
- cotangent: bfloat16 [8192, 2048], P('dp'), may hold values from -6 to 6
Outputs:
- layer_out: bfloat16 [8192, 2048], P('dp')
- tokens_grad: float32 [8192, 2048], P('dp')
- attn_gain_grad: float32 [2048], P('dp')
- w_query_grad: float32 [2048, 2048], P('dp', 'tensor')
- w_key_grad: float32 [2048, 2048], P('dp', 'tensor')
- w_value_grad: float32 [2048, 2048], P('dp', 'tensor')
- w_out_grad: float32 [2048, 2048], P('tensor', 'dp')
- ffn_gain_grad: float32 [2048], P('dp')
- w_gate_grad: float32 [2048, 5504], P('dp', 'tensor')
- w_up_grad: float32 [2048, 5504], P('dp', 'tensor')
- w_down_grad: float32 [5504, 2048], P('tensor', 'dp')
Inputs may be any that keep to these rules, and one draw needn't show every extreme that they name: positions is 0 where a document of the packed stream begins and one more than the previous token's elsewhere; documents hold 1 to 2047 tokens.
All inputs are finite; a program needn't handle non-finite values.
Results may differ from a plain program's by a relative error of at most 0.014.
Values may be sent and summed in bfloat16 or wider, within the bound.
A program may use at most 256 MiB of HBM per device.

v0:
```python
import jax
import jax.numpy as jnp
from jax import lax
from jax.sharding import PartitionSpec as P

E = 128
WINDOW = 1024


EPS = 1e-06
THETA = 10000.0


def shifted_2(block, axis, distance):
    devices = range(lax.axis_size(axis))
    route = [(i - distance, i) for i in devices if i - distance in devices]
    return lax.ppermute(block, axis, route)


def rms_scale(matrix, gain):
    mean_square = jnp.mean(matrix * matrix, axis=-1, keepdims=True)
    return matrix * lax.rsqrt(mean_square + EPS) * gain


def rotary(matrix, places, head_size):
    half_size = head_size // 2
    frequency = THETA ** (-(jnp.arange(half_size, dtype=jnp.float32) * 2.0 / head_size))
    angles = places[:, None, None] * frequency[None, None, :]
    cosine = jnp.cos(angles)
    sine_part = jnp.sin(angles)
    shaped = matrix.reshape(matrix.shape[0], -1, head_size)
    first_half = shaped[..., :half_size]
    second_half = shaped[..., half_size:]
    turned = jnp.concatenate(
        [
            first_half * cosine - second_half * sine_part,
            second_half * cosine + first_half * sine_part,
        ],
        axis=-1,
    )
    return turned.reshape(matrix.shape)


def swiglu(gate_part, up_part):
    return jax.nn.silu(gate_part) * up_part


def contract_rows(left, right):
    return lax.dot_general(
        left, right, (((0,), (0,)), ((), ())), preferred_element_type=jnp.float32
    )


def contract_cols(left, right):
    return lax.dot_general(
        left, right, (((1,), (1,)), ((), ())), preferred_element_type=jnp.float32
    )


def shards(
    tokens,
    positions,
    attn_gain,
    w_query,
    w_key,
    w_value,
    w_out,
    ffn_gain,
    w_gate,
    w_up,
    w_down,
    cotangent,
):
    gathered = (
        lax.all_gather(attn_gain, "dp", axis=0, tiled=True),
        lax.all_gather(w_query, "dp", axis=0, tiled=True),
        lax.all_gather(w_key, "dp", axis=0, tiled=True),
        lax.all_gather(w_value, "dp", axis=0, tiled=True),
        lax.all_gather(w_out, "dp", axis=1, tiled=True),
        lax.all_gather(ffn_gain, "dp", axis=0, tiled=True),
        lax.all_gather(w_gate, "dp", axis=0, tiled=True),
        lax.all_gather(w_up, "dp", axis=0, tiled=True),
        lax.all_gather(w_down, "dp", axis=1, tiled=True),
    )
    (
        gain_attn,
        query_proj,
        key_proj,
        value_proj,
        out_proj,
        gain_ffn,
        gate_proj,
        up_proj,
        down_proj,
    ) = gathered
    span_rows = tokens.shape[0]
    reach = (WINDOW - 2 + span_rows) // span_rows
    head_scale = E ** (-0.5)
    head_count = query_proj.shape[1] // E
    places = positions.astype(jnp.float32)

    def turn(matrix):
        return rotary(matrix, places, E)

    rows = tokens.astype(jnp.float32)
    normed_attn, attn_norm_pull = jax.vjp(rms_scale, rows, gain_attn.astype(jnp.float32))
    normed_attn_low = normed_attn.astype(jnp.bfloat16)
    query_rot, query_pull = jax.vjp(
        turn, jnp.dot(normed_attn_low, query_proj, preferred_element_type=jnp.float32)
    )
    key_rot, key_pull = jax.vjp(
        turn, jnp.dot(normed_attn_low, key_proj, preferred_element_type=jnp.float32)
    )
    query_low = query_rot.astype(jnp.bfloat16)
    key_low = key_rot.astype(jnp.bfloat16)
    value_low = jnp.dot(normed_attn_low, value_proj, preferred_element_type=jnp.float32).astype(
        jnp.bfloat16
    )
    key_parts = [key_low]
    value_parts = [value_low]
    for distance in range(1, reach + 1):
        far_keys, far_values = shifted_2((key_low, value_low), "dp", distance)
        key_parts = [far_keys] + key_parts
        value_parts = [far_values] + value_parts
    key_all = jnp.concatenate(key_parts, axis=0)
    value_all = jnp.concatenate(value_parts, axis=0)
    query_index = jnp.arange(span_rows, dtype=jnp.int32)[:, None]
    key_index = jnp.arange((reach + 1) * span_rows, dtype=jnp.int32)[None, :] - reach * span_rows
    allowed = (
        (key_index <= query_index)
        & (key_index > query_index - WINDOW)
        & (key_index >= query_index - positions[:, None])
    )

    def masked_scores(query_block, key_block):
        return jnp.where(allowed, contract_cols(query_block, key_block) * head_scale, -1e30)

    def head_forward(head_index, carry):
        mixed, log_sums = carry
        column = head_index * E
        query_block = lax.dynamic_slice_in_dim(query_low, column, E, 1)
        key_block = lax.dynamic_slice_in_dim(key_all, column, E, 1)
        value_block = lax.dynamic_slice_in_dim(value_all, column, E, 1)
        scores = masked_scores(query_block, key_block)
        largest = jnp.max(scores, axis=1, keepdims=True)
        shifted = jnp.exp(scores - largest)
        totals = jnp.sum(shifted, axis=1, keepdims=True)
        weights = (shifted / totals).astype(jnp.bfloat16)
        piece = jnp.dot(weights, value_block, preferred_element_type=jnp.float32).astype(
            jnp.bfloat16
        )
        mixed = lax.dynamic_update_slice_in_dim(mixed, piece, column, 1)
        log_sums = lax.dynamic_update_slice_in_dim(
            log_sums, largest + jnp.log(totals), head_index, 1
        )
        return (mixed, log_sums)

    start_mixed = jnp.zeros((span_rows, head_count * E), jnp.bfloat16)
    start_sums = jnp.zeros((span_rows, head_count), jnp.float32)
    mixed_low, log_sums = lax.fori_loop(0, head_count, head_forward, (start_mixed, start_sums))
    attn_total = lax.psum(
        jnp.dot(mixed_low, out_proj, preferred_element_type=jnp.float32), "tensor"
    )
    hidden = rows + attn_total
    normed_ffn, ffn_norm_pull = jax.vjp(rms_scale, hidden, gain_ffn.astype(jnp.float32))
    normed_ffn_low = normed_ffn.astype(jnp.bfloat16)
    gate_lin = jnp.dot(normed_ffn_low, gate_proj, preferred_element_type=jnp.float32)
    up_lin = jnp.dot(normed_ffn_low, up_proj, preferred_element_type=jnp.float32)
    activated, swiglu_pull = jax.vjp(swiglu, gate_lin, up_lin)
    activated_low = activated.astype(jnp.bfloat16)
    ffn_total = lax.psum(
        jnp.dot(activated_low, down_proj, preferred_element_type=jnp.float32).astype(jnp.bfloat16),
        "tensor",
    ).astype(jnp.float32)
    layer_out = (hidden + ffn_total).astype(jnp.bfloat16)
    query_proj, key_proj, value_proj, out_proj, gate_proj, up_proj, down_proj = (
        lax.all_gather(w_query, "dp", axis=0, tiled=True),
        lax.all_gather(w_key, "dp", axis=0, tiled=True),
        lax.all_gather(w_value, "dp", axis=0, tiled=True),
        lax.all_gather(w_out, "dp", axis=1, tiled=True),
        lax.all_gather(w_gate, "dp", axis=0, tiled=True),
        lax.all_gather(w_up, "dp", axis=0, tiled=True),
        lax.all_gather(w_down, "dp", axis=1, tiled=True),
    )
    down_grad = contract_rows(activated_low, cotangent)
    d_activated = contract_cols(cotangent, down_proj)
    d_gate, d_up = swiglu_pull(d_activated)
    d_gate_low = d_gate.astype(jnp.bfloat16)
    d_up_low = d_up.astype(jnp.bfloat16)
    gate_grad = contract_rows(normed_ffn_low, d_gate_low)
    up_grad = contract_rows(normed_ffn_low, d_up_low)
    d_normed_ffn = lax.psum(
        contract_cols(d_gate_low, gate_proj) + contract_cols(d_up_low, up_proj), "tensor"
    )
    d_hidden_norm, gain_ffn_grad = ffn_norm_pull(d_normed_ffn)
    d_hidden = cotangent.astype(jnp.float32) + d_hidden_norm
    d_hidden_low = d_hidden.astype(jnp.bfloat16)
    out_grad = contract_rows(mixed_low, d_hidden_low)
    d_mixed_low = contract_cols(d_hidden_low, out_proj).astype(jnp.bfloat16)

    def head_backward(head_index, carry):
        d_query, d_keys, d_values = carry
        column = head_index * E
        query_block = lax.dynamic_slice_in_dim(query_low, column, E, 1)
        key_block = lax.dynamic_slice_in_dim(key_all, column, E, 1)
        value_block = lax.dynamic_slice_in_dim(value_all, column, E, 1)
        grad_block = lax.dynamic_slice_in_dim(d_mixed_low, column, E, 1)
        scores = masked_scores(query_block, key_block)
        probs = jnp.exp(scores - lax.dynamic_slice_in_dim(log_sums, head_index, 1, 1))
        d_probs = contract_cols(grad_block, value_block)
        d_scores = (probs * (d_probs - jnp.sum(probs * d_probs, axis=1, keepdims=True))).astype(
            jnp.bfloat16
        )
        query_part = jnp.dot(d_scores, key_block, preferred_element_type=jnp.float32) * head_scale
        key_part = contract_rows(d_scores, query_block) * head_scale
        value_part = contract_rows(probs.astype(jnp.bfloat16), grad_block)
        d_query = lax.dynamic_update_slice_in_dim(d_query, query_part, column, 1)
        d_keys = lax.dynamic_update_slice_in_dim(d_keys, key_part, column, 1)
        d_values = lax.dynamic_update_slice_in_dim(d_values, value_part, column, 1)
        return (d_query, d_keys, d_values)

    key_rows = (reach + 1) * span_rows
    start_query = jnp.zeros((span_rows, head_count * E), jnp.float32)
    start_keys = jnp.zeros((key_rows, head_count * E), jnp.float32)
    d_query, d_keys, d_values = lax.fori_loop(
        0, head_count, head_backward, (start_query, start_keys, start_keys)
    )
    own_start = reach * span_rows
    d_keys_own = lax.slice_in_dim(d_keys, own_start, own_start + span_rows, axis=0)
    d_values_own = lax.slice_in_dim(d_values, own_start, own_start + span_rows, axis=0)
    for distance in range(1, reach + 1):
        start_row = (reach - distance) * span_rows
        sent_keys = lax.slice_in_dim(d_keys, start_row, start_row + span_rows, axis=0)
        sent_values = lax.slice_in_dim(d_values, start_row, start_row + span_rows, axis=0)
        returned_keys, returned_values = shifted_2((sent_keys, sent_values), "dp", -distance)
        d_keys_own = d_keys_own + returned_keys
        d_values_own = d_values_own + returned_values
    d_query_low = query_pull(d_query)[0].astype(jnp.bfloat16)
    d_key_low = key_pull(d_keys_own)[0].astype(jnp.bfloat16)
    d_value_low = d_values_own.astype(jnp.bfloat16)
    query_grad = contract_rows(normed_attn_low, d_query_low)
    key_grad = contract_rows(normed_attn_low, d_key_low)
    value_grad = contract_rows(normed_attn_low, d_value_low)
    d_normed_attn = lax.psum(
        contract_cols(d_query_low, query_proj)
        + contract_cols(d_key_low, key_proj)
        + contract_cols(d_value_low, value_proj),
        "tensor",
    )
    d_rows, gain_attn_grad = attn_norm_pull(d_normed_attn)
    tokens_grad = d_hidden + d_rows
    every_sum = (
        lax.psum_scatter(gain_attn_grad, "dp", scatter_dimension=0, tiled=True),
        lax.psum_scatter(query_grad, "dp", scatter_dimension=0, tiled=True),
        lax.psum_scatter(key_grad, "dp", scatter_dimension=0, tiled=True),
        lax.psum_scatter(value_grad, "dp", scatter_dimension=0, tiled=True),
        lax.psum_scatter(out_grad, "dp", scatter_dimension=1, tiled=True),
        lax.psum_scatter(gain_ffn_grad, "dp", scatter_dimension=0, tiled=True),
        lax.psum_scatter(gate_grad, "dp", scatter_dimension=0, tiled=True),
        lax.psum_scatter(up_grad, "dp", scatter_dimension=0, tiled=True),
        lax.psum_scatter(down_grad, "dp", scatter_dimension=1, tiled=True),
    )
    (
        gain_attn_sum,
        query_sum,
        key_sum,
        value_sum,
        out_sum,
        gain_ffn_sum,
        gate_sum,
        up_sum,
        down_sum,
    ) = every_sum
    return (
        layer_out,
        tokens_grad,
        gain_attn_sum,
        query_sum,
        key_sum,
        value_sum,
        out_sum,
        gain_ffn_sum,
        gate_sum,
        up_sum,
        down_sum,
    )


def solution(mesh):
    placed = (
        P("dp", None),
        P("dp"),
        P("dp"),
        P("dp", "tensor"),
        P("dp", "tensor"),
        P("dp", "tensor"),
        P("tensor", "dp"),
        P("dp"),
        P("dp", "tensor"),
        P("dp", "tensor"),
        P("tensor", "dp"),
        P("dp", None),
    )
    return jax.shard_map(
        shards,
        mesh=mesh,
        in_specs=placed,
        out_specs=(
            P("dp", None),
            P("dp", None),
            P("dp"),
            P("dp", "tensor"),
            P("dp", "tensor"),
            P("dp", "tensor"),
            P("tensor", "dp"),
            P("dp"),
            P("dp", "tensor"),
            P("dp", "tensor"),
            P("tensor", "dp"),
        ),
        check_vma=False,
    )
```

profile of v0, /device:TPU:0, one launch (start us, length us, event | category | flops | bytes accessed | tf_op | source)
XLA Modules:
  0.0 2380.0 jit_solution(404622339256267450)
XLA Ops:
  9.5 23.1 all-gather
  36.5 27.0 %all-gather.12.cloned.1.call-done = bf16[2048,1024]{1,0:T(8,128)(2,1)} async-done(((bf16[128,1024]{1,0:T(8,128)(2,1)}), bf16[2048,1024]{1,0:T(8,128)(2,1)}) %all-gather.12.cloned.1.call-update) | async-done | bytes 4194320 | tf_op jit(solution)/shard_map/all_gather | solution.py:77
  69.8 44.9 %all-gather.10.cloned.1.call-done = bf16[2048,1024]{1,0:T(8,128)(2,1)} async-done(((bf16[128,1024]{1,0:T(8,128)(2,1)}), bf16[2048,1024]{1,0:T(8,128)(2,1)}) %all-gather.10.cloned.1.call-update) | async-done | bytes 4194320 | tf_op jit(solution)/shard_map/all_gather | solution.py:76
  132.1 47.4 %all-gather.14.cloned.1.call-done = bf16[2048,1024]{1,0:T(8,128)(2,1)} async-done(((bf16[128,1024]{1,0:T(8,128)(2,1)}), bf16[2048,1024]{1,0:T(8,128)(2,1)}) %all-gather.14.cloned.1.call-update) | async-done | bytes 4194320 | tf_op jit(solution)/shard_map/all_gather | solution.py:78
  216.9 42.2 %while.34 = (s32[]{:T(128)}, bf16[512,1024]{1,0:T(8,128)(2,1)}, f32[512,8]{0,1:T(8,128)S(1)}, bf16[512,1024]{1,0:T(8,128)(2,1)}, bf16[1536,1024]{1,0:T(8,128)(2,...) while((s32[]{:T(128)}, bf16[512,1024]{1,0:T(8,128)(2,1)}, ...), condition=%wide.region_4.5_spmd.clone, body=%wide.region_1.4_spmd.clone.sunk | while | flops 412941824 | bytes 10518703 | solution.py:160
  268.1 46.8 %all-gather.1 = bf16[16,1,128]{2,1,0:T(2,128)(2,1)S(1)} all-gather(bf16[1,1,128]{2,1,0:T(2,128)(2,1)S(1)} %bitcast.107), channel_id=1, replica_groups=mesh['dp'=16,'tensor'=2] {'dp'}, dimensions={0}, use_global_device_ids=true | all-gather | bytes 4352 | tf_op jit(solution)/shard_map/all_gather | solution.py:80
  314.9 88.8 %all-reduce.12.cloned.1.call-done = f32[512,2048]{1,0:T(8,128)} async-done(((f32[512,2048]{1,0:T(8,128)}), f32[512,2048]{1,0:T(8,128)}) %all-reduce.12.cloned.1.call-update) | async-done | bytes 4194320 | tf_op jit(solution)/shard_map/psum | solution.py:161
  408.9 92.7 %all-gather.18.cloned.1.call-done = bf16[2048,2752]{0,1:T(8,128)(2,1)} async-done(((bf16[128,2752]{0,1:T(8,128)(2,1)}), bf16[2048,2752]{0,1:T(8,128)(2,1)}) %all-gather.18.cloned.1.call-update) | async-done | bytes 11272208 | tf_op jit(solution)/shard_map/all_gather | solution.py:81
  512.1 85.9 %all-gather.20.cloned.1.call-done = bf16[2048,2752]{0,1:T(8,128)(2,1)} async-done(((bf16[128,2752]{0,1:T(8,128)(2,1)}), bf16[2048,2752]{0,1:T(8,128)(2,1)}) %all-gather.20.cloned.1.call-update) | async-done | bytes 11272208 | tf_op jit(solution)/shard_map/all_gather | solution.py:82
  610.5 83.8 %all-gather.22.cloned.1.call-done = bf16[2752,2048]{1,0:T(8,128)(2,1)} async-done(((bf16[2752,128]{1,0:T(8,128)(2,1)}), bf16[2752,2048]{1,0:T(8,128)(2,1)}) %all-gather.22.cloned.1.call-update) | async-done | bytes 11272208 | tf_op jit(solution)/shard_map/all_gather | solution.py:83
  740.4 95.3 %all-reduce.16.cloned.1.call-done = f32[512,2048]{1,0:T(8,128)} async-done(((f32[512,2048]{1,0:T(8,128)}), f32[512,2048]{1,0:T(8,128)}) %all-reduce.16.cloned.1.call-update) | async-done | bytes 4194320 | tf_op jit(solution)/shard_map/psum | solution.py:192
  840.8 60.6 %all-reduce.14.cloned.1.call-done = bf16[512,2048]{1,0:T(8,128)(2,1)} async-done(((bf16[512,2048]{1,0:T(8,128)(2,1)}), bf16[512,2048]{1,0:T(8,128)(2,1)}) %all-reduce.14.cloned.1.call-update) | async-done | bytes 2097168 | tf_op jit(solution)/shard_map/psum | solution.py:171
  917.1 83.0 %while.35 = (s32[]{:T(128)}, f32[512,1024]{1,0:T(8,128)S(1)}, f32[1536,1024]{1,0:T(8,128)}, f32[1536,1024]{1,0:T(8,128)}, bf16[512,1024]{1,0:T(8,128)(2,1)}, /*i...) while((s32[]{:T(128)}, f32[512,1024]{1,0:T(8,128)S(1)}, ...), condition=%wide.region_12.13_spmd.clone, body=%wide.region_10.12_spmd.clone.sunk | while | flops 1017904640 | bytes 27157704 | solution.py:225
  1009.3 86.5 %collective-permute-done.5 = f32[512,1024]{1,0:T(8,128)S(1)} collective-permute-done((f32[512,1024]{1,0:T(8,128)S(1)}, f32[512,1024]{1,0:T(8,128)S(1)}, u32[]{:S(2)}, u32[]{:S(2)}) %collective-permute-start.5) | collective-permute-done | bytes 2097184 | tf_op jit(solution)/shard_map/ppermute | solution.py:17
  1108.5 34.2 %collective-permute-done.7 = f32[512,1024]{1,0:T(8,128)S(1)} collective-permute-done((f32[512,1024]{1,0:T(8,128)S(1)}, f32[512,1024]{1,0:T(8,128)S(1)}, u32[]{:S(2)}, u32[]{:S(2)}) %collective-permute-start.7) | collective-permute-done | bytes 2097184 | tf_op jit(solution)/shard_map/ppermute | solution.py:17
  1220.5 36.4 %all-reduce.18.cloned.1.call-done = f32[512,2048]{1,0:T(8,128)} async-done(((f32[512,2048]{1,0:T(8,128)}), f32[512,2048]{1,0:T(8,128)}) %all-reduce.18.cloned.1.call-update) | async-done | bytes 4194320 | tf_op jit(solution)/shard_map/psum | solution.py:244
  1260.4 63.1 %all-reduce.6 = (f32[2048]{0:T(1024)S(1)}, f32[2048]{0:T(1024)S(1)}) all-reduce(f32[2048]{0:T(1024)S(1)} %get-tuple-element.366, f32[2048]{0:T(1024)S(1)} %copy-done.21), channel_id=2, replica_groups=mesh['dp'=16,'tensor'=2] {'dp'}, use_global_device_ids=true, to_apply=%region_16.17.clone | all-reduce | flops 4096 | bytes 32768
  1331.3 35.2 %reduce-scatter.14.cloned.1.call-done = f32[1024,128]{1,0:T(8,128)} async-done(((f32[1024,2048]{1,0:T(8,128)}), f32[1024,128]{1,0:T(8,128)}) %reduce-scatter.14.cloned.1.call-update) | async-done | bytes 524304 | tf_op jit(solution)/shard_map/reduce_scatter | solution.py:257
  1366.5 109.1 %reduce-scatter.12.cloned.1.call-done = f32[128,1024]{1,0:T(8,128)} async-done(((f32[2048,1024]{1,0:T(8,128)}), f32[128,1024]{1,0:T(8,128)}) %reduce-scatter.12.cloned.1.call-update) | async-done | bytes 524304 | tf_op jit(solution)/shard_map/reduce_scatter | solution.py:256
  1475.6 108.9 %reduce-scatter.10.cloned.1.call-done = f32[128,1024]{1,0:T(8,128)} async-done(((f32[2048,1024]{1,0:T(8,128)}), f32[128,1024]{1,0:T(8,128)}) %reduce-scatter.10.cloned.1.call-update) | async-done | bytes 524304 | tf_op jit(solution)/shard_map/reduce_scatter | solution.py:255
  1584.5 108.8 %reduce-scatter.8.cloned.1.call-done = f32[128,1024]{1,0:T(8,128)} async-done(((f32[2048,1024]{1,0:T(8,128)}), f32[128,1024]{1,0:T(8,128)}) %reduce-scatter.8.cloned.1.call-update) | async-done | bytes 524304 | tf_op jit(solution)/shard_map/reduce_scatter | solution.py:254
  1693.3 227.0 %reduce-scatter.16.cloned.1.call-done = f32[128,2752]{0,1:T(8,128)} async-done(((f32[2048,2752]{0,1:T(8,128)}), f32[128,2752]{0,1:T(8,128)}) %reduce-scatter.16.cloned.1.call-update) | async-done | bytes 1409040 | tf_op jit(solution)/shard_map/reduce_scatter | solution.py:259
  1920.3 226.3 %reduce-scatter.18.cloned.1.call-done = f32[128,2752]{0,1:T(8,128)} async-done(((f32[2048,2752]{0,1:T(8,128)}), f32[128,2752]{0,1:T(8,128)}) %reduce-scatter.18.cloned.1.call-update) | async-done | bytes 1409040 | tf_op jit(solution)/shard_map/reduce_scatter | solution.py:260
  2146.7 226.3 %reduce-scatter.20.cloned.1.call-done = f32[2752,128]{1,0:T(8,128)} async-done(((f32[2752,2048]{1,0:T(8,128)}), f32[2752,128]{1,0:T(8,128)}) %reduce-scatter.20.cloned.1.call-update) | async-done | bytes 1409040 | tf_op jit(solution)/shard_map/reduce_scatter | solution.py:261
  (279 shorter events, 405.8 us)
Async XLA Ops:
  7.2 56.3 %all-gather.12.cloned.1.call-start = ((), (), s32[]{:S(2)}) async-start(), calls=%async_computation.8 | async-start | bytes 4456448 | tf_op jit(solution)/shard_map/all_gather | solution.py:77
  7.9 106.8 %all-gather.10.cloned.1.call-start = ((), (), s32[]{:S(2)}) async-start(), calls=%async_computation.7 | async-start | bytes 4456448 | tf_op jit(solution)/shard_map/all_gather | solution.py:76
  8.7 170.8 %all-gather.14.cloned.1.call-start = ((), (), s32[]{:S(2)}) async-start(), calls=%async_computation.9 | async-start | bytes 4456448 | tf_op jit(solution)/shard_map/all_gather | solution.py:78
  9.4 249.7 %all-gather.16.cloned.1.call-start = ((), (), s32[]{:S(2)}) async-start(), calls=%async_computation.10 | async-start | bytes 4456448 | tf_op jit(solution)/shard_map/all_gather | solution.py:79
  125.8 65.6 %collective-permute-start = (bf16[512,1024]{1,0:T(8,128)(2,1)}, bf16[512,1024]{1,0:T(8,128)(2,1)}, u32[]{:S(2)}, u32[]{:S(2)}) collective-permute-start(bf16[512,1024]{1,0:T(8,128)(2,1)} %bitcast.70), channel_id=1, source_target_pairs={{0,4},{2,6},{4,8},{6,10},{8,12},{10,14},{12,16},{14,18},{16,20},{1... | collective-permute-start | bytes 3145736 | tf_op jit(solution)/shard_map/ppermute | solution.py:17
  129.2 63.5 %collective-permute-start.1 = (bf16[512,1024]{1,0:T(8,128)(2,1)}, bf16[512,1024]{1,0:T(8,128)(2,1)}, u32[]{:S(2)}, u32[]{:S(2)}) collective-permute-start(bf16[512,1024]{1,0:T(8,128)(2,1)} %bitcast.70), channel_id=1, source_target_pairs={{0,2},{2,4},{4,6},{6,8},{8,10},{10,12},{12,14},{14,16},{16,18},{18... | collective-permute-start | bytes 3145736 | tf_op jit(solution)/shard_map/ppermute | solution.py:17
  185.0 27.9 %collective-permute-start.2 = (bf16[512,1024]{1,0:T(8,128)(2,1)}, bf16[512,1024]{1,0:T(8,128)(2,1)S(1)}, u32[]{:S(2)}, u32[]{:S(2)}) collective-permute-start(bf16[512,1024]{1,0:T(8,128)(2,1)} %convolution_convert_fusion.2), channel_id=1, source_target_pairs={{0,4},{2,6},{4,8},{6,10},{8,12},{10,14},{12,16},{14,18},{16,20},{1... | collective-permute-start | bytes 3145736 | tf_op jit(solution)/shard_map/ppermute | solution.py:17
  188.6 215.1 %all-reduce.12.cloned.1.call-start = ((), (), s32[]{:S(2)}) async-start(), calls=%async_computation.11 | async-start | bytes 8388608 | tf_op jit(solution)/shard_map/psum | solution.py:161
  266.0 235.7 %all-gather.18.cloned.1.call-start = ((), (), s32[]{:S(2)}) async-start(), calls=%async_computation.12 | async-start | bytes 11976704 | tf_op jit(solution)/shard_map/all_gather | solution.py:81
  266.6 331.4 %all-gather.20.cloned.1.call-start = ((), (), s32[]{:S(2)}) async-start(), calls=%async_computation.13 | async-start | bytes 11976704 | tf_op jit(solution)/shard_map/all_gather | solution.py:82
  267.3 427.0 %all-gather.22.cloned.1.call-start = ((), (), s32[]{:S(2)}) async-start(), calls=%async_computation.14 | async-start | bytes 11976704 | tf_op jit(solution)/shard_map/all_gather | solution.py:83
  268.1 567.6 %all-reduce.16.cloned.1.call-start = ((), (), s32[]{:S(2)}) async-start(), calls=%async_computation.16 | async-start | bytes 8388608 | tf_op jit(solution)/shard_map/psum | solution.py:192
  729.5 171.8 %all-reduce.14.cloned.1.call-start = ((), (), s32[]{:S(2)}) async-start(), calls=%async_computation.15 | async-start | bytes 4194304 | tf_op jit(solution)/shard_map/psum | solution.py:171
  740.4 516.5 %all-reduce.18.cloned.1.call-start = ((), (), s32[]{:S(2)}) async-start(), calls=%async_computation.17 | async-start | bytes 8388608 | tf_op jit(solution)/shard_map/psum | solution.py:244
  1004.3 91.4 %collective-permute-start.5 = (f32[512,1024]{1,0:T(8,128)S(1)}, f32[512,1024]{1,0:T(8,128)S(1)}, u32[]{:S(2)}, u32[]{:S(2)}) collective-permute-start(f32[512,1024]{1,0:T(8,128)S(1)} %get-tuple-element.424), channel_id=1, source_target_pairs={{4,0},{6,2},{8,4},{10,6},{12,8},{14,10},{16,12},{18,14},{20,16},{2... | collective-permute-start | bytes 6291464 | tf_op jit(solution)/shard_map/ppermute | solution.py:17
  1006.2 102.3 %collective-permute-start.6 = (f32[512,1024]{1,0:T(8,128)S(1)}, f32[512,1024]{1,0:T(8,128)S(1)}, u32[]{:S(2)}, u32[]{:S(2)}) collective-permute-start(f32[512,1024]{1,0:T(8,128)S(1)} %get-tuple-element.421), channel_id=1, source_target_pairs={{2,0},{4,2},{6,4},{8,6},{10,8},{12,10},{14,12},{16,14},{18,16},{20... | collective-permute-start | bytes 6291464 | tf_op jit(solution)/shard_map/ppermute | solution.py:17
  1007.5 135.2 %collective-permute-start.7 = (f32[512,1024]{1,0:T(8,128)S(1)}, f32[512,1024]{1,0:T(8,128)S(1)}, u32[]{:S(2)}, u32[]{:S(2)}) collective-permute-start(f32[512,1024]{1,0:T(8,128)S(1)} %get-tuple-element.422), channel_id=1, source_target_pairs={{4,0},{6,2},{8,4},{10,6},{12,8},{14,10},{16,12},{18,14},{20,16},{2... | collective-permute-start | bytes 6291464 | tf_op jit(solution)/shard_map/ppermute | solution.py:17
  1148.9 217.6 %reduce-scatter.14.cloned.1.call-start = ((), (), s32[]{:S(2)}) async-start(), calls=%async_computation.21 | async-start | bytes 8912896 | tf_op jit(solution)/shard_map/reduce_scatter | solution.py:257
  1158.1 317.5 %reduce-scatter.12.cloned.1.call-start = ((), (), s32[]{:S(2)}) async-start(), calls=%async_computation.20 | async-start | bytes 8912896 | tf_op jit(solution)/shard_map/reduce_scatter | solution.py:256
  1166.7 417.7 %reduce-scatter.10.cloned.1.call-start = ((), (), s32[]{:S(2)}) async-start(), calls=%async_computation.19 | async-start | bytes 8912896 | tf_op jit(solution)/shard_map/reduce_scatter | solution.py:255
  1173.9 519.4 %reduce-scatter.8.cloned.1.call-start = ((), (), s32[]{:S(2)}) async-start(), calls=%async_computation.18 | async-start | bytes 8912896 | tf_op jit(solution)/shard_map/reduce_scatter | solution.py:254
  1179.8 740.5 %reduce-scatter.16.cloned.1.call-start = ((), (), s32[]{:S(2)}) async-start(), calls=%async_computation.22 | async-start | bytes 23953408 | tf_op jit(solution)/shard_map/reduce_scatter | solution.py:259
  1192.8 953.9 %reduce-scatter.18.cloned.1.call-start = ((), (), s32[]{:S(2)}) async-start(), calls=%async_computation.23 | async-start | bytes 23953408 | tf_op jit(solution)/shard_map/reduce_scatter | solution.py:260
  1205.8 1167.2 %reduce-scatter.20.cloned.1.call-start = ((), (), s32[]{:S(2)}) async-start(), calls=%async_computation.24 | async-start | bytes 23953408 | tf_op jit(solution)/shard_map/reduce_scatter | solution.py:261
  (35 other events, 1216.8 us)
Sparse Core Ops, SparseCore 0:
  10.2 53.2 all-gather.11
  65.7 49.0 all-gather.9
  116.9 62.5 all-gather.13
  188.7 65.0 all-gather.15
  266.1 137.5 all-reduce.11
  405.9 95.7 all-gather.17
  504.1 93.8 all-gather.19
  600.4 93.8 all-gather.21
  729.6 106.0 all-reduce.15
  838.4 62.8 all-reduce.13
  1149.0 107.8 all-reduce.17
  1261.4 105.0 reduce-scatter.13
  1371.1 104.4 reduce-scatter.11
  1480.1 104.3 reduce-scatter.9
  1588.9 104.3 reduce-scatter.7
  1698.0 222.3 reduce-scatter.15
  1925.0 221.6 reduce-scatter.17
  2151.3 221.6 reduce-scatter.19
where the time goes:
time: 2390 us; the launch traced here: 2380 us
  waiting for transfers between devices  1850 us (77%)
  matrix products  285 us (12%)
  blocking collectives  133 us (6%)
  other arithmetic  48.2 us (2%)
  local copies, waits for them, and re-layouts  34.8 us (1%)
    reduce_scatter x1, waiting for transfers between devices, shards(): lax.psum_scatter(gate_grad, 'dp', scatter_dimension=0, tiled=True)  227 us
    reduce_scatter x1, waiting for transfers between devices, shards(): lax.psum_scatter(up_grad, 'dp', scatter_dimension=0, tiled=True)  226 us
    reduce_scatter x1, waiting for transfers between devices, shards(): lax.psum_scatter(down_grad, 'dp', scatter_dimension=1, tiled=True)  226 us
    ppermute x8, waiting for transfers between devices, shifted_2(): return lax.ppermute(block, axis, route)  138 us
    reduce_scatter x1, waiting for transfers between devices, shards(): lax.psum_scatter(value_grad, 'dp', scatter_dimension=0, tiled=True)  109 us
    reduce_scatter x1, waiting for transfers between devices, shards(): lax.psum_scatter(key_grad, 'dp', scatter_dimension=0, tiled=True)  109 us
    reduce_scatter x1, waiting for transfers between devices, shards(): lax.psum_scatter(query_grad, 'dp', scatter_dimension=0, tiled=True)  109 us
    dot_general x31, matrix products, contract_cols(): lax.dot_general(left, right, (((1,), (1,)), ((), ())), preferred_element_...  99.8 us
  transfers between devices with their start and end apart: 26, of which 20 were waited for; matrix products, arithmetic and copies ran while one was open for 9% of the time, Pallas kernels for 0%

commit v1 on v0

v1 whole, which is shorter than its diff:
```python
import functools

import jax
import jax.numpy as jnp
from jax import lax
from jax.experimental import pallas as pl
from jax.experimental.pallas import tpu as pltpu
from jax.sharding import PartitionSpec as P

E = 128
WINDOW = 1024
EPS = 1e-06
THETA = 10000.0
LOG2E = 1.4426950408889634
MESH = pl.DeviceIdType.MESH
BF = jnp.bfloat16
F32 = jnp.float32
QB = 256
KB = WINDOW + QB
TILE = 256
VMEM = 56 * 1024 * 1024


def whole_spec(shape):
    return pl.BlockSpec(shape, lambda i: (0,) * len(shape))


def cost(flops, nbytes, special=0):
    return pl.CostEstimate(flops=flops, bytes_accessed=nbytes, transcendentals=special)


def ring_chip(place, chips):
    place = lax.rem(place + 2 * chips, chips)
    late = place // (chips // 2)
    return (1 - late) * 2 * place + late * (2 * (chips - 1 - place) + 1)


def ring_place(chip, chips):
    column = lax.rem(chip, 2)
    row = chip // 2
    return (1 - column) * row + column * (chips - 1 - row)


def ring_route(chips, step):
    order = [2 * q if q < chips // 2 else 2 * (chips - 1 - q) + 1 for q in range(chips)]
    return [
        (order[q] * 2 + core, order[(q + step) % chips] * 2 + core)
        for q in range(chips)
        for core in range(2)
    ]


def swap_route(devices):
    return [(i, i ^ 1) for i in range(devices)]


def gather_kernel(devices, chunks, count, *refs):
    ins = refs[:count]
    outs = refs[count : 2 * count]
    local_sem, a_send, a_recv, b_send, b_recv, c_send, c_recv = refs[2 * count :]
    chips = devices // 2
    me = lax.axis_index("dp")
    side = lax.axis_index("tensor")
    core = lax.rem(me, 2)
    place = ring_place(me // 2, chips)

    def device(q):
        return ring_chip(q, chips) * 2 + core

    right = device(place + 1)
    left = device(place - 1)
    partner = me + 1 - 2 * core
    barrier = pltpu.get_barrier_semaphore()
    for other in (right, left, partner):
        pl.semaphore_signal(barrier, inc=1, device_id=(other, side), device_id_type=MESH)
    pl.semaphore_wait(barrier, 3)

    pieces = []
    for index, parts in enumerate(chunks):
        width = ins[index].shape[1] // parts
        for part in range(parts):
            pieces.append((index, part * width, width))
    hops = chips - 1

    def view(ref, row, half, piece, rows):
        index, column, width = piece
        start = row * rows + half * (rows // 2)
        if not isinstance(start, int):
            start = pl.multiple_of(start, 16)
        return ref.at[pl.ds(start, rows // 2), pl.ds(column, width)]

    def remote(source, target, send, recv, other):
        copy = pltpu.make_async_remote_copy(
            src_ref=source,
            dst_ref=target,
            send_sem=send,
            recv_sem=recv,
            device_id=(other, side),
            device_id_type=MESH,
        )
        copy.start()
        return copy

    local = []
    for index in range(count):
        rows = ins[index].shape[0]
        copy = pltpu.make_async_copy(
            ins[index], outs[index].at[pl.ds(pl.multiple_of(me * rows, 16), rows)], local_sem.at[index]
        )
        copy.start()
        local.append(copy)
    forward, partner_copies = {}, []
    for number, piece in enumerate(pieces):
        ref, out = ins[piece[0]], outs[piece[0]]
        rows = ref.shape[0]
        forward[number, 0] = (
            remote(view(ref, 0, 0, piece, rows), view(out, me, 0, piece, rows), a_send.at[number, 0], a_recv.at[number, 0], right),
            remote(view(ref, 0, 1, piece, rows), view(out, me, 1, piece, rows), b_send.at[number, 0], b_recv.at[number, 0], left),
        )
    for number, piece in enumerate(pieces):
        ref, out = ins[piece[0]], outs[piece[0]]
        rows = ref.shape[0]
        for half in range(2):
            partner_copies.append(
                remote(view(ref, 0, half, piece, rows), view(out, me, half, piece, rows), c_send.at[number, 0, half], c_recv.at[number, 0, half], partner)
            )
    for hop in range(hops):
        for number, piece in enumerate(pieces):
            out = outs[piece[0]]
            rows = ins[piece[0]].shape[0]
            came = forward[number, hop]
            sent = []
            for half in range(2):
                came[half].wait_recv()
                owner = device(place - 1 - hop if half == 0 else place + 1 + hop)
                block = view(out, owner, half, piece, rows)
                send, recv = (a_send, a_recv) if half == 0 else (b_send, b_recv)
                if hop < hops - 1:
                    sent.append(
                        remote(block, block, send.at[number, hop + 1], recv.at[number, hop + 1], right if half == 0 else left)
                    )
                partner_copies.append(
                    remote(block, block, c_send.at[number, hop + 1, half], c_recv.at[number, hop + 1, half], partner)
                )
            if sent:
                forward[number, hop + 1] = tuple(sent)
    for copy in local:
        copy.wait()
    for pair in forward.values():
        for copy in pair:
            copy.wait_send()
    for copy in partner_copies:
        copy.wait()


def ring_gather(arrays, chunks, identity):
    devices = lax.axis_size("dp")
    hops = devices // 2 - 1
    pieces = sum(chunks)
    dma = pltpu.SemaphoreType.DMA
    any_space = pl.BlockSpec(memory_space=pl.ANY)
    return pl.pallas_call(
        functools.partial(gather_kernel, devices, chunks, len(arrays)),
        out_shape=[jax.ShapeDtypeStruct((a.shape[0] * devices, a.shape[1]), a.dtype) for a in arrays],
        in_specs=[any_space] * len(arrays),
        out_specs=[any_space] * len(arrays),
        scratch_shapes=[
            dma((len(arrays),)),
            dma((pieces, hops)),
            dma((pieces, hops)),
            dma((pieces, hops)),
            dma((pieces, hops)),
            dma((pieces, hops + 1, 2)),
            dma((pieces, hops + 1, 2)),
        ],
        compiler_params=pltpu.CompilerParams(collective_id=identity, has_side_effects=True),
        name="ring_gather",
    )(*arrays)


def ring_scatter(own_rows):
    devices = lax.axis_size("dp")
    chips = devices // 2
    me = lax.axis_index("dp")
    core = me % 2
    place = ring_place(me // 2, chips)
    rows = own_rows.shape[0] // devices
    width = own_rows.shape[1]
    split = own_rows.reshape(chips, 2, rows, width)
    given = lax.dynamic_slice(split, (0, 1 - core, 0, 0), (chips, 1, rows, width))[:, 0]
    taken = lax.ppermute(given, "dp", swap_route(devices))
    half_rows = rows // 2

    def term(at, half):
        chip = ring_chip(at, chips)
        mine = lax.dynamic_slice(split, (chip, core, half * half_rows, 0), (1, 1, half_rows, width))[0, 0]
        other = lax.dynamic_slice(taken, (chip, half * half_rows, 0), (1, half_rows, width))[0]
        return mine.astype(F32) + other.astype(F32)

    to_right, to_left = term(place - 1, 0).astype(BF), term(place + 1, 1).astype(BF)
    for step in range(chips - 1):
        to_right = lax.ppermute(to_right, "dp", ring_route(chips, 1))
        to_left = lax.ppermute(to_left, "dp", ring_route(chips, -1))
        to_right = to_right.astype(F32) + term(place - 2 - step, 0)
        to_left = to_left.astype(F32) + term(place + 2 + step, 1)
        if step < chips - 2:
            to_right, to_left = to_right.astype(BF), to_left.astype(BF)
    return jnp.concatenate([to_right, to_left], axis=0)


def dot_nn(a, b):
    return jnp.dot(a, b, preferred_element_type=F32)


def dot_nt(a, b):
    return lax.dot_general(a, b, (((1,), (1,)), ((), ())), preferred_element_type=F32)


def matmul_nn(x, w, first, count, name):
    m, k = x.shape

    def kernel(x_ref, w_ref, o_ref):
        o_ref[...] = dot_nn(x_ref[...], w_ref[...]).astype(BF)

    return pl.pallas_call(
        kernel,
        grid=(count,),
        out_shape=jax.ShapeDtypeStruct((m, count * TILE), BF),
        in_specs=[whole_spec((m, k)), pl.BlockSpec((k, TILE), lambda i: (0, i + first))],
        out_specs=pl.BlockSpec((m, TILE), lambda i: (0, i)),
        compiler_params=pltpu.CompilerParams(vmem_limit_bytes=VMEM),
        cost_estimate=cost(2 * m * k * count * TILE, 2 * (m * k + (m + k) * count * TILE)),
        name=name,
    )(x, w)


def matmul_nt(pairs, name):
    m = pairs[0][0].shape[0]
    n = pairs[0][1].shape[0]
    amount = len(pairs)

    def kernel(*refs):
        total = None
        for index in range(amount):
            part = dot_nt(refs[2 * index][...], refs[2 * index + 1][...])
            total = part if total is None else total + part
        refs[-1][...] = total.astype(BF)

    specs, operands, width = [], [], 0
    for x, w, where in pairs:
        specs.append(whole_spec(x.shape))
        specs.append(pl.BlockSpec((TILE, x.shape[1]), functools.partial(lambda where, i: (i, where), where)))
        operands += [x, w]
        width += x.shape[1]
    return pl.pallas_call(
        kernel,
        grid=(n // TILE,),
        out_shape=jax.ShapeDtypeStruct((m, n), BF),
        in_specs=specs,
        out_specs=pl.BlockSpec((m, TILE), lambda i: (0, i)),
        compiler_params=pltpu.CompilerParams(vmem_limit_bytes=VMEM),
        cost_estimate=cost(2 * m * n * width, 2 * (m * width + n * width + m * n)),
        name=name,
    )(*operands)


def turned(block, cosine, sine, back):
    other = pltpu.roll(block, E // 2, 1)
    if back:
        return block * cosine - other * sine
    return block * cosine + other * sine


def project(x, w, cosine, sine, heads):
    m, k = x.shape
    per = TILE // E
    steps = 3 * heads // per
    rotated = 2 * heads // per

    def kernel(x_ref, w_ref, c_ref, s_ref, o_ref):
        step = pl.program_id(0)
        made = dot_nn(x_ref[...], w_ref[...])

        @pl.when(step < rotated)
        def _():
            for part in range(per):
                piece = slice(part * E, (part + 1) * E)
                o_ref[:, piece] = turned(made[:, piece], c_ref[...], s_ref[...], False).astype(BF)

        @pl.when(step >= rotated)
        def _():
            o_ref[...] = made.astype(BF)

    return pl.pallas_call(
        kernel,
        grid=(steps,),
        out_shape=jax.ShapeDtypeStruct((m, steps * TILE), BF),
        in_specs=[
            whole_spec((m, k)),
            pl.BlockSpec((k, TILE), lambda i: (0, i)),
            whole_spec((m, E)),
            whole_spec((m, E)),
        ],
        out_specs=pl.BlockSpec((m, TILE), lambda i: (0, i)),
        compiler_params=pltpu.CompilerParams(vmem_limit_bytes=VMEM),
        cost_estimate=cost(2 * m * k * steps * TILE, 2 * (m * k + (m + k) * steps * TILE)),
        name="project",
    )(x, w, cosine, sine)


def attend(qkv, near, far, places, heads):
    m = qkv.shape[0]
    blocks = m // QB
    factor = E ** (-0.5) * LOG2E

    def kernel(q_ref, k0, v0, k1, v1, k2, v2, p_ref, o_ref, probs_ref, bias):
        @pl.when(pl.program_id(0) == 0)
        def _():
            for block in range(blocks):
                key = lax.broadcasted_iota(jnp.int32, (KB, QB), 0) + block * QB
                query = lax.broadcasted_iota(jnp.int32, (KB, QB), 1) + block * QB
                place = p_ref[:, block * QB : (block + 1) * QB]
                allowed = (key <= query + WINDOW) & (key > query) & (key >= query + WINDOW - place)
                bias[block] = jnp.where(allowed, 0.0, -1e30)

        keys = jnp.concatenate([k2[...], k1[...], k0[...]], axis=0)
        values = jnp.concatenate([v2[...], v1[...], v0[...]], axis=0)
        values_t = values.T
        for block in range(blocks):
            span = slice(block * QB, block * QB + KB)
            scores = dot_nt(keys[span], q_ref[block * QB : (block + 1) * QB, :]) * factor + bias[block]
            largest = jnp.max(scores, axis=0, keepdims=True)
            grown = jnp.exp2(scores - largest)
            inverse = 1.0 / jnp.sum(grown, axis=0, keepdims=True)
            probs = (grown * inverse).astype(BF)
            probs_ref[0, block] = probs
            mixed_t = dot_nn(values_t[:, span], probs)
            o_ref[block * QB : (block + 1) * QB, :] = mixed_t.T.astype(BF)

    def head(offset):
        return pl.BlockSpec((m, E), lambda i: (0, i + offset))

    return pl.pallas_call(
        kernel,
        grid=(heads,),
        out_shape=[
            jax.ShapeDtypeStruct((m, heads * E), BF),
            jax.ShapeDtypeStruct((heads, blocks, KB, QB), BF),
        ],
        in_specs=[head(0), head(heads), head(2 * heads), head(0), head(heads), head(0), head(heads), whole_spec((1, m))],
        out_specs=[head(0), pl.BlockSpec((1, blocks, KB, QB), lambda i: (i, 0, 0, 0))],
        scratch_shapes=[pltpu.VMEM((blocks, KB, QB), F32)],
        compiler_params=pltpu.CompilerParams(vmem_limit_bytes=VMEM),
        cost_estimate=cost(4 * heads * m * KB * E * 2, 2 * heads * m * KB, heads * m * KB),
        name="attend",
    )(qkv, qkv, qkv, near, near, far, far, places)


def attend_back(qkv, near, far, probs, d_mixed, cosine, sine, heads):
    m = qkv.shape[0]
    blocks = m // QB
    factor = E ** (-0.5)
    reach = WINDOW + m

    def kernel(q_ref, k0, v0, k1, v1, k2, v2, p_ref, g_ref, c_ref, s_ref, dq_ref, dk0, dv0, dk1, dv1, dk2, dv2, keys_sum, values_sum):
        keys = jnp.concatenate([k2[...], k1[...], k0[...]], axis=0)
        values = jnp.concatenate([v2[...], v1[...], v0[...]], axis=0)
        keys_t = keys.T
        keys_sum[...] = jnp.zeros_like(keys_sum)
        values_sum[...] = jnp.zeros_like(values_sum)
        for block in range(blocks):
            span = slice(block * QB, block * QB + KB)
            here = slice(block * QB, (block + 1) * QB)
            low = p_ref[0, block]
            grad = g_ref[here, :]
            d_probs = dot_nt(values[span], grad)
            weighted = low.astype(F32) * d_probs
            total = jnp.sum(weighted, axis=0, keepdims=True)
            d_scores = (weighted - low.astype(F32) * total).astype(BF)
            values_sum[span, :] += dot_nn(low, grad)
            keys_sum[span, :] += dot_nn(d_scores, q_ref[here, :])
            d_query = dot_nn(keys_t[:, span], d_scores).T * factor
            dq_ref[here, :] = turned(d_query, c_ref[here, :], s_ref[here, :], True).astype(BF)
        for index, (dk, dv) in enumerate(((dk2, dv2), (dk1, dv1), (dk0, dv0))):
            rows = slice(index * m, (index + 1) * m)
            dk[...] = (keys_sum[rows, :] * factor).astype(BF)
            dv[...] = values_sum[rows, :].astype(BF)

    def head(offset):
        return pl.BlockSpec((m, E), lambda i: (0, i + offset))

    low = jax.ShapeDtypeStruct((m, heads * E), BF)
    return pl.pallas_call(
        kernel,
        grid=(heads,),
        out_shape=[low] * 7,
        in_specs=[
            head(0), head(heads), head(2 * heads), head(0), head(heads), head(0), head(heads),
            pl.BlockSpec((1, blocks, KB, QB), lambda i: (i, 0, 0, 0)),
            head(0),
            whole_spec((m, E)),
            whole_spec((m, E)),
        ],
        out_specs=[head(0)] * 7,
        scratch_shapes=[pltpu.VMEM((reach, E), F32), pltpu.VMEM((reach, E), F32)],
        compiler_params=pltpu.CompilerParams(vmem_limit_bytes=VMEM),
        cost_estimate=cost(8 * heads * m * KB * E * 2, 2 * heads * m * KB),
        name="attend_back",
    )(qkv, qkv, qkv, near, near, far, far, probs, d_mixed, cosine, sine)


def feed(x, dy, w, tiles):
    m, k = x.shape

    def kernel(x_ref, dy_ref, g_ref, u_ref, d_ref, act_ref, dg_ref, du_ref):
        gate = dot_nn(x_ref[...], g_ref[...])
        up = dot_nn(x_ref[...], u_ref[...])
        d_act = dot_nn(dy_ref[...], d_ref[...])
        soft = 1.0 / (1.0 + jnp.exp(-gate))
        silu = gate * soft
        act_ref[...] = (silu * up).astype(BF)
        dg_ref[...] = (d_act * up * (soft * (1.0 + gate * (1.0 - soft)))).astype(BF)
        du_ref[...] = (d_act * silu).astype(BF)

    tile = pl.BlockSpec((m, TILE), lambda i: (0, i))
    return pl.pallas_call(
        kernel,
        grid=(tiles,),
        out_shape=[jax.ShapeDtypeStruct((m, tiles * TILE), BF)] * 3,
        in_specs=[
            whole_spec((m, k)),
            whole_spec((m, k)),
            pl.BlockSpec((k, TILE), lambda i: (0, i)),
            pl.BlockSpec((k, TILE), lambda i: (0, i + tiles)),
            pl.BlockSpec((k, TILE), lambda i: (0, i + 2 * tiles)),
        ],
        out_specs=[tile] * 3,
        compiler_params=pltpu.CompilerParams(vmem_limit_bytes=VMEM),
        cost_estimate=cost(6 * m * k * tiles * TILE, 6 * (m + k) * tiles * TILE, m * tiles * TILE),
        name="feed",
    )(x, dy, w, w, w)


def norm_root(rows):
    return lax.rsqrt(jnp.mean(rows * rows, axis=-1, keepdims=True) + EPS)


def norm_back(rows, root, gain, grad):
    pushed = grad * gain
    inner = jnp.mean(pushed * rows, axis=-1, keepdims=True)
    d_rows = root * pushed - rows * (root * root * root * inner)
    return d_rows, jnp.sum(grad * rows * root, axis=0)


def pair_sum(part, route):
    return part.astype(F32) + lax.ppermute(part, "tensor", route).astype(F32)


def shards(tokens, positions, attn_gain, w_query, w_key, w_value, w_out, ffn_gain, w_gate, w_up, w_down, cotangent):
    devices = lax.axis_size("dp")
    core = lax.axis_index("dp") % 2
    sides = lax.axis_size("tensor")
    flip = [(i, (i + 1) % sides) for i in range(sides)]
    span = tokens.shape[0]
    own_rows = w_query.shape[0]
    width = tokens.shape[1]
    head_columns = w_query.shape[1]
    heads = head_columns // E
    hidden_units = w_gate.shape[1]
    tiles = (hidden_units + TILE - 1) // TILE
    padded = tiles * TILE

    attn_pack = jnp.concatenate([w_query, w_key, w_value, w_out.T], axis=1)
    lanes = max(128, own_rows)
    gains = jnp.zeros((32, lanes), BF).at[0, :own_rows].set(attn_gain).at[16, :own_rows].set(ffn_gain)
    w_attn, all_gains = ring_gather((attn_pack, gains), (2, 1), 0)

    def wide(matrix):
        return jnp.pad(matrix, ((0, 0), (0, padded - hidden_units)))

    ffn_pack = jnp.concatenate([wide(w_gate), wide(w_up), wide(w_down.T)], axis=1)
    w_attn, all_gains, ffn_pack = lax.optimization_barrier((w_attn, all_gains, ffn_pack))
    w_ffn = lax.all_gather(ffn_pack, "dp", axis=0, tiled=True)
    all_gains = all_gains.reshape(devices, 32, lanes)
    gain_attn = all_gains[:, 0, :own_rows].reshape(1, width).astype(F32)
    gain_ffn = all_gains[:, 16, :own_rows].reshape(1, width).astype(F32)

    frequency = THETA ** (-(jnp.arange(E // 2, dtype=F32) * 2.0 / E))
    angles = positions.astype(F32)[:, None] * frequency[None, :]
    cosine_half, sine_half = jnp.cos(angles), jnp.sin(angles)
    cosine = jnp.concatenate([cosine_half, cosine_half], axis=1)
    sine = jnp.concatenate([-sine_half, sine_half], axis=1)

    rows = tokens.astype(F32)
    root_attn = norm_root(rows)
    normed_attn = (rows * root_attn * gain_attn).astype(BF)
    qkv = project(normed_attn, w_attn, cosine, sine, heads)
    own_kv = qkv[:, head_columns:]
    far = lax.ppermute(own_kv, "dp", [(i - 2, i) for i in range(2, devices)])
    near = lax.ppermute(jnp.where(core == 0, own_kv, far), "dp", swap_route(devices))
    mixed, probs = attend(qkv, near, far, positions[None, :], heads)
    hidden = rows + pair_sum(matmul_nt([(mixed, w_attn, 3)], "out_project"), flip)

    root_ffn = norm_root(hidden)
    normed_ffn = (hidden * root_ffn * gain_ffn).astype(BF)
    activated, d_gate, d_up = feed(normed_ffn, cotangent, w_ffn, tiles)
    down_grad = ring_scatter(matmul_nn(cotangent.T, activated, 0, tiles, "down_grad"))
    normed_ffn_t = normed_ffn.T
    gate_grad = ring_scatter(matmul_nn(normed_ffn_t, d_gate, 0, tiles, "gate_grad"))
    up_grad = ring_scatter(matmul_nn(normed_ffn_t, d_up, 0, tiles, "up_grad"))
    d_normed_ffn = pair_sum(matmul_nt([(d_gate, w_ffn, 0), (d_up, w_ffn, 1)], "ffn_back"), flip)
    d_hidden_norm, gain_ffn_grad = norm_back(hidden, root_ffn, gain_ffn, d_normed_ffn)
    d_hidden = cotangent.astype(F32) + d_hidden_norm
    d_hidden_low = d_hidden.astype(BF)
    layer_out = (hidden + pair_sum(matmul_nt([(activated, w_ffn, 2)], "down_project"), flip)).astype(BF)

    d_mixed = matmul_nn(d_hidden_low, w_attn, 3 * head_columns // TILE, head_columns // TILE, "out_back")
    out_part = matmul_nn(d_hidden_low.T, mixed, 0, head_columns // TILE, "out_grad")
    d_query, dk0, dv0, dk1, dv1, dk2, dv2 = attend_back(qkv, near, far, probs, d_mixed, cosine, sine, heads)
    near_sum = lax.ppermute(jnp.concatenate([dk1, dv1], axis=1), "dp", swap_route(devices)).astype(F32)
    far_part = jnp.concatenate([dk2, dv2], axis=1)
    far_part = (far_part.astype(F32) + jnp.where(core == 1, near_sum, 0.0)).astype(BF)
    far_sum = lax.ppermute(far_part, "dp", [(i, i - 2) for i in range(2, devices)]).astype(F32)
    d_kv = jnp.concatenate([dk0, dv0], axis=1).astype(F32) + jnp.where(core == 0, near_sum, 0.0) + far_sum
    d_key = d_kv[:, :head_columns].reshape(span, heads, E)
    d_key = d_key * cosine[:, None, :] - jnp.roll(d_key, E // 2, axis=2) * sine[:, None, :]
    d_qkv = jnp.concatenate([d_query, d_key.reshape(span, head_columns).astype(BF), d_kv[:, head_columns:].astype(BF)], axis=1)
    normed_attn_t = normed_attn.T
    qkv_part = matmul_nn(normed_attn_t, d_qkv, 0, 3 * head_columns // TILE, "qkv_grad")
    attn_grads = ring_scatter(jnp.concatenate([qkv_part, out_part], axis=1))
    d_normed_attn = pair_sum(matmul_nt([(d_qkv, w_attn, 0)], "qkv_back"), flip)
    d_rows, gain_attn_grad = norm_back(rows, root_attn, gain_attn, d_normed_attn)
    tokens_grad = d_hidden + d_rows
    gain_sums = lax.psum_scatter(
        jnp.stack([gain_attn_grad.reshape(devices, own_rows), gain_ffn_grad.reshape(devices, own_rows)], axis=1),
        "dp", scatter_dimension=0, tiled=False,
    )
    return (
        layer_out,
        tokens_grad,
        gain_sums[0],
        attn_grads[:, :head_columns],
        attn_grads[:, head_columns : 2 * head_columns],
        attn_grads[:, 2 * head_columns : 3 * head_columns],
        attn_grads[:, 3 * head_columns :].T,
        gain_sums[1],
        gate_grad[:, :hidden_units],
        up_grad[:, :hidden_units],
        down_grad[:, :hidden_units].T,
    )


def solution(mesh):
    by_rows, by_both, turned_both, line = P("dp", None), P("dp", "tensor"), P("tensor", "dp"), P("dp")
    return jax.shard_map(
        shards,
        mesh=mesh,
        in_specs=(by_rows, line, line, by_both, by_both, by_both, turned_both, line, by_both, by_both, turned_both, by_rows),
        out_specs=(by_rows, by_rows, line, by_both, by_both, by_both, turned_both, line, by_both, by_both, turned_both),
        check_vma=False,
    )
```

time: 2390 us -> 977 us (0.41)
  waiting for transfers between devices: 1850 us -> 324 us
  Pallas kernels: 0 us -> 290 us
  matrix products: 285 us -> 0 us
  blocking collectives: 133 us -> 57.6 us
  other arithmetic: 48.2 us -> 122 us
  local copies, waits for them, and re-layouts: 34.8 us -> 90 us
  starting transfers between devices: 16.7 us -> 67.8 us
    reduce_scatter x7 -> x0, waiting for transfers between devices: 1040 us -> none  [the longest x1 227 us: shards(): lax.psum_scatter(gate_grad, 'dp', scatter_dimension=0, tiled=True)]
    all_gather x7 -> x1, waiting for transfers between devices: 382 us -> 0.01 us  [shards(): w_ffn = lax.all_gather(ffn_pack, 'dp', axis=0, tiled=True)]
    pallas_call x0 -> x15, Pallas kernels: none -> 290 us  [the longest x1 88 us: ring_gather(): pl.pallas_call(functools.partial(gather_kernel, devices, chunks, len(arra...]
    dot_general x77 -> x0, matrix products: 285 us -> none  [the longest x31 99.8 us: contract_cols(): lax.dot_general(left, right, (((1,), (1,)), ((), ())), preferred_element_...]
    psum x4 -> x0, waiting for transfers between devices: 281 us -> none  [the longest x1 95.3 us: shards(): lax.psum(contract_cols(d_gate_low, gate_proj) + contract_cols(d_up_low, u...]
    ppermute x8 -> x68, waiting for transfers between devices: 138 us -> 324 us  [the longest x28 132 us: ring_scatter(): to_right = lax.ppermute(to_right, 'dp', ring_route(chips, 1))]
    all_gather x2 -> x0, blocking collectives: 69.9 us -> none  [the longest x1 46.8 us: shards(): lax.all_gather(ffn_gain, 'dp', axis=0, tiled=True)]
    convert_element_type x14 -> x35, other arithmetic: 5.16 us -> 60.5 us  [the longest x24 43.2 us: ring_scatter(): to_right, to_left = (to_right.astype(BF), to_left.astype(BF))]
  transfers between devices with their start and end apart: 26 -> 69, of which waited for: 20 -> 37; matrix products, arithmetic and copies ran while one was open for 9% -> 20% of each run, Pallas kernels for 0% -> 16%
where the time goes in v1:
time: 977 us; the launch traced here: 967 us
  waiting for transfers between devices  324 us (33%)
  Pallas kernels  290 us (30%)
  other arithmetic  122 us (12%)
  local copies, waits for them, and re-layouts  90 us (9%)
  starting transfers between devices  67.8 us (7%)
  blocking collectives  57.6 us (6%)
  between operations  15 us (2%)
    ppermute x28, waiting for transfers between devices, ring_scatter(): to_right = lax.ppermute(to_right, 'dp', ring_route(chips, 1))  132 us
    ppermute x1, waiting for transfers between devices, shards(): far = lax.ppermute(own_kv, 'dp', [(i - 2, i) for i in range(2, devices)])  89.6 us
    pallas_call x1, Pallas kernels, ring_gather(): pl.pallas_call(functools.partial(gather_kernel, devices, chunks, len(arra...  88 us
    pallas_call x6, Pallas kernels, matmul_nn(): pl.pallas_call(kernel, grid=(count,), out_shape=jax.ShapeDtypeStruct((m,...  66.1 us
    unnamed x1, blocking collectives  57.6 us
    ppermute x28, waiting for transfers between devices, ring_scatter(): to_left = lax.ppermute(to_left, 'dp', ring_route(chips, -1))  55.4 us
    pallas_call x4, Pallas kernels, matmul_nt(): pl.pallas_call(kernel, grid=(n // TILE,), out_shape=jax.ShapeDtypeStruct(...  52.2 us
    convert_element_type x24, other arithmetic, ring_scatter(): to_right, to_left = (to_right.astype(BF), to_left.astype(BF))  43.2 us
  transfers between devices with their start and end apart: 69, of which 37 were waited for; matrix products, arithmetic and copies ran while one was open for 20% of the time, Pallas kernels for 16%

profile of v1, /device:TPU:0, one launch (start us, length us, event | category | flops | bytes accessed | tf_op | source)
XLA Modules:
  0.0 966.6 jit_solution(4967854347047884210)
XLA Ops:
  13.7 88.0 %ring_gather.1 = (bf16[2048,4096]{1,0:T(8,128)(2,1)}, bf16[512,128]{1,0:T(8,128)(2,1)}) custom-call(bf16[128,4096]{1,0:T(8,128)(2,1)} %pad_maximum_fusion.6.refs_0_, bf16[32,128]{1,0:T(8,128)(2,1)} %copy-done.28), custom_call_target="tpu_custom_call" | custom-call | tf_op jit(solution)/shard_map/ring_gather/pallas_call | solution.py:162
  116.0 15.8 %project.1.q_ref.k0.v0 = bf16[512,3072]{1,0:T(8,128)(2,1)} custom-call(bf16[512,2048]{1,0:T(8,128)(2,1)} %copy.119.x_ref, bf16[2048,4096]{1,0:T(8,128)(2,1)} %get-tuple-element.55.w_ref.refs_1_, f32[512,128]{1,0:T(8,128)} %get-tuple-element.176.c_ref, f32[512,128]{1,0:T(8,128)} %get-tuple-element.177.s_ref), custom_call_target="tpu_custom_call" | custom-call | flops 6442450944 | bytes 17825792 | tf_op jit(solution)/shard_map/project/pallas_call | solution.py:294
  139.9 89.6 %collective-permute-done.k2.v2 = bf16[512,2048]{1,0:T(8,128)(2,1)} collective-permute-done((bf16[512,2048]{1,0:T(8,128)(2,1)}, bf16[512,2048]{1,0:T(8,128)(2,1)}, u32[]{:S(2)}, u32[]{:S(2)}) %collective-permute-start) | collective-permute-done | bytes 2097184 | tf_op jit(solution)/shard_map/ppermute | solution.py:499
  237.1 21.0 %attend.1 = (bf16[512,1024]{1,0:T(8,128)(2,1)}, bf16[8,2,1280,256]{3,2,1,0:T(8,128)(2,1)}) custom-call(bf16[512,3072]{1,0:T(8,128)(2,1)} %project.1.q_ref.k0.v0, bf16[512,3072]{1,0:T(8,128)(2,1)} %project.1.q_ref.k0.v0, bf16[512,3072]{1,0:T(8,128)(2,1)} %project.1.q_ref.k0.v0, bf16[512,2048]{1,0:T(8,128)(2,1)} %copy-done.37, bf16[512,2048]{1,0:T(8,128)(2,1)} %copy-done.37, ...), custom_call_target="tpu_custom_call" | custom-call | flops 5368709120 | bytes 10485760 | tf_op jit(solution)/shard_map/attend/pallas_call | solution.py:343
  258.1 8.2 out_project.1
  275.7 42.6 %collective-permute-done.2 = bf16[512,2048]{0,1:T(8,128)(2,1)} collective-permute-done((bf16[512,2048]{0,1:T(8,128)(2,1)}, bf16[512,2048]{0,1:T(8,128)(2,1)}, u32[]{:S(2)}, u32[]{:S(2)}) %collective-permute-start.2) | collective-permute-done | bytes 2097184 | tf_op jit(solution)/shard_map/ppermute | solution.py:456
  333.2 26.5 %feed.1 = (bf16[512,2816]{1,0:T(8,128)(2,1)}, bf16[512,2816]{1,0:T(8,128)(2,1)}, bf16[512,2816]{1,0:T(8,128)(2,1)}) custom-call(bf16[512,2048]{1,0:T(8,128)(2,1)} %copy.122.x_ref, bf16[512,2048]{1,0:T(8,128)(2,1)} %dy_ref.1, bf16[2048,8448]{1,0:T(8,128)(2,1)} %all-gather.2.cloned.1.call-done.g_ref.u_ref.d_ref.refs_1_.refs_3_, ...), custom_call_target="tpu_custom_call" | custom-call | flops 17716740096 | bytes 43253760 | tf_op jit(solution)/shard_map/feed/pallas_call | solution.py:426
  359.7 18.6 %ffn_back.1 = bf16[512,2048]{1,0:T(8,128)(2,1)} custom-call(bf16[512,2816]{1,0:T(8,128)(2,1)} %get-tuple-element.59.refs_0_.w_ref, bf16[2048,8448]{1,0:T(8,128)(2,1)} %all-gather.2.cloned.1.call-done.g_ref.u_ref.d_ref.refs_1_.refs_3_, bf16[512,2816]{1,0:T(8,128)(2,1)} %get-tuple-element.60.refs_2_.w_ref, ...), custom_call_target="tpu_custom_call" | custom-call | flops 11811160064 | bytes 30932992 | tf_op jit(solution)/shard_map/ffn_back/pallas_call | solution.py:255
  383.9 13.1 %up_grad.1 = bf16[2048,2816]{1,0:T(8,128)(2,1)} custom-call(bf16[2048,512]{1,0:T(8,128)(2,1)} %fusion.143.x_ref, bf16[512,2816]{1,0:T(8,128)(2,1)} %get-tuple-element.60.refs_2_.w_ref), custom_call_target="tpu_custom_call" | custom-call | flops 5905580032 | bytes 16515072 | tf_op jit(solution)/shard_map/up_grad/pallas_call | solution.py:225
  402.4 13.1 %gate_grad.1 = bf16[2048,2816]{1,0:T(8,128)(2,1)} custom-call(bf16[2048,512]{1,0:T(8,128)(2,1)} %fusion.143.x_ref, bf16[512,2816]{1,0:T(8,128)(2,1)} %get-tuple-element.59.refs_0_.w_ref), custom_call_target="tpu_custom_call" | custom-call | flops 5905580032 | bytes 16515072 | tf_op jit(solution)/shard_map/gate_grad/pallas_call | solution.py:225
  421.5 13.1 %down_grad.1 = bf16[2048,2816]{1,0:T(8,128)(2,1)} custom-call(bf16[2048,512]{1,0:T(8,128)(2,1)} %bitcast.444, bf16[512,2816]{1,0:T(8,128)(2,1)} %get-tuple-element.58.refs_0_.w_ref), custom_call_target="tpu_custom_call" | custom-call | flops 5905580032 | bytes 16515072 | tf_op jit(solution)/shard_map/down_grad/pallas_call | solution.py:225
  455.4 20.3 %attend_back.1 = (bf16[512,1024]{1,0:T(8,128)(2,1)}, bf16[512,1024]{1,0:T(8,128)(2,1)}, bf16[512,1024]{1,0:T(8,128)(2,1)}, bf16[512,1024]{1,0:T(8,128)(2,1)}, bf...) custom-call(bf16[512,3072]{1,0:T(8,128)(2,1)} %project.1.q_ref.k0.v0, ...), custom_call_target="tpu_custom_call" | custom-call | flops 10737418240 | bytes 10485760 | tf_op jit(solution)/shard_map/attend_back/pallas_call | solution.py:393
  481.8 12.4 %down_project.1 = bf16[512,2048]{1,0:T(8,128)(2,1)} custom-call(bf16[512,2816]{1,0:T(8,128)(2,1)} %get-tuple-element.58.refs_0_.w_ref, bf16[2048,8448]{1,0:T(8,128)(2,1)} %all-gather.2.cloned.1.call-done.g_ref.u_ref.d_ref.refs_1_.refs_3_), custom_call_target="tpu_custom_call" | custom-call | flops 5905580032 | bytes 16515072 | tf_op jit(solution)/shard_map/down_project/pallas_call | solution.py:255
  519.7 46.1 %collective-permute-done.39 = bf16[64,2816]{1,0:T(8,128)(2,1)S(1)} collective-permute-done((bf16[64,2816]{1,0:T(8,128)(2,1)S(1)}, bf16[64,2816]{1,0:T(8,128)(2,1)S(1)}, u32[]{:S(2)}, u32[]{:S(2)}) %collective-permute-start.39) | collective-permute-done | bytes 360480 | tf_op jit(solution)/shard_map/ppermute | solution.py:202
  595.1 13.0 %qkv_back.1 = bf16[512,2048]{1,0:T(8,128)(2,1)} custom-call(bf16[512,3072]{1,0:T(8,128)(2,1)} %pad_maximum_fusion.1.refs_0_.w_ref, bf16[2048,4096]{1,0:T(8,128)(2,1)} %get-tuple-element.55.w_ref.refs_1_), custom_call_target="tpu_custom_call" | custom-call | flops 6442450944 | bytes 17825792 | tf_op jit(solution)/shard_map/qkv_back/pallas_call | solution.py:255
  612.0 14.3 %qkv_grad.1 = bf16[2048,3072]{1,0:T(8,128)(2,1)} custom-call(bf16[2048,512]{1,0:T(8,128)(2,1)} %fusion.144.x_ref, bf16[512,3072]{1,0:T(8,128)(2,1)} %pad_maximum_fusion.1.refs_0_.w_ref), custom_call_target="tpu_custom_call" | custom-call | flops 6442450944 | bytes 17825792 | tf_op jit(solution)/shard_map/qkv_grad/pallas_call | solution.py:225
  626.3 12.2 %pad_maximum_fusion = bf16[2048,4096]{1,0:T(8,128)(2,1)} fusion(bf16[2048,1024]{1,0:T(8,128)(2,1)S(1)} %copy-done.12, bf16[2048,3072]{1,0:T(8,128)(2,1)} %qkv_grad.1), kind=kLoop, calls=%fused_computation | loop fusion | flops 33554432 | bytes 33554432 | tf_op jit(solution)/shard_map/concatenate | solution.py:530
  638.5 7.9 dynamic-slice_bitcast_fusion
  724.4 7.1 collective-permute-done.28
  755.2 7.7 collective-permute-done.29
  777.3 10.9 %collective-permute-done.16 = bf16[64,4096]{1,0:T(8,128)(2,1)S(1)} collective-permute-done((bf16[64,4096]{1,0:T(8,128)(2,1)S(1)}, bf16[64,4096]{1,0:T(8,128)(2,1)S(1)}, u32[]{:S(2)}, u32[]{:S(2)}) %collective-permute-start.16) | collective-permute-done | bytes 524320 | tf_op jit(solution)/shard_map/ppermute | solution.py:203
  801.2 9.0 collective-permute-done.17
  823.3 7.9 collective-permute-done.18
  896.5 57.6 %all-reduce.4 = f32[16,2,128]{2,1,0:T(2,128)S(1)} all-reduce(f32[16,2,128]{2,1,0:T(2,128)S(1)} %pad_maximum_fusion.10), channel_id=2, replica_groups=mesh['dp'=16,'tensor'=2] {'dp'}, use_global_device_ids=true, to_apply=%region_6.7.clone | all-reduce | flops 4096 | bytes 32768
  (309 shorter events, 375.6 us)
Async XLA Ops:
  7.2 325.9 %all-gather.2.cloned.1.call-start = ((), (), s32[]{:S(2)}) async-start(), calls=%async_computation | async-start | bytes 36765696 | tf_op jit(solution)/shard_map/all_gather | solution.py:483
  135.0 94.5 %collective-permute-start = (bf16[512,2048]{1,0:T(8,128)(2,1)}, bf16[512,2048]{1,0:T(8,128)(2,1)}, u32[]{:S(2)}, u32[]{:S(2)}) collective-permute-start(bf16[512,2048]{1,0:T(8,128)(2,1)} %slice.99), channel_id=1, source_target_pairs={{0,4},{2,6},{4,8},{6,10},{8,12},{10,14},{12,16},{14,18},{16,20},{1... | collective-permute-start | bytes 6291464 | tf_op jit(solution)/shard_map/ppermute | solution.py:499
  270.2 48.1 %collective-permute-start.2 = (bf16[512,2048]{0,1:T(8,128)(2,1)}, bf16[512,2048]{0,1:T(8,128)(2,1)}, u32[]{:S(2)}, u32[]{:S(2)}) collective-permute-start(bf16[512,2048]{0,1:T(8,128)(2,1)} %copy.120), channel_id=1, source_target_pairs={{0,1},{1,0},{2,3},{3,2},{4,5},{5,4},{6,7},{7,6},{8,9},{9,8},{10,11... | collective-permute-start | bytes 6291464 | tf_op jit(solution)/shard_map/ppermute | solution.py:456
  382.3 58.0 %collective-permute-start.4 = (bf16[512,2048]{0,1:T(8,128)(2,1)}, bf16[512,2048]{0,1:T(8,128)(2,1)S(1)}, u32[]{:S(2)}, u32[]{:S(2)}) collective-permute-start(bf16[512,2048]{0,1:T(8,128)(2,1)} %copy.126), channel_id=1, source_target_pairs={{0,1},{1,0},{2,3},{3,2},{4,5},{5,4},{6,7},{7,6},{8,9},{9,8},{10,11... | collective-permute-start | bytes 6291464 | tf_op jit(solution)/shard_map/ppermute | solution.py:456
  402.4 106.4 %collective-permute-start.38 = (bf16[8,128,2816]{2,1,0:T(8,128)(2,1)}, bf16[8,128,2816]{2,1,0:T(8,128)(2,1)}, u32[]{:S(2)}, u32[]{:S(2)}) collective-permute-start(bf16[8,128,2816]{2,1,0:T(8,128)(2,1)} %dynamic-slice_bitcast_fusion.2), channel_id=1, source_target_pairs={{0,2},{2,0},{4,6},{6,4},{8,10},{10,8},{12,14},{14,12},{16,18},{18,... | collective-permute-start | bytes 17301512 | tf_op jit(solution)/shard_map/ppermute | solution.py:191
  421.0 93.7 %collective-permute-start.23 = (bf16[8,128,2816]{2,1,0:T(8,128)(2,1)}, bf16[8,128,2816]{2,1,0:T(8,128)(2,1)}, u32[]{:S(2)}, u32[]{:S(2)}) collective-permute-start(bf16[8,128,2816]{2,1,0:T(8,128)(2,1)} %dynamic-slice_bitcast_fusion.3), channel_id=1, source_target_pairs={{0,2},{2,0},{4,6},{6,4},{8,10},{10,8},{12,14},{14,12},{16,18},{18,... | collective-permute-start | bytes 17301512 | tf_op jit(solution)/shard_map/ppermute | solution.py:191
  440.2 75.9 %collective-permute-start.53 = (bf16[8,128,2816]{2,1,0:T(8,128)(2,1)}, bf16[8,128,2816]{2,1,0:T(8,128)(2,1)}, u32[]{:S(2)}, u32[]{:S(2)}) collective-permute-start(bf16[8,128,2816]{2,1,0:T(8,128)(2,1)} %dynamic-slice_bitcast_fusion.1), channel_id=1, source_target_pairs={{0,2},{2,0},{4,6},{6,4},{8,10},{10,8},{12,14},{14,12},{16,18},{18,... | collective-permute-start | bytes 17301512 | tf_op jit(solution)/shard_map/ppermute | solution.py:191
  478.8 26.1 %collective-permute-start.5 = (bf16[512,2048]{1,0:T(8,128)(2,1)}, bf16[512,2048]{1,0:T(8,128)(2,1)}, u32[]{:S(2)}, u32[]{:S(2)}) collective-permute-start(bf16[512,2048]{1,0:T(8,128)(2,1)} %pad_maximum_fusion.2), channel_id=1, source_target_pairs={{0,2},{2,0},{4,6},{6,4},{8,10},{10,8},{12,14},{14,12},{16,18},{18,... | collective-permute-start | bytes 6291464 | tf_op jit(solution)/shard_map/ppermute | solution.py:520
  498.1 383.7 %collective-permute-start.3 = (bf16[512,2048]{0,1:T(8,128)(2,1)}, bf16[512,2048]{0,1:T(8,128)(2,1)}, u32[]{:S(2)}, u32[]{:S(2)}) collective-permute-start(bf16[512,2048]{0,1:T(8,128)(2,1)} %copy.123), channel_id=1, source_target_pairs={{0,1},{1,0},{2,3},{3,2},{4,5},{5,4},{6,7},{7,6},{8,9},{9,8},{10,11... | collective-permute-start | bytes 6291464 | tf_op jit(solution)/shard_map/ppermute | solution.py:456
  507.4 78.6 %collective-permute-start.6 = (bf16[512,2048]{1,0:T(8,128)(2,1)S(1)}, bf16[512,2048]{1,0:T(8,128)(2,1)S(1)}, u32[]{:S(2)}, u32[]{:S(2)}) collective-permute-start(bf16[512,2048]{1,0:T(8,128)(2,1)S(1)} %fusion.7), channel_id=1, source_target_pairs={{4,0},{6,2},{8,4},{10,6},{12,8},{14,10},{16,12},{18,14},{20,16},{2... | collective-permute-start | bytes 6291464 | tf_op jit(solution)/shard_map/ppermute | solution.py:523
  510.2 55.6 %collective-permute-start.39 = (bf16[64,2816]{1,0:T(8,128)(2,1)S(1)}, bf16[64,2816]{1,0:T(8,128)(2,1)S(1)}, u32[]{:S(2)}, u32[]{:S(2)}) collective-permute-start(bf16[64,2816]{1,0:T(8,128)(2,1)S(1)} %get-tuple-element.143), channel_id=1, source_target_pairs={{0,8},{2,10},{8,16},{10,18},{16,24},{18,26},{24,28},{26,30},{28,20... | collective-permute-start | bytes 1081352 | tf_op jit(solution)/shard_map/ppermute | solution.py:202
  514.7 51.4 %collective-permute-start.46 = (bf16[64,2816]{1,0:T(8,128)(2,1)S(1)}, bf16[64,2816]{1,0:T(8,128)(2,1)S(1)}, u32[]{:S(2)}, u32[]{:S(2)}) collective-permute-start(bf16[64,2816]{1,0:T(8,128)(2,1)S(1)} %get-tuple-element.144), channel_id=1, source_target_pairs={{0,4},{2,6},{8,0},{10,2},{16,8},{18,10},{24,16},{26,18},{28,24},{3... | collective-permute-start | bytes 1081352 | tf_op jit(solution)/shard_map/ppermute | solution.py:203
  516.2 57.4 %collective-permute-start.24 = (bf16[64,2816]{1,0:T(8,128)(2,1)S(1)}, bf16[64,2816]{1,0:T(8,128)(2,1)S(1)}, u32[]{:S(2)}, u32[]{:S(2)}) collective-permute-start(bf16[64,2816]{1,0:T(8,128)(2,1)S(1)} %get-tuple-element.159), channel_id=1, source_target_pairs={{0,8},{2,10},{8,16},{10,18},{16,24},{18,26},{24,28},{26,30},{28,20... | collective-permute-start | bytes 1081352 | tf_op jit(solution)/shard_map/ppermute | solution.py:202
  574.3 72.1 %collective-permute-start.40 = (bf16[64,2816]{1,0:T(8,128)(2,1)S(1)}, bf16[64,2816]{1,0:T(8,128)(2,1)}, u32[]{:S(2)}, u32[]{:S(2)}) collective-permute-start(bf16[64,2816]{1,0:T(8,128)(2,1)S(1)} %get-tuple-element.141), channel_id=1, source_target_pairs={{0,8},{2,10},{8,16},{10,18},{16,24},{18,26},{24,28},{26,30},{28,20... | collective-permute-start | bytes 1081352 | tf_op jit(solution)/shard_map/ppermute | solution.py:202
  581.3 66.8 %collective-permute-start.47 = (bf16[64,2816]{1,0:T(8,128)(2,1)S(1)}, bf16[64,2816]{1,0:T(8,128)(2,1)}, u32[]{:S(2)}, u32[]{:S(2)}) collective-permute-start(bf16[64,2816]{1,0:T(8,128)(2,1)S(1)} %get-tuple-element.142), channel_id=1, source_target_pairs={{0,4},{2,6},{8,0},{10,2},{16,8},{18,10},{24,16},{26,18},{28,24},{3... | collective-permute-start | bytes 1081352 | tf_op jit(solution)/shard_map/ppermute | solution.py:203
  582.0 68.2 %collective-permute-start.25 = (bf16[64,2816]{1,0:T(8,128)(2,1)}, bf16[64,2816]{1,0:T(8,128)(2,1)}, u32[]{:S(2)}, u32[]{:S(2)}) collective-permute-start(bf16[64,2816]{1,0:T(8,128)(2,1)} %get-tuple-element.157), channel_id=1, source_target_pairs={{0,8},{2,10},{8,16},{10,18},{16,24},{18,26},{24,28},{26,30},{28,20... | collective-permute-start | bytes 1081352 | tf_op jit(solution)/shard_map/ppermute | solution.py:202
  586.1 65.8 %collective-permute-start.32 = (bf16[64,2816]{1,0:T(8,128)(2,1)S(1)}, bf16[64,2816]{1,0:T(8,128)(2,1)}, u32[]{:S(2)}, u32[]{:S(2)}) collective-permute-start(bf16[64,2816]{1,0:T(8,128)(2,1)S(1)} %get-tuple-element.158), channel_id=1, source_target_pairs={{0,4},{2,6},{8,0},{10,2},{16,8},{18,10},{24,16},{26,18},{28,24},{3... | collective-permute-start | bytes 1081352 | tf_op jit(solution)/shard_map/ppermute | solution.py:203
  650.2 218.1 %collective-permute-start.7 = (bf16[512,2048]{0,1:T(8,128)(2,1)}, bf16[512,2048]{0,1:T(8,128)(2,1)}, u32[]{:S(2)}, u32[]{:S(2)}) collective-permute-start(bf16[512,2048]{0,1:T(8,128)(2,1)} %copy.129), channel_id=1, source_target_pairs={{0,1},{1,0},{2,3},{3,2},{4,5},{5,4},{6,7},{7,6},{8,9},{9,8},{10,11... | collective-permute-start | bytes 6291464 | tf_op jit(solution)/shard_map/ppermute | solution.py:456
  651.9 114.7 %collective-permute-start.8 = (bf16[8,128,4096]{2,1,0:T(8,128)(2,1)}, bf16[8,128,4096]{2,1,0:T(8,128)(2,1)S(1)}, u32[]{:S(2)}, u32[]{:S(2)}) collective-permute-start(bf16[8,128,4096]{2,1,0:T(8,128)(2,1)} %dynamic-slice_bitcast_fusion), channel_id=1, source_target_pairs={{0,2},{2,0},{4,6},{6,4},{8,10},{10,8},{12,14},{14,12},{16,18},{18,... | collective-permute-start | bytes 25165832 | tf_op jit(solution)/shard_map/ppermute | solution.py:191
  766.6 25.9 %collective-permute-start.45 = (bf16[64,2816]{1,0:T(8,128)(2,1)S(1)}, bf16[64,2816]{1,0:T(8,128)(2,1)S(1)}, u32[]{:S(2)}, u32[]{:S(2)}) collective-permute-start(bf16[64,2816]{1,0:T(8,128)(2,1)S(1)} %get-tuple-element.131), channel_id=1, source_target_pairs={{0,8},{2,10},{8,16},{10,18},{16,24},{18,26},{24,28},{26,30},{28,20... | collective-permute-start | bytes 1081352 | tf_op jit(solution)/shard_map/ppermute | solution.py:202
  790.5 24.5 %collective-permute-start.30 = (bf16[64,2816]{1,0:T(8,128)(2,1)S(1)}, bf16[64,2816]{1,0:T(8,128)(2,1)S(1)}, u32[]{:S(2)}, u32[]{:S(2)}) collective-permute-start(bf16[64,2816]{1,0:T(8,128)(2,1)S(1)} %get-tuple-element.147), channel_id=1, source_target_pairs={{0,8},{2,10},{8,16},{10,18},{16,24},{18,26},{24,28},{26,30},{28,20... | collective-permute-start | bytes 1081352 | tf_op jit(solution)/shard_map/ppermute | solution.py:202
  813.0 20.7 %collective-permute-start.60 = (bf16[64,2816]{1,0:T(8,128)(2,1)S(1)}, bf16[64,2816]{1,0:T(8,128)(2,1)S(1)}, u32[]{:S(2)}, u32[]{:S(2)}) collective-permute-start(bf16[64,2816]{1,0:T(8,128)(2,1)S(1)} %get-tuple-element.115), channel_id=1, source_target_pairs={{0,8},{2,10},{8,16},{10,18},{16,24},{18,26},{24,28},{26,30},{28,20... | collective-permute-start | bytes 1081352 | tf_op jit(solution)/shard_map/ppermute | solution.py:202
  879.6 75.7 %collective-permute-start.22 = (bf16[64,4096]{1,0:T(8,128)(2,1)}, bf16[64,4096]{1,0:T(8,128)(2,1)S(1)}, u32[]{:S(2)}, u32[]{:S(2)}) collective-permute-start(bf16[64,4096]{1,0:T(8,128)(2,1)} %get-tuple-element.99), channel_id=1, source_target_pairs={{0,4},{2,6},{8,0},{10,2},{16,8},{18,10},{24,16},{26,18},{28,24},{3... | collective-permute-start | bytes 1572872 | tf_op jit(solution)/shard_map/ppermute | solution.py:203
  880.0 75.3 %collective-permute-start.15 = (bf16[64,4096]{1,0:T(8,128)(2,1)S(1)}, bf16[64,4096]{1,0:T(8,128)(2,1)}, u32[]{:S(2)}, u32[]{:S(2)}) collective-permute-start(bf16[64,4096]{1,0:T(8,128)(2,1)S(1)} %get-tuple-element.100), channel_id=1, source_target_pairs={{0,8},{2,10},{8,16},{10,18},{16,24},{18,26},{24,28},{26,30},{28,20... | collective-permute-start | bytes 1572872 | tf_op jit(solution)/shard_map/ppermute | solution.py:202
  (84 other events, 1413.7 us)
Sparse Core Ops, SparseCore 0:
  103.3 213.9 all-gather.1

commit v2 on v1

--- a/solution.py
+++ b/solution.py
@@ -39,15 +39,6 @@
     column = lax.rem(chip, 2)
     row = chip // 2
     return (1 - column) * row + column * (chips - 1 - row)
-
-
-def ring_route(chips, step):
-    order = [2 * q if q < chips // 2 else 2 * (chips - 1 - q) + 1 for q in range(chips)]
-    return [
-        (order[q] * 2 + core, order[(q + step) % chips] * 2 + core)
-        for q in range(chips)
-        for core in range(2)
-    ]
 
 
 def swap_route(devices):
@@ -178,34 +169,141 @@
     )(*arrays)
 
 
-def ring_scatter(own_rows):
-    devices = lax.axis_size("dp")
-    chips = devices // 2
-    me = lax.axis_index("dp")
-    core = me % 2
-    place = ring_place(me // 2, chips)
-    rows = own_rows.shape[0] // devices
-    width = own_rows.shape[1]
-    split = own_rows.reshape(chips, 2, rows, width)
-    given = lax.dynamic_slice(split, (0, 1 - core, 0, 0), (chips, 1, rows, width))[:, 0]
-    taken = lax.ppermute(given, "dp", swap_route(devices))
-    half_rows = rows // 2
-
-    def term(at, half):
-        chip = ring_chip(at, chips)
-        mine = lax.dynamic_slice(split, (chip, core, half * half_rows, 0), (1, 1, half_rows, width))[0, 0]
-        other = lax.dynamic_slice(taken, (chip, half * half_rows, 0), (1, half_rows, width))[0]
-        return mine.astype(F32) + other.astype(F32)
-
-    to_right, to_left = term(place - 1, 0).astype(BF), term(place + 1, 1).astype(BF)
-    for step in range(chips - 1):
-        to_right = lax.ppermute(to_right, "dp", ring_route(chips, 1))
-        to_left = lax.ppermute(to_left, "dp", ring_route(chips, -1))
-        to_right = to_right.astype(F32) + term(place - 2 - step, 0)
-        to_left = to_left.astype(F32) + term(place + 2 + step, 1)
-        if step < chips - 2:
-            to_right, to_left = to_right.astype(BF), to_left.astype(BF)
-    return jnp.concatenate([to_right, to_left], axis=0)
+class Ring:
+    def __init__(self, devices, sources, outs, scratch):
+        self.devices, self.chips = devices, devices // 2
+        self.sources, self.outs = sources, outs
+        count = len(sources)
+        self.mine, self.taken, self.inbox = scratch[0 : 3 * count : 3], scratch[1 : 3 * count : 3], scratch[2 : 3 * count : 3]
+        self.own_sem, self.give_sem, self.take_sem, self.send_sem, self.recv_sem = scratch[3 * count :]
+        self.me = lax.axis_index("dp")
+        self.side = lax.axis_index("tensor")
+        self.core = lax.rem(self.me, 2)
+        self.place = ring_place(self.me // 2, self.chips)
+        self.partner = self.me + 1 - 2 * self.core
+        self.next = (
+            ring_chip(self.place + 1, self.chips) * 2 + self.core,
+            ring_chip(self.place - 1, self.chips) * 2 + self.core,
+        )
+
+    @staticmethod
+    def scratch(devices, shapes):
+        chips, count = devices // 2, len(shapes)
+        dma = pltpu.SemaphoreType.DMA
+        buffers = []
+        for rows, width in shapes:
+            buffers += [pltpu.VMEM((amount, 2, rows // 2, width), BF) for amount in (chips, chips, chips - 1)]
+        return buffers + [dma((count, amount, 2)) for amount in (chips, chips, chips, chips - 1, chips - 1)]
+
+    def barrier(self, others=()):
+        semaphore = pltpu.get_barrier_semaphore()
+        everyone = [(self.next[0], self.side), (self.next[1], self.side), (self.partner, self.side), *others]
+        for other in everyone:
+            pl.semaphore_signal(semaphore, inc=1, device_id=other, device_id_type=MESH)
+        pl.semaphore_wait(semaphore, len(everyone))
+
+    def term(self, index, stage, half, core):
+        at = self.place - 1 - stage if half == 0 else self.place + 1 + stage
+        size = self.mine[index].shape[2]
+        return self.sources[index].at[ring_chip(at, self.chips) * 2 + core, pl.ds(half * size, size), :]
+
+    def own(self, index, stage, half):
+        return pltpu.make_async_copy(
+            self.term(index, stage, half, self.core), self.mine[index].at[stage, half], self.own_sem.at[index, stage, half]
+        )
+
+    def given(self, index, stage, half):
+        return pltpu.make_async_remote_copy(
+            src_ref=self.term(index, stage, half, 1 - self.core),
+            dst_ref=self.taken[index].at[stage, half],
+            send_sem=self.give_sem.at[index, stage, half],
+            recv_sem=self.take_sem.at[index, stage, half],
+            device_id=(self.partner, self.side),
+            device_id_type=MESH,
+        )
+
+    def hop(self, index, stage, half, first):
+        source = self.mine[index].at[0, half] if first else self.inbox[index].at[stage - 1, half]
+        return pltpu.make_async_remote_copy(
+            src_ref=source,
+            dst_ref=self.inbox[index].at[stage, half],
+            send_sem=self.send_sem.at[index, stage, half],
+            recv_sem=self.recv_sem.at[index, stage, half],
+            device_id=(self.next[half], self.side),
+            device_id_type=MESH,
+        )
+
+    def each(self):
+        return [(index, half) for index in range(len(self.sources)) for half in range(2)]
+
+    def begin(self):
+        def step(stage, carry):
+            for index, half in self.each():
+                self.given(index, stage, half).start()
+                self.own(index, stage, half).start()
+            return carry
+
+        lax.fori_loop(0, self.chips, step, 0)
+
+    def chip_term(self, index, stage, half):
+        self.own(index, stage, half).wait()
+        self.given(index, stage, half).wait_recv()
+        return self.mine[index][stage, half].astype(F32) + self.taken[index][stage, half].astype(F32)
+
+    def stage(self, stage):
+        last = self.chips - 1
+
+        @pl.when(stage == 0)
+        def _():
+            for index, half in self.each():
+                self.mine[index][0, half] = self.chip_term(index, 0, half).astype(BF)
+                self.hop(index, 0, half, True).start()
+
+        @pl.when((stage > 0) & (stage < last))
+        def _():
+            for index, half in self.each():
+                self.hop(index, stage - 1, half, True).wait_recv()
+                came = self.inbox[index][stage - 1, half].astype(F32)
+                self.inbox[index][stage - 1, half] = (came + self.chip_term(index, stage, half)).astype(BF)
+                self.hop(index, stage, half, False).start()
+
+        @pl.when(stage == last)
+        def _():
+            for index, half in self.each():
+                self.hop(index, last - 1, half, True).wait_recv()
+                came = self.inbox[index][last - 1, half].astype(F32)
+                size = came.shape[0]
+                total = came + self.chip_term(index, last, half)
+                out = self.outs[index]
+                out[half * size : (half + 1) * size, :] = total[:, : out.shape[1]]
+
+    def pace(self, step, first, total):
+        def done(at):
+            return jnp.maximum(at - first, 0) * self.chips // (total - first)
+
+        def one(stage, carry):
+            self.stage(stage)
+            return carry
+
+        lax.fori_loop(done(step), done(step + 1), one, 0)
+
+    def finish(self):
+        for index, half in self.each():
+            self.hop(index, 0, half, True).wait_send()
+
+        def sent(stage, carry):
+            for index, half in self.each():
+                self.hop(index, stage, half, False).wait_send()
+            return carry
+
+        lax.fori_loop(1, self.chips - 1, sent, 0)
+
+        def gave(stage, carry):
+            for index, half in self.each():
+                self.given(index, stage, half).wait_send()
+            return carry
+
+        lax.fori_loop(0, self.chips, gave, 0)
 
 
 def dot_nn(a, b):
@@ -356,13 +454,42 @@
     )(qkv, qkv, qkv, near, near, far, far, places)
 
 
-def attend_back(qkv, near, far, probs, d_mixed, cosine, sine, heads):
-    m = qkv.shape[0]
+def single(shape):
+    return pl.BlockSpec(shape, lambda i: (0,) * len(shape), pipeline_mode=pl.Buffered(1))
+
+
+def attend_back(qkv, near, far, probs, mixed, w_attn, d_hidden, d_hidden_t, cosine, sine, ring_source, heads, out_width, identity):
+    m, width = d_hidden.shape
+    devices, rows, ring_width = ring_source.shape[1:]
     blocks = m // QB
     factor = E ** (-0.5)
     reach = WINDOW + m
-
-    def kernel(q_ref, k0, v0, k1, v1, k2, v2, p_ref, g_ref, c_ref, s_ref, dq_ref, dk0, dv0, dk1, dv1, dk2, dv2, keys_sum, values_sum):
+    columns = heads * E
+
+    def kernel(q_ref, k0, v0, k1, v1, k2, v2, p_ref, x_ref, w_ref, g_ref, gt_ref, c_ref, s_ref, source, d_ref, out_ref, sum_ref, keys_sum, values_sum, near_out, near_in, far_out, far_in, kept, near_send, near_recv, far_send, far_recv, *scratch):
+        head = pl.program_id(0)
+        ring = Ring(devices, [source.at[0]], [sum_ref], scratch)
+        me, side, core = ring.me, ring.side, ring.core
+
+        @pl.when(head == 0)
+        def _():
+            ring.barrier(((lax.rem(me + 2, devices), side), (lax.rem(me + devices - 2, devices), side)))
+            ring.begin()
+
+        def near_copy(which):
+            return pltpu.make_async_remote_copy(
+                src_ref=near_out.at[which], dst_ref=near_in.at[which], send_sem=near_send.at[which], recv_sem=near_recv.at[which],
+                device_id=(ring.partner, side), device_id_type=MESH,
+            )
+
+        def far_copy(which):
+            return pltpu.make_async_remote_copy(
+                src_ref=far_out.at[which], dst_ref=far_in.at[which], send_sem=far_send.at[which], recv_sem=far_recv.at[which],
+                device_id=(lax.rem(me + devices - 2, devices), side), device_id_type=MESH,
+            )
+
+        grad_all = dot_nn(g_ref[...], w_ref[...]).astype(BF)
+        out_ref[...] = dot_nn(gt_ref[...], x_ref[...]).astype(BF)
         keys = jnp.concatenate([k2[...], k1[...], k0[...]], axis=0)
         values = jnp.concatenate([v2[...], v1[...], v0[...]], axis=0)
         keys_t = keys.T
@@ -372,7 +499,7 @@
             span = slice(block * QB, block * QB + KB)
             here = slice(block * QB, (block + 1) * QB)
             low = p_ref[0, block]
-            grad = g_ref[here, :]
+            grad = grad_all[here, :]
             d_probs = dot_nt(values[span], grad)
             weighted = low.astype(F32) * d_probs
             total = jnp.sum(weighted, axis=0, keepdims=True)
@@ -380,53 +507,255 @@
             values_sum[span, :] += dot_nn(low, grad)
             keys_sum[span, :] += dot_nn(d_scores, q_ref[here, :])
             d_query = dot_nn(keys_t[:, span], d_scores).T * factor
-            dq_ref[here, :] = turned(d_query, c_ref[here, :], s_ref[here, :], True).astype(BF)
-        for index, (dk, dv) in enumerate(((dk2, dv2), (dk1, dv1), (dk0, dv0))):
-            rows = slice(index * m, (index + 1) * m)
-            dk[...] = (keys_sum[rows, :] * factor).astype(BF)
-            dv[...] = values_sum[rows, :].astype(BF)
-
-    def head(offset):
+            d_ref[here, pl.ds(pl.multiple_of(head * E, E), E)] = turned(d_query, c_ref[here, :], s_ref[here, :], True).astype(BF)
+        for which, (total, scale) in enumerate(((keys_sum, factor), (values_sum, 1.0))):
+            far_out[head, which] = (total[:m, :] * scale).astype(BF)
+            near_out[head, which] = (total[m : 2 * m, :] * scale).astype(BF)
+            kept[head, which] = total[2 * m :, :] * scale
+        near_copy(head).start()
+
+        def settle(which):
+            near_copy(which).wait_recv()
+            came = near_in[which].astype(F32)
+            share = core.astype(F32)
+            far_out[which] = (far_out[which].astype(F32) + came * share).astype(BF)
+            kept[which] = kept[which] + came * (1.0 - share)
+
+            @pl.when(me >= 2)
+            def _():
+                far_copy(which).start()
+
+        def close(which):
+            @pl.when(me < devices - 2)
+            def _():
+                far_copy(which).wait_recv()
+                kept[which] = kept[which] + far_in[which].astype(F32)
+
+            d_key = turned(kept[which, 0], c_ref[...], s_ref[...], True).astype(BF)
+            d_ref[:, pl.ds(pl.multiple_of((heads + which) * E, E), E)] = d_key
+            d_ref[:, pl.ds(pl.multiple_of((2 * heads + which) * E, E), E)] = kept[which, 1].astype(BF)
+            near_copy(which).wait_send()
+
+            @pl.when(me >= 2)
+            def _():
+                far_copy(which).wait_send()
+
+        @pl.when(head > 0)
+        def _():
+            settle(head - 1)
+
+        @pl.when(head == heads - 1)
+        def _():
+            settle(head)
+
+        ring.pace(head, 0, heads)
+
+        @pl.when(head == heads - 1)
+        def _():
+            def one(which, carry):
+                close(which)
+                return carry
+
+            lax.fori_loop(0, heads, one, 0)
+            ring.finish()
+
+    def head_spec(offset):
         return pl.BlockSpec((m, E), lambda i: (0, i + offset))
 
-    low = jax.ShapeDtypeStruct((m, heads * E), BF)
+    dma = pltpu.SemaphoreType.DMA
+    pieces = (heads, 2, m, E)
     return pl.pallas_call(
         kernel,
         grid=(heads,),
-        out_shape=[low] * 7,
+        out_shape=[
+            jax.ShapeDtypeStruct((m, 3 * columns), BF),
+            jax.ShapeDtypeStruct((width, columns), BF),
+            jax.ShapeDtypeStruct((rows, out_width), F32),
+        ],
         in_specs=[
-            head(0), head(heads), head(2 * heads), head(0), head(heads), head(0), head(heads),
+            head_spec(0), head_spec(heads), head_spec(2 * heads), head_spec(0), head_spec(heads), head_spec(0), head_spec(heads),
             pl.BlockSpec((1, blocks, KB, QB), lambda i: (i, 0, 0, 0)),
-            head(0),
-            whole_spec((m, E)),
-            whole_spec((m, E)),
+            head_spec(0),
+            pl.BlockSpec((width, E), lambda i: (0, i + 3 * heads)),
+            single((m, width)),
+            single((width, m)),
+            single((m, E)),
+            single((m, E)),
+            pl.BlockSpec(memory_space=pl.ANY),
         ],
-        out_specs=[head(0)] * 7,
-        scratch_shapes=[pltpu.VMEM((reach, E), F32), pltpu.VMEM((reach, E), F32)],
-        compiler_params=pltpu.CompilerParams(vmem_limit_bytes=VMEM),
+        out_specs=[single((m, 3 * columns)), pl.BlockSpec((width, E), lambda i: (0, i)), single((rows, out_width))],
+        scratch_shapes=[
+            pltpu.VMEM((reach, E), F32), pltpu.VMEM((reach, E), F32),
+            pltpu.VMEM(pieces, BF), pltpu.VMEM(pieces, BF), pltpu.VMEM(pieces, BF), pltpu.VMEM(pieces, BF), pltpu.VMEM(pieces, F32),
+            dma((heads,)), dma((heads,)), dma((heads,)), dma((heads,)),
+            *Ring.scratch(devices, [(rows, ring_width)]),
+        ],
+        compiler_params=pltpu.CompilerParams(vmem_limit_bytes=VMEM, collective_id=identity, has_side_effects=True),
         cost_estimate=cost(8 * heads * m * KB * E * 2, 2 * heads * m * KB),
         name="attend_back",
-    )(qkv, qkv, qkv, near, near, far, far, probs, d_mixed, cosine, sine)
+    )(qkv, qkv, qkv, near, near, far, far, probs, mixed, w_attn, d_hidden, d_hidden_t, cosine, sine, ring_source)
+
+
+def back_pass(x_t, d_out, weights, extra, ring_sources, out_widths, identity, name):
+    amount, m, columns = d_out.shape
+    width = x_t.shape[0]
+    devices = lax.axis_size("dp")
+    sides = lax.axis_size("tensor")
+    tiles = width // TILE
+    per = columns // TILE
+    total = tiles + amount * per
+    ring_shapes = [(source.shape[-2], source.shape[-1]) for source, _ in ring_sources]
+    count = len(ring_sources)
+
+    def kernel(*refs):
+        refs = list(refs)
+
+        def take(number):
+            taken = refs[:number]
+            del refs[:number]
+            return taken
+
+        xt_ref, tile_ref, d_ref = take(3)
+        w_refs = take(amount)
+        extra_refs = take(2) if extra else None
+        sources = [ref if lead is None else ref.at[lead] for ref, (_, lead) in zip(take(count), ring_sources)]
+        grad_ref, back_ref = take(2)
+        extra_out = take(1)[0] if extra else None
+        sums = take(count)
+        sent, got, y_send, y_recv = take(4)
+        ring = Ring(devices, sources, sums, refs)
+        other = (ring.me, lax.rem(ring.side + 1, sides))
+        step = pl.program_id(0)
+
+        def across(which):
+            return pltpu.make_async_remote_copy(
+                src_ref=sent.at[which], dst_ref=got.at[which], send_sem=y_send.at[which], recv_sem=y_recv.at[which],
+                device_id=other, device_id_type=MESH,
+            )
+
+        @pl.when(step == 0)
+        def _():
+            ring.barrier((other,))
+            ring.begin()
+
+        @pl.when(step < tiles)
+        def _():
+            part = None
+            for index in range(amount):
+                made = dot_nt(d_ref[index], w_refs[index][...])
+                part = made if part is None else part + made
+            sent[step] = part.astype(BF)
+            across(step).start()
+            if extra:
+                extra_out[...] = dot_nt(extra_refs[0][...], extra_refs[1][...]).astype(BF)
+
+        @pl.when(step >= tiles)
+        def _():
+            grad_ref[0] = dot_nn(xt_ref[...], tile_ref[0]).astype(BF)
+
+        ring.pace(step, 0, total)
+
+        @pl.when(step == total - 1)
+        def _():
+            for which in range(tiles):
+                across(which).wait()
+                back_ref[:, which * TILE : (which + 1) * TILE] = sent[which].astype(F32) + got[which].astype(F32)
+            ring.finish()
+
+    def late(i):
+        return jnp.maximum(i - tiles, 0)
+
+    def early(i):
+        return jnp.minimum(i, tiles - 1)
+
+    specs = [
+        single((width, m)),
+        pl.BlockSpec((1, m, TILE), lambda i: (late(i) // per, 0, late(i) % per)),
+        single((amount, m, columns)),
+    ]
+    operands = [x_t, d_out, d_out]
+    for index in range(amount):
+        specs.append(pl.BlockSpec((TILE, columns), functools.partial(lambda where, i: (early(i), where), index)))
+        operands.append(weights)
+    out_specs = [pl.BlockSpec((1, width, TILE), lambda i: (late(i) // per, 0, late(i) % per)), single((m, width))]
+    out_shape = [jax.ShapeDtypeStruct((amount, width, columns), BF), jax.ShapeDtypeStruct((m, width), F32)]
+    if extra:
+        x, w, where = extra
+        specs += [single(x.shape), pl.BlockSpec((TILE, x.shape[1]), lambda i: (early(i), where))]
+        operands += [x, w]
+        out_specs.append(pl.BlockSpec((m, TILE), lambda i: (0, early(i))))
+        out_shape.append(jax.ShapeDtypeStruct((m, width), BF))
+    specs += [pl.BlockSpec(memory_space=pl.ANY)] * count
+    operands += [source for source, _ in ring_sources]
+    for (rows, _), out_width in zip(ring_shapes, out_widths):
+        out_specs.append(single((rows, out_width)))
+        out_shape.append(jax.ShapeDtypeStruct((rows, out_width), F32))
+    dma = pltpu.SemaphoreType.DMA
+    return pl.pallas_call(
+        kernel,
+        grid=(total,),
+        out_shape=out_shape,
+        in_specs=specs,
+        out_specs=out_specs,
+        scratch_shapes=[
+            pltpu.VMEM((tiles, m, TILE), BF),
+            pltpu.VMEM((tiles, m, TILE), BF),
+            dma((tiles,)),
+            dma((tiles,)),
+            *Ring.scratch(devices, ring_shapes),
+        ],
+        compiler_params=pltpu.CompilerParams(vmem_limit_bytes=VMEM, collective_id=identity, has_side_effects=True),
+        cost_estimate=cost(4 * m * width * amount * columns, 6 * width * amount * columns),
+        name=name,
+    )(*operands)
+
+
+def ring_only(ring_sources, out_widths, identity):
+    devices = lax.axis_size("dp")
+    shapes = [source.shape[1:] for source in ring_sources]
+    count = len(shapes)
+
+    def kernel(*refs):
+        ring = Ring(devices, list(refs[:count]), list(refs[count : 2 * count]), refs[2 * count :])
+        ring.barrier()
+        ring.begin()
+
+        def one(stage, carry):
+            ring.stage(stage)
+            return carry
+
+        lax.fori_loop(0, ring.chips, one, 0)
+        ring.finish()
+
+    return pl.pallas_call(
+        kernel,
+        out_shape=[jax.ShapeDtypeStruct((rows, out_width), F32) for (rows, _), out_width in zip(shapes, out_widths)],
+        in_specs=[pl.BlockSpec(memory_space=pl.ANY)] * count,
+        out_specs=[pl.BlockSpec(memory_space=pltpu.VMEM)] * count,
+        scratch_shapes=Ring.scratch(devices, shapes),
+        compiler_params=pltpu.CompilerParams(vmem_limit_bytes=VMEM, collective_id=identity, has_side_effects=True),
+        name="ring_sum",
+    )(*ring_sources)
 
 
 def feed(x, dy, w, tiles):
     m, k = x.shape
 
-    def kernel(x_ref, dy_ref, g_ref, u_ref, d_ref, act_ref, dg_ref, du_ref):
+    def kernel(x_ref, dy_ref, g_ref, u_ref, d_ref, act_ref, both_ref):
         gate = dot_nn(x_ref[...], g_ref[...])
         up = dot_nn(x_ref[...], u_ref[...])
         d_act = dot_nn(dy_ref[...], d_ref[...])
         soft = 1.0 / (1.0 + jnp.exp(-gate))
         silu = gate * soft
         act_ref[...] = (silu * up).astype(BF)
-        dg_ref[...] = (d_act * up * (soft * (1.0 + gate * (1.0 - soft)))).astype(BF)
-        du_ref[...] = (d_act * silu).astype(BF)
+        both_ref[0] = (d_act * up * (soft * (1.0 + gate * (1.0 - soft)))).astype(BF)
+        both_ref[1] = (d_act * silu).astype(BF)
 
     tile = pl.BlockSpec((m, TILE), lambda i: (0, i))
     return pl.pallas_call(
         kernel,
         grid=(tiles,),
-        out_shape=[jax.ShapeDtypeStruct((m, tiles * TILE), BF)] * 3,
+        out_shape=[jax.ShapeDtypeStruct((m, tiles * TILE), BF), jax.ShapeDtypeStruct((2, m, tiles * TILE), BF)],
         in_specs=[
             whole_spec((m, k)),
             whole_spec((m, k)),
@@ -434,7 +763,7 @@
             pl.BlockSpec((k, TILE), lambda i: (0, i + tiles)),
             pl.BlockSpec((k, TILE), lambda i: (0, i + 2 * tiles)),
         ],
-        out_specs=[tile] * 3,
+        out_specs=[tile, pl.BlockSpec((2, m, TILE), lambda i: (0, 0, i))],
         compiler_params=pltpu.CompilerParams(vmem_limit_bytes=VMEM),
         cost_estimate=cost(6 * m * k * tiles * TILE, 6 * (m + k) * tiles * TILE, m * tiles * TILE),
         name="feed",
@@ -503,50 +832,44 @@
 
     root_ffn = norm_root(hidden)
     normed_ffn = (hidden * root_ffn * gain_ffn).astype(BF)
-    activated, d_gate, d_up = feed(normed_ffn, cotangent, w_ffn, tiles)
-    down_grad = ring_scatter(matmul_nn(cotangent.T, activated, 0, tiles, "down_grad"))
-    normed_ffn_t = normed_ffn.T
-    gate_grad = ring_scatter(matmul_nn(normed_ffn_t, d_gate, 0, tiles, "gate_grad"))
-    up_grad = ring_scatter(matmul_nn(normed_ffn_t, d_up, 0, tiles, "up_grad"))
-    d_normed_ffn = pair_sum(matmul_nt([(d_gate, w_ffn, 0), (d_up, w_ffn, 1)], "ffn_back"), flip)
+    activated, d_both = feed(normed_ffn, cotangent, w_ffn, tiles)
+    down_part = matmul_nn(cotangent.T, activated, 0, tiles, "down_grad").reshape(devices, own_rows, padded)
+    both_part, d_normed_ffn, ffn_part, down_grad = back_pass(
+        normed_ffn.T, d_both, w_ffn, (activated, w_ffn, 2), [(down_part, None)], [hidden_units], 1, "ffn_back"
+    )
+    both_part = both_part.reshape(2, devices, own_rows, padded)
+    layer_out = (hidden + pair_sum(ffn_part, flip)).astype(BF)
     d_hidden_norm, gain_ffn_grad = norm_back(hidden, root_ffn, gain_ffn, d_normed_ffn)
     d_hidden = cotangent.astype(F32) + d_hidden_norm
     d_hidden_low = d_hidden.astype(BF)
-    layer_out = (hidden + pair_sum(matmul_nt([(activated, w_ffn, 2)], "down_project"), flip)).astype(BF)
-
-    d_mixed = matmul_nn(d_hidden_low, w_attn, 3 * head_columns // TILE, head_columns // TILE, "out_back")
-    out_part = matmul_nn(d_hidden_low.T, mixed, 0, head_columns // TILE, "out_grad")
-    d_query, dk0, dv0, dk1, dv1, dk2, dv2 = attend_back(qkv, near, far, probs, d_mixed, cosine, sine, heads)
-    near_sum = lax.ppermute(jnp.concatenate([dk1, dv1], axis=1), "dp", swap_route(devices)).astype(F32)
-    far_part = jnp.concatenate([dk2, dv2], axis=1)
-    far_part = (far_part.astype(F32) + jnp.where(core == 1, near_sum, 0.0)).astype(BF)
-    far_sum = lax.ppermute(far_part, "dp", [(i, i - 2) for i in range(2, devices)]).astype(F32)
-    d_kv = jnp.concatenate([dk0, dv0], axis=1).astype(F32) + jnp.where(core == 0, near_sum, 0.0) + far_sum
-    d_key = d_kv[:, :head_columns].reshape(span, heads, E)
-    d_key = d_key * cosine[:, None, :] - jnp.roll(d_key, E // 2, axis=2) * sine[:, None, :]
-    d_qkv = jnp.concatenate([d_query, d_key.reshape(span, head_columns).astype(BF), d_kv[:, head_columns:].astype(BF)], axis=1)
-    normed_attn_t = normed_attn.T
-    qkv_part = matmul_nn(normed_attn_t, d_qkv, 0, 3 * head_columns // TILE, "qkv_grad")
-    attn_grads = ring_scatter(jnp.concatenate([qkv_part, out_part], axis=1))
-    d_normed_attn = pair_sum(matmul_nt([(d_qkv, w_attn, 0)], "qkv_back"), flip)
+
+    d_qkv, out_part, gate_grad = attend_back(
+        qkv, near, far, probs, mixed, w_attn, d_hidden_low, d_hidden_low.T, cosine, sine, both_part, heads, hidden_units, 2
+    )
+    qkv_part, d_normed_attn, up_grad, out_grad = back_pass(
+        normed_attn.T, d_qkv[None], w_attn, None,
+        [(both_part, 1), (out_part.reshape(devices, own_rows, head_columns), None)], [hidden_units, head_columns], 3, "qkv_back",
+    )
     d_rows, gain_attn_grad = norm_back(rows, root_attn, gain_attn, d_normed_attn)
     tokens_grad = d_hidden + d_rows
-    gain_sums = lax.psum_scatter(
-        jnp.stack([gain_attn_grad.reshape(devices, own_rows), gain_ffn_grad.reshape(devices, own_rows)], axis=1),
-        "dp", scatter_dimension=0, tiled=False,
+    gain_part = jnp.zeros((devices, 32, lanes), BF)
+    gain_part = gain_part.at[:, 0, :own_rows].set(gain_attn_grad.reshape(devices, own_rows).astype(BF))
+    gain_part = gain_part.at[:, 16, :own_rows].set(gain_ffn_grad.reshape(devices, own_rows).astype(BF))
+    qkv_grad, gain_grads = ring_only(
+        [qkv_part.reshape(devices, own_rows, 3 * head_columns), gain_part], [3 * head_columns, lanes], 4
     )
     return (
         layer_out,
         tokens_grad,
-        gain_sums[0],
-        attn_grads[:, :head_columns],
-        attn_grads[:, head_columns : 2 * head_columns],
-        attn_grads[:, 2 * head_columns : 3 * head_columns],
-        attn_grads[:, 3 * head_columns :].T,
-        gain_sums[1],
-        gate_grad[:, :hidden_units],
-        up_grad[:, :hidden_units],
-        down_grad[:, :hidden_units].T,
+        gain_grads[0, :own_rows],
+        qkv_grad[:, :head_columns],
+        qkv_grad[:, head_columns : 2 * head_columns],
+        qkv_grad[:, 2 * head_columns :],
+        out_grad.T,
+        gain_grads[16, :own_rows],
+        gate_grad,
+        up_grad,
+        down_grad.T,
     )
 
 

time: 977 us -> 829 us (0.85)
  Pallas kernels: 290 us -> 547 us
  waiting for transfers between devices: 324 us -> 134 us
  other arithmetic: 122 us -> 39.4 us
  blocking collectives: 57.6 us -> 0 us
  starting transfers between devices: 67.8 us -> 10.4 us
  local copies, waits for them, and re-layouts: 90 us -> 75.4 us
    pallas_call x1 -> x4, Pallas kernels: 20.3 us -> 375 us  [the longest x2 190 us: back_pass(): pl.pallas_call(kernel, grid=(total,), out_shape=out_shape, in_specs=specs...]
    ppermute x62 -> x0, waiting for transfers between devices: 188 us -> none  [the longest x28 132 us: ring_scatter(): to_right = lax.ppermute(to_right, 'dp', ring_route(chips, 1))]
    unnamed x1 -> x0, blocking collectives: 57.6 us -> none
    ppermute x62 -> x0, starting transfers between devices: 57.4 us -> none  [the longest x28 37.9 us: ring_scatter(): to_right = lax.ppermute(to_right, 'dp', ring_route(chips, 1))]
    convert_element_type x30 -> x0, other arithmetic: 53.7 us -> none  [the longest x24 43.2 us: ring_scatter(): to_right, to_left = (to_right.astype(BF), to_left.astype(BF))]
    pallas_call x6 -> x1, Pallas kernels: 66.1 us -> 13.2 us  [matmul_nn(): pl.pallas_call(kernel, grid=(count,), out_shape=jax.ShapeDtypeStruct((m,...]
    pallas_call x4 -> x1, Pallas kernels: 52.2 us -> 8.42 us  [matmul_nt(): pl.pallas_call(kernel, grid=(n // TILE,), out_shape=jax.ShapeDtypeStruct(...]
    squeeze x5 -> x1, local copies, waits for them, and re-layouts: 25 us -> 1.35 us  [shards(): gain_grads[16, :own_rows]]
  transfers between devices with their start and end apart: 69 -> 5, of which waited for: 37 -> 3; matrix products, arithmetic and copies ran while one was open for 20% -> 8% of each run, Pallas kernels for 16% -> 39%
where the time goes in v2:
time: 829 us; the launch traced here: 821 us
  Pallas kernels  547 us (66%)
  waiting for transfers between devices  134 us (16%)
  local copies, waits for them, and re-layouts  75.4 us (9%)
  other arithmetic  39.4 us (5%)
  between operations  14.6 us (2%)
  starting transfers between devices  10.4 us (1%)
    pallas_call x2, Pallas kernels, back_pass(): pl.pallas_call(kernel, grid=(total,), out_shape=out_shape, in_specs=specs...  190 us
    pallas_call x1, Pallas kernels, attend_back(): pl.pallas_call(kernel, grid=(heads,), out_shape=[jax.ShapeDtypeStruct((m,...  111 us
    ppermute x1, waiting for transfers between devices, shards(): far = lax.ppermute(own_kv, 'dp', [(i - 2, i) for i in range(2, devices)])  89.3 us
    pallas_call x1, Pallas kernels, ring_gather(): pl.pallas_call(functools.partial(gather_kernel, devices, chunks, len(arra...  88 us
    pallas_call x1, Pallas kernels, ring_only(): pl.pallas_call(kernel, out_shape=[jax.ShapeDtypeStruct((rows, out_width),...  72.8 us
    ppermute x2, waiting for transfers between devices, pair_sum(): return part.astype(F32) + lax.ppermute(part, 'tensor', route).astype(F32)  40.4 us
    unnamed x64, local copies, waits for them, and re-layouts  34.8 us
    pallas_call x1, Pallas kernels, feed(): pl.pallas_call(kernel, grid=(tiles,), out_shape=[jax.ShapeDtypeStruct((m,...  26.5 us
  transfers between devices with their start and end apart: 5, of which 3 were waited for; matrix products, arithmetic and copies ran while one was open for 8% of the time, Pallas kernels for 39%

profile of v2, /device:TPU:0, one launch (start us, length us, event | category | flops | bytes accessed | tf_op | source)
XLA Modules:
  0.0 820.6 jit_solution(650783861553918267)
XLA Ops:
  14.3 88.0 %ring_gather.1 = (bf16[2048,4096]{1,0:T(8,128)(2,1)}, bf16[512,128]{1,0:T(8,128)(2,1)}) custom-call(bf16[128,4096]{1,0:T(8,128)(2,1)} %pad_maximum_fusion.refs_0_, bf16[32,128]{1,0:T(8,128)(2,1)} %copy-done.16), custom_call_target="tpu_custom_call" | custom-call | tf_op jit(solution)/shard_map/ring_gather/pallas_call | solution.py:153
  110.4 4.1 copy.52.x_ref
  116.6 15.9 %project.1.q_ref.k0.v0 = bf16[512,3072]{1,0:T(8,128)(2,1)} custom-call(bf16[512,2048]{1,0:T(8,128)(2,1)} %copy.52.x_ref, bf16[2048,4096]{1,0:T(8,128)(2,1)} %get-tuple-element.84.w_ref.refs_1_.refs_3_, f32[512,128]{1,0:T(8,128)} %get-tuple-element.143.c_ref, f32[512,128]{1,0:T(8,128)} %get-tuple-element.144.s_ref), custom_call_target="tpu_custom_call" | custom-call | flops 6442450944 | bytes 17825792 | tf_op jit(solution)/shard_map/project/pallas_call | solution.py:392
  135.6 5.2 collective-permute-start
  140.8 89.3 %collective-permute-done.k2.v2 = bf16[512,2048]{1,0:T(8,128)(2,1)} collective-permute-done((bf16[512,2048]{1,0:T(8,128)(2,1)}, bf16[512,2048]{1,0:T(8,128)(2,1)}, u32[]{:S(2)}, u32[]{:S(2)}) %collective-permute-start) | collective-permute-done | bytes 2097184 | tf_op jit(solution)/shard_map/ppermute | solution.py:828
  232.4 4.0 collective-permute-done.1.k1.v1
  237.7 20.6 %attend.1 = (bf16[512,1024]{1,0:T(8,128)(2,1)}, bf16[8,2,1280,256]{3,2,1,0:T(8,128)(2,1)}) custom-call(bf16[512,3072]{1,0:T(8,128)(2,1)} %project.1.q_ref.k0.v0, bf16[512,3072]{1,0:T(8,128)(2,1)} %project.1.q_ref.k0.v0, bf16[512,3072]{1,0:T(8,128)(2,1)} %project.1.q_ref.k0.v0, bf16[512,2048]{1,0:T(8,128)(2,1)} %copy-done.5, bf16[512,2048]{1,0:T(8,128)(2,1)} %copy-done.5, ...), custom_call_target="tpu_custom_call" | custom-call | flops 5368709120 | bytes 10485760 | tf_op jit(solution)/shard_map/attend/pallas_call | solution.py:441
  258.2 8.4 %out_project.1 = bf16[512,2048]{1,0:T(8,128)(2,1)} custom-call(bf16[512,1024]{1,0:T(8,128)(2,1)} %get-tuple-element.85.refs_0_.x_ref, bf16[2048,4096]{1,0:T(8,128)(2,1)} %get-tuple-element.84.w_ref.refs_1_.refs_3_), custom_call_target="tpu_custom_call" | custom-call | flops 2147483648 | bytes 7340032 | tf_op jit(solution)/shard_map/out_project/pallas_call | solution.py:353
  272.1 4.0 copy.56
  278.0 40.4 %collective-permute-done.2 = bf16[512,2048]{0,1:T(8,128)(2,1)} collective-permute-done((bf16[512,2048]{0,1:T(8,128)(2,1)}, bf16[512,2048]{0,1:T(8,128)(2,1)}, u32[]{:S(2)}, u32[]{:S(2)}) %collective-permute-start.2) | collective-permute-done | bytes 2097184 | tf_op jit(solution)/shard_map/ppermute | solution.py:785
  324.9 4.0 copy.55.x_ref
  332.7 26.5 %feed.1 = (bf16[512,2816]{1,0:T(8,128)(2,1)}, bf16[2,512,2816]{2,1,0:T(8,128)(2,1)}) custom-call(bf16[512,2048]{1,0:T(8,128)(2,1)} %copy.55.x_ref, bf16[512,2048]{1,0:T(8,128)(2,1)} %dy_ref.1, bf16[2048,8448]{1,0:T(8,128)(2,1)} %all-gather.2.cloned.1.call-done.g_ref.u_ref.d_ref.refs_3_.refs_4_.refs_6_, ...), custom_call_target="tpu_custom_call" | custom-call | flops 17716740096 | bytes 43253760 | tf_op jit(solution)/shard_map/feed/pallas_call | solution.py:755
  359.2 13.2 %down_grad.1 = bf16[2048,2816]{1,0:T(8,128)(2,1)} custom-call(bf16[2048,512]{1,0:T(8,128)(2,1)} %bitcast.34, bf16[512,2816]{1,0:T(8,128)(2,1)} %get-tuple-element.88.w_ref.refs_5_), custom_call_target="tpu_custom_call" | custom-call | flops 5905580032 | bytes 16515072 | tf_op jit(solution)/shard_map/down_grad/pallas_call | solution.py:323
  372.4 99.4 %ffn_back.1 = (bf16[2,2048,2816]{2,1,0:T(8,128)(2,1)}, f32[512,2048]{1,0:T(8,128)}, bf16[512,2048]{1,0:T(8,128)(2,1)}, f32[128,2752]{1,0:T(8,128)}) custom-call(bf16[2048,512]{1,0:T(8,128)(2,1)} %fusion.19.refs_0_, bf16[2,512,2816]{2,1,0:T(8,128)(2,1)} %get-tuple-element.87.refs_1_.refs_2_, bf16[2,512,2816]{2,1,0:T(8,128)(2,1)} %get-tuple-element.87.refs_1_.refs_2_, ...), custom_call_target="tpu_custom_call" | custom-call | flops 23622320128 | bytes 69206016 | tf_op jit(solution)/shard_map/ffn_back/pallas_call | solution.py:694
  471.9 5.4 copy.60
  477.3 4.9 multiply_reduce_fusion
  486.5 4.0 copy.61.g_ref
  490.5 3.9 copy.57
  497.8 111.4 %attend_back.1 = (bf16[512,3072]{1,0:T(8,128)(2,1)}, bf16[2048,1024]{1,0:T(8,128)(2,1)}, f32[128,2752]{1,0:T(8,128)}) custom-call(bf16[512,3072]{1,0:T(8,128)(2,1)} %project.1.q_ref.k0.v0, bf16[512,3072]{1,0:T(8,128)(2,1)} %project.1.q_ref.k0.v0, bf16[512,3072]{1,0:T(8,128)(2,1)} %project.1.q_ref.k0.v0, bf16[512,2048]{1,0:T(8,128)(2,1)} %copy-done.5, ...), custom_call_target="tpu_custom_call" | custom-call | flops 10737418240 | bytes 10485760 | tf_op jit(solution)/shard_map/attend_back/pallas_call | solution.py:567
  609.2 91.0 %qkv_back.1 = (bf16[1,2048,3072]{2,1,0:T(8,128)(2,1)}, f32[512,2048]{1,0:T(8,128)}, f32[128,2752]{1,0:T(8,128)}, f32[128,1024]{1,0:T(8,128)}) custom-call(bf16[2048,512]{1,0:T(8,128)(2,1)} %fusion.20.refs_0_, bf16[1,512,3072]{2,1,0:T(8,128)(2,1)} %bitcast.35, bf16[1,512,3072]{2,1,0:T(8,128)(2,1)} %bitcast.36, ...), custom_call_target="tpu_custom_call" | custom-call | flops 12884901888 | bytes 37748736 | tf_op jit(solution)/shard_map/qkv_back/pallas_call | solution.py:694
  700.2 5.4 copy.62
  721.4 72.8 %ring_sum.1 = (f32[128,3072]{1,0:T(8,128)}, f32[32,128]{1,0:T(8,128)}) custom-call(bf16[16,128,3072]{2,1,0:T(8,128)(2,1)} %bitcast.37, bf16[16,32,128]{2,1,0:T(8,128)(2,1)} %scatter.19.refs_1_), custom_call_target="tpu_custom_call" | custom-call | tf_op jit(solution)/shard_map/ring_sum/pallas_call | solution.py:730
  798.2 7.4 fusion.9
  805.6 5.5 copy.68
  (99 shorter events, 71.4 us)
Async XLA Ops:
  7.2 5.4 copy-start.24
  7.2 5.4 copy-start.11
  7.2 5.4 copy-start.10
  7.2 5.4 copy-start.9
  7.2 6.4 copy-start.25
  7.2 325.5 %all-gather.2.cloned.1.call-start = ((), (), s32[]{:S(2)}) async-start(), calls=%async_computation | async-start | bytes 36765696 | tf_op jit(solution)/shard_map/all_gather | solution.py:812
  107.8 597.8 %copy-start.14 = (f32[512]{0:T(512)}, f32[512]{0:T(512)S(1)}, u32[]{:S(2)}) copy-start(f32[512]{0:T(512)S(1)} %add_rsqrt_fusion.1) | copy-start | bytes 6148
  108.5 6.0 copy-start.23
  135.6 94.5 %collective-permute-start = (bf16[512,2048]{1,0:T(8,128)(2,1)}, bf16[512,2048]{1,0:T(8,128)(2,1)}, u32[]{:S(2)}, u32[]{:S(2)}) collective-permute-start(bf16[512,2048]{1,0:T(8,128)(2,1)} %slice.101), channel_id=1, source_target_pairs={{0,4},{2,6},{4,8},{6,10},{8,12},{10,14},{12,16},{14,18},{16,20},{1... | collective-permute-start | bytes 6291464 | tf_op jit(solution)/shard_map/ppermute | solution.py:828
  232.1 4.2 collective-permute-start.1
  270.6 47.8 %collective-permute-start.2 = (bf16[512,2048]{0,1:T(8,128)(2,1)}, bf16[512,2048]{0,1:T(8,128)(2,1)}, u32[]{:S(2)}, u32[]{:S(2)}) collective-permute-start(bf16[512,2048]{0,1:T(8,128)(2,1)} %copy.53), channel_id=1, source_target_pairs={{0,1},{1,0},{2,3},{3,2},{4,5},{5,4},{6,7},{7,6},{8,9},{9,8},{10,11... | collective-permute-start | bytes 6291464 | tf_op jit(solution)/shard_map/ppermute | solution.py:785
  276.1 42.3 %copy-start.6 = (bf16[512,2048]{0,1:T(8,128)(2,1)S(1)}, bf16[512,2048]{0,1:T(8,128)(2,1)}, u32[]{:S(2)}) copy-start(bf16[512,2048]{0,1:T(8,128)(2,1)} %copy.53) | copy-start | bytes 6291460
  321.1 161.1 %copy-start.12 = (f32[512]{0:T(512)}, f32[512]{0:T(512)S(1)}, u32[]{:S(2)}) copy-start(f32[512]{0:T(512)S(1)} %add_rsqrt_fusion) | copy-start | bytes 6148
  477.3 4.9 copy-start.1
  477.3 5.9 copy-start.3
  494.4 303.7 %collective-permute-start.3 = (bf16[512,2048]{0,1:T(8,128)(2,1)}, bf16[512,2048]{0,1:T(8,128)(2,1)}, u32[]{:S(2)}, u32[]{:S(2)}) collective-permute-start(bf16[512,2048]{0,1:T(8,128)(2,1)} %copy.57), channel_id=1, source_target_pairs={{0,1},{1,0},{2,3},{3,2},{4,5},{5,4},{6,7},{7,6},{8,9},{9,8},{10,11... | collective-permute-start | bytes 6291464 | tf_op jit(solution)/shard_map/ppermute | solution.py:785
  709.3 9.1 %copy-start.8 = (f32[128,2752]{1,0:T(8,128)S(1)}, f32[128,2752]{1,0:T(8,128)}, u32[]{:S(2)}) copy-start(f32[128,2752]{1,0:T(8,128)} %get-tuple-element.102) | copy-start | bytes 4227076
  721.4 74.2 %copy-start.20 = (f32[512]{0:T(512)S(1)}, f32[512]{0:T(512)}, u32[]{:S(2)}) copy-start(f32[512]{0:T(512)} %copy-done.19) | copy-start | bytes 6148
  721.4 74.2 %copy-start.22 = (f32[512]{0:T(512)S(1)}, f32[512]{0:T(512)}, u32[]{:S(2)}) copy-start(f32[512]{0:T(512)} %get-tuple-element.128) | copy-start | bytes 6148
  721.4 76.8 %copy-start.2 = (f32[512,2048]{0,1:T(8,128)S(1)}, f32[512,2048]{0,1:T(8,128)}, u32[]{:S(2)}) copy-start(f32[512,2048]{0,1:T(8,128)} %copy-done) | copy-start | bytes 12582916
  721.4 76.8 %copy-start.13 = (f32[512]{0:T(512)S(1)}, f32[512]{0:T(512)}, u32[]{:S(2)}) copy-start(f32[512]{0:T(512)} %copy-done.12) | copy-start | bytes 6148
  721.4 76.8 %copy-start.15 = (f32[512]{0:T(512)S(1)}, f32[512]{0:T(512)}, u32[]{:S(2)}) copy-start(f32[512]{0:T(512)} %copy-done.14) | copy-start | bytes 6148
  721.4 76.8 %copy-start.18 = (f32[512]{0:T(512)S(1)}, f32[512]{0:T(512)}, u32[]{:S(2)}) copy-start(f32[512]{0:T(512)} %copy-done.17) | copy-start | bytes 6148
  805.6 5.5 copy-start.7
  (7 other events, 16.2 us)
Sparse Core Ops, SparseCore 0:
  103.9 213.9 all-gather.1

commit v3 on v2

--- a/solution.py
+++ b/solution.py
@@ -18,6 +18,7 @@
 QB = 256
 KB = WINDOW + QB
 TILE = 256
+ROWS = 128
 VMEM = 56 * 1024 * 1024
 
 
@@ -170,12 +171,14 @@
 
 
 class Ring:
-    def __init__(self, devices, sources, outs, scratch):
+    AHEAD = 3
+
+    def __init__(self, devices, terms, goals, groups, scratch):
         self.devices, self.chips = devices, devices // 2
-        self.sources, self.outs = sources, outs
-        count = len(sources)
+        self.terms, self.goals, self.groups = terms, goals, groups
+        count = len(terms)
         self.mine, self.taken, self.inbox = scratch[0 : 3 * count : 3], scratch[1 : 3 * count : 3], scratch[2 : 3 * count : 3]
-        self.own_sem, self.give_sem, self.take_sem, self.send_sem, self.recv_sem = scratch[3 * count :]
+        self.own_sem, self.give_sem, self.take_sem, self.send_sem, self.recv_sem = scratch[3 * count : 3 * count + 5]
         self.me = lax.axis_index("dp")
         self.side = lax.axis_index("tensor")
         self.core = lax.rem(self.me, 2)
@@ -185,6 +188,7 @@
             ring_chip(self.place + 1, self.chips) * 2 + self.core,
             ring_chip(self.place - 1, self.chips) * 2 + self.core,
         )
+        self.events = self.chips * len(groups)
 
     @staticmethod
     def scratch(devices, shapes):
@@ -202,19 +206,20 @@
             pl.semaphore_signal(semaphore, inc=1, device_id=other, device_id_type=MESH)
         pl.semaphore_wait(semaphore, len(everyone))
 
-    def term(self, index, stage, half, core):
+    def block(self, index, stage, half, core):
         at = self.place - 1 - stage if half == 0 else self.place + 1 + stage
         size = self.mine[index].shape[2]
-        return self.sources[index].at[ring_chip(at, self.chips) * 2 + core, pl.ds(half * size, size), :]
+        source, column, width = self.terms[index]
+        return source.at[ring_chip(at, self.chips) * 2 + core, pl.ds(half * size, size), pl.ds(column, width)]
 
     def own(self, index, stage, half):
         return pltpu.make_async_copy(
-            self.term(index, stage, half, self.core), self.mine[index].at[stage, half], self.own_sem.at[index, stage, half]
+            self.block(index, stage, half, self.core), self.mine[index].at[stage, half], self.own_sem.at[index, stage, half]
         )
 
     def given(self, index, stage, half):
         return pltpu.make_async_remote_copy(
-            src_ref=self.term(index, stage, half, 1 - self.core),
+            src_ref=self.block(index, stage, half, 1 - self.core),
             dst_ref=self.taken[index].at[stage, half],
             send_sem=self.give_sem.at[index, stage, half],
             recv_sem=self.take_sem.at[index, stage, half],
@@ -233,59 +238,81 @@
             device_id_type=MESH,
         )
 
-    def each(self):
-        return [(index, half) for index in range(len(self.sources)) for half in range(2)]
+    def each(self, group=None):
+        members = range(len(self.terms)) if group is None else self.groups[group]
+        return [(index, half) for index in members for half in range(2)]
+
+    def fetch(self, stage, group):
+        for index, half in self.each(group):
+            self.given(index, stage, half).start()
+            self.own(index, stage, half).start()
 
     def begin(self):
-        def step(stage, carry):
-            for index, half in self.each():
-                self.given(index, stage, half).start()
-                self.own(index, stage, half).start()
-            return carry
-
-        lax.fori_loop(0, self.chips, step, 0)
+        for stage in range(min(self.AHEAD, self.chips)):
+            for group in range(len(self.groups)):
+                self.fetch(stage, group)
 
     def chip_term(self, index, stage, half):
         self.own(index, stage, half).wait()
         self.given(index, stage, half).wait_recv()
         return self.mine[index][stage, half].astype(F32) + self.taken[index][stage, half].astype(F32)
 
-    def stage(self, stage):
+    def stage(self, stage, group):
         last = self.chips - 1
 
         @pl.when(stage == 0)
         def _():
-            for index, half in self.each():
+            for index, half in self.each(group):
                 self.mine[index][0, half] = self.chip_term(index, 0, half).astype(BF)
                 self.hop(index, 0, half, True).start()
 
         @pl.when((stage > 0) & (stage < last))
         def _():
-            for index, half in self.each():
+            for index, half in self.each(group):
                 self.hop(index, stage - 1, half, True).wait_recv()
                 came = self.inbox[index][stage - 1, half].astype(F32)
                 self.inbox[index][stage - 1, half] = (came + self.chip_term(index, stage, half)).astype(BF)
                 self.hop(index, stage, half, False).start()
 
+        @pl.when(stage + self.AHEAD < self.chips)
+        def _():
+            self.fetch(stage + self.AHEAD, group)
+
         @pl.when(stage == last)
         def _():
-            for index, half in self.each():
+            for index, half in self.each(group):
                 self.hop(index, last - 1, half, True).wait_recv()
                 came = self.inbox[index][last - 1, half].astype(F32)
                 size = came.shape[0]
                 total = came + self.chip_term(index, last, half)
-                out = self.outs[index]
-                out[half * size : (half + 1) * size, :] = total[:, : out.shape[1]]
-
-    def pace(self, step, first, total):
+                goal, column = self.goals[index]
+                width = min(goal.shape[1] - column, total.shape[1])
+                goal[half * size : (half + 1) * size, column : column + width] = total[:, :width]
+
+    def run(self, first, stop):
+        count = len(self.groups)
+
+        def one(event, carry):
+            for group in range(count):
+                if count == 1:
+                    self.stage(event, 0)
+                else:
+                    pl.when(lax.rem(event, count) == group)(functools.partial(self.stage, event // count, group))
+            return carry
+
+        lax.fori_loop(first, stop, one, 0)
+
+    def pace(self, step, costs):
+        whole = sum(steps * each for steps, each in costs)
+
         def done(at):
-            return jnp.maximum(at - first, 0) * self.chips // (total - first)
-
-        def one(stage, carry):
-            self.stage(stage)
-            return carry
-
-        lax.fori_loop(done(step), done(step + 1), one, 0)
+            spent, before = 0, 0
+            for steps, each in costs:
+                spent = spent + jnp.minimum(jnp.maximum(at - before, 0), steps) * each
+                before += steps
+            return spent * self.events // whole
+
+        self.run(done(step), done(step + 1))
 
     def finish(self):
         for index, half in self.each():
@@ -375,39 +402,49 @@
     steps = 3 * heads // per
     rotated = 2 * heads // per
 
-    def kernel(x_ref, w_ref, c_ref, s_ref, o_ref):
+    def kernel(x_ref, w_ref, c_ref, s_ref, q_ref, kv_ref):
         step = pl.program_id(0)
         made = dot_nn(x_ref[...], w_ref[...])
 
-        @pl.when(step < rotated)
-        def _():
+        def rotate_to(ref):
             for part in range(per):
                 piece = slice(part * E, (part + 1) * E)
-                o_ref[:, piece] = turned(made[:, piece], c_ref[...], s_ref[...], False).astype(BF)
+                ref[:, piece] = turned(made[:, piece], c_ref[...], s_ref[...], False).astype(BF)
+
+        @pl.when(step < rotated // 2)
+        def _():
+            rotate_to(q_ref)
+
+        @pl.when((step >= rotated // 2) & (step < rotated))
+        def _():
+            rotate_to(kv_ref)
 
         @pl.when(step >= rotated)
         def _():
-            o_ref[...] = made.astype(BF)
+            kv_ref[...] = made.astype(BF)
 
     return pl.pallas_call(
         kernel,
         grid=(steps,),
-        out_shape=jax.ShapeDtypeStruct((m, steps * TILE), BF),
+        out_shape=[jax.ShapeDtypeStruct((m, heads * E), BF), jax.ShapeDtypeStruct((m, 2 * heads * E), BF)],
         in_specs=[
             whole_spec((m, k)),
             pl.BlockSpec((k, TILE), lambda i: (0, i)),
             whole_spec((m, E)),
             whole_spec((m, E)),
         ],
-        out_specs=pl.BlockSpec((m, TILE), lambda i: (0, i)),
+        out_specs=[
+            pl.BlockSpec((m, TILE), lambda i: (0, jnp.minimum(i, rotated // 2 - 1))),
+            pl.BlockSpec((m, TILE), lambda i: (0, jnp.maximum(i - rotated // 2, 0))),
+        ],
         compiler_params=pltpu.CompilerParams(vmem_limit_bytes=VMEM),
         cost_estimate=cost(2 * m * k * steps * TILE, 2 * (m * k + (m + k) * steps * TILE)),
         name="project",
     )(x, w, cosine, sine)
 
 
-def attend(qkv, near, far, places, heads):
-    m = qkv.shape[0]
+def attend(query, own, near, far, places, heads):
+    m = query.shape[0]
     blocks = m // QB
     factor = E ** (-0.5) * LOG2E
 
@@ -445,20 +482,20 @@
             jax.ShapeDtypeStruct((m, heads * E), BF),
             jax.ShapeDtypeStruct((heads, blocks, KB, QB), BF),
         ],
-        in_specs=[head(0), head(heads), head(2 * heads), head(0), head(heads), head(0), head(heads), whole_spec((1, m))],
+        in_specs=[head(0), head(0), head(heads), head(0), head(heads), head(0), head(heads), whole_spec((1, m))],
         out_specs=[head(0), pl.BlockSpec((1, blocks, KB, QB), lambda i: (i, 0, 0, 0))],
         scratch_shapes=[pltpu.VMEM((blocks, KB, QB), F32)],
         compiler_params=pltpu.CompilerParams(vmem_limit_bytes=VMEM),
         cost_estimate=cost(4 * heads * m * KB * E * 2, 2 * heads * m * KB, heads * m * KB),
         name="attend",
-    )(qkv, qkv, qkv, near, near, far, far, places)
+    )(query, own, own, near, near, far, far, places)
 
 
 def single(shape):
     return pl.BlockSpec(shape, lambda i: (0,) * len(shape), pipeline_mode=pl.Buffered(1))
 
 
-def attend_back(qkv, near, far, probs, mixed, w_attn, d_hidden, d_hidden_t, cosine, sine, ring_source, heads, out_width, identity):
+def attend_back(query, own, near, far, probs, mixed, w_attn, d_hidden, d_hidden_t, cosine, sine, flip, ring_source, heads, out_width, identity):
     m, width = d_hidden.shape
     devices, rows, ring_width = ring_source.shape[1:]
     blocks = m // QB
@@ -466,9 +503,10 @@
     reach = WINDOW + m
     columns = heads * E
 
-    def kernel(q_ref, k0, v0, k1, v1, k2, v2, p_ref, x_ref, w_ref, g_ref, gt_ref, c_ref, s_ref, source, d_ref, out_ref, sum_ref, keys_sum, values_sum, near_out, near_in, far_out, far_in, kept, near_send, near_recv, far_send, far_recv, *scratch):
+    def kernel(q_ref, k0, v0, k1, v1, k2, v2, p_ref, x_ref, w_ref, g_ref, gt_ref, c_ref, s_ref, flip_ref, source, d_ref, out_ref, sum_ref, flipped_ref, keys_sum, values_sum, near_out, near_in, far_out, far_in, kept, near_send, near_recv, far_send, far_recv, *scratch):
         head = pl.program_id(0)
-        ring = Ring(devices, [source.at[0]], [sum_ref], scratch)
+        half = ring_width // 2
+        ring = Ring(devices, [(source.at[0], 0, half), (source.at[0], half, half)], [(sum_ref, 0), (sum_ref, half)], [[0], [1]], scratch)
         me, side, core = ring.me, ring.side, ring.core
 
         @pl.when(head == 0)
@@ -508,6 +546,8 @@
             keys_sum[span, :] += dot_nn(d_scores, q_ref[here, :])
             d_query = dot_nn(keys_t[:, span], d_scores).T * factor
             d_ref[here, pl.ds(pl.multiple_of(head * E, E), E)] = turned(d_query, c_ref[here, :], s_ref[here, :], True).astype(BF)
+            if block == 0:
+                ring.pace(2 * head, [(2 * heads, 1)])
         for which, (total, scale) in enumerate(((keys_sum, factor), (values_sum, 1.0))):
             far_out[head, which] = (total[:m, :] * scale).astype(BF)
             near_out[head, which] = (total[m : 2 * m, :] * scale).astype(BF)
@@ -548,7 +588,11 @@
         def _():
             settle(head)
 
-        ring.pace(head, 0, heads)
+        ring.pace(2 * head + 1, [(2 * heads, 1)])
+
+        @pl.when(head == 1)
+        def _():
+            flipped_ref[...] = flip_ref[...].T[: flipped_ref.shape[0]]
 
         @pl.when(head == heads - 1)
         def _():
@@ -571,9 +615,10 @@
             jax.ShapeDtypeStruct((m, 3 * columns), BF),
             jax.ShapeDtypeStruct((width, columns), BF),
             jax.ShapeDtypeStruct((rows, out_width), F32),
+            jax.ShapeDtypeStruct((out_width, rows), F32),
         ],
         in_specs=[
-            head_spec(0), head_spec(heads), head_spec(2 * heads), head_spec(0), head_spec(heads), head_spec(0), head_spec(heads),
+            head_spec(0), head_spec(0), head_spec(heads), head_spec(0), head_spec(heads), head_spec(0), head_spec(heads),
             pl.BlockSpec((1, blocks, KB, QB), lambda i: (i, 0, 0, 0)),
             head_spec(0),
             pl.BlockSpec((width, E), lambda i: (0, i + 3 * heads)),
@@ -581,22 +626,28 @@
             single((width, m)),
             single((m, E)),
             single((m, E)),
+            single(flip.shape),
             pl.BlockSpec(memory_space=pl.ANY),
         ],
-        out_specs=[single((m, 3 * columns)), pl.BlockSpec((width, E), lambda i: (0, i)), single((rows, out_width))],
+        out_specs=[
+            single((m, 3 * columns)),
+            pl.BlockSpec((width, E), lambda i: (0, i)),
+            single((rows, out_width)),
+            single((out_width, rows)),
+        ],
         scratch_shapes=[
             pltpu.VMEM((reach, E), F32), pltpu.VMEM((reach, E), F32),
             pltpu.VMEM(pieces, BF), pltpu.VMEM(pieces, BF), pltpu.VMEM(pieces, BF), pltpu.VMEM(pieces, BF), pltpu.VMEM(pieces, F32),
             dma((heads,)), dma((heads,)), dma((heads,)), dma((heads,)),
-            *Ring.scratch(devices, [(rows, ring_width)]),
+            *Ring.scratch(devices, [(rows, ring_width // 2)] * 2),
         ],
         compiler_params=pltpu.CompilerParams(vmem_limit_bytes=VMEM, collective_id=identity, has_side_effects=True),
         cost_estimate=cost(8 * heads * m * KB * E * 2, 2 * heads * m * KB),
         name="attend_back",
-    )(qkv, qkv, qkv, near, near, far, far, probs, mixed, w_attn, d_hidden, d_hidden_t, cosine, sine, ring_source)
-
-
-def back_pass(x_t, d_out, weights, extra, ring_sources, out_widths, identity, name):
+    )(query, own, own, near, near, far, far, probs, mixed, w_attn, d_hidden, d_hidden_t, cosine, sine, flip, ring_source)
+
+
+def back_pass(x_t, d_out, weights, extra, ring_sources, out_widths, costs, identity, name):
     amount, m, columns = d_out.shape
     width = x_t.shape[0]
     devices = lax.axis_size("dp")
@@ -604,8 +655,9 @@
     tiles = width // TILE
     per = columns // TILE
     total = tiles + amount * per
-    ring_shapes = [(source.shape[-2], source.shape[-1]) for source, _ in ring_sources]
     count = len(ring_sources)
+    shapes = [(source.shape[-2], source.shape[-1] // pieces) for source, _, pieces in ring_sources for _ in range(pieces)]
+    groups = [[index] for index in range(len(shapes))]
 
     def kernel(*refs):
         refs = list(refs)
@@ -618,12 +670,17 @@
         xt_ref, tile_ref, d_ref = take(3)
         w_refs = take(amount)
         extra_refs = take(2) if extra else None
-        sources = [ref if lead is None else ref.at[lead] for ref, (_, lead) in zip(take(count), ring_sources)]
+        sources = [ref if lead is None else ref.at[lead] for ref, (_, lead, _) in zip(take(count), ring_sources)]
         grad_ref, back_ref = take(2)
         extra_out = take(1)[0] if extra else None
         sums = take(count)
         sent, got, y_send, y_recv = take(4)
-        ring = Ring(devices, sources, sums, refs)
+        terms, goals = [], []
+        for source, goal, (array, _, pieces) in zip(sources, sums, ring_sources):
+            piece = array.shape[-1] // pieces
+            terms += [(source, number * piece, piece) for number in range(pieces)]
+            goals += [(goal, number * piece) for number in range(pieces)]
+        ring = Ring(devices, terms, goals, groups, refs)
         other = (ring.me, lax.rem(ring.side + 1, sides))
         step = pl.program_id(0)
 
@@ -653,7 +710,7 @@
         def _():
             grad_ref[0] = dot_nn(xt_ref[...], tile_ref[0]).astype(BF)
 
-        ring.pace(step, 0, total)
+        ring.pace(step, [(tiles, costs[0]), (amount * per, costs[1])])
 
         @pl.when(step == total - 1)
         def _():
@@ -686,8 +743,9 @@
         out_specs.append(pl.BlockSpec((m, TILE), lambda i: (0, early(i))))
         out_shape.append(jax.ShapeDtypeStruct((m, width), BF))
     specs += [pl.BlockSpec(memory_space=pl.ANY)] * count
-    operands += [source for source, _ in ring_sources]
-    for (rows, _), out_width in zip(ring_shapes, out_widths):
+    operands += [source for source, _, _ in ring_sources]
+    for (source, _, _), out_width in zip(ring_sources, out_widths):
+        rows = source.shape[-2]
         out_specs.append(single((rows, out_width)))
         out_shape.append(jax.ShapeDtypeStruct((rows, out_width), F32))
     dma = pltpu.SemaphoreType.DMA
@@ -702,7 +760,7 @@
             pltpu.VMEM((tiles, m, TILE), BF),
             dma((tiles,)),
             dma((tiles,)),
-            *Ring.scratch(devices, ring_shapes),
+            *Ring.scratch(devices, shapes),
         ],
         compiler_params=pltpu.CompilerParams(vmem_limit_bytes=VMEM, collective_id=identity, has_side_effects=True),
         cost_estimate=cost(4 * m * width * amount * columns, 6 * width * amount * columns),
@@ -710,32 +768,231 @@
     )(*operands)
 
 
-def ring_only(ring_sources, out_widths, identity):
-    devices = lax.axis_size("dp")
-    shapes = [source.shape[1:] for source in ring_sources]
-    count = len(shapes)
-
-    def kernel(*refs):
-        ring = Ring(devices, list(refs[:count]), list(refs[count : 2 * count]), refs[2 * count :])
-        ring.barrier()
-        ring.begin()
-
-        def one(stage, carry):
-            ring.stage(stage)
-            return carry
-
-        lax.fori_loop(0, ring.chips, one, 0)
-        ring.finish()
-
+def root_of(rows):
+    return lax.rsqrt(jnp.mean(rows * rows, axis=-1, keepdims=True) + EPS)
+
+
+def norm_grad(rows, gain, grad):
+    root = root_of(rows)
+    pushed = grad * gain
+    inner = jnp.mean(pushed * rows, axis=-1, keepdims=True)
+    return root * pushed - rows * (root * root * root * inner), jnp.sum(grad * rows * root, axis=0, keepdims=True)
+
+
+def first_norm(tokens, gain):
+    m, width = tokens.shape
+
+    def kernel(x_ref, g_ref, o_ref, t_ref):
+        rows = x_ref[...].astype(F32)
+        normed = (rows * root_of(rows) * g_ref[...]).astype(BF)
+        o_ref[...] = normed
+        t_ref[...] = normed.T
+
+    rows_spec = pl.BlockSpec((ROWS, width), lambda i: (i, 0))
     return pl.pallas_call(
         kernel,
-        out_shape=[jax.ShapeDtypeStruct((rows, out_width), F32) for (rows, _), out_width in zip(shapes, out_widths)],
-        in_specs=[pl.BlockSpec(memory_space=pl.ANY)] * count,
-        out_specs=[pl.BlockSpec(memory_space=pltpu.VMEM)] * count,
-        scratch_shapes=Ring.scratch(devices, shapes),
+        grid=(m // ROWS,),
+        out_shape=[jax.ShapeDtypeStruct((m, width), BF), jax.ShapeDtypeStruct((width, m), BF)],
+        in_specs=[rows_spec, whole_spec((1, width))],
+        out_specs=[rows_spec, pl.BlockSpec((width, ROWS), lambda i: (0, i))],
+        compiler_params=pltpu.CompilerParams(vmem_limit_bytes=VMEM),
+        cost_estimate=cost(8 * m * width, 6 * m * width),
+        name="first_norm",
+    )(tokens, gain)
+
+
+def out_norm(mixed, w_attn, place, tokens, gain, identity):
+    m, columns = mixed.shape
+    width = tokens.shape[1]
+    steps = m // ROWS
+    sides = lax.axis_size("tensor")
+
+    def kernel(x_ref, w_ref, r_ref, g_ref, hidden_ref, normed_ref, turned_ref, sent, got, send, recv):
+        step = pl.program_id(0)
+        other = (lax.axis_index("dp"), lax.rem(lax.axis_index("tensor") + 1, sides))
+
+        @pl.when(step == 0)
+        def _():
+            semaphore = pltpu.get_barrier_semaphore()
+            pl.semaphore_signal(semaphore, inc=1, device_id=other, device_id_type=MESH)
+            pl.semaphore_wait(semaphore, 1)
+
+        def across(which):
+            return pltpu.make_async_remote_copy(
+                src_ref=sent.at[which], dst_ref=got.at[which], send_sem=send.at[which], recv_sem=recv.at[which],
+                device_id=other, device_id_type=MESH,
+            )
+
+        @pl.when(step < steps)
+        def _():
+            sent[step] = dot_nt(x_ref[...], w_ref[...]).astype(BF)
+            across(step).start()
+
+        @pl.when(step >= steps)
+        def _():
+            which = step - steps
+            across(which).wait()
+            hidden = r_ref[...].astype(F32) + (sent[which].astype(F32) + got[which].astype(F32))
+            normed = (hidden * root_of(hidden) * g_ref[...]).astype(BF)
+            hidden_ref[...] = hidden
+            normed_ref[...] = normed
+            turned_ref[...] = normed.T
+
+    def late(i):
+        return jnp.maximum(i - steps, 0)
+
+    late_rows = pl.BlockSpec((ROWS, width), lambda i: (late(i), 0))
+    dma = pltpu.SemaphoreType.DMA
+    return pl.pallas_call(
+        kernel,
+        grid=(2 * steps,),
+        out_shape=[
+            jax.ShapeDtypeStruct((m, width), F32),
+            jax.ShapeDtypeStruct((m, width), BF),
+            jax.ShapeDtypeStruct((width, m), BF),
+        ],
+        in_specs=[
+            pl.BlockSpec((ROWS, columns), lambda i: (jnp.minimum(i, steps - 1), 0)),
+            pl.BlockSpec((width, columns), lambda i: (0, place), pipeline_mode=pl.Buffered(1)),
+            late_rows,
+            single((1, width)),
+        ],
+        out_specs=[late_rows, late_rows, pl.BlockSpec((width, ROWS), lambda i: (0, late(i)))],
+        scratch_shapes=[pltpu.VMEM((steps, ROWS, width), BF), pltpu.VMEM((steps, ROWS, width), BF), dma((steps,)), dma((steps,))],
         compiler_params=pltpu.CompilerParams(vmem_limit_bytes=VMEM, collective_id=identity, has_side_effects=True),
-        name="ring_sum",
-    )(*ring_sources)
+        cost_estimate=cost(2 * m * width * columns, 12 * m * width),
+        name="out_norm",
+    )(mixed, w_attn, tokens, gain)
+
+
+def hidden_grad(hidden, gain, grad, cotangent):
+    m, width = hidden.shape
+
+    def kernel(h_ref, g_ref, d_ref, y_ref, o_ref, low_ref, turned_ref, gain_ref):
+        change, gain_part = norm_grad(h_ref[...], g_ref[...], d_ref[...])
+        total = y_ref[...].astype(F32) + change
+        low = total.astype(BF)
+        o_ref[...] = total
+        low_ref[...] = low
+        turned_ref[...] = low.T
+
+        @pl.when(pl.program_id(0) == 0)
+        def _():
+            gain_ref[...] = gain_part
+
+        @pl.when(pl.program_id(0) > 0)
+        def _():
+            gain_ref[...] += gain_part
+
+    rows_spec = pl.BlockSpec((ROWS, width), lambda i: (i, 0))
+    return pl.pallas_call(
+        kernel,
+        grid=(m // ROWS,),
+        out_shape=[
+            jax.ShapeDtypeStruct((m, width), F32),
+            jax.ShapeDtypeStruct((m, width), BF),
+            jax.ShapeDtypeStruct((width, m), BF),
+            jax.ShapeDtypeStruct((1, width), F32),
+        ],
+        in_specs=[rows_spec, whole_spec((1, width)), rows_spec, rows_spec],
+        out_specs=[rows_spec, rows_spec, pl.BlockSpec((width, ROWS), lambda i: (0, i)), whole_spec((1, width))],
+        compiler_params=pltpu.CompilerParams(vmem_limit_bytes=VMEM),
+        cost_estimate=cost(16 * m * width, 18 * m * width),
+        name="hidden_grad",
+    )(hidden, gain, grad, cotangent)
+
+
+def last_pass(tokens, gain, grad, d_hidden, hidden, ffn_part, ffn_other, gain_ffn_grad, flip, qkv_part, lanes, identity):
+    m, width = tokens.shape
+    devices, rows, all_columns = qkv_part.shape
+    columns = all_columns // 3
+    chips = devices // 2
+    size = ROWS // 2
+    steps = m // size
+    total = steps + chips
+    names = 3
+
+    def kernel(x_ref, g_ref, dn_ref, dh_ref, h_ref, p_ref, o_ref, gf_ref, flip_ref, source, grad_ref, layer_ref, flipped_ref, q_ref, k_ref, v_ref, gains_ref, gain_sum, gain_source, *scratch):
+        step = pl.program_id(0)
+        ring = Ring(
+            devices, [(source, number * columns, columns) for number in range(names)], [(q_ref, 0), (k_ref, 0), (v_ref, 0)],
+            [[0], [1], [2]], scratch[: 3 * names + 5],
+        )
+        gain_ring = Ring(devices, [(gain_source, 0, lanes)], [(gains_ref, 0)], [[0]], scratch[3 * names + 5 :])
+
+        @pl.when(step == 0)
+        def _():
+            ring.barrier()
+            ring.begin()
+
+        @pl.when(step < steps)
+        def _():
+            change, gain_part = norm_grad(x_ref[...].astype(F32), g_ref[...], dn_ref[...])
+            grad_ref[...] = dh_ref[...] + change
+            layer_ref[...] = (h_ref[...] + (p_ref[...].astype(F32) + o_ref[...].astype(F32))).astype(BF)
+
+            @pl.when(step == 0)
+            def _():
+                gain_sum[...] = gain_part
+                flipped_ref[...] = flip_ref[...].T
+
+            @pl.when(step > 0)
+            def _():
+                gain_sum[...] += gain_part
+
+        @pl.when(step == steps - 1)
+        def _():
+            gain_source[...] = jnp.zeros_like(gain_source)
+            for device in range(devices):
+                span = slice(device * rows, (device + 1) * rows)
+                gain_source[device, :16, :rows] = jnp.broadcast_to(gain_sum[:, span], (16, rows)).astype(BF)
+                gain_source[device, 16:, :rows] = jnp.broadcast_to(gf_ref[:, span], (16, rows)).astype(BF)
+            gain_ring.begin()
+
+        ring.pace(step, [(steps, 3), (chips, 4)])
+
+        @pl.when(step >= steps)
+        def _():
+            gain_ring.run(step - steps, step - steps + 1)
+
+        @pl.when(step == total - 1)
+        def _():
+            ring.finish()
+            gain_ring.finish()
+
+    def early(i):
+        return jnp.minimum(i, steps - 1)
+
+    rows_spec = pl.BlockSpec((size, width), lambda i: (early(i), 0))
+    sums = jax.ShapeDtypeStruct((rows, columns), F32)
+    return pl.pallas_call(
+        kernel,
+        grid=(total,),
+        out_shape=[
+            jax.ShapeDtypeStruct((m, width), F32),
+            jax.ShapeDtypeStruct((m, width), BF),
+            jax.ShapeDtypeStruct((flip.shape[1], flip.shape[0]), F32),
+            sums, sums, sums,
+            jax.ShapeDtypeStruct((32, lanes), F32),
+        ],
+        in_specs=[
+            rows_spec, single((1, width)), rows_spec, rows_spec, rows_spec, rows_spec, rows_spec, single((1, width)),
+            single(flip.shape), pl.BlockSpec(memory_space=pl.ANY),
+        ],
+        out_specs=[
+            rows_spec, rows_spec, single((flip.shape[1], flip.shape[0])),
+            single(sums.shape), single(sums.shape), single(sums.shape), single((32, lanes)),
+        ],
+        scratch_shapes=[
+            pltpu.VMEM((1, width), F32),
+            pltpu.VMEM((devices, 32, lanes), BF),
+            *Ring.scratch(devices, [(rows, columns)] * names),
+            *Ring.scratch(devices, [(32, lanes)]),
+        ],
+        compiler_params=pltpu.CompilerParams(vmem_limit_bytes=VMEM, collective_id=identity, has_side_effects=True),
+        cost_estimate=cost(20 * m * width, 24 * m * width),
+        name="last_pass",
+    )(tokens, gain, grad, d_hidden, hidden, ffn_part, ffn_other, gain_ffn_grad, flip, qkv_part)
 
 
 def feed(x, dy, w, tiles):
@@ -768,21 +1025,6 @@
         cost_estimate=cost(6 * m * k * tiles * TILE, 6 * (m + k) * tiles * TILE, m * tiles * TILE),
         name="feed",
     )(x, dy, w, w, w)
-
-
-def norm_root(rows):
-    return lax.rsqrt(jnp.mean(rows * rows, axis=-1, keepdims=True) + EPS)
-
-
-def norm_back(rows, root, gain, grad):
-    pushed = grad * gain
-    inner = jnp.mean(pushed * rows, axis=-1, keepdims=True)
-    d_rows = root * pushed - rows * (root * root * root * inner)
-    return d_rows, jnp.sum(grad * rows * root, axis=0)
-
-
-def pair_sum(part, route):
-    return part.astype(F32) + lax.ppermute(part, "tensor", route).astype(F32)
 
 
 def shards(tokens, positions, attn_gain, w_query, w_key, w_value, w_out, ffn_gain, w_gate, w_up, w_down, cotangent):
@@ -820,56 +1062,45 @@
     cosine = jnp.concatenate([cosine_half, cosine_half], axis=1)
     sine = jnp.concatenate([-sine_half, sine_half], axis=1)
 
-    rows = tokens.astype(F32)
-    root_attn = norm_root(rows)
-    normed_attn = (rows * root_attn * gain_attn).astype(BF)
-    qkv = project(normed_attn, w_attn, cosine, sine, heads)
-    own_kv = qkv[:, head_columns:]
+    normed_attn, normed_attn_t = first_norm(tokens, gain_attn)
+    query, own_kv = project(normed_attn, w_attn, cosine, sine, heads)
     far = lax.ppermute(own_kv, "dp", [(i - 2, i) for i in range(2, devices)])
     near = lax.ppermute(jnp.where(core == 0, own_kv, far), "dp", swap_route(devices))
-    mixed, probs = attend(qkv, near, far, positions[None, :], heads)
-    hidden = rows + pair_sum(matmul_nt([(mixed, w_attn, 3)], "out_project"), flip)
-
-    root_ffn = norm_root(hidden)
-    normed_ffn = (hidden * root_ffn * gain_ffn).astype(BF)
+    mixed, probs = attend(query, own_kv, near, far, positions[None, :], heads)
+    hidden, normed_ffn, normed_ffn_t = out_norm(mixed, w_attn, 3, tokens, gain_ffn, 5)
+
     activated, d_both = feed(normed_ffn, cotangent, w_ffn, tiles)
     down_part = matmul_nn(cotangent.T, activated, 0, tiles, "down_grad").reshape(devices, own_rows, padded)
     both_part, d_normed_ffn, ffn_part, down_grad = back_pass(
-        normed_ffn.T, d_both, w_ffn, (activated, w_ffn, 2), [(down_part, None)], [hidden_units], 1, "ffn_back"
+        normed_ffn_t, d_both, w_ffn, (activated, w_ffn, 2), [(down_part, None, 2)], [padded], (13, 4), 1, "ffn_back"
     )
     both_part = both_part.reshape(2, devices, own_rows, padded)
-    layer_out = (hidden + pair_sum(ffn_part, flip)).astype(BF)
-    d_hidden_norm, gain_ffn_grad = norm_back(hidden, root_ffn, gain_ffn, d_normed_ffn)
-    d_hidden = cotangent.astype(F32) + d_hidden_norm
-    d_hidden_low = d_hidden.astype(BF)
-
-    d_qkv, out_part, gate_grad = attend_back(
-        qkv, near, far, probs, mixed, w_attn, d_hidden_low, d_hidden_low.T, cosine, sine, both_part, heads, hidden_units, 2
+    ffn_other = lax.ppermute(ffn_part, "tensor", flip)
+    d_hidden, d_hidden_low, d_hidden_t, gain_ffn_grad = hidden_grad(hidden, gain_ffn, d_normed_ffn, cotangent)
+
+    d_qkv, out_part, gate_grad, w_down_grad = attend_back(
+        query, own_kv, near, far, probs, mixed, w_attn, d_hidden_low, d_hidden_t, cosine, sine, down_grad, both_part, heads, hidden_units, 2
     )
     qkv_part, d_normed_attn, up_grad, out_grad = back_pass(
-        normed_attn.T, d_qkv[None], w_attn, None,
-        [(both_part, 1), (out_part.reshape(devices, own_rows, head_columns), None)], [hidden_units, head_columns], 3, "qkv_back",
+        normed_attn_t, d_qkv[None], w_attn, None,
+        [(both_part, 1, 2), (out_part.reshape(devices, own_rows, head_columns), None, 1)], [hidden_units, head_columns], (4, 3), 3, "qkv_back",
     )
-    d_rows, gain_attn_grad = norm_back(rows, root_attn, gain_attn, d_normed_attn)
-    tokens_grad = d_hidden + d_rows
-    gain_part = jnp.zeros((devices, 32, lanes), BF)
-    gain_part = gain_part.at[:, 0, :own_rows].set(gain_attn_grad.reshape(devices, own_rows).astype(BF))
-    gain_part = gain_part.at[:, 16, :own_rows].set(gain_ffn_grad.reshape(devices, own_rows).astype(BF))
-    qkv_grad, gain_grads = ring_only(
-        [qkv_part.reshape(devices, own_rows, 3 * head_columns), gain_part], [3 * head_columns, lanes], 4
+    tokens_grad, layer_out, w_out_grad, query_grad, key_grad, value_grad, gain_grads = last_pass(
+        tokens, gain_attn, d_normed_attn, d_hidden, hidden, ffn_part, ffn_other, gain_ffn_grad, out_grad,
+        qkv_part.reshape(devices, own_rows, 3 * head_columns), lanes, 4,
     )
     return (
         layer_out,
         tokens_grad,
         gain_grads[0, :own_rows],
-        qkv_grad[:, :head_columns],
-        qkv_grad[:, head_columns : 2 * head_columns],
-        qkv_grad[:, 2 * head_columns :],
-        out_grad.T,
+        query_grad,
+        key_grad,
+        value_grad,
+        w_out_grad,
         gain_grads[16, :own_rows],
         gate_grad,
         up_grad,
-        down_grad.T,
+        w_down_grad,
     )
 
 

time: 829 us -> 748 us (0.902)
  local copies, waits for them, and re-layouts: 75.4 us -> 25.5 us
  Pallas kernels: 547 us -> 588 us
  waiting for transfers between devices: 134 us -> 103 us
  other arithmetic: 39.4 us -> 10.6 us
    pallas_call x3 -> x5, Pallas kernels: 97.1 us -> 155 us  [the longest x1 71.3 us: last_pass(): pl.pallas_call(kernel, grid=(total,), out_shape=[jax.ShapeDtypeStruct((m,...]
    ppermute x2 -> x1, waiting for transfers between devices: 40.4 us -> 0.01 us  [shards(): ffn_other = lax.ppermute(ffn_part, 'tensor', flip)]
    pallas_call x2, Pallas kernels: 190 us -> 171 us  [back_pass(): pl.pallas_call(kernel, grid=(total,), out_shape=out_shape, in_specs=specs...]
    pallas_call x4 -> x0, local copies, waits for them, and re-layouts: 18.6 us -> none  [the longest x3 14.7 us: back_pass(): pl.pallas_call(kernel, grid=(total,), out_shape=out_shape, in_specs=specs...]
    convert_element_type x5 -> x0, local copies, waits for them, and re-layouts: 12.7 us -> none  [the longest x1 4.13 us: shards(): normed_attn = (rows * root_attn * gain_attn).astype(BF)]
    reduce_sum x4 -> x0, other arithmetic: 11.8 us -> none  [the longest x2 8.66 us: norm_back(): return (d_rows, jnp.sum(grad * rows * root, axis=0))]
    all_gather x1, waiting for transfers between devices: 0.01 us -> 11.8 us  [shards(): w_ffn = lax.all_gather(ffn_pack, 'dp', axis=0, tiled=True)]
    unnamed x64 -> x46, local copies, waits for them, and re-layouts: 34.8 us -> 23.4 us
  transfers between devices with their start and end apart: 5 -> 4, of which waited for: 3 -> 2; matrix products, arithmetic and copies ran while one was open for 8% -> 2% of each run, Pallas kernels for 39% -> 41%
where the time goes in v3:
time: 748 us; the launch traced here: 747 us
  Pallas kernels  588 us (79%)
  waiting for transfers between devices  103 us (14%)
  local copies, waits for them, and re-layouts  25.5 us (3%)
  between operations  14.3 us (2%)
  other arithmetic  10.6 us (1%)
    pallas_call x2, Pallas kernels, back_pass(): pl.pallas_call(kernel, grid=(total,), out_shape=out_shape, in_specs=specs...  171 us
    pallas_call x1, Pallas kernels, attend_back(): pl.pallas_call(kernel, grid=(heads,), out_shape=[jax.ShapeDtypeStruct((m,...  115 us
    ppermute x1, waiting for transfers between devices, shards(): far = lax.ppermute(own_kv, 'dp', [(i - 2, i) for i in range(2, devices)])  90.8 us
    pallas_call x1, Pallas kernels, ring_gather(): pl.pallas_call(functools.partial(gather_kernel, devices, chunks, len(arra...  88 us
    pallas_call x1, Pallas kernels, last_pass(): pl.pallas_call(kernel, grid=(total,), out_shape=[jax.ShapeDtypeStruct((m,...  71.3 us
    pallas_call x1, Pallas kernels, out_norm(): pl.pallas_call(kernel, grid=(2 * steps,), out_shape=[jax.ShapeDtypeStruct...  53.9 us
    pallas_call x1, Pallas kernels, feed(): pl.pallas_call(kernel, grid=(tiles,), out_shape=[jax.ShapeDtypeStruct((m,...  26.5 us
    unnamed x46, local copies, waits for them, and re-layouts  23.4 us
  transfers between devices with their start and end apart: 4, of which 2 were waited for; matrix products, arithmetic and copies ran while one was open for 2% of the time, Pallas kernels for 41%

profile of v3, /device:TPU:0, one launch (start us, length us, event | category | flops | bytes accessed | tf_op | source)
XLA Modules:
  0.0 746.7 jit_solution(2040601775257964692)
XLA Ops:
  10.6 2.1 pad_maximum_fusion.refs_0_
  12.6 88.0 %ring_gather.1 = (bf16[2048,4096]{1,0:T(8,128)(2,1)}, bf16[512,128]{1,0:T(8,128)(2,1)}) custom-call(bf16[128,4096]{1,0:T(8,128)(2,1)} %pad_maximum_fusion.refs_0_, bf16[32,128]{1,0:T(8,128)(2,1)} %copy-done.12), custom_call_target="tpu_custom_call" | custom-call | tf_op jit(solution)/shard_map/ring_gather/pallas_call | solution.py:154
  100.6 1.4 fusion.5
  104.1 4.6 first_norm.1
  110.7 15.9 %project.1 = (bf16[512,1024]{1,0:T(8,128)(2,1)}, bf16[512,2048]{1,0:T(8,128)(2,1)}) custom-call(bf16[512,2048]{1,0:T(8,128)(2,1)} %get-tuple-element.78.x_ref, bf16[2048,4096]{1,0:T(8,128)(2,1)} %get-tuple-element.79.w_ref.refs_3_, f32[512,128]{1,0:T(8,128)} %get-tuple-element.131.c_ref, f32[512,128]{1,0:T(8,128)} %get-tuple-element.132.s_ref), custom_call_target="tpu_custom_call" | custom-call | flops 6442450944 | bytes 17825792 | tf_op jit(solution)/shard_map/project/pallas_call | solution.py:426
  126.7 3.8 collective-permute-start
  130.5 90.8 %collective-permute-done.k2.v2 = bf16[512,2048]{1,0:T(8,128)(2,1)S(1)} collective-permute-done((bf16[512,2048]{1,0:T(8,128)(2,1)}, bf16[512,2048]{1,0:T(8,128)(2,1)S(1)}, u32[]{:S(2)}, u32[]{:S(2)}) %collective-permute-start) | collective-permute-done | bytes 2097184 | tf_op jit(solution)/shard_map/ppermute | solution.py:1067
  221.3 3.9 broadcast_select_fusion
  225.2 4.1 copy.29
  230.0 20.5 %attend.1 = (bf16[512,1024]{1,0:T(8,128)(2,1)}, bf16[8,2,1280,256]{3,2,1,0:T(8,128)(2,1)}) custom-call(bf16[512,1024]{1,0:T(8,128)(2,1)} %get-tuple-element.80.q_ref, bf16[512,2048]{1,0:T(8,128)(2,1)} %get-tuple-element.81.k0.v0, bf16[512,2048]{1,0:T(8,128)(2,1)} %get-tuple-element.81.k0.v0, bf16[512,2048]{1,0:T(8,128)(2,1)} %collective-permute-done.1.k1.v1, ...), custom_call_target="tpu_custom_call" | custom-call | flops 5368709120 | bytes 10485760 | tf_op jit(solution)/shard_map/attend/pallas_call | solution.py:478
  250.5 53.9 %out_norm.1 = (f32[512,2048]{1,0:T(8,128)}, bf16[512,2048]{1,0:T(8,128)(2,1)}, bf16[2048,512]{1,0:T(8,128)(2,1)}) custom-call(bf16[512,1024]{1,0:T(8,128)(2,1)} %get-tuple-element.83.x_ref, bf16[2048,4096]{1,0:T(8,128)(2,1)} %get-tuple-element.79.w_ref.refs_3_, bf16[512,2048]{1,0:T(8,128)(2,1)} %x_ref.3, f32[1,2048]{1,0:T(1,128)} %bitcast.30), custom_call_target="tpu_custom_call" | custom-call | flops 2147483648 | bytes 12582912 | tf_op jit(solution)/shard_map/out_norm/pallas_call | solution.py:846
  304.4 11.8 %all-gather.2.cloned.1.call-done.g_ref.u_ref.d_ref.refs_3_.refs_4_.refs_6_ = bf16[2048,8448]{1,0:T(8,128)(2,1)} async-done(((bf16[128,8448]{1,0:T(8,128)(2,1)}), bf16[2048,8448]{1,0:T(8,128)(2,1)}) %all-gather.2.cloned.1.call-update) | async-done | bytes 34603024 | tf_op jit(solution)/shard_map/all_gather | solution.py:1054
  316.2 26.5 %feed.1 = (bf16[512,2816]{1,0:T(8,128)(2,1)}, bf16[2,512,2816]{2,1,0:T(8,128)(2,1)}) custom-call(bf16[512,2048]{1,0:T(8,128)(2,1)} %get-tuple-element.86.x_ref, bf16[512,2048]{1,0:T(8,128)(2,1)} %y_ref.1, bf16[2048,8448]{1,0:T(8,128)(2,1)} %all-gather.2.cloned.1.call-done.g_ref.u_ref.d_ref.refs_3_.refs_4_.refs_6_, ...), custom_call_target="tpu_custom_call" | custom-call | flops 17716740096 | bytes 43253760 | tf_op jit(solution)/shard_map/feed/pallas_call | solution.py:1012
  342.6 13.1 %down_grad.1 = bf16[2048,2816]{1,0:T(8,128)(2,1)} custom-call(bf16[2048,512]{1,0:T(8,128)(2,1)} %bitcast.26, bf16[512,2816]{1,0:T(8,128)(2,1)} %get-tuple-element.89.w_ref.refs_5_), custom_call_target="tpu_custom_call" | custom-call | flops 5905580032 | bytes 16515072 | tf_op jit(solution)/shard_map/down_grad/pallas_call | solution.py:350
  355.8 80.9 %ffn_back.1 = (bf16[2,2048,2816]{2,1,0:T(8,128)(2,1)}, f32[512,2048]{1,0:T(8,128)}, bf16[512,2048]{1,0:T(8,128)(2,1)}, f32[128,2816]{1,0:T(8,128)}) custom-call(bf16[2048,512]{1,0:T(8,128)(2,1)} %get-tuple-element.85.refs_0_, bf16[2,512,2816]{2,1,0:T(8,128)(2,1)} %get-tuple-element.88.refs_1_.refs_2_, ...), custom_call_target="tpu_custom_call" | custom-call | flops 23622320128 | bytes 69206016 | tf_op jit(solution)/shard_map/ffn_back/pallas_call | solution.py:752
  436.7 1.5 collective-permute-start.2
  438.1 8.8 %hidden_grad.1 = (f32[512,2048]{1,0:T(8,128)}, bf16[512,2048]{1,0:T(8,128)(2,1)}, bf16[2048,512]{1,0:T(8,128)(2,1)}, f32[1,2048]{1,0:T(1,128)}) custom-call(f32[512,2048]{1,0:T(8,128)} %get-tuple-element.84.h_ref, f32[1,2048]{1,0:T(1,128)} %bitcast.31, f32[512,2048]{1,0:T(8,128)} %get-tuple-element.90.d_ref, bf16[512,2048]{1,0:T(8,128)(2,1)} %y_ref.1), custom_call_target="tpu_custom_call" | custom-call | flops 16777216 | bytes 18874368 | tf_op jit(solution)/shard_map/hidden_grad/pallas_call | solution.py:888
  447.0 114.7 %attend_back.1 = (bf16[512,3072]{1,0:T(8,128)(2,1)}, bf16[2048,1024]{1,0:T(8,128)(2,1)}, f32[128,2752]{1,0:T(8,128)}, f32[2752,128]{1,0:T(8,128)}) custom-call(bf16[512,1024]{1,0:T(8,128)(2,1)} %get-tuple-element.80.q_ref, bf16[512,2048]{1,0:T(8,128)(2,1)} %get-tuple-element.81.k0.v0, bf16[512,2048]{1,0:T(8,128)(2,1)} %get-tuple-element.81.k0.v0, ...), custom_call_target="tpu_custom_call" | custom-call | flops 10737418240 | bytes 10485760 | tf_op jit(solution)/shard_map/attend_back/pallas_call | solution.py:611
  561.7 90.1 %qkv_back.1 = (bf16[1,2048,3072]{2,1,0:T(8,128)(2,1)}, f32[512,2048]{1,0:T(8,128)}, f32[128,2752]{1,0:T(8,128)}, f32[128,1024]{1,0:T(8,128)}) custom-call(bf16[2048,512]{1,0:T(8,128)(2,1)} %get-tuple-element.77.refs_0_, bf16[1,512,3072]{2,1,0:T(8,128)(2,1)} %bitcast.21, bf16[1,512,3072]{2,1,0:T(8,128)(2,1)} %bitcast.22, ...), custom_call_target="tpu_custom_call" | custom-call | flops 12884901888 | bytes 37748736 | tf_op jit(solution)/shard_map/qkv_back/pallas_call | solution.py:752
  651.8 3.0 copy.31
  654.8 1.5 copy.30
  657.6 71.3 %last_pass.1 = (f32[512,2048]{1,0:T(8,128)}, bf16[512,2048]{1,0:T(8,128)(2,1)}, f32[1024,128]{1,0:T(8,128)}, f32[128,1024]{1,0:T(8,128)}, f32[128,1024]{1,0:T(8,...) custom-call(bf16[512,2048]{1,0:T(8,128)(2,1)} %x_ref.3, f32[1,2048]{1,0:T(1,128)} %bitcast.29, ...), custom_call_target="tpu_custom_call" | custom-call | flops 20971520 | bytes 25165824 | tf_op jit(solution)/shard_map/last_pass/pallas_call | solution.py:968
  730.2 3.3 copy.44
  733.5 2.0 copy.45
  (56 shorter events, 14.8 us)
Async XLA Ops:
  7.2 2.7 copy-start.5
  7.2 3.0 copy-start.6
  7.2 309.0 %all-gather.2.cloned.1.call-start = ((), (), s32[]{:S(2)}) async-start(), calls=%async_computation | async-start | bytes 36765696 | tf_op jit(solution)/shard_map/all_gather | solution.py:1054
  8.4 2.1 copy-start.14
  8.4 2.1 copy-start.15
  8.5 2.1 copy-start.11
  10.6 2.1 copy-start.12
  102.1 0.7 copy-start.13
  126.7 94.7 %collective-permute-start = (bf16[512,2048]{1,0:T(8,128)(2,1)}, bf16[512,2048]{1,0:T(8,128)(2,1)S(1)}, u32[]{:S(2)}, u32[]{:S(2)}) collective-permute-start(bf16[512,2048]{1,0:T(8,128)(2,1)} %get-tuple-element.81.k0.v0), channel_id=1, source_target_pairs={{0,4},{2,6},{4,8},{6,10},{8,12},{10,14},{12,16},{14,18},{16,20},{1... | collective-permute-start | bytes 6291464 | tf_op jit(solution)/shard_map/ppermute | solution.py:1067
  221.3 3.9 copy-start
  225.2 4.7 collective-permute-start.1
  436.7 219.7 %collective-permute-start.2 = (bf16[512,2048]{1,0:T(8,128)(2,1)}, bf16[512,2048]{1,0:T(8,128)(2,1)S(1)}, u32[]{:S(2)}, u32[]{:S(2)}) collective-permute-start(bf16[512,2048]{1,0:T(8,128)(2,1)} %get-tuple-element.99.p_ref), channel_id=1, source_target_pairs={{0,1},{1,0},{2,3},{3,2},{4,5},{5,4},{6,7},{7,6},{8,9},{9,8},{10,11... | collective-permute-start | bytes 6291464 | tf_op jit(solution)/shard_map/ppermute | solution.py:1078
  651.8 3.0 copy-start.3
  656.3 1.3 copy-start.2
  730.2 3.3 copy-start.1
  733.5 2.0 copy-start.10
  733.5 2.8 copy-start.9
  733.5 3.6 copy-start.8
  735.5 2.4 copy-start.7
  735.5 3.2 copy-start.4
Sparse Core Ops, SparseCore 0:
  102.2 213.9 all-gather.1

commit v4 on v3

--- a/solution.py
+++ b/solution.py
@@ -26,6 +26,10 @@
     return pl.BlockSpec(shape, lambda i: (0,) * len(shape))
 
 
+def single(shape):
+    return pl.BlockSpec(shape, lambda i: (0,) * len(shape), pipeline_mode=pl.Buffered(1))
+
+
 def cost(flops, nbytes, special=0):
     return pl.CostEstimate(flops=flops, bytes_accessed=nbytes, transcendentals=special)
 
@@ -42,14 +46,10 @@
     return (1 - column) * row + column * (chips - 1 - row)
 
 
-def swap_route(devices):
-    return [(i, i ^ 1) for i in range(devices)]
-
-
 def gather_kernel(devices, chunks, count, *refs):
-    ins = refs[:count]
-    outs = refs[count : 2 * count]
-    local_sem, a_send, a_recv, b_send, b_recv, c_send, c_recv = refs[2 * count :]
+    ins, tokens = refs[:count], refs[count]
+    outs, near, far = refs[count + 1 : 2 * count + 1], refs[2 * count + 1], refs[2 * count + 2]
+    local_sem, a_send, a_recv, b_send, b_recv, c_send, c_recv, far_send, far_recv, near_send, near_recv = refs[2 * count + 3 :]
     chips = devices // 2
     me = lax.axis_index("dp")
     side = lax.axis_index("tensor")
@@ -62,10 +62,12 @@
     right = device(place + 1)
     left = device(place - 1)
     partner = me + 1 - 2 * core
+    across = lax.rem(side + 1, lax.axis_size("tensor"))
+    later, before = lax.rem(me + 2, devices), lax.rem(me + devices - 2, devices)
     barrier = pltpu.get_barrier_semaphore()
-    for other in (right, left, partner):
-        pl.semaphore_signal(barrier, inc=1, device_id=(other, side), device_id_type=MESH)
-    pl.semaphore_wait(barrier, 3)
+    for other in ((right, side), (left, side), (partner, side), (me, across), (later, side), (before, side)):
+        pl.semaphore_signal(barrier, inc=1, device_id=other, device_id_type=MESH)
+    pl.semaphore_wait(barrier, 6)
 
     pieces = []
     for index, parts in enumerate(chunks):
@@ -81,17 +83,47 @@
             start = pl.multiple_of(start, 16)
         return ref.at[pl.ds(start, rows // 2), pl.ds(column, width)]
 
+    def described(source, target, send, recv, other):
+        return pltpu.make_async_remote_copy(
+            src_ref=source, dst_ref=target, send_sem=send, recv_sem=recv, device_id=other, device_id_type=MESH
+        )
+
     def remote(source, target, send, recv, other):
-        copy = pltpu.make_async_remote_copy(
-            src_ref=source,
-            dst_ref=target,
-            send_sem=send,
-            recv_sem=recv,
-            device_id=(other, side),
-            device_id_type=MESH,
-        )
+        copy = described(source, target, send, recv, (other, side))
         copy.start()
         return copy
+
+    span = tokens.shape[0] // 2
+
+    def half_rows(ref, which):
+        return ref.at[pl.ds(pl.multiple_of(which * span, span), span)]
+
+    far_copy = described(half_rows(tokens, side), half_rows(far, side), far_send.at[0], far_recv.at[0], (later, side))
+    cross_copy = described(half_rows(far, side), half_rows(far, side), far_send.at[1], far_recv.at[1], (me, across))
+    own_near = [described(half_rows(tokens, which), half_rows(near, which), near_send.at[which], near_recv.at[which], (partner, side)) for which in range(2)]
+    far_near = [described(half_rows(far, which), half_rows(near, which), near_send.at[slot], near_recv.at[slot], (partner, side)) for slot, which in enumerate((side, across))]
+
+    @pl.when(me < devices - 2)
+    def _():
+        far_copy.start()
+
+    @pl.when(core == 0)
+    def _():
+        for copy in own_near:
+            copy.start()
+
+    def pass_on(slot):
+        @pl.when(me >= 2)
+        def _():
+            if slot == 0:
+                far_copy.wait_recv()
+                cross_copy.start()
+            else:
+                cross_copy.wait_recv()
+
+            @pl.when(core == 1)
+            def _():
+                far_near[slot].start()
 
     local = []
     for index in range(count):
@@ -136,6 +168,10 @@
                 )
             if sent:
                 forward[number, hop + 1] = tuple(sent)
+        if hop == hops // 2:
+            pass_on(0)
+        if hop == hops - 2:
+            pass_on(1)
     for copy in local:
         copy.wait()
     for pair in forward.values():
@@ -144,8 +180,31 @@
     for copy in partner_copies:
         copy.wait()
 
-
-def ring_gather(arrays, chunks, identity):
+    @pl.when(me < devices - 2)
+    def _():
+        far_copy.wait_send()
+
+    @pl.when(me >= 2)
+    def _():
+        cross_copy.wait_send()
+
+        @pl.when(core == 1)
+        def _():
+            for copy in far_near:
+                copy.wait_send()
+
+    @pl.when(core == 0)
+    def _():
+        for copy in own_near:
+            copy.wait_send()
+
+    @pl.when((core == 1) | (me >= 2))
+    def _():
+        for copy in own_near:
+            copy.wait_recv()
+
+
+def ring_gather(arrays, chunks, tokens, identity):
     devices = lax.axis_size("dp")
     hops = devices // 2 - 1
     pieces = sum(chunks)
@@ -153,9 +212,10 @@
     any_space = pl.BlockSpec(memory_space=pl.ANY)
     return pl.pallas_call(
         functools.partial(gather_kernel, devices, chunks, len(arrays)),
-        out_shape=[jax.ShapeDtypeStruct((a.shape[0] * devices, a.shape[1]), a.dtype) for a in arrays],
-        in_specs=[any_space] * len(arrays),
-        out_specs=[any_space] * len(arrays),
+        out_shape=[jax.ShapeDtypeStruct((a.shape[0] * devices, a.shape[1]), a.dtype) for a in arrays]
+        + [jax.ShapeDtypeStruct(tokens.shape, tokens.dtype)] * 2,
+        in_specs=[any_space] * (len(arrays) + 1),
+        out_specs=[any_space] * (len(arrays) + 2),
         scratch_shapes=[
             dma((len(arrays),)),
             dma((pieces, hops)),
@@ -164,10 +224,14 @@
             dma((pieces, hops)),
             dma((pieces, hops + 1, 2)),
             dma((pieces, hops + 1, 2)),
+            dma((2,)),
+            dma((2,)),
+            dma((2,)),
+            dma((2,)),
         ],
         compiler_params=pltpu.CompilerParams(collective_id=identity, has_side_effects=True),
         name="ring_gather",
-    )(*arrays)
+    )(*arrays, tokens)
 
 
 class Ring:
@@ -359,36 +423,6 @@
     )(x, w)
 
 
-def matmul_nt(pairs, name):
-    m = pairs[0][0].shape[0]
-    n = pairs[0][1].shape[0]
-    amount = len(pairs)
-
-    def kernel(*refs):
-        total = None
-        for index in range(amount):
-            part = dot_nt(refs[2 * index][...], refs[2 * index + 1][...])
-            total = part if total is None else total + part
-        refs[-1][...] = total.astype(BF)
-
-    specs, operands, width = [], [], 0
-    for x, w, where in pairs:
-        specs.append(whole_spec(x.shape))
-        specs.append(pl.BlockSpec((TILE, x.shape[1]), functools.partial(lambda where, i: (i, where), where)))
-        operands += [x, w]
-        width += x.shape[1]
-    return pl.pallas_call(
-        kernel,
-        grid=(n // TILE,),
-        out_shape=jax.ShapeDtypeStruct((m, n), BF),
-        in_specs=specs,
-        out_specs=pl.BlockSpec((m, TILE), lambda i: (0, i)),
-        compiler_params=pltpu.CompilerParams(vmem_limit_bytes=VMEM),
-        cost_estimate=cost(2 * m * n * width, 2 * (m * width + n * width + m * n)),
-        name=name,
-    )(*operands)
-
-
 def turned(block, cosine, sine, back):
     other = pltpu.roll(block, E // 2, 1)
     if back:
@@ -396,59 +430,53 @@
     return block * cosine + other * sine
 
 
-def project(x, w, cosine, sine, heads):
+def project(x, w, cosine, sine, own, heads):
     m, k = x.shape
     per = TILE // E
-    steps = 3 * heads // per
-    rotated = 2 * heads // per
+    some = heads // per
 
     def kernel(x_ref, w_ref, c_ref, s_ref, q_ref, kv_ref):
         step = pl.program_id(0)
-        made = dot_nn(x_ref[...], w_ref[...])
-
-        def rotate_to(ref):
+
+        def rotate_to(ref, made, rows):
             for part in range(per):
                 piece = slice(part * E, (part + 1) * E)
-                ref[:, piece] = turned(made[:, piece], c_ref[...], s_ref[...], False).astype(BF)
-
-        @pl.when(step < rotated // 2)
-        def _():
-            rotate_to(q_ref)
-
-        @pl.when((step >= rotated // 2) & (step < rotated))
-        def _():
-            rotate_to(kv_ref)
-
-        @pl.when(step >= rotated)
-        def _():
-            kv_ref[...] = made.astype(BF)
+                ref[:, piece] = turned(made[:, piece], c_ref[rows, :], s_ref[rows, :], False).astype(BF)
+
+        @pl.when(step < some)
+        def _():
+            rows = slice(m - own, m)
+            rotate_to(q_ref, dot_nn(x_ref[rows, :], w_ref[...]), rows)
+
+        @pl.when((step >= some) & (step < 2 * some))
+        def _():
+            rotate_to(kv_ref, dot_nn(x_ref[...], w_ref[...]), slice(0, m))
+
+        @pl.when(step >= 2 * some)
+        def _():
+            kv_ref[...] = dot_nn(x_ref[...], w_ref[...]).astype(BF)
 
     return pl.pallas_call(
         kernel,
-        grid=(steps,),
-        out_shape=[jax.ShapeDtypeStruct((m, heads * E), BF), jax.ShapeDtypeStruct((m, 2 * heads * E), BF)],
-        in_specs=[
-            whole_spec((m, k)),
-            pl.BlockSpec((k, TILE), lambda i: (0, i)),
-            whole_spec((m, E)),
-            whole_spec((m, E)),
-        ],
+        grid=(3 * some,),
+        out_shape=[jax.ShapeDtypeStruct((own, heads * E), BF), jax.ShapeDtypeStruct((m, 2 * heads * E), BF)],
+        in_specs=[single((m, k)), pl.BlockSpec((k, TILE), lambda i: (0, i)), single((m, E)), single((m, E))],
         out_specs=[
-            pl.BlockSpec((m, TILE), lambda i: (0, jnp.minimum(i, rotated // 2 - 1))),
-            pl.BlockSpec((m, TILE), lambda i: (0, jnp.maximum(i - rotated // 2, 0))),
+            pl.BlockSpec((own, TILE), lambda i: (0, jnp.minimum(i, some - 1))),
+            pl.BlockSpec((m, TILE), lambda i: (0, jnp.maximum(i - some, 0))),
         ],
         compiler_params=pltpu.CompilerParams(vmem_limit_bytes=VMEM),
-        cost_estimate=cost(2 * m * k * steps * TILE, 2 * (m * k + (m + k) * steps * TILE)),
+        cost_estimate=cost(2 * (own + 2 * m) * k * heads * E, 2 * (m * k + 3 * (m + k) * heads * E)),
         name="project",
     )(x, w, cosine, sine)
 
 
-def attend(query, own, near, far, places, heads):
+def attend(query, kv, places, heads):
     m = query.shape[0]
     blocks = m // QB
     factor = E ** (-0.5) * LOG2E
 
-    def kernel(q_ref, k0, v0, k1, v1, k2, v2, p_ref, o_ref, probs_ref, bias):
+    def kernel(q_ref, k_ref, v_ref, p_ref, o_ref, probs_ref, bias):
         @pl.when(pl.program_id(0) == 0)
         def _():
             for block in range(blocks):
@@ -458,12 +486,10 @@
                 allowed = (key <= query + WINDOW) & (key > query) & (key >= query + WINDOW - place)
                 bias[block] = jnp.where(allowed, 0.0, -1e30)
 
-        keys = jnp.concatenate([k2[...], k1[...], k0[...]], axis=0)
-        values = jnp.concatenate([v2[...], v1[...], v0[...]], axis=0)
-        values_t = values.T
+        values_t = v_ref[...].T
         for block in range(blocks):
             span = slice(block * QB, block * QB + KB)
-            scores = dot_nt(keys[span], q_ref[block * QB : (block + 1) * QB, :]) * factor + bias[block]
+            scores = dot_nt(k_ref[span, :], q_ref[block * QB : (block + 1) * QB, :]) * factor + bias[block]
             largest = jnp.max(scores, axis=0, keepdims=True)
             grown = jnp.exp2(scores - largest)
             inverse = 1.0 / jnp.sum(grown, axis=0, keepdims=True)
@@ -472,8 +498,8 @@
             mixed_t = dot_nn(values_t[:, span], probs)
             o_ref[block * QB : (block + 1) * QB, :] = mixed_t.T.astype(BF)
 
-    def head(offset):
-        return pl.BlockSpec((m, E), lambda i: (0, i + offset))
+    head = pl.BlockSpec((m, E), lambda i: (0, i))
+    reach = kv.shape[0]
 
     return pl.pallas_call(
         kernel,
@@ -482,20 +508,21 @@
             jax.ShapeDtypeStruct((m, heads * E), BF),
             jax.ShapeDtypeStruct((heads, blocks, KB, QB), BF),
         ],
-        in_specs=[head(0), head(0), head(heads), head(0), head(heads), head(0), head(heads), whole_spec((1, m))],
-        out_specs=[head(0), pl.BlockSpec((1, blocks, KB, QB), lambda i: (i, 0, 0, 0))],
+        in_specs=[
+            head,
+            pl.BlockSpec((reach, E), lambda i: (0, i)),
+            pl.BlockSpec((reach, E), lambda i: (0, i + heads)),
+            whole_spec((1, m)),
+        ],
+        out_specs=[head, pl.BlockSpec((1, blocks, KB, QB), lambda i: (i, 0, 0, 0))],
         scratch_shapes=[pltpu.VMEM((blocks, KB, QB), F32)],
         compiler_params=pltpu.CompilerParams(vmem_limit_bytes=VMEM),
         cost_estimate=cost(4 * heads * m * KB * E * 2, 2 * heads * m * KB, heads * m * KB),
         name="attend",
-    )(query, own, own, near, near, far, far, places)
-
-
-def single(shape):
-    return pl.BlockSpec(shape, lambda i: (0,) * len(shape), pipeline_mode=pl.Buffered(1))
-
-
-def attend_back(query, own, near, far, probs, mixed, w_attn, d_hidden, d_hidden_t, cosine, sine, flip, ring_source, heads, out_width, identity):
+    )(query, kv, kv, places)
+
+
+def attend_back(query, kv, probs, mixed, w_attn, d_hidden, d_hidden_t, cosine, sine, flip, ring_source, heads, out_width, identity):
     m, width = d_hidden.shape
     devices, rows, ring_width = ring_source.shape[1:]
     blocks = m // QB
@@ -503,7 +530,7 @@
     reach = WINDOW + m
     columns = heads * E
 
-    def kernel(q_ref, k0, v0, k1, v1, k2, v2, p_ref, x_ref, w_ref, g_ref, gt_ref, c_ref, s_ref, flip_ref, source, d_ref, out_ref, sum_ref, flipped_ref, keys_sum, values_sum, near_out, near_in, far_out, far_in, kept, near_send, near_recv, far_send, far_recv, *scratch):
+    def kernel(q_ref, k_ref, v_ref, p_ref, x_ref, w_ref, g_ref, gt_ref, c_ref, s_ref, flip_ref, source, d_ref, out_ref, sum_ref, flipped_ref, keys_sum, values_sum, near_out, near_in, far_out, far_in, kept, near_send, near_recv, far_send, far_recv, *scratch):
         head = pl.program_id(0)
         half = ring_width // 2
         ring = Ring(devices, [(source.at[0], 0, half), (source.at[0], half, half)], [(sum_ref, 0), (sum_ref, half)], [[0], [1]], scratch)
@@ -528,9 +555,7 @@
 
         grad_all = dot_nn(g_ref[...], w_ref[...]).astype(BF)
         out_ref[...] = dot_nn(gt_ref[...], x_ref[...]).astype(BF)
-        keys = jnp.concatenate([k2[...], k1[...], k0[...]], axis=0)
-        values = jnp.concatenate([v2[...], v1[...], v0[...]], axis=0)
-        keys_t = keys.T
+        keys_t = k_ref[...].T
         keys_sum[...] = jnp.zeros_like(keys_sum)
         values_sum[...] = jnp.zeros_like(values_sum)
         for block in range(blocks):
@@ -538,7 +563,7 @@
             here = slice(block * QB, (block + 1) * QB)
             low = p_ref[0, block]
             grad = grad_all[here, :]
-            d_probs = dot_nt(values[span], grad)
+            d_probs = dot_nt(v_ref[span, :], grad)
             weighted = low.astype(F32) * d_probs
             total = jnp.sum(weighted, axis=0, keepdims=True)
             d_scores = (weighted - low.astype(F32) * total).astype(BF)
@@ -618,7 +643,9 @@
             jax.ShapeDtypeStruct((out_width, rows), F32),
         ],
         in_specs=[
-            head_spec(0), head_spec(0), head_spec(heads), head_spec(0), head_spec(heads), head_spec(0), head_spec(heads),
+            head_spec(0),
+            pl.BlockSpec((reach, E), lambda i: (0, i)),
+            pl.BlockSpec((reach, E), lambda i: (0, i + heads)),
             pl.BlockSpec((1, blocks, KB, QB), lambda i: (i, 0, 0, 0)),
             head_spec(0),
             pl.BlockSpec((width, E), lambda i: (0, i + 3 * heads)),
@@ -644,10 +671,10 @@
         compiler_params=pltpu.CompilerParams(vmem_limit_bytes=VMEM, collective_id=identity, has_side_effects=True),
         cost_estimate=cost(8 * heads * m * KB * E * 2, 2 * heads * m * KB),
         name="attend_back",
-    )(query, own, own, near, near, far, far, probs, mixed, w_attn, d_hidden, d_hidden_t, cosine, sine, flip, ring_source)
-
-
-def back_pass(x_t, d_out, weights, extra, ring_sources, out_widths, costs, identity, name):
+    )(query, kv, kv, probs, mixed, w_attn, d_hidden, d_hidden_t, cosine, sine, flip, ring_source)
+
+
+def back_pass(x_t, d_out, weights, ring_sources, out_widths, costs, identity, name):
     amount, m, columns = d_out.shape
     width = x_t.shape[0]
     devices = lax.axis_size("dp")
@@ -669,10 +696,8 @@
 
         xt_ref, tile_ref, d_ref = take(3)
         w_refs = take(amount)
-        extra_refs = take(2) if extra else None
         sources = [ref if lead is None else ref.at[lead] for ref, (_, lead, _) in zip(take(count), ring_sources)]
         grad_ref, back_ref = take(2)
-        extra_out = take(1)[0] if extra else None
         sums = take(count)
         sent, got, y_send, y_recv = take(4)
         terms, goals = [], []
@@ -703,8 +728,6 @@
                 part = made if part is None else part + made
             sent[step] = part.astype(BF)
             across(step).start()
-            if extra:
-                extra_out[...] = dot_nt(extra_refs[0][...], extra_refs[1][...]).astype(BF)
 
         @pl.when(step >= tiles)
         def _():
@@ -736,12 +759,6 @@
         operands.append(weights)
     out_specs = [pl.BlockSpec((1, width, TILE), lambda i: (late(i) // per, 0, late(i) % per)), single((m, width))]
     out_shape = [jax.ShapeDtypeStruct((amount, width, columns), BF), jax.ShapeDtypeStruct((m, width), F32)]
-    if extra:
-        x, w, where = extra
-        specs += [single(x.shape), pl.BlockSpec((TILE, x.shape[1]), lambda i: (early(i), where))]
-        operands += [x, w]
-        out_specs.append(pl.BlockSpec((m, TILE), lambda i: (0, early(i))))
-        out_shape.append(jax.ShapeDtypeStruct((m, width), BF))
     specs += [pl.BlockSpec(memory_space=pl.ANY)] * count
     operands += [source for source, _, _ in ring_sources]
     for (source, _, _), out_width in zip(ring_sources, out_widths):
@@ -779,26 +796,57 @@
     return root * pushed - rows * (root * root * root * inner), jnp.sum(grad * rows * root, axis=0, keepdims=True)
 
 
-def first_norm(tokens, gain):
+def first_norm(far, near, tokens, gain):
     m, width = tokens.shape
-
-    def kernel(x_ref, g_ref, o_ref, t_ref):
-        rows = x_ref[...].astype(F32)
-        normed = (rows * root_of(rows) * g_ref[...]).astype(BF)
-        o_ref[...] = normed
-        t_ref[...] = normed.T
-
-    rows_spec = pl.BlockSpec((ROWS, width), lambda i: (i, 0))
+    steps = m // ROWS
+
+    def kernel(far_ref, near_ref, x_ref, g_ref, o_ref, t_ref):
+        step = pl.program_id(0)
+        me = lax.axis_index("dp")
+
+        def normed(ref):
+            rows = ref[...].astype(F32)
+            return (rows * root_of(rows) * g_ref[...]).astype(BF)
+
+        def earlier(ref, there):
+            @pl.when(there)
+            def _():
+                o_ref[...] = normed(ref)
+
+            @pl.when(jnp.logical_not(there))
+            def _():
+                o_ref[...] = jnp.zeros_like(o_ref)
+
+        @pl.when(step < steps)
+        def _():
+            earlier(far_ref, me >= 2)
+
+        @pl.when((step >= steps) & (step < 2 * steps))
+        def _():
+            earlier(near_ref, me >= 1)
+
+        @pl.when(step >= 2 * steps)
+        def _():
+            made = normed(x_ref)
+            o_ref[...] = made
+            t_ref[...] = made.T
+
+    def part(which):
+        return pl.BlockSpec((ROWS, width), lambda i: (jnp.clip(i - which * steps, 0, steps - 1), 0))
+
     return pl.pallas_call(
         kernel,
-        grid=(m // ROWS,),
-        out_shape=[jax.ShapeDtypeStruct((m, width), BF), jax.ShapeDtypeStruct((width, m), BF)],
-        in_specs=[rows_spec, whole_spec((1, width))],
-        out_specs=[rows_spec, pl.BlockSpec((width, ROWS), lambda i: (0, i))],
+        grid=(3 * steps,),
+        out_shape=[jax.ShapeDtypeStruct((3 * m, width), BF), jax.ShapeDtypeStruct((width, m), BF)],
+        in_specs=[part(0), part(1), part(2), whole_spec((1, width))],
+        out_specs=[
+            pl.BlockSpec((ROWS, width), lambda i: (i, 0)),
+            pl.BlockSpec((width, ROWS), lambda i: (0, jnp.maximum(i - 2 * steps, 0))),
+        ],
         compiler_params=pltpu.CompilerParams(vmem_limit_bytes=VMEM),
-        cost_estimate=cost(8 * m * width, 6 * m * width),
+        cost_estimate=cost(24 * m * width, 14 * m * width),
         name="first_norm",
-    )(tokens, gain)
+    )(far, near, tokens, gain)
 
 
 def out_norm(mixed, w_attn, place, tokens, gain, identity):
@@ -902,7 +950,7 @@
     )(hidden, gain, grad, cotangent)
 
 
-def last_pass(tokens, gain, grad, d_hidden, hidden, ffn_part, ffn_other, gain_ffn_grad, flip, qkv_part, lanes, identity):
+def last_pass(tokens, gain, grad, d_hidden, hidden, activated, w_ffn, gain_ffn_grad, flip, qkv_part, lanes, identity):
     m, width = tokens.shape
     devices, rows, all_columns = qkv_part.shape
     columns = all_columns // 3
@@ -911,25 +959,40 @@
     steps = m // size
     total = steps + chips
     names = 3
-
-    def kernel(x_ref, g_ref, dn_ref, dh_ref, h_ref, p_ref, o_ref, gf_ref, flip_ref, source, grad_ref, layer_ref, flipped_ref, q_ref, k_ref, v_ref, gains_ref, gain_sum, gain_source, *scratch):
+    tiles = width // TILE
+    units = activated.shape[1]
+    sides = lax.axis_size("tensor")
+    assert tiles == steps and chips >= tiles
+
+    def kernel(x_ref, g_ref, dn_ref, dh_ref, h_ref, a_ref, w_ref, gf_ref, flip_ref, source, grad_ref, layer_ref, flipped_ref, q_ref, k_ref, v_ref, gains_ref, gain_sum, gain_source, sent, got, y_send, y_recv, *scratch):
         step = pl.program_id(0)
         ring = Ring(
             devices, [(source, number * columns, columns) for number in range(names)], [(q_ref, 0), (k_ref, 0), (v_ref, 0)],
             [[0], [1], [2]], scratch[: 3 * names + 5],
         )
         gain_ring = Ring(devices, [(gain_source, 0, lanes)], [(gains_ref, 0)], [[0]], scratch[3 * names + 5 :])
+        other = (ring.me, lax.rem(ring.side + 1, sides))
+
+        def across(which):
+            return pltpu.make_async_remote_copy(
+                src_ref=sent.at[which], dst_ref=got.at[which], send_sem=y_send.at[which], recv_sem=y_recv.at[which],
+                device_id=other, device_id_type=MESH,
+            )
 
         @pl.when(step == 0)
         def _():
-            ring.barrier()
+            ring.barrier((other,))
             ring.begin()
+
+        @pl.when(step < tiles)
+        def _():
+            sent[step] = dot_nt(a_ref[...], w_ref[...]).astype(BF)
+            across(step).start()
 
         @pl.when(step < steps)
         def _():
             change, gain_part = norm_grad(x_ref[...].astype(F32), g_ref[...], dn_ref[...])
             grad_ref[...] = dh_ref[...] + change
-            layer_ref[...] = (h_ref[...] + (p_ref[...].astype(F32) + o_ref[...].astype(F32))).astype(BF)
 
             @pl.when(step == 0)
             def _():
@@ -949,11 +1012,17 @@
                 gain_source[device, 16:, :rows] = jnp.broadcast_to(gf_ref[:, span], (16, rows)).astype(BF)
             gain_ring.begin()
 
-        ring.pace(step, [(steps, 3), (chips, 4)])
+        ring.pace(step, [(steps, 3), (chips, 5)])
 
         @pl.when(step >= steps)
         def _():
             gain_ring.run(step - steps, step - steps + 1)
+
+        @pl.when((step >= steps) & (step < steps + tiles))
+        def _():
+            which = step - steps
+            across(which).wait()
+            layer_ref[...] = (h_ref[...] + (sent[which].astype(F32) + got[which].astype(F32))).astype(BF)
 
         @pl.when(step == total - 1)
         def _():
@@ -964,6 +1033,8 @@
         return jnp.minimum(i, steps - 1)
 
     rows_spec = pl.BlockSpec((size, width), lambda i: (early(i), 0))
+    tile_spec = pl.BlockSpec((m, TILE), lambda i: (0, jnp.clip(i - steps, 0, tiles - 1)))
+    dma = pltpu.SemaphoreType.DMA
     sums = jax.ShapeDtypeStruct((rows, columns), F32)
     return pl.pallas_call(
         kernel,
@@ -976,23 +1047,28 @@
             jax.ShapeDtypeStruct((32, lanes), F32),
         ],
         in_specs=[
-            rows_spec, single((1, width)), rows_spec, rows_spec, rows_spec, rows_spec, rows_spec, single((1, width)),
+            rows_spec, single((1, width)), rows_spec, rows_spec, tile_spec, single((m, units)),
+            pl.BlockSpec((TILE, units), lambda i: (early(i), 2)), single((1, width)),
             single(flip.shape), pl.BlockSpec(memory_space=pl.ANY),
         ],
         out_specs=[
-            rows_spec, rows_spec, single((flip.shape[1], flip.shape[0])),
+            rows_spec, tile_spec, single((flip.shape[1], flip.shape[0])),
             single(sums.shape), single(sums.shape), single(sums.shape), single((32, lanes)),
         ],
         scratch_shapes=[
             pltpu.VMEM((1, width), F32),
             pltpu.VMEM((devices, 32, lanes), BF),
+            pltpu.VMEM((tiles, m, TILE), BF),
+            pltpu.VMEM((tiles, m, TILE), BF),
+            dma((tiles,)),
+            dma((tiles,)),
             *Ring.scratch(devices, [(rows, columns)] * names),
             *Ring.scratch(devices, [(32, lanes)]),
         ],
         compiler_params=pltpu.CompilerParams(vmem_limit_bytes=VMEM, collective_id=identity, has_side_effects=True),
         cost_estimate=cost(20 * m * width, 24 * m * width),
         name="last_pass",
-    )(tokens, gain, grad, d_hidden, hidden, ffn_part, ffn_other, gain_ffn_grad, flip, qkv_part)
+    )(tokens, gain, grad, d_hidden, hidden, activated, w_ffn, gain_ffn_grad, flip, qkv_part)
 
 
 def feed(x, dy, w, tiles):
@@ -1029,10 +1105,8 @@
 
 def shards(tokens, positions, attn_gain, w_query, w_key, w_value, w_out, ffn_gain, w_gate, w_up, w_down, cotangent):
     devices = lax.axis_size("dp")
-    core = lax.axis_index("dp") % 2
-    sides = lax.axis_size("tensor")
-    flip = [(i, (i + 1) % sides) for i in range(sides)]
     span = tokens.shape[0]
+    assert 2 * span == WINDOW
     own_rows = w_query.shape[0]
     width = tokens.shape[1]
     head_columns = w_query.shape[1]
@@ -1044,7 +1118,7 @@
     attn_pack = jnp.concatenate([w_query, w_key, w_value, w_out.T], axis=1)
     lanes = max(128, own_rows)
     gains = jnp.zeros((32, lanes), BF).at[0, :own_rows].set(attn_gain).at[16, :own_rows].set(ffn_gain)
-    w_attn, all_gains = ring_gather((attn_pack, gains), (2, 1), 0)
+    w_attn, all_gains, near, far = ring_gather((attn_pack, gains), (2, 1), tokens, 0)
 
     def wide(matrix):
         return jnp.pad(matrix, ((0, 0), (0, padded - hidden_units)))
@@ -1057,36 +1131,35 @@
     gain_ffn = all_gains[:, 16, :own_rows].reshape(1, width).astype(F32)
 
     frequency = THETA ** (-(jnp.arange(E // 2, dtype=F32) * 2.0 / E))
-    angles = positions.astype(F32)[:, None] * frequency[None, :]
+    earlier = positions[0] - WINDOW + jnp.arange(WINDOW, dtype=jnp.int32)
+    angles = jnp.concatenate([earlier, positions]).astype(F32)[:, None] * frequency[None, :]
     cosine_half, sine_half = jnp.cos(angles), jnp.sin(angles)
     cosine = jnp.concatenate([cosine_half, cosine_half], axis=1)
     sine = jnp.concatenate([-sine_half, sine_half], axis=1)
 
-    normed_attn, normed_attn_t = first_norm(tokens, gain_attn)
-    query, own_kv = project(normed_attn, w_attn, cosine, sine, heads)
-    far = lax.ppermute(own_kv, "dp", [(i - 2, i) for i in range(2, devices)])
-    near = lax.ppermute(jnp.where(core == 0, own_kv, far), "dp", swap_route(devices))
-    mixed, probs = attend(query, own_kv, near, far, positions[None, :], heads)
+    normed_attn, normed_attn_t = first_norm(far, near, tokens, gain_attn)
+    query, kv = project(normed_attn, w_attn, cosine, sine, span, heads)
+    mixed, probs = attend(query, kv, positions[None, :], heads)
+    cosine, sine = cosine[WINDOW:], sine[WINDOW:]
     hidden, normed_ffn, normed_ffn_t = out_norm(mixed, w_attn, 3, tokens, gain_ffn, 5)
 
     activated, d_both = feed(normed_ffn, cotangent, w_ffn, tiles)
     down_part = matmul_nn(cotangent.T, activated, 0, tiles, "down_grad").reshape(devices, own_rows, padded)
-    both_part, d_normed_ffn, ffn_part, down_grad = back_pass(
-        normed_ffn_t, d_both, w_ffn, (activated, w_ffn, 2), [(down_part, None, 2)], [padded], (13, 4), 1, "ffn_back"
+    both_part, d_normed_ffn, down_grad = back_pass(
+        normed_ffn_t, d_both, w_ffn, [(down_part, None, 2)], [padded], (2, 1), 1, "ffn_back"
     )
     both_part = both_part.reshape(2, devices, own_rows, padded)
-    ffn_other = lax.ppermute(ffn_part, "tensor", flip)
     d_hidden, d_hidden_low, d_hidden_t, gain_ffn_grad = hidden_grad(hidden, gain_ffn, d_normed_ffn, cotangent)
 
     d_qkv, out_part, gate_grad, w_down_grad = attend_back(
-        query, own_kv, near, far, probs, mixed, w_attn, d_hidden_low, d_hidden_t, cosine, sine, down_grad, both_part, heads, hidden_units, 2
+        query, kv, probs, mixed, w_attn, d_hidden_low, d_hidden_t, cosine, sine, down_grad, both_part, heads, hidden_units, 2
     )
     qkv_part, d_normed_attn, up_grad, out_grad = back_pass(
-        normed_attn_t, d_qkv[None], w_attn, None,
+        normed_attn_t, d_qkv[None], w_attn,
         [(both_part, 1, 2), (out_part.reshape(devices, own_rows, head_columns), None, 1)], [hidden_units, head_columns], (4, 3), 3, "qkv_back",
     )
     tokens_grad, layer_out, w_out_grad, query_grad, key_grad, value_grad, gain_grads = last_pass(
-        tokens, gain_attn, d_normed_attn, d_hidden, hidden, ffn_part, ffn_other, gain_ffn_grad, out_grad,
+        tokens, gain_attn, d_normed_attn, d_hidden, hidden, activated, w_ffn, gain_ffn_grad, out_grad,
         qkv_part.reshape(devices, own_rows, 3 * head_columns), lanes, 4,
     )
     return (

time: 748 us -> 720 us (0.963)
  waiting for transfers between devices: 103 us -> 54.3 us
  Pallas kernels: 588 us -> 615 us
    ppermute x3 -> x0, waiting for transfers between devices: 90.8 us -> none  [the longest x1 90.8 us: shards(): far = lax.ppermute(own_kv, 'dp', [(i - 2, i) for i in range(2, devices)])]
    all_gather x1, waiting for transfers between devices: 11.8 us -> 54.3 us  [shards(): w_ffn = lax.all_gather(ffn_pack, 'dp', axis=0, tiled=True)]
    pallas_call x1, Pallas kernels: 88 us -> 110 us  [ring_gather(): pl.pallas_call(functools.partial(gather_kernel, devices, chunks, len(arra...]
    pallas_call x2, Pallas kernels: 20.5 us -> 35.6 us  [the longest x1 24.7 us: project(): pl.pallas_call(kernel, grid=(3 * some,), out_shape=[jax.ShapeDtypeStruct(...]
    pallas_call x2, Pallas kernels: 171 us -> 161 us  [back_pass(): pl.pallas_call(kernel, grid=(total,), out_shape=out_shape, in_specs=specs...]
    unnamed x46 -> x50, local copies, waits for them, and re-layouts: 23.4 us -> 20 us
  transfers between devices with their start and end apart: 4 -> 1, of which waited for: 2 -> 1; matrix products, arithmetic and copies ran while one was open for 2% -> 1% of each run, Pallas kernels for 41% -> 15%
where the time goes in v4:
time: 720 us; the launch traced here: 716 us
  Pallas kernels  615 us (85%)
  waiting for transfers between devices  54.3 us (8%)
  local copies, waits for them, and re-layouts  22.7 us (3%)
  between operations  15.2 us (2%)
  other arithmetic  8.53 us (1%)
    pallas_call x2, Pallas kernels, back_pass(): pl.pallas_call(kernel, grid=(total,), out_shape=out_shape, in_specs=specs...  161 us
    pallas_call x1, Pallas kernels, attend_back(): pl.pallas_call(kernel, grid=(heads,), out_shape=[jax.ShapeDtypeStruct((m,...  114 us
    pallas_call x1, Pallas kernels, ring_gather(): pl.pallas_call(functools.partial(gather_kernel, devices, chunks, len(arra...  110 us
    pallas_call x1, Pallas kernels, last_pass(): pl.pallas_call(kernel, grid=(total,), out_shape=[jax.ShapeDtypeStruct((m,...  73.8 us
    all_gather x1, waiting for transfers between devices, shards(): w_ffn = lax.all_gather(ffn_pack, 'dp', axis=0, tiled=True)  54.3 us
    pallas_call x1, Pallas kernels, out_norm(): pl.pallas_call(kernel, grid=(2 * steps,), out_shape=[jax.ShapeDtypeStruct...  52.8 us
    pallas_call x1, Pallas kernels, feed(): pl.pallas_call(kernel, grid=(tiles,), out_shape=[jax.ShapeDtypeStruct((m,...  26.6 us
    pallas_call x1, Pallas kernels, project(): pl.pallas_call(kernel, grid=(3 * some,), out_shape=[jax.ShapeDtypeStruct(...  24.7 us
  transfers between devices with their start and end apart: 1, of which 1 were waited for; matrix products, arithmetic and copies ran while one was open for 1% of the time, Pallas kernels for 15%

profile of v4, /device:TPU:0, one launch (start us, length us, event | category | flops | bytes accessed | tf_op | source)
XLA Modules:
  0.0 716.1 jit_solution(10076718583955128570)
XLA Ops:
  8.4 1.4 copy.24
  10.5 1.4 fusion.5
  13.0 109.8 %ring_gather.1 = (bf16[2048,4096]{1,0:T(8,128)(2,1)}, bf16[512,128]{1,0:T(8,128)(2,1)}, bf16[512,2048]{1,0:T(8,128)(2,1)}, bf16[512,2048]{1,0:T(8,128)(2,1)}) custom-call(bf16[128,4096]{1,0:T(8,128)(2,1)} %pad_maximum_fusion.refs_0_, bf16[32,128]{1,0:T(8,128)(2,1)} %copy-done.14, bf16[512,2048]{1,0:T(8,128)(2,1)} %x_ref.3), custom_call_target="tpu_custom_call" | custom-call | tf_op jit(solution)/shard_map/ring_gather/pallas_call | solution.py:213
  123.4 3.0 copy.29
  128.5 10.9 %first_norm.1 = (bf16[1536,2048]{1,0:T(8,128)(2,1)}, bf16[2048,512]{1,0:T(8,128)(2,1)}) custom-call(bf16[512,2048]{1,0:T(8,128)(2,1)} %get-tuple-element.78.far_ref, bf16[512,2048]{1,0:T(8,128)(2,1)} %get-tuple-element.79.near_ref, bf16[512,2048]{1,0:T(8,128)(2,1)} %x_ref.3, f32[1,2048]{1,0:T(1,128)} %bitcast.29), custom_call_target="tpu_custom_call" | custom-call | flops 25165824 | bytes 14680064 | tf_op jit(solution)/shard_map/first_norm/pallas_call | solution.py:837
  139.4 2.8 fusion.8
  143.2 1.6 pad_maximum_fusion.1
  144.8 24.7 %project.1 = (bf16[512,1024]{1,0:T(8,128)(2,1)}, bf16[1536,2048]{1,0:T(8,128)(2,1)}) custom-call(bf16[1536,2048]{1,0:T(8,128)(2,1)} %get-tuple-element.81.x_ref, bf16[2048,4096]{1,0:T(8,128)(2,1)} %get-tuple-element.82.w_ref.refs_3_, f32[1536,128]{1,0:T(8,128)} %get-tuple-element.135.c_ref, f32[1536,128]{1,0:T(8,128)} %get-tuple-element.136.s_ref), custom_call_target="tpu_custom_call" | custom-call | flops 15032385536 | bytes 28311552 | tf_op jit(solution)/shard_map/project/pallas_call | solution.py:459
  169.5 20.4 %attend.1 = (bf16[512,1024]{1,0:T(8,128)(2,1)}, bf16[8,2,1280,256]{3,2,1,0:T(8,128)(2,1)}) custom-call(bf16[512,1024]{1,0:T(8,128)(2,1)} %get-tuple-element.83.q_ref, bf16[1536,2048]{1,0:T(8,128)(2,1)} %get-tuple-element.84.k_ref.v_ref, bf16[1536,2048]{1,0:T(8,128)(2,1)} %get-tuple-element.84.k_ref.v_ref, s32[1,512]{1,0:T(1,128)} %bitcast.33), custom_call_target="tpu_custom_call" | custom-call | flops 5368709120 | bytes 10485760 | tf_op jit(solution)/shard_map/attend/pallas_call | solution.py:504
  189.9 52.8 %out_norm.1 = (f32[512,2048]{1,0:T(8,128)}, bf16[512,2048]{1,0:T(8,128)(2,1)}, bf16[2048,512]{1,0:T(8,128)(2,1)}) custom-call(bf16[512,1024]{1,0:T(8,128)(2,1)} %get-tuple-element.86.x_ref, bf16[2048,4096]{1,0:T(8,128)(2,1)} %get-tuple-element.82.w_ref.refs_3_, bf16[512,2048]{1,0:T(8,128)(2,1)} %x_ref.3, f32[1,2048]{1,0:T(1,128)} %bitcast.31), custom_call_target="tpu_custom_call" | custom-call | flops 2147483648 | bytes 12582912 | tf_op jit(solution)/shard_map/out_norm/pallas_call | solution.py:894
  242.7 54.3 %all-gather.2.cloned.1.call-done.g_ref.u_ref.d_ref.refs_3_.refs_4_.w_ref = bf16[2048,8448]{1,0:T(8,128)(2,1)} async-done(((bf16[128,8448]{1,0:T(8,128)(2,1)}), bf16[2048,8448]{1,0:T(8,128)(2,1)}) %all-gather.2.cloned.1.call-update) | async-done | bytes 34603024 | tf_op jit(solution)/shard_map/all_gather | solution.py:1128
  297.0 26.6 %feed.1 = (bf16[512,2816]{1,0:T(8,128)(2,1)}, bf16[2,512,2816]{2,1,0:T(8,128)(2,1)}) custom-call(bf16[512,2048]{1,0:T(8,128)(2,1)} %get-tuple-element.89.x_ref, bf16[512,2048]{1,0:T(8,128)(2,1)} %y_ref.1, bf16[2048,8448]{1,0:T(8,128)(2,1)} %all-gather.2.cloned.1.call-done.g_ref.u_ref.d_ref.refs_3_.refs_4_.w_ref, ...), custom_call_target="tpu_custom_call" | custom-call | flops 17716740096 | bytes 43253760 | tf_op jit(solution)/shard_map/feed/pallas_call | solution.py:1088
  323.7 13.0 %down_grad.1 = bf16[2048,2816]{1,0:T(8,128)(2,1)} custom-call(bf16[2048,512]{1,0:T(8,128)(2,1)} %bitcast.27, bf16[512,2816]{1,0:T(8,128)(2,1)} %get-tuple-element.92.w_ref.a_ref), custom_call_target="tpu_custom_call" | custom-call | flops 5905580032 | bytes 16515072 | tf_op jit(solution)/shard_map/down_grad/pallas_call | solution.py:414
  336.7 71.2 %ffn_back.1 = (bf16[2,2048,2816]{2,1,0:T(8,128)(2,1)}, f32[512,2048]{1,0:T(8,128)}, f32[128,2816]{1,0:T(8,128)}) custom-call(bf16[2048,512]{1,0:T(8,128)(2,1)} %get-tuple-element.88.refs_0_, bf16[2,512,2816]{2,1,0:T(8,128)(2,1)} %get-tuple-element.91.refs_1_.refs_2_, bf16[2,512,2816]{2,1,0:T(8,128)(2,1)} %get-tuple-element.91.refs_1_.refs_2_, ...), custom_call_target="tpu_custom_call" | custom-call | flops 23622320128 | bytes 69206016 | tf_op jit(solution)/shard_map/ffn_back/pallas_call | solution.py:769
  407.9 8.8 %hidden_grad.1 = (f32[512,2048]{1,0:T(8,128)}, bf16[512,2048]{1,0:T(8,128)(2,1)}, bf16[2048,512]{1,0:T(8,128)(2,1)}, f32[1,2048]{1,0:T(1,128)}) custom-call(f32[512,2048]{1,0:T(8,128)} %get-tuple-element.87.h_ref, f32[1,2048]{1,0:T(1,128)} %bitcast.32, f32[512,2048]{1,0:T(8,128)} %get-tuple-element.93.d_ref, bf16[512,2048]{1,0:T(8,128)(2,1)} %y_ref.1), custom_call_target="tpu_custom_call" | custom-call | flops 16777216 | bytes 18874368 | tf_op jit(solution)/shard_map/hidden_grad/pallas_call | solution.py:936
  416.8 113.8 %attend_back.1 = (bf16[512,3072]{1,0:T(8,128)(2,1)}, bf16[2048,1024]{1,0:T(8,128)(2,1)}, f32[128,2752]{1,0:T(8,128)}, f32[2752,128]{1,0:T(8,128)}) custom-call(bf16[512,1024]{1,0:T(8,128)(2,1)} %get-tuple-element.83.q_ref, bf16[1536,2048]{1,0:T(8,128)(2,1)} %get-tuple-element.84.k_ref.v_ref, bf16[1536,2048]{1,0:T(8,128)(2,1)} %get-tuple-element.84.k_ref.v_ref, ...), custom_call_target="tpu_custom_call" | custom-call | flops 10737418240 | bytes 10485760 | tf_op jit(solution)/shard_map/attend_back/pallas_call | solution.py:636
  530.6 89.4 %qkv_back.1 = (bf16[1,2048,3072]{2,1,0:T(8,128)(2,1)}, f32[512,2048]{1,0:T(8,128)}, f32[128,2752]{1,0:T(8,128)}, f32[128,1024]{1,0:T(8,128)}) custom-call(bf16[2048,512]{1,0:T(8,128)(2,1)} %get-tuple-element.80.refs_0_, bf16[1,512,3072]{2,1,0:T(8,128)(2,1)} %bitcast.22, bf16[1,512,3072]{2,1,0:T(8,128)(2,1)} %bitcast.23, ...), custom_call_target="tpu_custom_call" | custom-call | flops 12884901888 | bytes 37748736 | tf_op jit(solution)/shard_map/qkv_back/pallas_call | solution.py:769
  620.0 73.8 %last_pass.1 = (f32[512,2048]{1,0:T(8,128)}, bf16[512,2048]{1,0:T(8,128)(2,1)}, f32[1024,128]{1,0:T(8,128)}, f32[128,1024]{1,0:T(8,128)}, f32[128,1024]{1,0:T(8,...) custom-call(bf16[512,2048]{1,0:T(8,128)(2,1)} %x_ref.3, f32[1,2048]{1,0:T(1,128)} %bitcast.30, ...), custom_call_target="tpu_custom_call" | custom-call | flops 20971520 | bytes 25165824 | tf_op jit(solution)/shard_map/last_pass/pallas_call | solution.py:1039
  693.8 1.3 slice_bitcast_fusion
  695.2 3.0 copy.31
  698.2 1.5 copy.30
  699.7 1.3 copy.44
  701.0 1.6 copy-done.1
  702.7 2.0 copy.45
  (55 shorter events, 10.1 us)
Async XLA Ops:
  7.2 2.7 copy-start.5
  7.2 2.9 copy-start.6
  7.2 289.8 %all-gather.2.cloned.1.call-start = ((), (), s32[]{:S(2)}) async-start(), calls=%async_computation | async-start | bytes 36765696 | tf_op jit(solution)/shard_map/all_gather | solution.py:1128
  8.4 2.0 copy-start.16
  10.4 1.5 copy-start.17
  10.5 1.5 copy-start.11
  10.5 1.5 copy-start.12
  10.5 1.5 copy-start.13
  12.0 1.1 copy-start.14
  13.0 109.8 %copy-start.15 = (s32[512]{0:T(512)S(1)}, s32[512]{0:T(512)}, u32[]{:S(2)}) copy-start(s32[512]{0:T(512)} %param.17) | copy-start | bytes 6148
  13.0 110.4 %copy-start = (bf16[512,2048]{1,0:T(8,128)(2,1)S(1)}, bf16[512,2048]{1,0:T(8,128)(2,1)}, u32[]{:S(2)}) copy-start(bf16[512,2048]{1,0:T(8,128)(2,1)} %y_ref.1) | copy-start | bytes 6291460
  693.8 4.4 copy-start.3
  695.2 4.6 copy-start.2
  699.7 2.9 copy-start.1
  702.7 2.0 copy-start.10
  702.7 2.8 copy-start.9
  702.7 3.6 copy-start.8
  704.7 2.4 copy-start.7
  704.7 3.2 copy-start.4
Sparse Core Ops, SparseCore 0:
  123.0 173.9 all-gather.1

commit v5 on v4

--- a/solution.py
+++ b/solution.py
@@ -19,7 +19,8 @@
 KB = WINDOW + QB
 TILE = 256
 ROWS = 128
-VMEM = 56 * 1024 * 1024
+LATE = 2
+VMEM = 59 * 1024 * 1024
 
 
 def whole_spec(shape):
@@ -234,6 +235,117 @@
     )(*arrays, tokens)
 
 
+class Spread:
+    def __init__(self, devices, pieces, scratch):
+        self.devices, self.chips, self.pieces = devices, devices // 2, pieces
+        self.local_sem, self.send_sem, self.recv_sem, self.give_sem, self.take_sem = scratch
+        self.me = lax.axis_index("dp")
+        self.side = lax.axis_index("tensor")
+        self.core = lax.rem(self.me, 2)
+        self.place = ring_place(self.me // 2, self.chips)
+        self.partner = self.me + 1 - 2 * self.core
+        self.next = (
+            ring_chip(self.place + 1, self.chips) * 2 + self.core,
+            ring_chip(self.place - 1, self.chips) * 2 + self.core,
+        )
+        self.events = (self.chips - 1) * len(pieces)
+
+    @staticmethod
+    def scratch(devices, count):
+        dma = pltpu.SemaphoreType.DMA
+        chips = devices // 2
+        return [dma((count,))] + [dma((count, amount, 2)) for amount in (chips - 1, chips - 1, chips, chips)]
+
+    def barrier(self):
+        semaphore = pltpu.get_barrier_semaphore()
+        for other in (*self.next, self.partner):
+            pl.semaphore_signal(semaphore, inc=1, device_id=(other, self.side), device_id_type=MESH)
+        pl.semaphore_wait(semaphore, 3)
+
+    def block(self, index, stage, half):
+        source, whole, column, width = self.pieces[index]
+        rows = source.shape[0]
+        owner = ring_chip(self.place - stage if half == 0 else self.place + stage, self.chips) * 2 + self.core
+        return whole.at[pl.ds(pl.multiple_of(owner * rows + half * (rows // 2), 16), rows // 2), pl.ds(column, width)]
+
+    def first(self, index, half):
+        source, _, column, width = self.pieces[index]
+        rows = source.shape[0]
+        return source.at[pl.ds(half * (rows // 2), rows // 2), pl.ds(column, width)]
+
+    def local(self, index):
+        source, whole, column, width = self.pieces[index]
+        rows = source.shape[0]
+        span = pl.ds(pl.multiple_of(self.me * rows, 16), rows)
+        return pltpu.make_async_copy(
+            source.at[:, pl.ds(column, width)], whole.at[span, pl.ds(column, width)], self.local_sem.at[index]
+        )
+
+    def copy(self, index, stage, half, start, across):
+        block = self.block(index, stage, half)
+        send, recv = (self.give_sem, self.take_sem) if across else (self.send_sem, self.recv_sem)
+        return pltpu.make_async_remote_copy(
+            src_ref=self.first(index, half) if start else block,
+            dst_ref=block,
+            send_sem=send.at[index, stage, half],
+            recv_sem=recv.at[index, stage, half],
+            device_id=(self.partner if across else self.next[half], self.side),
+            device_id_type=MESH,
+        )
+
+    def each(self):
+        return [(index, half) for index in range(len(self.pieces)) for half in range(2)]
+
+    def begin(self):
+        for index, half in self.each():
+            self.copy(index, 0, half, True, False).start()
+        for index, half in self.each():
+            self.copy(index, 0, half, True, True).start()
+        for index in range(len(self.pieces)):
+            self.local(index).start()
+
+    def stage(self, stage, index):
+        for half in range(2):
+            self.copy(index, stage - 1, half, False, False).wait_recv()
+
+            @pl.when(stage < self.chips - 1)
+            def _():
+                self.copy(index, stage, half, False, False).start()
+
+            self.copy(index, stage, half, False, True).start()
+
+    def pace(self, step, total):
+        count = len(self.pieces)
+
+        def one(event, carry):
+            for index in range(count):
+                pl.when(lax.rem(event, count) == index)(functools.partial(self.stage, event // count + 1, index))
+            return carry
+
+        lax.fori_loop(step * self.events // total, (step + 1) * self.events // total, one, 0)
+
+    def finish(self):
+        for index in range(len(self.pieces)):
+            self.local(index).wait()
+        for index, half in self.each():
+            self.copy(index, 0, half, True, False).wait_send()
+            self.copy(index, 0, half, True, True).wait()
+
+        def sent(stage, carry):
+            for index, half in self.each():
+                self.copy(index, stage, half, False, False).wait_send()
+            return carry
+
+        lax.fori_loop(1, self.chips - 1, sent, 0)
+
+        def gave(stage, carry):
+            for index, half in self.each():
+                self.copy(index, stage, half, False, True).wait()
+            return carry
+
+        lax.fori_loop(1, self.chips, gave, 0)
+
+
 class Ring:
     AHEAD = 3
 
@@ -405,24 +517,6 @@
     return lax.dot_general(a, b, (((1,), (1,)), ((), ())), preferred_element_type=F32)
 
 
-def matmul_nn(x, w, first, count, name):
-    m, k = x.shape
-
-    def kernel(x_ref, w_ref, o_ref):
-        o_ref[...] = dot_nn(x_ref[...], w_ref[...]).astype(BF)
-
-    return pl.pallas_call(
-        kernel,
-        grid=(count,),
-        out_shape=jax.ShapeDtypeStruct((m, count * TILE), BF),
-        in_specs=[whole_spec((m, k)), pl.BlockSpec((k, TILE), lambda i: (0, i + first))],
-        out_specs=pl.BlockSpec((m, TILE), lambda i: (0, i)),
-        compiler_params=pltpu.CompilerParams(vmem_limit_bytes=VMEM),
-        cost_estimate=cost(2 * m * k * count * TILE, 2 * (m * k + (m + k) * count * TILE)),
-        name=name,
-    )(x, w)
-
-
 def turned(block, cosine, sine, back):
     other = pltpu.roll(block, E // 2, 1)
     if back:
@@ -522,21 +616,22 @@
     )(query, kv, kv, places)
 
 
-def attend_back(query, kv, probs, mixed, w_attn, d_hidden, d_hidden_t, cosine, sine, flip, ring_source, heads, out_width, identity):
-    m, width = d_hidden.shape
+def attend_back(query, kv, probs, mixed, w_attn, hidden, gain, d_normed, cotangent, cosine, sine, flip, ring_source, heads, out_width, identity):
+    m, width = hidden.shape
+    firsts = m // ROWS
     devices, rows, ring_width = ring_source.shape[1:]
     blocks = m // QB
     factor = E ** (-0.5)
     reach = WINDOW + m
     columns = heads * E
 
-    def kernel(q_ref, k_ref, v_ref, p_ref, x_ref, w_ref, g_ref, gt_ref, c_ref, s_ref, flip_ref, source, d_ref, out_ref, sum_ref, flipped_ref, keys_sum, values_sum, near_out, near_in, far_out, far_in, kept, near_send, near_recv, far_send, far_recv, *scratch):
-        head = pl.program_id(0)
+    def kernel(q_ref, k_ref, v_ref, p_ref, x_ref, w_ref, h_ref, gain_ref, dn_ref, y_ref, c_ref, s_ref, flip_ref, source, d_ref, out_ref, sum_ref, flipped_ref, dh_ref, gain_out, g_ref, gt_ref, keys_sum, values_sum, near_out, near_in, far_out, far_in, kept, near_send, near_recv, far_send, far_recv, *scratch):
+        step = pl.program_id(0)
         half = ring_width // 2
         ring = Ring(devices, [(source.at[0], 0, half), (source.at[0], half, half)], [(sum_ref, 0), (sum_ref, half)], [[0], [1]], scratch)
         me, side, core = ring.me, ring.side, ring.core
 
-        @pl.when(head == 0)
+        @pl.when(step == 0)
         def _():
             ring.barrier(((lax.rem(me + 2, devices), side), (lax.rem(me + devices - 2, devices), side)))
             ring.begin()
@@ -553,104 +648,135 @@
                 device_id=(lax.rem(me + devices - 2, devices), side), device_id_type=MESH,
             )
 
-        grad_all = dot_nn(g_ref[...], w_ref[...]).astype(BF)
-        out_ref[...] = dot_nn(gt_ref[...], x_ref[...]).astype(BF)
-        keys_t = k_ref[...].T
-        keys_sum[...] = jnp.zeros_like(keys_sum)
-        values_sum[...] = jnp.zeros_like(values_sum)
-        for block in range(blocks):
-            span = slice(block * QB, block * QB + KB)
-            here = slice(block * QB, (block + 1) * QB)
-            low = p_ref[0, block]
-            grad = grad_all[here, :]
-            d_probs = dot_nt(v_ref[span, :], grad)
-            weighted = low.astype(F32) * d_probs
-            total = jnp.sum(weighted, axis=0, keepdims=True)
-            d_scores = (weighted - low.astype(F32) * total).astype(BF)
-            values_sum[span, :] += dot_nn(low, grad)
-            keys_sum[span, :] += dot_nn(d_scores, q_ref[here, :])
-            d_query = dot_nn(keys_t[:, span], d_scores).T * factor
-            d_ref[here, pl.ds(pl.multiple_of(head * E, E), E)] = turned(d_query, c_ref[here, :], s_ref[here, :], True).astype(BF)
-            if block == 0:
-                ring.pace(2 * head, [(2 * heads, 1)])
-        for which, (total, scale) in enumerate(((keys_sum, factor), (values_sum, 1.0))):
-            far_out[head, which] = (total[:m, :] * scale).astype(BF)
-            near_out[head, which] = (total[m : 2 * m, :] * scale).astype(BF)
-            kept[head, which] = total[2 * m :, :] * scale
-        near_copy(head).start()
-
-        def settle(which):
-            near_copy(which).wait_recv()
-            came = near_in[which].astype(F32)
-            share = core.astype(F32)
-            far_out[which] = (far_out[which].astype(F32) + came * share).astype(BF)
-            kept[which] = kept[which] + came * (1.0 - share)
-
-            @pl.when(me >= 2)
+        turns = [(firsts + 2 * heads, 1)]
+
+        @pl.when(step < firsts)
+        def _():
+            change, gain_part = norm_grad(h_ref[...], gain_ref[...], dn_ref[...])
+            total = y_ref[...].astype(F32) + change
+            low = total.astype(BF)
+            dh_ref[...] = total
+            here = pl.ds(pl.multiple_of(step * ROWS, ROWS), ROWS)
+            g_ref[here, :] = low
+            gt_ref[:, here] = low.T
+
+            @pl.when(step == 0)
             def _():
-                far_copy(which).start()
-
-        def close(which):
-            @pl.when(me < devices - 2)
+                gain_out[...] = gain_part
+
+            @pl.when(step > 0)
             def _():
-                far_copy(which).wait_recv()
-                kept[which] = kept[which] + far_in[which].astype(F32)
-
-            d_key = turned(kept[which, 0], c_ref[...], s_ref[...], True).astype(BF)
-            d_ref[:, pl.ds(pl.multiple_of((heads + which) * E, E), E)] = d_key
-            d_ref[:, pl.ds(pl.multiple_of((2 * heads + which) * E, E), E)] = kept[which, 1].astype(BF)
-            near_copy(which).wait_send()
-
-            @pl.when(me >= 2)
+                gain_out[...] += gain_part
+
+            ring.pace(step, turns)
+
+        @pl.when(step >= firsts)
+        def _():
+            head = step - firsts
+            grad_all = dot_nn(g_ref[...], w_ref[...]).astype(BF)
+            out_ref[...] = dot_nn(gt_ref[...], x_ref[...]).astype(BF)
+            keys_t = k_ref[...].T
+            keys_sum[...] = jnp.zeros_like(keys_sum)
+            values_sum[...] = jnp.zeros_like(values_sum)
+            for block in range(blocks):
+                span = slice(block * QB, block * QB + KB)
+                here = slice(block * QB, (block + 1) * QB)
+                low = p_ref[0, block]
+                grad = grad_all[here, :]
+                d_probs = dot_nt(v_ref[span, :], grad)
+                weighted = low.astype(F32) * d_probs
+                total = jnp.sum(weighted, axis=0, keepdims=True)
+                d_scores = (weighted - low.astype(F32) * total).astype(BF)
+                values_sum[span, :] += dot_nn(low, grad)
+                keys_sum[span, :] += dot_nn(d_scores, q_ref[here, :])
+                d_query = dot_nn(keys_t[:, span], d_scores).T * factor
+                d_ref[here, pl.ds(pl.multiple_of(head * E, E), E)] = turned(d_query, c_ref[here, :], s_ref[here, :], True).astype(BF)
+                if block == 0:
+                    ring.pace(firsts + 2 * head, turns)
+            for which, (total, scale) in enumerate(((keys_sum, factor), (values_sum, 1.0))):
+                far_out[head, which] = (total[:m, :] * scale).astype(BF)
+                near_out[head, which] = (total[m : 2 * m, :] * scale).astype(BF)
+                kept[head, which] = total[2 * m :, :] * scale
+            near_copy(head).start()
+
+            def settle(which):
+                near_copy(which).wait_recv()
+                came = near_in[which].astype(F32)
+                share = core.astype(F32)
+                far_out[which] = (far_out[which].astype(F32) + came * share).astype(BF)
+                kept[which] = kept[which] + came * (1.0 - share)
+
+                @pl.when(me >= 2)
+                def _():
+                    far_copy(which).start()
+
+            def close(which):
+                @pl.when(me < devices - 2)
+                def _():
+                    far_copy(which).wait_recv()
+                    kept[which] = kept[which] + far_in[which].astype(F32)
+
+                d_key = turned(kept[which, 0], c_ref[...], s_ref[...], True).astype(BF)
+                d_ref[:, pl.ds(pl.multiple_of((heads + which) * E, E), E)] = d_key
+                d_ref[:, pl.ds(pl.multiple_of((2 * heads + which) * E, E), E)] = kept[which, 1].astype(BF)
+                near_copy(which).wait_send()
+
+                @pl.when(me >= 2)
+                def _():
+                    far_copy(which).wait_send()
+
+            @pl.when(head > 0)
             def _():
-                far_copy(which).wait_send()
-
-        @pl.when(head > 0)
-        def _():
-            settle(head - 1)
-
-        @pl.when(head == heads - 1)
-        def _():
-            settle(head)
-
-        ring.pace(2 * head + 1, [(2 * heads, 1)])
-
-        @pl.when(head == 1)
-        def _():
-            flipped_ref[...] = flip_ref[...].T[: flipped_ref.shape[0]]
-
-        @pl.when(head == heads - 1)
-        def _():
-            def one(which, carry):
-                close(which)
-                return carry
-
-            lax.fori_loop(0, heads, one, 0)
-            ring.finish()
-
-    def head_spec(offset):
-        return pl.BlockSpec((m, E), lambda i: (0, i + offset))
-
+                settle(head - 1)
+
+            @pl.when(head == heads - 1)
+            def _():
+                settle(head)
+
+            ring.pace(firsts + 2 * head + 1, turns)
+
+            @pl.when(head == 1)
+            def _():
+                flipped_ref[...] = flip_ref[...].T[: flipped_ref.shape[0]]
+
+            @pl.when(head == heads - 1)
+            def _():
+                def one(which, carry):
+                    close(which)
+                    return carry
+
+                lax.fori_loop(0, heads, one, 0)
+                ring.finish()
+
+    def at(i):
+        return jnp.maximum(i - firsts, 0)
+
+    head_spec = pl.BlockSpec((m, E), lambda i: (0, at(i)))
+    rows_spec = pl.BlockSpec((ROWS, width), lambda i: (jnp.minimum(i, firsts - 1), 0))
     dma = pltpu.SemaphoreType.DMA
     pieces = (heads, 2, m, E)
     return pl.pallas_call(
         kernel,
-        grid=(heads,),
+        grid=(firsts + heads,),
         out_shape=[
             jax.ShapeDtypeStruct((m, 3 * columns), BF),
             jax.ShapeDtypeStruct((width, columns), BF),
             jax.ShapeDtypeStruct((rows, out_width), F32),
             jax.ShapeDtypeStruct((out_width, rows), F32),
+            jax.ShapeDtypeStruct((m, width), F32),
+            jax.ShapeDtypeStruct((1, width), F32),
         ],
         in_specs=[
-            head_spec(0),
-            pl.BlockSpec((reach, E), lambda i: (0, i)),
-            pl.BlockSpec((reach, E), lambda i: (0, i + heads)),
-            pl.BlockSpec((1, blocks, KB, QB), lambda i: (i, 0, 0, 0)),
-            head_spec(0),
-            pl.BlockSpec((width, E), lambda i: (0, i + 3 * heads)),
-            single((m, width)),
-            single((width, m)),
+            head_spec,
+            pl.BlockSpec((reach, E), lambda i: (0, at(i))),
+            pl.BlockSpec((reach, E), lambda i: (0, at(i) + heads)),
+            pl.BlockSpec((1, blocks, KB, QB), lambda i: (at(i), 0, 0, 0)),
+            head_spec,
+            pl.BlockSpec((width, E), lambda i: (0, at(i) + 3 * heads)),
+            rows_spec,
+            single((1, width)),
+            rows_spec,
+            rows_spec,
             single((m, E)),
             single((m, E)),
             single(flip.shape),
@@ -658,11 +784,14 @@
         ],
         out_specs=[
             single((m, 3 * columns)),
-            pl.BlockSpec((width, E), lambda i: (0, i)),
+            pl.BlockSpec((width, E), lambda i: (0, at(i))),
             single((rows, out_width)),
             single((out_width, rows)),
+            rows_spec,
+            single((1, width)),
         ],
         scratch_shapes=[
+            pltpu.VMEM((m, width), BF), pltpu.VMEM((width, m), BF),
             pltpu.VMEM((reach, E), F32), pltpu.VMEM((reach, E), F32),
             pltpu.VMEM(pieces, BF), pltpu.VMEM(pieces, BF), pltpu.VMEM(pieces, BF), pltpu.VMEM(pieces, BF), pltpu.VMEM(pieces, F32),
             dma((heads,)), dma((heads,)), dma((heads,)), dma((heads,)),
@@ -671,7 +800,7 @@
         compiler_params=pltpu.CompilerParams(vmem_limit_bytes=VMEM, collective_id=identity, has_side_effects=True),
         cost_estimate=cost(8 * heads * m * KB * E * 2, 2 * heads * m * KB),
         name="attend_back",
-    )(query, kv, kv, probs, mixed, w_attn, d_hidden, d_hidden_t, cosine, sine, flip, ring_source)
+    )(query, kv, kv, probs, mixed, w_attn, hidden, gain, d_normed, cotangent, cosine, sine, flip, ring_source)
 
 
 def back_pass(x_t, d_out, weights, ring_sources, out_widths, costs, identity, name):
@@ -695,7 +824,7 @@
             return taken
 
         xt_ref, tile_ref, d_ref = take(3)
-        w_refs = take(amount)
+        w_refs = [take(amount) for _ in weights]
         sources = [ref if lead is None else ref.at[lead] for ref, (_, lead, _) in zip(take(count), ring_sources)]
         grad_ref, back_ref = take(2)
         sums = take(count)
@@ -724,8 +853,11 @@
         def _():
             part = None
             for index in range(amount):
-                made = dot_nt(d_ref[index], w_refs[index][...])
-                part = made if part is None else part + made
+                column = 0
+                for (_, several), blocks in zip(weights, w_refs):
+                    made = dot_nt(d_ref[index, :, column : column + several], blocks[index][...])
+                    part = made if part is None else part + made
+                    column += several
             sent[step] = part.astype(BF)
             across(step).start()
 
@@ -754,9 +886,10 @@
         single((amount, m, columns)),
     ]
     operands = [x_t, d_out, d_out]
-    for index in range(amount):
-        specs.append(pl.BlockSpec((TILE, columns), functools.partial(lambda where, i: (early(i), where), index)))
-        operands.append(weights)
+    for array, several in weights:
+        for index in range(amount):
+            specs.append(pl.BlockSpec((TILE, several), functools.partial(lambda where, i: (early(i), where), index)))
+            operands.append(array)
     out_specs = [pl.BlockSpec((1, width, TILE), lambda i: (late(i) // per, 0, late(i) % per)), single((m, width))]
     out_shape = [jax.ShapeDtypeStruct((amount, width, columns), BF), jax.ShapeDtypeStruct((m, width), F32)]
     specs += [pl.BlockSpec(memory_space=pl.ANY)] * count
@@ -913,44 +1046,7 @@
     )(mixed, w_attn, tokens, gain)
 
 
-def hidden_grad(hidden, gain, grad, cotangent):
-    m, width = hidden.shape
-
-    def kernel(h_ref, g_ref, d_ref, y_ref, o_ref, low_ref, turned_ref, gain_ref):
-        change, gain_part = norm_grad(h_ref[...], g_ref[...], d_ref[...])
-        total = y_ref[...].astype(F32) + change
-        low = total.astype(BF)
-        o_ref[...] = total
-        low_ref[...] = low
-        turned_ref[...] = low.T
-
-        @pl.when(pl.program_id(0) == 0)
-        def _():
-            gain_ref[...] = gain_part
-
-        @pl.when(pl.program_id(0) > 0)
-        def _():
-            gain_ref[...] += gain_part
-
-    rows_spec = pl.BlockSpec((ROWS, width), lambda i: (i, 0))
-    return pl.pallas_call(
-        kernel,
-        grid=(m // ROWS,),
-        out_shape=[
-            jax.ShapeDtypeStruct((m, width), F32),
-            jax.ShapeDtypeStruct((m, width), BF),
-            jax.ShapeDtypeStruct((width, m), BF),
-            jax.ShapeDtypeStruct((1, width), F32),
-        ],
-        in_specs=[rows_spec, whole_spec((1, width)), rows_spec, rows_spec],
-        out_specs=[rows_spec, rows_spec, pl.BlockSpec((width, ROWS), lambda i: (0, i)), whole_spec((1, width))],
-        compiler_params=pltpu.CompilerParams(vmem_limit_bytes=VMEM),
-        cost_estimate=cost(16 * m * width, 18 * m * width),
-        name="hidden_grad",
-    )(hidden, gain, grad, cotangent)
-
-
-def last_pass(tokens, gain, grad, d_hidden, hidden, activated, w_ffn, gain_ffn_grad, flip, qkv_part, lanes, identity):
+def last_pass(tokens, gain, grad, d_hidden, hidden, activated, w_ffn, rest, gain_ffn_grad, flip, qkv_part, lanes, identity):
     m, width = tokens.shape
     devices, rows, all_columns = qkv_part.shape
     columns = all_columns // 3
@@ -964,7 +1060,9 @@
     sides = lax.axis_size("tensor")
     assert tiles == steps and chips >= tiles
 
-    def kernel(x_ref, g_ref, dn_ref, dh_ref, h_ref, a_ref, w_ref, gf_ref, flip_ref, source, grad_ref, layer_ref, flipped_ref, q_ref, k_ref, v_ref, gains_ref, gain_sum, gain_source, sent, got, y_send, y_recv, *scratch):
+    some = w_ffn.shape[1] // 3
+
+    def kernel(x_ref, g_ref, dn_ref, dh_ref, h_ref, a_ref, w_ref, rest_ref, gf_ref, flip_ref, source, grad_ref, layer_ref, flipped_ref, q_ref, k_ref, v_ref, gains_ref, gain_sum, gain_source, sent, got, y_send, y_recv, *scratch):
         step = pl.program_id(0)
         ring = Ring(
             devices, [(source, number * columns, columns) for number in range(names)], [(q_ref, 0), (k_ref, 0), (v_ref, 0)],
@@ -986,7 +1084,7 @@
 
         @pl.when(step < tiles)
         def _():
-            sent[step] = dot_nt(a_ref[...], w_ref[...]).astype(BF)
+            sent[step] = (dot_nt(a_ref[:, :some], w_ref[...]) + dot_nt(a_ref[:, some:], rest_ref[...])).astype(BF)
             across(step).start()
 
         @pl.when(step < steps)
@@ -1048,7 +1146,7 @@
         ],
         in_specs=[
             rows_spec, single((1, width)), rows_spec, rows_spec, tile_spec, single((m, units)),
-            pl.BlockSpec((TILE, units), lambda i: (early(i), 2)), single((1, width)),
+            pl.BlockSpec((TILE, some), lambda i: (early(i), 2)), pl.BlockSpec((TILE, units - some), lambda i: (early(i), 2)), single((1, width)),
             single(flip.shape), pl.BlockSpec(memory_space=pl.ANY),
         ],
         out_specs=[
@@ -1068,39 +1166,108 @@
         compiler_params=pltpu.CompilerParams(vmem_limit_bytes=VMEM, collective_id=identity, has_side_effects=True),
         cost_estimate=cost(20 * m * width, 24 * m * width),
         name="last_pass",
-    )(tokens, gain, grad, d_hidden, hidden, activated, w_ffn, gain_ffn_grad, flip, qkv_part)
-
-
-def feed(x, dy, w, tiles):
+    )(tokens, gain, grad, d_hidden, hidden, activated, w_ffn, rest, gain_ffn_grad, flip, qkv_part)
+
+
+def feed_tile(x_ref, dy_ref, dyt_ref, g_ref, u_ref, d_ref, act_ref, both_ref, down_ref):
+    gate = dot_nn(x_ref[...], g_ref[...])
+    up = dot_nn(x_ref[...], u_ref[...])
+    d_act = dot_nn(dy_ref[...], d_ref[...])
+    soft = 1.0 / (1.0 + jnp.exp(-gate))
+    silu = gate * soft
+    act = (silu * up).astype(BF)
+    act_ref[...] = act
+    both_ref[0] = (d_act * up * (soft * (1.0 + gate * (1.0 - soft)))).astype(BF)
+    both_ref[1] = (d_act * silu).astype(BF)
+    down_ref[...] = dot_nn(dyt_ref[...], act).astype(BF)
+
+
+def feed(x, dy, dy_t, w, block, tiles, identity):
     m, k = x.shape
-
-    def kernel(x_ref, dy_ref, g_ref, u_ref, d_ref, act_ref, both_ref):
-        gate = dot_nn(x_ref[...], g_ref[...])
-        up = dot_nn(x_ref[...], u_ref[...])
-        d_act = dot_nn(dy_ref[...], d_ref[...])
-        soft = 1.0 / (1.0 + jnp.exp(-gate))
-        silu = gate * soft
-        act_ref[...] = (silu * up).astype(BF)
-        both_ref[0] = (d_act * up * (soft * (1.0 + gate * (1.0 - soft)))).astype(BF)
-        both_ref[1] = (d_act * silu).astype(BF)
-
-    tile = pl.BlockSpec((m, TILE), lambda i: (0, i))
+    early = tiles - LATE
+    devices = lax.axis_size("dp")
+    width = block.shape[1] // 2
+
+    def kernel(x_ref, dy_ref, dyt_ref, g_ref, u_ref, d_ref, block_ref, act_ref, both_ref, down_ref, rest_ref, *scratch):
+        step = pl.program_id(0)
+        spread = Spread(devices, [(block_ref, rest_ref, 0, width), (block_ref, rest_ref, width, width)], scratch)
+
+        @pl.when(step == 0)
+        def _():
+            spread.barrier()
+            spread.begin()
+
+        feed_tile(x_ref, dy_ref, dyt_ref, g_ref, u_ref, d_ref, act_ref, both_ref, down_ref)
+        spread.pace(step, early)
+
+        @pl.when(step == early - 1)
+        def _():
+            spread.finish()
+
+    any_space = pl.BlockSpec(memory_space=pl.ANY)
     return pl.pallas_call(
         kernel,
-        grid=(tiles,),
-        out_shape=[jax.ShapeDtypeStruct((m, tiles * TILE), BF), jax.ShapeDtypeStruct((2, m, tiles * TILE), BF)],
+        grid=(early,),
+        out_shape=[
+            jax.ShapeDtypeStruct((m, tiles * TILE), BF),
+            jax.ShapeDtypeStruct((2, m, tiles * TILE), BF),
+            jax.ShapeDtypeStruct((k, tiles * TILE), BF),
+            jax.ShapeDtypeStruct((k, block.shape[1]), BF),
+        ],
         in_specs=[
-            whole_spec((m, k)),
-            whole_spec((m, k)),
+            single((m, k)),
+            single((m, k)),
+            single((k, m)),
             pl.BlockSpec((k, TILE), lambda i: (0, i)),
-            pl.BlockSpec((k, TILE), lambda i: (0, i + tiles)),
-            pl.BlockSpec((k, TILE), lambda i: (0, i + 2 * tiles)),
-        ],
-        out_specs=[tile, pl.BlockSpec((2, m, TILE), lambda i: (0, 0, i))],
+            pl.BlockSpec((k, TILE), lambda i: (0, i + early)),
+            pl.BlockSpec((k, TILE), lambda i: (0, i + 2 * early)),
+            any_space,
+        ],
+        out_specs=[
+            pl.BlockSpec((m, TILE), lambda i: (0, i)),
+            pl.BlockSpec((2, m, TILE), lambda i: (0, 0, i)),
+            pl.BlockSpec((k, TILE), lambda i: (0, i)),
+            any_space,
+        ],
+        scratch_shapes=Spread.scratch(devices, 2),
+        compiler_params=pltpu.CompilerParams(vmem_limit_bytes=VMEM, collective_id=identity, has_side_effects=True),
+        cost_estimate=cost(8 * m * k * early * TILE, 8 * (m + k) * early * TILE, m * early * TILE),
+        name="feed",
+    )(x, dy, dy_t, w, w, w, block)
+
+
+def feed_rest(x, dy, dy_t, rest, activated, d_both, down_part):
+    m, k = x.shape
+    tiles = activated.shape[1] // TILE
+    early = tiles - LATE
+
+    def kernel(x_ref, dy_ref, dyt_ref, g_ref, u_ref, d_ref, act_in, both_in, down_in, act_ref, both_ref, down_ref):
+        feed_tile(x_ref, dy_ref, dyt_ref, g_ref, u_ref, d_ref, act_ref, both_ref, down_ref)
+
+    any_space = pl.BlockSpec(memory_space=pl.ANY)
+    return pl.pallas_call(
+        kernel,
+        grid=(LATE,),
+        out_shape=[jax.ShapeDtypeStruct(a.shape, BF) for a in (activated, d_both, down_part)],
+        in_specs=[
+            single((m, k)),
+            single((m, k)),
+            single((k, m)),
+            pl.BlockSpec((k, TILE), lambda i: (0, i)),
+            pl.BlockSpec((k, TILE), lambda i: (0, i + LATE)),
+            pl.BlockSpec((k, TILE), lambda i: (0, i + 2 * LATE)),
+            any_space, any_space, any_space,
+        ],
+        out_specs=[
+            pl.BlockSpec((m, TILE), lambda i: (0, i + early)),
+            pl.BlockSpec((2, m, TILE), lambda i: (0, 0, i + early)),
+            pl.BlockSpec((k, TILE), lambda i: (0, i + early)),
+        ],
+        input_output_aliases={6: 0, 7: 1, 8: 2},
         compiler_params=pltpu.CompilerParams(vmem_limit_bytes=VMEM),
-        cost_estimate=cost(6 * m * k * tiles * TILE, 6 * (m + k) * tiles * TILE, m * tiles * TILE),
-        name="feed",
-    )(x, dy, w, w, w)
+        cost_estimate=cost(8 * m * k * LATE * TILE, 8 * (m + k) * LATE * TILE, m * LATE * TILE),
+        name="feed_rest",
+    )(x, dy, dy_t, rest, rest, rest, activated, d_both, down_part)
 
 
 def shards(tokens, positions, attn_gain, w_query, w_key, w_value, w_out, ffn_gain, w_gate, w_up, w_down, cotangent):
@@ -1123,7 +1290,10 @@
     def wide(matrix):
         return jnp.pad(matrix, ((0, 0), (0, padded - hidden_units)))
 
-    ffn_pack = jnp.concatenate([wide(w_gate), wide(w_up), wide(w_down.T)], axis=1)
+    ffn_parts = [wide(w_gate), wide(w_up), wide(w_down.T)]
+    some = padded - LATE * TILE
+    ffn_pack = jnp.concatenate([part[:, :some] for part in ffn_parts], axis=1)
+    rest_pack = jnp.concatenate([part[:, some:] for part in ffn_parts], axis=1)
     w_attn, all_gains, ffn_pack = lax.optimization_barrier((w_attn, all_gains, ffn_pack))
     w_ffn = lax.all_gather(ffn_pack, "dp", axis=0, tiled=True)
     all_gains = all_gains.reshape(devices, 32, lanes)
@@ -1143,23 +1313,24 @@
     cosine, sine = cosine[WINDOW:], sine[WINDOW:]
     hidden, normed_ffn, normed_ffn_t = out_norm(mixed, w_attn, 3, tokens, gain_ffn, 5)
 
-    activated, d_both = feed(normed_ffn, cotangent, w_ffn, tiles)
-    down_part = matmul_nn(cotangent.T, activated, 0, tiles, "down_grad").reshape(devices, own_rows, padded)
+    cotangent_t = cotangent.T
+    activated, d_both, down_part, rest = feed(normed_ffn, cotangent, cotangent_t, w_ffn, rest_pack, tiles, 6)
+    activated, d_both, down_part = feed_rest(normed_ffn, cotangent, cotangent_t, rest, activated, d_both, down_part)
     both_part, d_normed_ffn, down_grad = back_pass(
-        normed_ffn_t, d_both, w_ffn, [(down_part, None, 2)], [padded], (2, 1), 1, "ffn_back"
+        normed_ffn_t, d_both, [(w_ffn, some), (rest, padded - some)], [(down_part.reshape(devices, own_rows, padded), None, 2)], [padded],
+        (2, 1), 1, "ffn_back",
     )
     both_part = both_part.reshape(2, devices, own_rows, padded)
-    d_hidden, d_hidden_low, d_hidden_t, gain_ffn_grad = hidden_grad(hidden, gain_ffn, d_normed_ffn, cotangent)
-
-    d_qkv, out_part, gate_grad, w_down_grad = attend_back(
-        query, kv, probs, mixed, w_attn, d_hidden_low, d_hidden_t, cosine, sine, down_grad, both_part, heads, hidden_units, 2
+
+    d_qkv, out_part, gate_grad, w_down_grad, d_hidden, gain_ffn_grad = attend_back(
+        query, kv, probs, mixed, w_attn, hidden, gain_ffn, d_normed_ffn, cotangent, cosine, sine, down_grad, both_part, heads, hidden_units, 2
     )
     qkv_part, d_normed_attn, up_grad, out_grad = back_pass(
-        normed_attn_t, d_qkv[None], w_attn,
+        normed_attn_t, d_qkv[None], [(w_attn, 3 * head_columns)],
         [(both_part, 1, 2), (out_part.reshape(devices, own_rows, head_columns), None, 1)], [hidden_units, head_columns], (4, 3), 3, "qkv_back",
     )
     tokens_grad, layer_out, w_out_grad, query_grad, key_grad, value_grad, gain_grads = last_pass(
-        tokens, gain_attn, d_normed_attn, d_hidden, hidden, activated, w_ffn, gain_ffn_grad, out_grad,
+        tokens, gain_attn, d_normed_attn, d_hidden, hidden, activated, w_ffn, rest, gain_ffn_grad, out_grad,
         qkv_part.reshape(devices, own_rows, 3 * head_columns), lanes, 4,
     )
     return (

time: 720 us -> 699 us (0.971)
  waiting for transfers between devices: 54.3 us -> 24.2 us
    all_gather x1, waiting for transfers between devices: 54.3 us -> 24.2 us  [shards(): w_ffn = lax.all_gather(ffn_pack, 'dp', axis=0, tiled=True)]
    pallas_call x4 -> x3, Pallas kernels: 162 us -> 170 us  [the longest x1 113 us: attend_back(): pl.pallas_call(kernel, grid=(firsts + heads,), out_shape=[jax.ShapeDtypeS...]
    unnamed x50 -> x52, local copies, waits for them, and re-layouts: 20 us -> 20.7 us
  transfers between devices with their start and end apart: 1 -> 1, of which waited for: 1 -> 1; matrix products, arithmetic and copies ran while one was open for 1% -> 2% of each run, Pallas kernels for 15% -> 16%
where the time goes in v5:
time: 699 us; the launch traced here: 695 us
  Pallas kernels  621 us (89%)
  waiting for transfers between devices  24.2 us (3%)
  local copies, waits for them, and re-layouts  23.5 us (3%)
  between operations  15.2 us (2%)
  other arithmetic  10.2 us (1%)
    pallas_call x2, Pallas kernels, back_pass(): pl.pallas_call(kernel, grid=(total,), out_shape=out_shape, in_specs=specs...  161 us
    pallas_call x1, Pallas kernels, attend_back(): pl.pallas_call(kernel, grid=(firsts + heads,), out_shape=[jax.ShapeDtypeS...  113 us
    pallas_call x1, Pallas kernels, ring_gather(): pl.pallas_call(functools.partial(gather_kernel, devices, chunks, len(arra...  110 us
    pallas_call x1, Pallas kernels, last_pass(): pl.pallas_call(kernel, grid=(total,), out_shape=[jax.ShapeDtypeStruct((m,...  72.5 us
    pallas_call x1, Pallas kernels, out_norm(): pl.pallas_call(kernel, grid=(2 * steps,), out_shape=[jax.ShapeDtypeStruct...  53 us
    pallas_call x1, Pallas kernels, feed(): pl.pallas_call(kernel, grid=(early,), out_shape=[jax.ShapeDtypeStruct((m,...  46.2 us
    pallas_call x1, Pallas kernels, project(): pl.pallas_call(kernel, grid=(3 * some,), out_shape=[jax.ShapeDtypeStruct(...  24.3 us
    all_gather x1, waiting for transfers between devices, shards(): w_ffn = lax.all_gather(ffn_pack, 'dp', axis=0, tiled=True)  24.2 us
  transfers between devices with their start and end apart: 1, of which 1 were waited for; matrix products, arithmetic and copies ran while one was open for 2% of the time, Pallas kernels for 16%

profile of v5, /device:TPU:0, one launch (start us, length us, event | category | flops | bytes accessed | tf_op | source)
XLA Modules:
  0.0 694.7 jit_solution(7830288774238322052)
XLA Ops:
  7.2 1.9 copy.26
  9.1 1.4 copy.27
  10.9 1.4 copy.29
  12.4 1.3 pad_maximum_fusion
  13.8 2.1 pad_maximum_fusion.1.refs_0_
  15.8 109.9 %ring_gather.1 = (bf16[2048,4096]{1,0:T(8,128)(2,1)}, bf16[512,128]{1,0:T(8,128)(2,1)}, bf16[512,2048]{1,0:T(8,128)(2,1)}, bf16[512,2048]{1,0:T(8,128)(2,1)}) custom-call(bf16[128,4096]{1,0:T(8,128)(2,1)} %pad_maximum_fusion.1.refs_0_, bf16[32,128]{1,0:T(8,128)(2,1)} %copy-done.15, bf16[512,2048]{1,0:T(8,128)(2,1)} %x_ref.3), custom_call_target="tpu_custom_call" | custom-call | tf_op jit(solution)/shard_map/ring_gather/pallas_call | solution.py:214
  126.3 3.0 copy.32
  131.3 10.9 %first_norm.1 = (bf16[1536,2048]{1,0:T(8,128)(2,1)}, bf16[2048,512]{1,0:T(8,128)(2,1)}) custom-call(bf16[512,2048]{1,0:T(8,128)(2,1)} %get-tuple-element.81.far_ref, bf16[512,2048]{1,0:T(8,128)(2,1)} %get-tuple-element.82.near_ref, bf16[512,2048]{1,0:T(8,128)(2,1)} %x_ref.3, f32[1,2048]{1,0:T(1,128)} %bitcast.31), custom_call_target="tpu_custom_call" | custom-call | flops 25165824 | bytes 14680064 | tf_op jit(solution)/shard_map/first_norm/pallas_call | solution.py:970
  142.3 2.8 fusion.2
  146.2 1.6 pad_maximum_fusion.2
  147.8 24.3 %project.1 = (bf16[512,1024]{1,0:T(8,128)(2,1)}, bf16[1536,2048]{1,0:T(8,128)(2,1)}) custom-call(bf16[1536,2048]{1,0:T(8,128)(2,1)} %get-tuple-element.84.x_ref, bf16[2048,4096]{1,0:T(8,128)(2,1)} %get-tuple-element.85.w_ref.refs_3_, f32[1536,128]{1,0:T(8,128)} %get-tuple-element.141.c_ref, f32[1536,128]{1,0:T(8,128)} %get-tuple-element.142.s_ref), custom_call_target="tpu_custom_call" | custom-call | flops 15032385536 | bytes 28311552 | tf_op jit(solution)/shard_map/project/pallas_call | solution.py:553
  172.0 20.3 %attend.1 = (bf16[512,1024]{1,0:T(8,128)(2,1)}, bf16[8,2,1280,256]{3,2,1,0:T(8,128)(2,1)}) custom-call(bf16[512,1024]{1,0:T(8,128)(2,1)} %get-tuple-element.86.q_ref, bf16[1536,2048]{1,0:T(8,128)(2,1)} %get-tuple-element.87.k_ref.v_ref, bf16[1536,2048]{1,0:T(8,128)(2,1)} %get-tuple-element.87.k_ref.v_ref, s32[1,512]{1,0:T(1,128)} %bitcast.35), custom_call_target="tpu_custom_call" | custom-call | flops 5368709120 | bytes 10485760 | tf_op jit(solution)/shard_map/attend/pallas_call | solution.py:598
  192.3 53.0 %out_norm.1 = (f32[512,2048]{1,0:T(8,128)}, bf16[512,2048]{1,0:T(8,128)(2,1)}, bf16[2048,512]{1,0:T(8,128)(2,1)}) custom-call(bf16[512,1024]{1,0:T(8,128)(2,1)} %get-tuple-element.89.x_ref, bf16[2048,4096]{1,0:T(8,128)(2,1)} %get-tuple-element.85.w_ref.refs_3_, bf16[512,2048]{1,0:T(8,128)(2,1)} %x_ref.3, f32[1,2048]{1,0:T(1,128)} %bitcast.33), custom_call_target="tpu_custom_call" | custom-call | flops 2147483648 | bytes 12582912 | tf_op jit(solution)/shard_map/out_norm/pallas_call | solution.py:1027
  246.2 24.2 %all-gather.2.cloned.1.call-done.g_ref.u_ref.d_ref.refs_3_.refs_4_.w_ref = bf16[2048,6912]{1,0:T(8,128)(2,1)} async-done(((bf16[128,6912]{1,0:T(8,128)(2,1)}), bf16[2048,6912]{1,0:T(8,128)(2,1)}) %all-gather.2.cloned.1.call-update) | async-done | bytes 28311568 | tf_op jit(solution)/shard_map/all_gather | solution.py:1298
  270.3 46.2 %feed.1 = (bf16[512,2816]{1,0:T(8,128)(2,1)}, bf16[2,512,2816]{2,1,0:T(8,128)(2,1)}, bf16[2048,2816]{1,0:T(8,128)(2,1)}, bf16[2048,1536]{1,0:T(8,128)(2,1)}) custom-call(bf16[512,2048]{1,0:T(8,128)(2,1)} %get-tuple-element.92.x_ref, bf16[512,2048]{1,0:T(8,128)(2,1)} %y_ref.1, bf16[2048,512]{1,0:T(8,128)(2,1)} %bitcast.22, ...), custom_call_target="tpu_custom_call" | custom-call | flops 19327352832 | bytes 47185920 | tf_op jit(solution)/shard_map/feed/pallas_call | solution.py:1208
  316.5 10.3 %feed_rest.1 = (bf16[512,2816]{1,0:T(8,128)(2,1)}, bf16[2,512,2816]{2,1,0:T(8,128)(2,1)}, bf16[2048,2816]{1,0:T(8,128)(2,1)}) custom-call(bf16[512,2048]{1,0:T(8,128)(2,1)} %get-tuple-element.92.x_ref, bf16[512,2048]{1,0:T(8,128)(2,1)} %y_ref.1, bf16[2048,512]{1,0:T(8,128)(2,1)} %bitcast.23, ...), custom_call_target="tpu_custom_call", output_to_operand_aliasing={{0}: (6, {}), {1}: (7, {}), {2}: (8, {})} | custom-call | flops 4294967296 | bytes 10485760 | tf_op jit(solution)/shard_map/feed_rest/pallas_call | solution.py:1248
  326.8 70.5 %ffn_back.1 = (bf16[2,2048,2816]{2,1,0:T(8,128)(2,1)}, f32[512,2048]{1,0:T(8,128)}, f32[128,2816]{1,0:T(8,128)}) custom-call(bf16[2048,512]{1,0:T(8,128)(2,1)} %get-tuple-element.91.refs_0_, bf16[2,512,2816]{2,1,0:T(8,128)(2,1)} %get-tuple-element.98.refs_1_.refs_2_, bf16[2,512,2816]{2,1,0:T(8,128)(2,1)} %get-tuple-element.98.refs_1_.refs_2_, ...), custom_call_target="tpu_custom_call" | custom-call | flops 23622320128 | bytes 69206016 | tf_op jit(solution)/shard_map/ffn_back/pallas_call | solution.py:902
  397.3 113.3 %attend_back.1 = (bf16[512,3072]{1,0:T(8,128)(2,1)}, bf16[2048,1024]{1,0:T(8,128)(2,1)}, f32[128,2752]{1,0:T(8,128)}, f32[2752,128]{1,0:T(8,128)}, f32[512,2048]{1,0:T(8,128)}, /*index=5*/f32[1,2048]{1,0:T(1,128)}) custom-call(bf16[512,1024]{1,0:T(8,128)(2,1)} %get-tuple-element.86.q_ref, bf16[1536,2048]{1,0:T(8,128)(2,1)} %get-tuple-element.87.k_ref.v_ref, ...), custom_call_target="tpu_custom_call" | custom-call | flops 10737418240 | bytes 10485760 | tf_op jit(solution)/shard_map/attend_back/pallas_call | solution.py:758
  510.6 90.3 %qkv_back.1 = (bf16[1,2048,3072]{2,1,0:T(8,128)(2,1)}, f32[512,2048]{1,0:T(8,128)}, f32[128,2752]{1,0:T(8,128)}, f32[128,1024]{1,0:T(8,128)}) custom-call(bf16[2048,512]{1,0:T(8,128)(2,1)} %get-tuple-element.83.refs_0_, bf16[1,512,3072]{2,1,0:T(8,128)(2,1)} %bitcast.25, bf16[1,512,3072]{2,1,0:T(8,128)(2,1)} %bitcast.26, ...), custom_call_target="tpu_custom_call" | custom-call | flops 12884901888 | bytes 37748736 | tf_op jit(solution)/shard_map/qkv_back/pallas_call | solution.py:902
  601.0 72.5 %last_pass.1 = (f32[512,2048]{1,0:T(8,128)}, bf16[512,2048]{1,0:T(8,128)(2,1)}, f32[1024,128]{1,0:T(8,128)}, f32[128,1024]{1,0:T(8,128)}, f32[128,1024]{1,0:T(8,...) custom-call(bf16[512,2048]{1,0:T(8,128)(2,1)} %x_ref.3, f32[1,2048]{1,0:T(1,128)} %bitcast.32, ...), custom_call_target="tpu_custom_call" | custom-call | flops 20971520 | bytes 25165824 | tf_op jit(solution)/shard_map/last_pass/pallas_call | solution.py:1137
  674.8 1.5 copy.36
  676.3 1.5 copy.35
  679.7 1.6 copy-done.3
  681.3 2.0 copy.53
  (62 shorter events, 11.7 us)
Async XLA Ops:
  7.2 3.3 copy-start.9
  7.2 263.1 %all-gather.2.cloned.1.call-start = ((), (), s32[]{:S(2)}) async-start(), calls=%async_computation | async-start | bytes 30081024 | tf_op jit(solution)/shard_map/all_gather | solution.py:1298
  10.5 1.8 copy-start.1
  10.8 1.5 copy-start.17
  12.3 1.4 copy-start.18
  12.3 1.5 copy-start.8
  12.3 1.5 copy-start.14
  13.7 2.1 copy-start.15
  15.8 109.9 %copy-start.16 = (s32[512]{0:T(512)S(1)}, s32[512]{0:T(512)}, u32[]{:S(2)}) copy-start(s32[512]{0:T(512)} %param.17) | copy-start | bytes 6148
  15.8 110.4 %copy-start = (bf16[512,2048]{1,0:T(8,128)(2,1)S(1)}, bf16[512,2048]{1,0:T(8,128)(2,1)}, u32[]{:S(2)}) copy-start(bf16[512,2048]{1,0:T(8,128)(2,1)} %y_ref.1) | copy-start | bytes 6291460
  131.3 10.9 %copy-start.2 = (bf16[128,2752]{1,0:T(8,128)(2,1)S(1)}, bf16[128,2752]{1,0:T(8,128)(2,1)}, u32[]{:S(2)}) copy-start(bf16[128,2752]{1,0:T(8,128)(2,1)} %copy-done.1) | copy-start | bytes 2113540
  601.0 73.8 %copy-start.6 = (f32[128,2752]{1,0:T(8,128)S(1)}, f32[128,2752]{1,0:T(8,128)}, u32[]{:S(2)}) copy-start(f32[128,2752]{1,0:T(8,128)} %get-tuple-element.130) | copy-start | bytes 4227076
  673.5 2.9 copy-start.5
  676.3 2.0 copy-start.4
  678.3 2.9 copy-start.3
  681.3 2.0 copy-start.13
  681.3 2.8 copy-start.12
  681.3 3.6 copy-start.11
  683.3 2.4 copy-start.10
  683.3 3.2 copy-start.7
Sparse Core Ops, SparseCore 0:
  125.9 144.3 all-gather.1

commit v6 on v5

--- a/solution.py
+++ b/solution.py
@@ -19,7 +19,7 @@
 KB = WINDOW + QB
 TILE = 256
 ROWS = 128
-LATE = 2
+LATE = 3
 VMEM = 59 * 1024 * 1024
 
 
@@ -364,7 +364,7 @@
             ring_chip(self.place + 1, self.chips) * 2 + self.core,
             ring_chip(self.place - 1, self.chips) * 2 + self.core,
         )
-        self.events = self.chips * len(groups)
+        self.events = (self.chips - 1) * len(groups)
 
     @staticmethod
     def scratch(devices, shapes):
@@ -424,7 +424,12 @@
             self.own(index, stage, half).start()
 
     def begin(self):
-        for stage in range(min(self.AHEAD, self.chips)):
+        for group in range(len(self.groups)):
+            self.fetch(0, group)
+        for index, half in self.each():
+            self.mine[index][0, half] = self.chip_term(index, 0, half).astype(BF)
+            self.hop(index, 0, half, True).start()
+        for stage in range(1, self.AHEAD + 1):
             for group in range(len(self.groups)):
                 self.fetch(stage, group)
 
@@ -436,13 +441,7 @@
     def stage(self, stage, group):
         last = self.chips - 1
 
-        @pl.when(stage == 0)
-        def _():
-            for index, half in self.each(group):
-                self.mine[index][0, half] = self.chip_term(index, 0, half).astype(BF)
-                self.hop(index, 0, half, True).start()
-
-        @pl.when((stage > 0) & (stage < last))
+        @pl.when(stage < last)
         def _():
             for index, half in self.each(group):
                 self.hop(index, stage - 1, half, True).wait_recv()
@@ -471,9 +470,9 @@
         def one(event, carry):
             for group in range(count):
                 if count == 1:
-                    self.stage(event, 0)
+                    self.stage(event + 1, 0)
                 else:
-                    pl.when(lax.rem(event, count) == group)(functools.partial(self.stage, event // count, group))
+                    pl.when(lax.rem(event, count) == group)(functools.partial(self.stage, event // count + 1, group))
             return carry
 
         lax.fori_loop(first, stop, one, 0)
@@ -616,7 +615,7 @@
     )(query, kv, kv, places)
 
 
-def attend_back(query, kv, probs, mixed, w_attn, hidden, gain, d_normed, cotangent, cosine, sine, flip, ring_source, heads, out_width, identity):
+def attend_back(query, kv, probs, mixed, w_attn, hidden, gain, d_normed, d_normed_other, cotangent, cosine, sine, flip, ring_source, heads, out_width, identity):
     m, width = hidden.shape
     firsts = m // ROWS
     devices, rows, ring_width = ring_source.shape[1:]
@@ -625,7 +624,7 @@
     reach = WINDOW + m
     columns = heads * E
 
-    def kernel(q_ref, k_ref, v_ref, p_ref, x_ref, w_ref, h_ref, gain_ref, dn_ref, y_ref, c_ref, s_ref, flip_ref, source, d_ref, out_ref, sum_ref, flipped_ref, dh_ref, gain_out, g_ref, gt_ref, keys_sum, values_sum, near_out, near_in, far_out, far_in, kept, near_send, near_recv, far_send, far_recv, *scratch):
+    def kernel(q_ref, k_ref, v_ref, p_ref, x_ref, w_ref, h_ref, gain_ref, dn_ref, do_ref, y_ref, c_ref, s_ref, flip_ref, source, d_ref, out_ref, sum_ref, flipped_ref, dh_ref, gain_out, g_ref, gt_ref, keys_sum, values_sum, near_out, near_in, far_out, far_in, kept, near_send, near_recv, far_send, far_recv, *scratch):
         step = pl.program_id(0)
         half = ring_width // 2
         ring = Ring(devices, [(source.at[0], 0, half), (source.at[0], half, half)], [(sum_ref, 0), (sum_ref, half)], [[0], [1]], scratch)
@@ -652,7 +651,7 @@
 
         @pl.when(step < firsts)
         def _():
-            change, gain_part = norm_grad(h_ref[...], gain_ref[...], dn_ref[...])
+            change, gain_part = norm_grad(h_ref[...], gain_ref[...], dn_ref[...].astype(F32) + do_ref[...].astype(F32))
             total = y_ref[...].astype(F32) + change
             low = total.astype(BF)
             dh_ref[...] = total
@@ -777,6 +776,7 @@
             single((1, width)),
             rows_spec,
             rows_spec,
+            rows_spec,
             single((m, E)),
             single((m, E)),
             single(flip.shape),
@@ -800,7 +800,7 @@
         compiler_params=pltpu.CompilerParams(vmem_limit_bytes=VMEM, collective_id=identity, has_side_effects=True),
         cost_estimate=cost(8 * heads * m * KB * E * 2, 2 * heads * m * KB),
         name="attend_back",
-    )(query, kv, kv, probs, mixed, w_attn, hidden, gain, d_normed, cotangent, cosine, sine, flip, ring_source)
+    )(query, kv, kv, probs, mixed, w_attn, hidden, gain, d_normed, d_normed_other, cotangent, cosine, sine, flip, ring_source)
 
 
 def back_pass(x_t, d_out, weights, ring_sources, out_widths, costs, identity, name):
@@ -1046,7 +1046,7 @@
     )(mixed, w_attn, tokens, gain)
 
 
-def last_pass(tokens, gain, grad, d_hidden, hidden, activated, w_ffn, rest, gain_ffn_grad, flip, qkv_part, lanes, identity):
+def last_pass(tokens, gain, grad, d_hidden, hidden, act_early, act_late, w_ffn, rest, gain_ffn_grad, flip, qkv_part, lanes, identity):
     m, width = tokens.shape
     devices, rows, all_columns = qkv_part.shape
     columns = all_columns // 3
@@ -1056,13 +1056,11 @@
     total = steps + chips
     names = 3
     tiles = width // TILE
-    units = activated.shape[1]
+    some, late = act_early.shape[1], act_late.shape[1]
     sides = lax.axis_size("tensor")
     assert tiles == steps and chips >= tiles
 
-    some = w_ffn.shape[1] // 3
-
-    def kernel(x_ref, g_ref, dn_ref, dh_ref, h_ref, a_ref, w_ref, rest_ref, gf_ref, flip_ref, source, grad_ref, layer_ref, flipped_ref, q_ref, k_ref, v_ref, gains_ref, gain_sum, gain_source, sent, got, y_send, y_recv, *scratch):
+    def kernel(x_ref, g_ref, dn_ref, dh_ref, h_ref, a_ref, al_ref, w_ref, rest_ref, gf_ref, flip_ref, source, grad_ref, layer_ref, flipped_ref, q_ref, k_ref, v_ref, gains_ref, gain_sum, gain_source, sent, got, y_send, y_recv, *scratch):
         step = pl.program_id(0)
         ring = Ring(
             devices, [(source, number * columns, columns) for number in range(names)], [(q_ref, 0), (k_ref, 0), (v_ref, 0)],
@@ -1084,7 +1082,7 @@
 
         @pl.when(step < tiles)
         def _():
-            sent[step] = (dot_nt(a_ref[:, :some], w_ref[...]) + dot_nt(a_ref[:, some:], rest_ref[...])).astype(BF)
+            sent[step] = (dot_nt(a_ref[...], w_ref[...]) + dot_nt(al_ref[...], rest_ref[...])).astype(BF)
             across(step).start()
 
         @pl.when(step < steps)
@@ -1114,7 +1112,7 @@
 
         @pl.when(step >= steps)
         def _():
-            gain_ring.run(step - steps, step - steps + 1)
+            gain_ring.run(step - steps, jnp.minimum(step - steps + 1, gain_ring.events))
 
         @pl.when((step >= steps) & (step < steps + tiles))
         def _():
@@ -1145,8 +1143,8 @@
             jax.ShapeDtypeStruct((32, lanes), F32),
         ],
         in_specs=[
-            rows_spec, single((1, width)), rows_spec, rows_spec, tile_spec, single((m, units)),
-            pl.BlockSpec((TILE, some), lambda i: (early(i), 2)), pl.BlockSpec((TILE, units - some), lambda i: (early(i), 2)), single((1, width)),
+            rows_spec, single((1, width)), rows_spec, rows_spec, tile_spec, single((m, some)), single((m, late)),
+            pl.BlockSpec((TILE, some), lambda i: (early(i), 2)), pl.BlockSpec((TILE, late), lambda i: (early(i), 2)), single((1, width)),
             single(flip.shape), pl.BlockSpec(memory_space=pl.ANY),
         ],
         out_specs=[
@@ -1166,7 +1164,7 @@
         compiler_params=pltpu.CompilerParams(vmem_limit_bytes=VMEM, collective_id=identity, has_side_effects=True),
         cost_estimate=cost(20 * m * width, 24 * m * width),
         name="last_pass",
-    )(tokens, gain, grad, d_hidden, hidden, activated, w_ffn, rest, gain_ffn_grad, flip, qkv_part)
+    )(tokens, gain, grad, d_hidden, hidden, act_early, act_late, w_ffn, rest, gain_ffn_grad, flip, qkv_part)
 
 
 def feed_tile(x_ref, dy_ref, dyt_ref, g_ref, u_ref, d_ref, act_ref, both_ref, down_ref):
@@ -1209,9 +1207,9 @@
         kernel,
         grid=(early,),
         out_shape=[
-            jax.ShapeDtypeStruct((m, tiles * TILE), BF),
-            jax.ShapeDtypeStruct((2, m, tiles * TILE), BF),
-            jax.ShapeDtypeStruct((k, tiles * TILE), BF),
+            jax.ShapeDtypeStruct((m, early * TILE), BF),
+            jax.ShapeDtypeStruct((2, m, early * TILE), BF),
+            jax.ShapeDtypeStruct((k, early * TILE), BF),
             jax.ShapeDtypeStruct((k, block.shape[1]), BF),
         ],
         in_specs=[
@@ -1236,38 +1234,146 @@
     )(x, dy, dy_t, w, w, w, block)
 
 
-def feed_rest(x, dy, dy_t, rest, activated, d_both, down_part):
-    m, k = x.shape
-    tiles = activated.shape[1] // TILE
-    early = tiles - LATE
-
-    def kernel(x_ref, dy_ref, dyt_ref, g_ref, u_ref, d_ref, act_in, both_in, down_in, act_ref, both_ref, down_ref):
-        feed_tile(x_ref, dy_ref, dyt_ref, g_ref, u_ref, d_ref, act_ref, both_ref, down_ref)
-
+def ffn_back(x, x_t, dy, dy_t, d_early, w_ffn, rest, down_early, identity):
+    m, width = x.shape
+    devices, rows, some = down_early.shape
+    late = LATE * TILE
+    padded = some + late
+    early_tiles = some // TILE
+    tiles = width // TILE
+    grads = 2 * (early_tiles + LATE)
+    total = LATE + tiles + grads
+    sides = lax.axis_size("tensor")
+    pieces = [(rows, some // 2)] * 2
+
+    def kernel(x_ref, xt_ref, dy_ref, dyt_ref, rg_ref, ru_ref, rd_ref, d_ref, tile_ref, wg_ref, wu_ref, lg_ref, lu_ref, source, act_ref, grad_ref, sent_ref, got, sum_ref, d_late, down_late, down_tile, both_tile, sent, y_send, y_recv, *scratch):
+        step = pl.program_id(0)
+        ring = Ring(devices, [(source, 0, some // 2), (source, some // 2, some // 2)], [(sum_ref, 0), (sum_ref, some // 2)], [[0], [1]], scratch[:11])
+        late_ring = Ring(devices, [(down_late, 0, late)], [(sum_ref, some)], [[0]], scratch[11:])
+        other = (ring.me, lax.rem(ring.side + 1, sides))
+
+        def across(which):
+            return pltpu.make_async_remote_copy(
+                src_ref=sent.at[which], dst_ref=got.at[:, pl.ds(pl.multiple_of(which * TILE, TILE), TILE)],
+                send_sem=y_send.at[which], recv_sem=y_recv.at[which], device_id=other, device_id_type=MESH,
+            )
+
+        @pl.when(step == 0)
+        def _():
+            ring.barrier((other,))
+            ring.begin()
+
+        @pl.when(step < LATE)
+        def _():
+            feed_tile(x_ref, dy_ref, dyt_ref, rg_ref, ru_ref, rd_ref, act_ref, both_tile, down_tile)
+            here = pl.ds(pl.multiple_of(step * TILE, TILE), TILE)
+            d_late[:, :, here] = both_tile[...]
+            down_late[:, :, here] = down_tile[...].reshape(devices, rows, TILE)
+
+        @pl.when(step == LATE - 1)
+        def _():
+            late_ring.begin()
+
+        @pl.when((step >= LATE) & (step < LATE + tiles))
+        def _():
+            which = step - LATE
+            part = dot_nt(d_ref[0], wg_ref[...]) + dot_nt(d_ref[1], wu_ref[...])
+            part += dot_nt(d_late[0], lg_ref[...]) + dot_nt(d_late[1], lu_ref[...])
+            low = part.astype(BF)
+            sent[which] = low
+            sent_ref[...] = low
+            across(which).start()
+
+        @pl.when((step >= LATE + tiles) & (step < LATE + tiles + 2 * early_tiles))
+        def _():
+            grad_ref[0] = dot_nn(xt_ref[...], tile_ref[0]).astype(BF)
+
+        @pl.when(step >= LATE + tiles + 2 * early_tiles)
+        def _():
+            number = step - (LATE + tiles + 2 * early_tiles)
+            here = pl.ds(pl.multiple_of(lax.rem(number, LATE) * TILE, TILE), TILE)
+            grad_ref[0] = dot_nn(xt_ref[...], d_late[number // LATE, :, here]).astype(BF)
+
+        ring.pace(step, [(LATE, 12), (tiles, 8), (grads, 4)])
+        late_ring.pace(step, [(LATE, 0), (tiles, 8), (grads, 4)])
+
+        @pl.when(step == total - 1)
+        def _():
+            for which in range(tiles):
+                across(which).wait()
+            ring.finish()
+            late_ring.finish()
+
+    def first(i):
+        return jnp.minimum(i, LATE - 1)
+
+    def second(i):
+        return jnp.clip(i - LATE, 0, tiles - 1)
+
+    def third(i):
+        at = jnp.clip(i - LATE - tiles, 0, 2 * early_tiles - 1)
+        return (at // early_tiles, 0, at % early_tiles)
+
+    def grad_at(i):
+        at = jnp.maximum(i - LATE - tiles, 0)
+        more = jnp.maximum(at - 2 * early_tiles, 0)
+        is_late = at // (2 * early_tiles)
+        return (
+            (1 - is_late) * (at // early_tiles) + is_late * (more // LATE),
+            0,
+            (1 - is_late) * (at % early_tiles) + is_late * (early_tiles + more % LATE),
+        )
+
+    assert LATE <= early_tiles
     any_space = pl.BlockSpec(memory_space=pl.ANY)
+    dma = pltpu.SemaphoreType.DMA
+
+    def rest_tile(which):
+        return pl.BlockSpec((width, TILE), lambda i: (0, first(i) + which * LATE))
+
     return pl.pallas_call(
         kernel,
-        grid=(LATE,),
-        out_shape=[jax.ShapeDtypeStruct(a.shape, BF) for a in (activated, d_both, down_part)],
+        grid=(total,),
+        out_shape=[
+            jax.ShapeDtypeStruct((m, late), BF),
+            jax.ShapeDtypeStruct((2, width, padded), BF),
+            jax.ShapeDtypeStruct((m, width), BF),
+            jax.ShapeDtypeStruct((m, width), BF),
+            jax.ShapeDtypeStruct((rows, padded), F32),
+        ],
         in_specs=[
-            single((m, k)),
-            single((m, k)),
-            single((k, m)),
-            pl.BlockSpec((k, TILE), lambda i: (0, i)),
-            pl.BlockSpec((k, TILE), lambda i: (0, i + LATE)),
-            pl.BlockSpec((k, TILE), lambda i: (0, i + 2 * LATE)),
-            any_space, any_space, any_space,
+            single((m, width)), single((width, m)), single((m, width)), single((width, m)),
+            rest_tile(0), rest_tile(1), rest_tile(2),
+            single((2, m, some)),
+            pl.BlockSpec((1, m, TILE), third),
+            pl.BlockSpec((TILE, some), lambda i: (second(i), 0)),
+            pl.BlockSpec((TILE, some), lambda i: (second(i), 1)),
+            pl.BlockSpec((TILE, late), lambda i: (second(i), 0)),
+            pl.BlockSpec((TILE, late), lambda i: (second(i), 1)),
+            any_space,
         ],
         out_specs=[
-            pl.BlockSpec((m, TILE), lambda i: (0, i + early)),
-            pl.BlockSpec((2, m, TILE), lambda i: (0, 0, i + early)),
-            pl.BlockSpec((k, TILE), lambda i: (0, i + early)),
-        ],
-        input_output_aliases={6: 0, 7: 1, 8: 2},
-        compiler_params=pltpu.CompilerParams(vmem_limit_bytes=VMEM),
-        cost_estimate=cost(8 * m * k * LATE * TILE, 8 * (m + k) * LATE * TILE, m * LATE * TILE),
-        name="feed_rest",
-    )(x, dy, dy_t, rest, rest, rest, activated, d_both, down_part)
+            pl.BlockSpec((m, TILE), lambda i: (0, first(i))),
+            pl.BlockSpec((1, width, TILE), grad_at),
+            pl.BlockSpec((m, TILE), lambda i: (0, second(i))),
+            any_space,
+            single((rows, padded)),
+        ],
+        scratch_shapes=[
+            pltpu.VMEM((2, m, late), BF),
+            pltpu.VMEM((devices, rows, late), BF),
+            pltpu.VMEM((width, TILE), BF),
+            pltpu.VMEM((2, m, TILE), BF),
+            pltpu.VMEM((tiles, m, TILE), BF),
+            dma((tiles,)),
+            dma((tiles,)),
+            *Ring.scratch(devices, pieces),
+            *Ring.scratch(devices, [(rows, late)]),
+        ],
+        compiler_params=pltpu.CompilerParams(vmem_limit_bytes=VMEM, collective_id=identity, has_side_effects=True),
+        cost_estimate=cost(8 * m * width * padded + 8 * m * width * late, 10 * width * padded),
+        name="ffn_back",
+    )(x, x_t, dy, dy_t, rest, rest, rest, d_early, d_early, w_ffn, w_ffn, rest, rest, down_early)
 
 
 def shards(tokens, positions, attn_gain, w_query, w_key, w_value, w_out, ffn_gain, w_gate, w_up, w_down, cotangent):
@@ -1314,23 +1420,21 @@
     hidden, normed_ffn, normed_ffn_t = out_norm(mixed, w_attn, 3, tokens, gain_ffn, 5)
 
     cotangent_t = cotangent.T
-    activated, d_both, down_part, rest = feed(normed_ffn, cotangent, cotangent_t, w_ffn, rest_pack, tiles, 6)
-    activated, d_both, down_part = feed_rest(normed_ffn, cotangent, cotangent_t, rest, activated, d_both, down_part)
-    both_part, d_normed_ffn, down_grad = back_pass(
-        normed_ffn_t, d_both, [(w_ffn, some), (rest, padded - some)], [(down_part.reshape(devices, own_rows, padded), None, 2)], [padded],
-        (2, 1), 1, "ffn_back",
+    act_early, d_early, down_early, rest = feed(normed_ffn, cotangent, cotangent_t, w_ffn, rest_pack, tiles, 6)
+    act_late, both_part, d_normed_ffn, d_normed_other, down_grad = ffn_back(
+        normed_ffn, normed_ffn_t, cotangent, cotangent_t, d_early, w_ffn, rest, down_early.reshape(devices, own_rows, some), 1
     )
     both_part = both_part.reshape(2, devices, own_rows, padded)
 
     d_qkv, out_part, gate_grad, w_down_grad, d_hidden, gain_ffn_grad = attend_back(
-        query, kv, probs, mixed, w_attn, hidden, gain_ffn, d_normed_ffn, cotangent, cosine, sine, down_grad, both_part, heads, hidden_units, 2
+        query, kv, probs, mixed, w_attn, hidden, gain_ffn, d_normed_ffn, d_normed_other, cotangent, cosine, sine, down_grad, both_part, heads, hidden_units, 2
     )
     qkv_part, d_normed_attn, up_grad, out_grad = back_pass(
         normed_attn_t, d_qkv[None], [(w_attn, 3 * head_columns)],
         [(both_part, 1, 2), (out_part.reshape(devices, own_rows, head_columns), None, 1)], [hidden_units, head_columns], (4, 3), 3, "qkv_back",
     )
     tokens_grad, layer_out, w_out_grad, query_grad, key_grad, value_grad, gain_grads = last_pass(
-        tokens, gain_attn, d_normed_attn, d_hidden, hidden, activated, w_ffn, rest, gain_ffn_grad, out_grad,
+        tokens, gain_attn, d_normed_attn, d_hidden, hidden, act_early, act_late, w_ffn, rest, gain_ffn_grad, out_grad,
         qkv_part.reshape(devices, own_rows, 3 * head_columns), lanes, 4,
     )
     return (

time: 699 us -> 685 us (0.980)
  waiting for transfers between devices: 24.2 us -> 9.44 us
    pallas_call x2 -> x1, Pallas kernels: 161 us -> 88.1 us  [back_pass(): pl.pallas_call(kernel, grid=(total,), out_shape=out_shape, in_specs=specs...]
    pallas_call x1, Pallas kernels: 10.3 us -> 74.6 us  [ffn_back(): pl.pallas_call(kernel, grid=(total,), out_shape=[jax.ShapeDtypeStruct((m,...]
    all_gather x1, waiting for transfers between devices: 24.2 us -> 9.42 us  [shards(): w_ffn = lax.all_gather(ffn_pack, 'dp', axis=0, tiled=True)]
    pallas_call x1, Pallas kernels: 46.2 us -> 56.3 us  [feed(): pl.pallas_call(kernel, grid=(early,), out_shape=[jax.ShapeDtypeStruct((m,...]
    unnamed x52 -> x54, local copies, waits for them, and re-layouts: 20.7 us -> 19.7 us
where the time goes in v6:
time: 685 us; the launch traced here: 681 us
  Pallas kernels  625 us (91%)
  local copies, waits for them, and re-layouts  22.5 us (3%)
  between operations  15.2 us (2%)
  waiting for transfers between devices  9.44 us (1%)
  other arithmetic  9.18 us (1%)
    pallas_call x1, Pallas kernels, attend_back(): pl.pallas_call(kernel, grid=(firsts + heads,), out_shape=[jax.ShapeDtypeS...  114 us
    pallas_call x1, Pallas kernels, ring_gather(): pl.pallas_call(functools.partial(gather_kernel, devices, chunks, len(arra...  110 us
    pallas_call x1, Pallas kernels, back_pass(): pl.pallas_call(kernel, grid=(total,), out_shape=out_shape, in_specs=specs...  88.1 us
    pallas_call x1, Pallas kernels, ffn_back(): pl.pallas_call(kernel, grid=(total,), out_shape=[jax.ShapeDtypeStruct((m,...  74.6 us
    pallas_call x1, Pallas kernels, last_pass(): pl.pallas_call(kernel, grid=(total,), out_shape=[jax.ShapeDtypeStruct((m,...  73.2 us
    pallas_call x1, Pallas kernels, feed(): pl.pallas_call(kernel, grid=(early,), out_shape=[jax.ShapeDtypeStruct((m,...  56.3 us
    pallas_call x1, Pallas kernels, out_norm(): pl.pallas_call(kernel, grid=(2 * steps,), out_shape=[jax.ShapeDtypeStruct...  53 us
    pallas_call x1, Pallas kernels, project(): pl.pallas_call(kernel, grid=(3 * some,), out_shape=[jax.ShapeDtypeStruct(...  24.5 us
  transfers between devices with their start and end apart: 1, of which 1 were waited for; matrix products, arithmetic and copies ran while one was open for 2% of the time, Pallas kernels for 16%

profile of v6, /device:TPU:0, one launch (start us, length us, event | category | flops | bytes accessed | tf_op | source)
XLA Modules:
  0.0 681.0 jit_solution(11866965521848704837)
XLA Ops:
  7.2 1.1 copy.23
  8.4 1.4 copy.24
  10.2 1.4 copy.26
  11.7 1.2 pad_maximum_fusion
  14.1 109.8 %ring_gather.1 = (bf16[2048,4096]{1,0:T(8,128)(2,1)}, bf16[512,128]{1,0:T(8,128)(2,1)}, bf16[512,2048]{1,0:T(8,128)(2,1)}, bf16[512,2048]{1,0:T(8,128)(2,1)}) custom-call(bf16[128,4096]{1,0:T(8,128)(2,1)} %pad_maximum_fusion.1.refs_0_, bf16[32,128]{1,0:T(8,128)(2,1)} %copy-done.16, bf16[512,2048]{1,0:T(8,128)(2,1)} %x_ref.3), custom_call_target="tpu_custom_call" | custom-call | tf_op jit(solution)/shard_map/ring_gather/pallas_call | solution.py:214
  124.4 2.7 copy.29
  129.1 10.8 %first_norm.1 = (bf16[1536,2048]{1,0:T(8,128)(2,1)}, bf16[2048,512]{1,0:T(8,128)(2,1)}) custom-call(bf16[512,2048]{1,0:T(8,128)(2,1)} %get-tuple-element.80.far_ref, bf16[512,2048]{1,0:T(8,128)(2,1)} %get-tuple-element.81.near_ref, bf16[512,2048]{1,0:T(8,128)(2,1)} %x_ref.3, f32[1,2048]{1,0:T(1,128)} %bitcast.31), custom_call_target="tpu_custom_call" | custom-call | flops 25165824 | bytes 14680064 | tf_op jit(solution)/shard_map/first_norm/pallas_call | solution.py:970
  140.1 2.8 fusion.2
  143.9 1.6 pad_maximum_fusion.2
  145.5 24.5 %project.1 = (bf16[512,1024]{1,0:T(8,128)(2,1)}, bf16[1536,2048]{1,0:T(8,128)(2,1)}) custom-call(bf16[1536,2048]{1,0:T(8,128)(2,1)} %get-tuple-element.83.x_ref, bf16[2048,4096]{1,0:T(8,128)(2,1)} %get-tuple-element.84.w_ref.refs_3_, f32[1536,128]{1,0:T(8,128)} %get-tuple-element.139.c_ref, f32[1536,128]{1,0:T(8,128)} %get-tuple-element.140.s_ref), custom_call_target="tpu_custom_call" | custom-call | flops 15032385536 | bytes 28311552 | tf_op jit(solution)/shard_map/project/pallas_call | solution.py:552
  170.1 20.3 %attend.1 = (bf16[512,1024]{1,0:T(8,128)(2,1)}, bf16[8,2,1280,256]{3,2,1,0:T(8,128)(2,1)}) custom-call(bf16[512,1024]{1,0:T(8,128)(2,1)} %get-tuple-element.85.q_ref, bf16[1536,2048]{1,0:T(8,128)(2,1)} %get-tuple-element.86.k_ref.v_ref, bf16[1536,2048]{1,0:T(8,128)(2,1)} %get-tuple-element.86.k_ref.v_ref, s32[1,512]{1,0:T(1,128)} %bitcast.35), custom_call_target="tpu_custom_call" | custom-call | flops 5368709120 | bytes 10485760 | tf_op jit(solution)/shard_map/attend/pallas_call | solution.py:597
  190.4 53.0 %out_norm.1 = (f32[512,2048]{1,0:T(8,128)}, bf16[512,2048]{1,0:T(8,128)(2,1)}, bf16[2048,512]{1,0:T(8,128)(2,1)}) custom-call(bf16[512,1024]{1,0:T(8,128)(2,1)} %get-tuple-element.88.x_ref, bf16[2048,4096]{1,0:T(8,128)(2,1)} %get-tuple-element.84.w_ref.refs_3_, bf16[512,2048]{1,0:T(8,128)(2,1)} %x_ref.3, f32[1,2048]{1,0:T(1,128)} %bitcast.33), custom_call_target="tpu_custom_call" | custom-call | flops 2147483648 | bytes 12582912 | tf_op jit(solution)/shard_map/out_norm/pallas_call | solution.py:1027
  244.2 9.4 %all-gather.2.cloned.1.call-done.g_ref.u_ref.d_ref.wg_ref.wu_ref.w_ref = bf16[2048,6144]{1,0:T(8,128)(2,1)} async-done(((bf16[128,6144]{1,0:T(8,128)(2,1)}), bf16[2048,6144]{1,0:T(8,128)(2,1)}) %all-gather.2.cloned.1.call-update) | async-done | bytes 25165840 | tf_op jit(solution)/shard_map/all_gather | solution.py:1404
  253.6 56.3 %feed.1 = (bf16[512,2048]{1,0:T(8,128)(2,1)}, bf16[2,512,2048]{2,1,0:T(8,128)(2,1)}, bf16[2048,2048]{1,0:T(8,128)(2,1)}, bf16[2048,2304]{1,0:T(8,128)(2,1)}) custom-call(bf16[512,2048]{1,0:T(8,128)(2,1)} %get-tuple-element.90.x_ref, bf16[512,2048]{1,0:T(8,128)(2,1)} %y_ref.1, bf16[2048,512]{1,0:T(8,128)(2,1)} %bitcast.21, ...), custom_call_target="tpu_custom_call" | custom-call | flops 17179869184 | bytes 41943040 | tf_op jit(solution)/shard_map/feed/pallas_call | solution.py:1206
  310.0 74.6 %ffn_back.1 = (bf16[512,768]{1,0:T(8,128)(2,1)}, bf16[2,2048,2816]{2,1,0:T(8,128)(2,1)}, bf16[512,2048]{1,0:T(8,128)(2,1)}, bf16[512,2048]{1,0:T(8,128)(2,1)}, f32[128,2816]{1,0:T(8,128)}) custom-call(bf16[512,2048]{1,0:T(8,128)(2,1)} %get-tuple-element.90.x_ref, bf16[2048,512]{1,0:T(8,128)(2,1)} %get-tuple-element.91.xt_ref, bf16[512,2048]{1,0:T(8,128)(2,1)} %y_ref.1, ...), custom_call_target="tpu_custom_call" | custom-call | flops 30064771072 | bytes 57671680 | tf_op jit(solution)/shard_map/ffn_back/pallas_call | solution.py:1334
  384.6 113.9 %attend_back.1 = (bf16[512,3072]{1,0:T(8,128)(2,1)}, bf16[2048,1024]{1,0:T(8,128)(2,1)}, f32[128,2752]{1,0:T(8,128)}, f32[2752,128]{1,0:T(8,128)}, f32[512,2048]{1,0:T(8,128)}, /*index=5*/f32[1,2048]{1,0:T(1,128)}) custom-call(bf16[512,1024]{1,0:T(8,128)(2,1)} %get-tuple-element.85.q_ref, bf16[1536,2048]{1,0:T(8,128)(2,1)} %get-tuple-element.86.k_ref.v_ref, ...), custom_call_target="tpu_custom_call" | custom-call | flops 10737418240 | bytes 10485760 | tf_op jit(solution)/shard_map/attend_back/pallas_call | solution.py:757
  498.5 88.1 %qkv_back.1 = (bf16[1,2048,3072]{2,1,0:T(8,128)(2,1)}, f32[512,2048]{1,0:T(8,128)}, f32[128,2752]{1,0:T(8,128)}, f32[128,1024]{1,0:T(8,128)}) custom-call(bf16[2048,512]{1,0:T(8,128)(2,1)} %get-tuple-element.82.refs_0_, bf16[1,512,3072]{2,1,0:T(8,128)(2,1)} %bitcast.24, bf16[1,512,3072]{2,1,0:T(8,128)(2,1)} %bitcast.25, ...), custom_call_target="tpu_custom_call" | custom-call | flops 12884901888 | bytes 37748736 | tf_op jit(solution)/shard_map/qkv_back/pallas_call | solution.py:902
  586.6 73.2 %last_pass.1 = (f32[512,2048]{1,0:T(8,128)}, bf16[512,2048]{1,0:T(8,128)(2,1)}, f32[1024,128]{1,0:T(8,128)}, f32[128,1024]{1,0:T(8,128)}, f32[128,1024]{1,0:T(8,...) custom-call(bf16[512,2048]{1,0:T(8,128)(2,1)} %x_ref.3, f32[1,2048]{1,0:T(1,128)} %bitcast.32, ...), custom_call_target="tpu_custom_call" | custom-call | flops 20971520 | bytes 25165824 | tf_op jit(solution)/shard_map/last_pass/pallas_call | solution.py:1135
  659.9 1.3 slice_bitcast_fusion
  661.2 1.5 copy.33
  662.7 1.5 copy.32
  664.7 1.3 copy.46
  666.1 1.6 copy-done.3
  667.7 2.0 copy.47
  (63 shorter events, 10.2 us)
Async XLA Ops:
  7.2 2.7 copy-start.8
  7.2 246.4 %all-gather.2.cloned.1.call-start = ((), (), s32[]{:S(2)}) async-start(), calls=%async_computation | async-start | bytes 26738688 | tf_op jit(solution)/shard_map/all_gather | solution.py:1404
  9.8 1.8 copy-start.1
  10.1 1.6 copy-start.18
  11.6 1.4 copy-start.19
  11.6 1.4 copy-start.13
  11.6 1.4 copy-start.14
  11.6 1.4 copy-start.15
  13.0 1.1 copy-start.16
  14.0 109.8 %copy-start.17 = (s32[512]{0:T(512)S(1)}, s32[512]{0:T(512)}, u32[]{:S(2)}) copy-start(s32[512]{0:T(512)} %param.17) | copy-start | bytes 6148
  14.0 110.4 %copy-start = (bf16[512,2048]{1,0:T(8,128)(2,1)S(1)}, bf16[512,2048]{1,0:T(8,128)(2,1)}, u32[]{:S(2)}) copy-start(bf16[512,2048]{1,0:T(8,128)(2,1)} %y_ref.1) | copy-start | bytes 6291460
  129.1 10.9 %copy-start.2 = (bf16[128,2752]{1,0:T(8,128)(2,1)S(1)}, bf16[128,2752]{1,0:T(8,128)(2,1)}, u32[]{:S(2)}) copy-start(bf16[128,2752]{1,0:T(8,128)(2,1)} %copy-done.1) | copy-start | bytes 2113540
  586.6 74.6 %copy-start.6 = (f32[128,2752]{1,0:T(8,128)S(1)}, f32[128,2752]{1,0:T(8,128)}, u32[]{:S(2)}) copy-start(f32[128,2752]{1,0:T(8,128)} %get-tuple-element.128) | copy-start | bytes 4227076
  659.9 2.9 copy-start.5
  662.7 2.0 copy-start.4
  664.7 2.9 copy-start.3
  667.7 2.0 copy-start.12
  667.7 2.8 copy-start.11
  667.7 3.6 copy-start.10
  669.7 2.4 copy-start.9
  669.7 3.2 copy-start.7
Sparse Core Ops, SparseCore 0:
  124.0 129.5 all-gather.1

commit v7 on v6

--- a/solution.py
+++ b/solution.py
@@ -29,6 +29,10 @@
 
 def single(shape):
     return pl.BlockSpec(shape, lambda i: (0,) * len(shape), pipeline_mode=pl.Buffered(1))
+
+
+def loads(sources, targets, semaphores):
+    return [pltpu.make_async_copy(s, t, semaphores.at[i]) for i, (s, t) in enumerate(zip(sources, targets))]
 
 
 def cost(flops, nbytes, special=0):
@@ -624,30 +628,24 @@
     reach = WINDOW + m
     columns = heads * E
 
-    def kernel(q_ref, k_ref, v_ref, p_ref, x_ref, w_ref, h_ref, gain_ref, dn_ref, do_ref, y_ref, c_ref, s_ref, flip_ref, source, d_ref, out_ref, sum_ref, flipped_ref, dh_ref, gain_out, g_ref, gt_ref, keys_sum, values_sum, near_out, near_in, far_out, far_in, kept, near_send, near_recv, far_send, far_recv, *scratch):
+    def kernel(q_ref, k_ref, v_ref, p_ref, x_ref, w_ref, h_ref, gain_ref, dn_ref, do_ref, y_ref, c_hbm, s_hbm, flip_hbm, source, dq_ref, dk_ref, dv_ref, out_ref, sum_ref, flipped_ref, dh_ref, gain_out, c_ref, s_ref, flip_ref, load_sem, g_ref, gt_ref, keys_sum, values_sum, *scratch):
         step = pl.program_id(0)
         half = ring_width // 2
         ring = Ring(devices, [(source.at[0], 0, half), (source.at[0], half, half)], [(sum_ref, 0), (sum_ref, half)], [[0], [1]], scratch)
-        me, side, core = ring.me, ring.side, ring.core
+        brought = loads((c_hbm, s_hbm, flip_hbm), (c_ref, s_ref, flip_ref), load_sem)
+        turns = [(firsts + 2 * heads, 1)]
 
         @pl.when(step == 0)
         def _():
-            ring.barrier(((lax.rem(me + 2, devices), side), (lax.rem(me + devices - 2, devices), side)))
+            for copy in brought:
+                copy.start()
+            ring.barrier()
             ring.begin()
 
-        def near_copy(which):
-            return pltpu.make_async_remote_copy(
-                src_ref=near_out.at[which], dst_ref=near_in.at[which], send_sem=near_send.at[which], recv_sem=near_recv.at[which],
-                device_id=(ring.partner, side), device_id_type=MESH,
-            )
-
-        def far_copy(which):
-            return pltpu.make_async_remote_copy(
-                src_ref=far_out.at[which], dst_ref=far_in.at[which], send_sem=far_send.at[which], recv_sem=far_recv.at[which],
-                device_id=(lax.rem(me + devices - 2, devices), side), device_id_type=MESH,
-            )
-
-        turns = [(firsts + 2 * heads, 1)]
+        @pl.when(step == firsts)
+        def _():
+            for copy in brought:
+                copy.wait()
 
         @pl.when(step < firsts)
         def _():
@@ -680,6 +678,7 @@
             for block in range(blocks):
                 span = slice(block * QB, block * QB + KB)
                 here = slice(block * QB, (block + 1) * QB)
+                there = slice(WINDOW + block * QB, WINDOW + (block + 1) * QB)
                 low = p_ref[0, block]
                 grad = grad_all[here, :]
                 d_probs = dot_nt(v_ref[span, :], grad)
@@ -689,49 +688,11 @@
                 values_sum[span, :] += dot_nn(low, grad)
                 keys_sum[span, :] += dot_nn(d_scores, q_ref[here, :])
                 d_query = dot_nn(keys_t[:, span], d_scores).T * factor
-                d_ref[here, pl.ds(pl.multiple_of(head * E, E), E)] = turned(d_query, c_ref[here, :], s_ref[here, :], True).astype(BF)
+                dq_ref[here, :] = turned(d_query, c_ref[there, :], s_ref[there, :], True).astype(BF)
                 if block == 0:
                     ring.pace(firsts + 2 * head, turns)
-            for which, (total, scale) in enumerate(((keys_sum, factor), (values_sum, 1.0))):
-                far_out[head, which] = (total[:m, :] * scale).astype(BF)
-                near_out[head, which] = (total[m : 2 * m, :] * scale).astype(BF)
-                kept[head, which] = total[2 * m :, :] * scale
-            near_copy(head).start()
-
-            def settle(which):
-                near_copy(which).wait_recv()
-                came = near_in[which].astype(F32)
-                share = core.astype(F32)
-                far_out[which] = (far_out[which].astype(F32) + came * share).astype(BF)
-                kept[which] = kept[which] + came * (1.0 - share)
-
-                @pl.when(me >= 2)
-                def _():
-                    far_copy(which).start()
-
-            def close(which):
-                @pl.when(me < devices - 2)
-                def _():
-                    far_copy(which).wait_recv()
-                    kept[which] = kept[which] + far_in[which].astype(F32)
-
-                d_key = turned(kept[which, 0], c_ref[...], s_ref[...], True).astype(BF)
-                d_ref[:, pl.ds(pl.multiple_of((heads + which) * E, E), E)] = d_key
-                d_ref[:, pl.ds(pl.multiple_of((2 * heads + which) * E, E), E)] = kept[which, 1].astype(BF)
-                near_copy(which).wait_send()
-
-                @pl.when(me >= 2)
-                def _():
-                    far_copy(which).wait_send()
-
-            @pl.when(head > 0)
-            def _():
-                settle(head - 1)
-
-            @pl.when(head == heads - 1)
-            def _():
-                settle(head)
-
+            dk_ref[...] = turned(keys_sum[...] * factor, c_ref[...], s_ref[...], True).astype(BF)
+            dv_ref[...] = values_sum[...].astype(BF)
             ring.pace(firsts + 2 * head + 1, turns)
 
             @pl.when(head == 1)
@@ -740,25 +701,22 @@
 
             @pl.when(head == heads - 1)
             def _():
-                def one(which, carry):
-                    close(which)
-                    return carry
-
-                lax.fori_loop(0, heads, one, 0)
                 ring.finish()
 
     def at(i):
         return jnp.maximum(i - firsts, 0)
 
     head_spec = pl.BlockSpec((m, E), lambda i: (0, at(i)))
+    long_spec = pl.BlockSpec((reach, E), lambda i: (0, at(i)))
     rows_spec = pl.BlockSpec((ROWS, width), lambda i: (jnp.minimum(i, firsts - 1), 0))
-    dma = pltpu.SemaphoreType.DMA
-    pieces = (heads, 2, m, E)
+    any_space = pl.BlockSpec(memory_space=pl.ANY)
     return pl.pallas_call(
         kernel,
         grid=(firsts + heads,),
         out_shape=[
-            jax.ShapeDtypeStruct((m, 3 * columns), BF),
+            jax.ShapeDtypeStruct((m, columns), BF),
+            jax.ShapeDtypeStruct((reach, columns), BF),
+            jax.ShapeDtypeStruct((reach, columns), BF),
             jax.ShapeDtypeStruct((width, columns), BF),
             jax.ShapeDtypeStruct((rows, out_width), F32),
             jax.ShapeDtypeStruct((out_width, rows), F32),
@@ -767,7 +725,7 @@
         ],
         in_specs=[
             head_spec,
-            pl.BlockSpec((reach, E), lambda i: (0, at(i))),
+            long_spec,
             pl.BlockSpec((reach, E), lambda i: (0, at(i) + heads)),
             pl.BlockSpec((1, blocks, KB, QB), lambda i: (at(i), 0, 0, 0)),
             head_spec,
@@ -777,13 +735,12 @@
             rows_spec,
             rows_spec,
             rows_spec,
-            single((m, E)),
-            single((m, E)),
-            single(flip.shape),
-            pl.BlockSpec(memory_space=pl.ANY),
+            any_space, any_space, any_space, any_space,
         ],
         out_specs=[
-            single((m, 3 * columns)),
+            head_spec,
+            long_spec,
+            long_spec,
             pl.BlockSpec((width, E), lambda i: (0, at(i))),
             single((rows, out_width)),
             single((out_width, rows)),
@@ -791,10 +748,9 @@
             single((1, width)),
         ],
         scratch_shapes=[
+            pltpu.VMEM((reach, E), F32), pltpu.VMEM((reach, E), F32), pltpu.VMEM(flip.shape, F32), pltpu.SemaphoreType.DMA((3,)),
             pltpu.VMEM((m, width), BF), pltpu.VMEM((width, m), BF),
             pltpu.VMEM((reach, E), F32), pltpu.VMEM((reach, E), F32),
-            pltpu.VMEM(pieces, BF), pltpu.VMEM(pieces, BF), pltpu.VMEM(pieces, BF), pltpu.VMEM(pieces, BF), pltpu.VMEM(pieces, F32),
-            dma((heads,)), dma((heads,)), dma((heads,)), dma((heads,)),
             *Ring.scratch(devices, [(rows, ring_width // 2)] * 2),
         ],
         compiler_params=pltpu.CompilerParams(vmem_limit_bytes=VMEM, collective_id=identity, has_side_effects=True),
@@ -803,119 +759,186 @@
     )(query, kv, kv, probs, mixed, w_attn, hidden, gain, d_normed, d_normed_other, cotangent, cosine, sine, flip, ring_source)
 
 
-def back_pass(x_t, d_out, weights, ring_sources, out_widths, costs, identity, name):
-    amount, m, columns = d_out.shape
-    width = x_t.shape[0]
-    devices = lax.axis_size("dp")
-    sides = lax.axis_size("tensor")
+def qkv_back(x_t, d_query, d_key, d_value, w_attn, up_part, out_part, out_width, identity):
+    width, reach = x_t.shape
+    m, columns = d_query.shape
+    devices, rows, up_width = up_part.shape[1:]
     tiles = width // TILE
     per = columns // TILE
-    total = tiles + amount * per
-    count = len(ring_sources)
-    shapes = [(source.shape[-2], source.shape[-1] // pieces) for source, _, pieces in ring_sources for _ in range(pieces)]
-    groups = [[index] for index in range(len(shapes))]
-
-    def kernel(*refs):
-        refs = list(refs)
-
-        def take(number):
-            taken = refs[:number]
-            del refs[:number]
-            return taken
-
-        xt_ref, tile_ref, d_ref = take(3)
-        w_refs = [take(amount) for _ in weights]
-        sources = [ref if lead is None else ref.at[lead] for ref, (_, lead, _) in zip(take(count), ring_sources)]
-        grad_ref, back_ref = take(2)
-        sums = take(count)
-        sent, got, y_send, y_recv = take(4)
-        terms, goals = [], []
-        for source, goal, (array, _, pieces) in zip(sources, sums, ring_sources):
-            piece = array.shape[-1] // pieces
-            terms += [(source, number * piece, piece) for number in range(pieces)]
-            goals += [(goal, number * piece) for number in range(pieces)]
-        ring = Ring(devices, terms, goals, groups, refs)
-        other = (ring.me, lax.rem(ring.side + 1, sides))
+    total = tiles + 3 * per
+    sides = lax.axis_size("tensor")
+    half = m // 2
+    piece = up_width // 2
+    shapes = [(rows, piece), (rows, piece), (rows, columns)]
+    assert 3 * per > tiles and reach == 3 * m
+
+    def kernel(xt_hbm, dq_hbm, dk_hbm, dv_hbm, w_ref, up_ref, out_ref, grad_ref, sent_ref, got, add_ref, up_sum, out_sum, xt_ref, dq_ref, dk_ref, dv_ref, load_sem, sent, early, early_in, near_in, far_in, own_send, own_recv, early_send, early_recv, near_send, near_recv, far_send, far_recv, *scratch):
         step = pl.program_id(0)
-
-        def across(which):
+        source = up_ref.at[1]
+        ring = Ring(
+            devices, [(source, 0, piece), (source, piece, piece), (out_ref, 0, columns)], [(up_sum, 0), (up_sum, piece), (out_sum, 0)],
+            [[0], [1], [2]], scratch,
+        )
+        me, side = ring.me, ring.side
+        across = lax.rem(side + 1, sides)
+        later, before = lax.rem(me + 2, devices), lax.rem(me + devices - 2, devices)
+        share = ring.core.astype(F32)
+        brought = loads((dq_hbm, dk_hbm, dv_hbm, xt_hbm), (dq_ref, dk_ref, dv_ref, xt_ref), load_sem)
+
+        def remote(source, target, send, recv, which, other):
             return pltpu.make_async_remote_copy(
-                src_ref=sent.at[which], dst_ref=got.at[which], send_sem=y_send.at[which], recv_sem=y_recv.at[which],
-                device_id=other, device_id_type=MESH,
+                src_ref=source, dst_ref=target, send_sem=send.at[which], recv_sem=recv.at[which], device_id=other, device_id_type=MESH
             )
 
+        def own_copy(which):
+            target = got.at[:, pl.ds(pl.multiple_of(which * TILE, TILE), TILE)]
+            return remote(sent.at[which], target, own_send, own_recv, which, (me, across))
+
+        def early_copy(which):
+            return remote(early.at[which, across], early_in.at[which], early_send, early_recv, which, (me, across))
+
+        def near_copy(which):
+            return remote(early_in.at[which, 1], near_in.at[which], near_send, near_recv, which, (ring.partner, side))
+
+        def far_copy(which):
+            return remote(early_in.at[which, 0], far_in.at[which], far_send, far_recv, which, (before, side))
+
         @pl.when(step == 0)
         def _():
-            ring.barrier((other,))
+            for copy in brought:
+                copy.start()
+            ring.barrier(((me, across), (later, side), (before, side)))
             ring.begin()
+            for copy in brought[:3]:
+                copy.wait()
+
+        @pl.when(step == tiles)
+        def _():
+            brought[3].wait()
 
         @pl.when(step < tiles)
         def _():
-            part = None
-            for index in range(amount):
-                column = 0
-                for (_, several), blocks in zip(weights, w_refs):
-                    made = dot_nt(d_ref[index, :, column : column + several], blocks[index][...])
-                    part = made if part is None else part + made
-                    column += several
-            sent[step] = part.astype(BF)
-            across(step).start()
-
-        @pl.when(step >= tiles)
-        def _():
-            grad_ref[0] = dot_nn(xt_ref[...], tile_ref[0]).astype(BF)
-
-        ring.pace(step, [(tiles, costs[0]), (amount * per, costs[1])])
+            w_key, w_value = w_ref[:, columns : 2 * columns], w_ref[:, 2 * columns :]
+            part = dot_nt(dq_ref[...], w_ref[:, :columns])
+            part += dot_nt(dk_ref[2 * m :, :], w_key) + dot_nt(dv_ref[2 * m :, :], w_value)
+            low = part.astype(BF)
+            sent[step] = low
+            sent_ref[...] = low
+            for block in range(2):
+                span = slice(block * m, (block + 1) * m)
+                part = (dot_nt(dk_ref[span, :], w_key) + dot_nt(dv_ref[span, :], w_value)).astype(BF)
+                for number in range(2):
+                    early[step, number, block] = part[number * half : (number + 1) * half]
+            early_copy(step).start()
+
+        number = step - tiles
+
+        @pl.when((number >= 0) & (number < tiles))
+        def _():
+            own_copy(number).start()
+            early_copy(number).wait_recv()
+            early_in[number] = (early_in[number].astype(F32) + early[number, side].astype(F32)).astype(BF)
+            near_copy(number).start()
+
+        @pl.when((number >= 1) & (number <= tiles))
+        def _():
+            which = number - 1
+            near_copy(which).wait_recv()
+            early_in[which, 0] = (early_in[which, 0].astype(F32) + near_in[which].astype(F32) * share).astype(BF)
+
+            @pl.when(me >= 2)
+            def _():
+                far_copy(which).start()
+
+        @pl.when((number >= 0) & (number < per))
+        def _():
+            here = pl.ds(pl.multiple_of(number * TILE, TILE), TILE)
+            grad_ref[...] = dot_nn(xt_ref[:, 2 * m :], dq_ref[:, here]).astype(BF)
+
+        @pl.when((number >= per) & (number < 2 * per))
+        def _():
+            here = pl.ds(pl.multiple_of((number - per) * TILE, TILE), TILE)
+            grad_ref[...] = dot_nn(xt_ref[...], dk_ref[:, here]).astype(BF)
+
+        @pl.when(number >= 2 * per)
+        def _():
+            here = pl.ds(pl.multiple_of((number - 2 * per) * TILE, TILE), TILE)
+            grad_ref[...] = dot_nn(xt_ref[...], dv_ref[:, here]).astype(BF)
+
+        ring.pace(step, [(tiles, 5), (3 * per, 4)])
 
         @pl.when(step == total - 1)
         def _():
             for which in range(tiles):
-                across(which).wait()
-                back_ref[:, which * TILE : (which + 1) * TILE] = sent[which].astype(F32) + got[which].astype(F32)
+                here = slice(which * TILE, (which + 1) * TILE)
+                add_ref[:, here] = (near_in[which].astype(F32) * (1.0 - share)).astype(BF)
+
+                @pl.when(me < devices - 2)
+                def _():
+                    far_copy(which).wait_recv()
+                    add_ref[:, here] = (add_ref[:, here].astype(F32) + far_in[which].astype(F32)).astype(BF)
+
+                @pl.when(me >= 2)
+                def _():
+                    far_copy(which).wait_send()
+
+                near_copy(which).wait_send()
+                early_copy(which).wait_send()
+                own_copy(which).wait()
             ring.finish()
 
-    def late(i):
-        return jnp.maximum(i - tiles, 0)
-
-    def early(i):
+    any_space = pl.BlockSpec(memory_space=pl.ANY)
+    dma = pltpu.SemaphoreType.DMA
+
+    def second(i):
         return jnp.minimum(i, tiles - 1)
 
-    specs = [
-        single((width, m)),
-        pl.BlockSpec((1, m, TILE), lambda i: (late(i) // per, 0, late(i) % per)),
-        single((amount, m, columns)),
-    ]
-    operands = [x_t, d_out, d_out]
-    for array, several in weights:
-        for index in range(amount):
-            specs.append(pl.BlockSpec((TILE, several), functools.partial(lambda where, i: (early(i), where), index)))
-            operands.append(array)
-    out_specs = [pl.BlockSpec((1, width, TILE), lambda i: (late(i) // per, 0, late(i) % per)), single((m, width))]
-    out_shape = [jax.ShapeDtypeStruct((amount, width, columns), BF), jax.ShapeDtypeStruct((m, width), F32)]
-    specs += [pl.BlockSpec(memory_space=pl.ANY)] * count
-    operands += [source for source, _, _ in ring_sources]
-    for (source, _, _), out_width in zip(ring_sources, out_widths):
-        rows = source.shape[-2]
-        out_specs.append(single((rows, out_width)))
-        out_shape.append(jax.ShapeDtypeStruct((rows, out_width), F32))
-    dma = pltpu.SemaphoreType.DMA
     return pl.pallas_call(
         kernel,
         grid=(total,),
-        out_shape=out_shape,
-        in_specs=specs,
-        out_specs=out_specs,
+        out_shape=[
+            jax.ShapeDtypeStruct((width, 3 * columns), BF),
+            jax.ShapeDtypeStruct((m, width), BF),
+            jax.ShapeDtypeStruct((m, width), BF),
+            jax.ShapeDtypeStruct((half, width), BF),
+            jax.ShapeDtypeStruct((rows, out_width), F32),
+            jax.ShapeDtypeStruct((rows, columns), F32),
+        ],
+        in_specs=[
+            any_space, any_space, any_space, any_space,
+            pl.BlockSpec((TILE, 3 * columns), lambda i: (second(i), 0)),
+            any_space, any_space,
+        ],
+        out_specs=[
+            pl.BlockSpec((width, TILE), lambda i: (0, jnp.maximum(i - tiles, 0))),
+            pl.BlockSpec((m, TILE), lambda i: (0, second(i))),
+            any_space,
+            single((half, width)),
+            single((rows, out_width)),
+            single((rows, columns)),
+        ],
         scratch_shapes=[
+            pltpu.VMEM((width, reach), BF),
+            pltpu.VMEM((m, columns), BF),
+            pltpu.VMEM((reach, columns), BF),
+            pltpu.VMEM((reach, columns), BF),
+            dma((4,)),
             pltpu.VMEM((tiles, m, TILE), BF),
-            pltpu.VMEM((tiles, m, TILE), BF),
-            dma((tiles,)),
-            dma((tiles,)),
+            pltpu.VMEM((tiles, 2, 2, half, TILE), BF),
+            pltpu.VMEM((tiles, 2, half, TILE), BF),
+            pltpu.VMEM((tiles, half, TILE), BF),
+            pltpu.VMEM((tiles, half, TILE), BF),
+            *[dma((tiles,))] * 8,
             *Ring.scratch(devices, shapes),
         ],
         compiler_params=pltpu.CompilerParams(vmem_limit_bytes=VMEM, collective_id=identity, has_side_effects=True),
-        cost_estimate=cost(4 * m * width * amount * columns, 6 * width * amount * columns),
-        name=name,
-    )(*operands)
+        cost_estimate=cost(4 * (m + 2 * reach) * width * columns, 12 * width * columns),
+        name="qkv_back",
+    )(x_t, d_query, d_key, d_value, w_attn, up_part, out_part)
+
+
+def tiles_of(width):
+    return width // TILE
 
 
 def root_of(rows):
@@ -944,11 +967,14 @@
         def earlier(ref, there):
             @pl.when(there)
             def _():
-                o_ref[...] = normed(ref)
+                made = normed(ref)
+                o_ref[...] = made
+                t_ref[...] = made.T
 
             @pl.when(jnp.logical_not(there))
             def _():
                 o_ref[...] = jnp.zeros_like(o_ref)
+                t_ref[...] = jnp.zeros_like(t_ref)
 
         @pl.when(step < steps)
         def _():
@@ -970,11 +996,11 @@
     return pl.pallas_call(
         kernel,
         grid=(3 * steps,),
-        out_shape=[jax.ShapeDtypeStruct((3 * m, width), BF), jax.ShapeDtypeStruct((width, m), BF)],
+        out_shape=[jax.ShapeDtypeStruct((3 * m, width), BF), jax.ShapeDtypeStruct((width, 3 * m), BF)],
         in_specs=[part(0), part(1), part(2), whole_spec((1, width))],
         out_specs=[
             pl.BlockSpec((ROWS, width), lambda i: (i, 0)),
-            pl.BlockSpec((width, ROWS), lambda i: (0, jnp.maximum(i - 2 * steps, 0))),
+            pl.BlockSpec((width, ROWS), lambda i: (0, i)),
         ],
         compiler_params=pltpu.CompilerParams(vmem_limit_bytes=VMEM),
         cost_estimate=cost(24 * m * width, 14 * m * width),
@@ -1046,21 +1072,22 @@
     )(mixed, w_attn, tokens, gain)
 
 
-def last_pass(tokens, gain, grad, d_hidden, hidden, act_early, act_late, w_ffn, rest, gain_ffn_grad, flip, qkv_part, lanes, identity):
+def last_pass(tokens, gain, grad, grad_other, grad_add, d_hidden, hidden, act_early, act_late, w_ffn, rest, gain_ffn_grad, flip, qkv_part, lanes, identity):
     m, width = tokens.shape
     devices, rows, all_columns = qkv_part.shape
     columns = all_columns // 3
     chips = devices // 2
     size = ROWS // 2
     steps = m // size
-    total = steps + chips
+    total = tiles_of(width) + steps + chips
     names = 3
-    tiles = width // TILE
+    half = m // 2
+    tiles = tiles_of(width)
     some, late = act_early.shape[1], act_late.shape[1]
     sides = lax.axis_size("tensor")
-    assert tiles == steps and chips >= tiles
-
-    def kernel(x_ref, g_ref, dn_ref, dh_ref, h_ref, a_ref, al_ref, w_ref, rest_ref, gf_ref, flip_ref, source, grad_ref, layer_ref, flipped_ref, q_ref, k_ref, v_ref, gains_ref, gain_sum, gain_source, sent, got, y_send, y_recv, *scratch):
+    assert chips >= tiles
+
+    def kernel(x_ref, g_ref, dn_ref, do_ref, add_hbm, dh_ref, h_ref, a_hbm, al_hbm, w_ref, rest_ref, gf_ref, flip_hbm, source, grad_ref, layer_ref, flipped_ref, q_ref, k_ref, v_ref, gains_ref, a_ref, al_ref, flip_ref, add, load_sem, add_send, add_recv, gain_sum, gain_source, sent, got, y_send, y_recv, *scratch):
         step = pl.program_id(0)
         ring = Ring(
             devices, [(source, number * columns, columns) for number in range(names)], [(q_ref, 0), (k_ref, 0), (v_ref, 0)],
@@ -1068,6 +1095,12 @@
         )
         gain_ring = Ring(devices, [(gain_source, 0, lanes)], [(gains_ref, 0)], [[0]], scratch[3 * names + 5 :])
         other = (ring.me, lax.rem(ring.side + 1, sides))
+        brought = loads((a_hbm, al_hbm, flip_hbm, add_hbm), (a_ref, al_ref, flip_ref, add.at[ring.side]), load_sem)
+        add_copy = pltpu.make_async_remote_copy(
+            src_ref=add_hbm, dst_ref=add.at[ring.side], send_sem=add_send, recv_sem=add_recv, device_id=other, device_id_type=MESH
+        )
+        row_step = step - tiles
+        end_step = step - tiles - steps
 
         def across(which):
             return pltpu.make_async_remote_copy(
@@ -1077,29 +1110,41 @@
 
         @pl.when(step == 0)
         def _():
+            for copy in brought:
+                copy.start()
             ring.barrier((other,))
+            add_copy.start()
             ring.begin()
+            for copy in brought:
+                copy.wait()
+            flipped_ref[...] = flip_ref[...].T
+
+        @pl.when(row_step == 0)
+        def _():
+            add_copy.wait()
 
         @pl.when(step < tiles)
         def _():
             sent[step] = (dot_nt(a_ref[...], w_ref[...]) + dot_nt(al_ref[...], rest_ref[...])).astype(BF)
             across(step).start()
 
-        @pl.when(step < steps)
-        def _():
-            change, gain_part = norm_grad(x_ref[...].astype(F32), g_ref[...], dn_ref[...])
+        @pl.when((row_step >= 0) & (row_step < steps))
+        def _():
+            which = row_step * size // half
+            here = pl.ds(pl.multiple_of(row_step * size - which * half, size), size)
+            grad_rows = dn_ref[...].astype(F32) + do_ref[...].astype(F32) + add[which, here, :].astype(F32)
+            change, gain_part = norm_grad(x_ref[...].astype(F32), g_ref[...], grad_rows)
             grad_ref[...] = dh_ref[...] + change
 
-            @pl.when(step == 0)
+            @pl.when(row_step == 0)
             def _():
                 gain_sum[...] = gain_part
-                flipped_ref[...] = flip_ref[...].T
-
-            @pl.when(step > 0)
+
+            @pl.when(row_step > 0)
             def _():
                 gain_sum[...] += gain_part
 
-        @pl.when(step == steps - 1)
+        @pl.when(row_step == steps - 1)
         def _():
             gain_source[...] = jnp.zeros_like(gain_source)
             for device in range(devices):
@@ -1108,17 +1153,16 @@
                 gain_source[device, 16:, :rows] = jnp.broadcast_to(gf_ref[:, span], (16, rows)).astype(BF)
             gain_ring.begin()
 
-        ring.pace(step, [(steps, 3), (chips, 5)])
-
-        @pl.when(step >= steps)
-        def _():
-            gain_ring.run(step - steps, jnp.minimum(step - steps + 1, gain_ring.events))
-
-        @pl.when((step >= steps) & (step < steps + tiles))
-        def _():
-            which = step - steps
-            across(which).wait()
-            layer_ref[...] = (h_ref[...] + (sent[which].astype(F32) + got[which].astype(F32))).astype(BF)
+        ring.pace(step, [(tiles, 4), (steps, 3), (chips, 3)])
+
+        @pl.when(end_step >= 0)
+        def _():
+            gain_ring.run(end_step, jnp.minimum(end_step + 1, gain_ring.events))
+
+        @pl.when((end_step >= 0) & (end_step < tiles))
+        def _():
+            across(end_step).wait()
+            layer_ref[...] = (h_ref[...] + (sent[end_step].astype(F32) + got[end_step].astype(F32))).astype(BF)
 
         @pl.when(step == total - 1)
         def _():
@@ -1126,10 +1170,10 @@
             gain_ring.finish()
 
     def early(i):
-        return jnp.minimum(i, steps - 1)
-
-    rows_spec = pl.BlockSpec((size, width), lambda i: (early(i), 0))
-    tile_spec = pl.BlockSpec((m, TILE), lambda i: (0, jnp.clip(i - steps, 0, tiles - 1)))
+        return jnp.minimum(i, tiles - 1)
+
+    rows_spec = pl.BlockSpec((size, width), lambda i: (jnp.clip(i - tiles, 0, steps - 1), 0))
+    tile_spec = pl.BlockSpec((m, TILE), lambda i: (0, jnp.clip(i - tiles - steps, 0, tiles - 1)))
     dma = pltpu.SemaphoreType.DMA
     sums = jax.ShapeDtypeStruct((rows, columns), F32)
     return pl.pallas_call(
@@ -1143,15 +1187,22 @@
             jax.ShapeDtypeStruct((32, lanes), F32),
         ],
         in_specs=[
-            rows_spec, single((1, width)), rows_spec, rows_spec, tile_spec, single((m, some)), single((m, late)),
+            rows_spec, single((1, width)), rows_spec, rows_spec, pl.BlockSpec(memory_space=pl.ANY), rows_spec, tile_spec, pl.BlockSpec(memory_space=pl.ANY), pl.BlockSpec(memory_space=pl.ANY),
             pl.BlockSpec((TILE, some), lambda i: (early(i), 2)), pl.BlockSpec((TILE, late), lambda i: (early(i), 2)), single((1, width)),
-            single(flip.shape), pl.BlockSpec(memory_space=pl.ANY),
+            pl.BlockSpec(memory_space=pl.ANY), pl.BlockSpec(memory_space=pl.ANY),
         ],
         out_specs=[
             rows_spec, tile_spec, single((flip.shape[1], flip.shape[0])),
             single(sums.shape), single(sums.shape), single(sums.shape), single((32, lanes)),
         ],
         scratch_shapes=[
+            pltpu.VMEM((m, some), BF),
+            pltpu.VMEM((m, late), BF),
+            pltpu.VMEM(flip.shape, F32),
+            pltpu.VMEM((2, half, width), BF),
+            dma((4,)),
+            dma,
+            dma,
             pltpu.VMEM((1, width), F32),
             pltpu.VMEM((devices, 32, lanes), BF),
             pltpu.VMEM((tiles, m, TILE), BF),
@@ -1164,7 +1215,7 @@
         compiler_params=pltpu.CompilerParams(vmem_limit_bytes=VMEM, collective_id=identity, has_side_effects=True),
         cost_estimate=cost(20 * m * width, 24 * m * width),
         name="last_pass",
-    )(tokens, gain, grad, d_hidden, hidden, act_early, act_late, w_ffn, rest, gain_ffn_grad, flip, qkv_part)
+    )(tokens, gain, grad, grad_other, grad_add, d_hidden, hidden, act_early, act_late, w_ffn, rest, gain_ffn_grad, flip, qkv_part)
 
 
 def feed_tile(x_ref, dy_ref, dyt_ref, g_ref, u_ref, d_ref, act_ref, both_ref, down_ref):
@@ -1186,14 +1237,19 @@
     devices = lax.axis_size("dp")
     width = block.shape[1] // 2
 
-    def kernel(x_ref, dy_ref, dyt_ref, g_ref, u_ref, d_ref, block_ref, act_ref, both_ref, down_ref, rest_ref, *scratch):
+    def kernel(x_hbm, dy_hbm, dyt_hbm, g_ref, u_ref, d_ref, block_ref, act_ref, both_ref, down_ref, rest_ref, x_ref, dy_ref, dyt_ref, load_sem, *scratch):
         step = pl.program_id(0)
+        brought = loads((x_hbm, dy_hbm, dyt_hbm), (x_ref, dy_ref, dyt_ref), load_sem)
         spread = Spread(devices, [(block_ref, rest_ref, 0, width), (block_ref, rest_ref, width, width)], scratch)
 
         @pl.when(step == 0)
         def _():
+            for copy in brought:
+                copy.start()
             spread.barrier()
             spread.begin()
+            for copy in brought:
+                copy.wait()
 
         feed_tile(x_ref, dy_ref, dyt_ref, g_ref, u_ref, d_ref, act_ref, both_ref, down_ref)
         spread.pace(step, early)
@@ -1213,9 +1269,7 @@
             jax.ShapeDtypeStruct((k, block.shape[1]), BF),
         ],
         in_specs=[
-            single((m, k)),
-            single((m, k)),
-            single((k, m)),
+            any_space, any_space, any_space,
             pl.BlockSpec((k, TILE), lambda i: (0, i)),
             pl.BlockSpec((k, TILE), lambda i: (0, i + early)),
             pl.BlockSpec((k, TILE), lambda i: (0, i + 2 * early)),
@@ -1227,7 +1281,10 @@
             pl.BlockSpec((k, TILE), lambda i: (0, i)),
             any_space,
         ],
-        scratch_shapes=Spread.scratch(devices, 2),
+        scratch_shapes=[
+            pltpu.VMEM((m, k), BF), pltpu.VMEM((m, k), BF), pltpu.VMEM((k, m), BF), pltpu.SemaphoreType.DMA((3,)),
+            *Spread.scratch(devices, 2),
+        ],
         compiler_params=pltpu.CompilerParams(vmem_limit_bytes=VMEM, collective_id=identity, has_side_effects=True),
         cost_estimate=cost(8 * m * k * early * TILE, 8 * (m + k) * early * TILE, m * early * TILE),
         name="feed",
@@ -1246,8 +1303,9 @@
     sides = lax.axis_size("tensor")
     pieces = [(rows, some // 2)] * 2
 
-    def kernel(x_ref, xt_ref, dy_ref, dyt_ref, rg_ref, ru_ref, rd_ref, d_ref, tile_ref, wg_ref, wu_ref, lg_ref, lu_ref, source, act_ref, grad_ref, sent_ref, got, sum_ref, d_late, down_late, down_tile, both_tile, sent, y_send, y_recv, *scratch):
+    def kernel(x_hbm, xt_hbm, dy_hbm, dyt_hbm, rg_ref, ru_ref, rd_ref, d_hbm, tile_ref, wg_ref, wu_ref, lg_ref, lu_ref, source, act_ref, grad_ref, sent_ref, got, sum_ref, x_ref, xt_ref, dy_ref, dyt_ref, d_ref, load_sem, d_late, down_late, down_tile, both_tile, sent, y_send, y_recv, *scratch):
         step = pl.program_id(0)
+        brought = loads((x_hbm, dy_hbm, dyt_hbm, d_hbm, xt_hbm), (x_ref, dy_ref, dyt_ref, d_ref, xt_ref), load_sem)
         ring = Ring(devices, [(source, 0, some // 2), (source, some // 2, some // 2)], [(sum_ref, 0), (sum_ref, some // 2)], [[0], [1]], scratch[:11])
         late_ring = Ring(devices, [(down_late, 0, late)], [(sum_ref, some)], [[0]], scratch[11:])
         other = (ring.me, lax.rem(ring.side + 1, sides))
@@ -1260,8 +1318,20 @@
 
         @pl.when(step == 0)
         def _():
+            for copy in brought:
+                copy.start()
             ring.barrier((other,))
             ring.begin()
+            for copy in brought[:3]:
+                copy.wait()
+
+        @pl.when(step == LATE)
+        def _():
+            brought[3].wait()
+
+        @pl.when(step == LATE + tiles)
+        def _():
+            brought[4].wait()
 
         @pl.when(step < LATE)
         def _():
@@ -1342,9 +1412,9 @@
             jax.ShapeDtypeStruct((rows, padded), F32),
         ],
         in_specs=[
-            single((m, width)), single((width, m)), single((m, width)), single((width, m)),
+            any_space, any_space, any_space, any_space,
             rest_tile(0), rest_tile(1), rest_tile(2),
-            single((2, m, some)),
+            any_space,
             pl.BlockSpec((1, m, TILE), third),
             pl.BlockSpec((TILE, some), lambda i: (second(i), 0)),
             pl.BlockSpec((TILE, some), lambda i: (second(i), 1)),
@@ -1360,6 +1430,12 @@
             single((rows, padded)),
         ],
         scratch_shapes=[
+            pltpu.VMEM((m, width), BF),
+            pltpu.VMEM((width, m), BF),
+            pltpu.VMEM((m, width), BF),
+            pltpu.VMEM((width, m), BF),
+            pltpu.VMEM((2, m, some), BF),
+            dma((5,)),
             pltpu.VMEM((2, m, late), BF),
             pltpu.VMEM((devices, rows, late), BF),
             pltpu.VMEM((width, TILE), BF),
@@ -1416,7 +1492,6 @@
     normed_attn, normed_attn_t = first_norm(far, near, tokens, gain_attn)
     query, kv = project(normed_attn, w_attn, cosine, sine, span, heads)
     mixed, probs = attend(query, kv, positions[None, :], heads)
-    cosine, sine = cosine[WINDOW:], sine[WINDOW:]
     hidden, normed_ffn, normed_ffn_t = out_norm(mixed, w_attn, 3, tokens, gain_ffn, 5)
 
     cotangent_t = cotangent.T
@@ -1426,15 +1501,14 @@
     )
     both_part = both_part.reshape(2, devices, own_rows, padded)
 
-    d_qkv, out_part, gate_grad, w_down_grad, d_hidden, gain_ffn_grad = attend_back(
+    d_query, d_key, d_value, out_part, gate_grad, w_down_grad, d_hidden, gain_ffn_grad = attend_back(
         query, kv, probs, mixed, w_attn, hidden, gain_ffn, d_normed_ffn, d_normed_other, cotangent, cosine, sine, down_grad, both_part, heads, hidden_units, 2
     )
-    qkv_part, d_normed_attn, up_grad, out_grad = back_pass(
-        normed_attn_t, d_qkv[None], [(w_attn, 3 * head_columns)],
-        [(both_part, 1, 2), (out_part.reshape(devices, own_rows, head_columns), None, 1)], [hidden_units, head_columns], (4, 3), 3, "qkv_back",
+    qkv_part, d_normed_attn, d_attn_other, d_attn_add, up_grad, out_grad = qkv_back(
+        normed_attn_t, d_query, d_key, d_value, w_attn, both_part, out_part.reshape(devices, own_rows, head_columns), hidden_units, 3
     )
     tokens_grad, layer_out, w_out_grad, query_grad, key_grad, value_grad, gain_grads = last_pass(
-        tokens, gain_attn, d_normed_attn, d_hidden, hidden, act_early, act_late, w_ffn, rest, gain_ffn_grad, out_grad,
+        tokens, gain_attn, d_normed_attn, d_attn_other, d_attn_add, d_hidden, hidden, act_early, act_late, w_ffn, rest, gain_ffn_grad, out_grad,
         qkv_part.reshape(devices, own_rows, 3 * head_columns), lanes, 4,
     )
     return (

time: 685 us -> 660 us (0.964)
  Pallas kernels: 625 us -> 601 us
    pallas_call x1, Pallas kernels: 114 us -> 66 us  [attend_back(): pl.pallas_call(kernel, grid=(firsts + heads,), out_shape=[jax.ShapeDtypeS...]
    pallas_call x1, Pallas kernels: 88.1 us -> 111 us  [qkv_back(): pl.pallas_call(kernel, grid=(total,), out_shape=[jax.ShapeDtypeStruct((wi...]
  transfers between devices with their start and end apart: 1 -> 1, of which waited for: 1 -> 1; matrix products, arithmetic and copies ran while one was open for 2% -> 2% of each run, Pallas kernels for 16% -> 17%
where the time goes in v7:
time: 660 us; the launch traced here: 656 us
  Pallas kernels  601 us (91%)
  local copies, waits for them, and re-layouts  22.5 us (3%)
  between operations  15.2 us (2%)
  waiting for transfers between devices  9.02 us (1%)
  other arithmetic  8.25 us (1%)
    pallas_call x1, Pallas kernels, qkv_back(): pl.pallas_call(kernel, grid=(total,), out_shape=[jax.ShapeDtypeStruct((wi...  111 us
    pallas_call x1, Pallas kernels, ring_gather(): pl.pallas_call(functools.partial(gather_kernel, devices, chunks, len(arra...  110 us
    pallas_call x1, Pallas kernels, last_pass(): pl.pallas_call(kernel, grid=(total,), out_shape=[jax.ShapeDtypeStruct((m,...  76.9 us
    pallas_call x1, Pallas kernels, ffn_back(): pl.pallas_call(kernel, grid=(total,), out_shape=[jax.ShapeDtypeStruct((m,...  72.6 us
    pallas_call x1, Pallas kernels, attend_back(): pl.pallas_call(kernel, grid=(firsts + heads,), out_shape=[jax.ShapeDtypeS...  66 us
    pallas_call x1, Pallas kernels, feed(): pl.pallas_call(kernel, grid=(early,), out_shape=[jax.ShapeDtypeStruct((m,...  54.1 us
    pallas_call x1, Pallas kernels, out_norm(): pl.pallas_call(kernel, grid=(2 * steps,), out_shape=[jax.ShapeDtypeStruct...  53.1 us
    pallas_call x1, Pallas kernels, project(): pl.pallas_call(kernel, grid=(3 * some,), out_shape=[jax.ShapeDtypeStruct(...  24.5 us
  transfers between devices with their start and end apart: 1, of which 1 were waited for; matrix products, arithmetic and copies ran while one was open for 2% of the time, Pallas kernels for 17%

profile of v7, /device:TPU:0, one launch (start us, length us, event | category | flops | bytes accessed | tf_op | source)
XLA Modules:
  0.0 655.7 jit_solution(979174616377281088)
XLA Ops:
  7.2 1.1 copy.23
  8.4 1.4 copy.24
  10.2 1.4 copy.26
  11.7 1.3 pad_maximum_fusion
  14.1 109.8 %ring_gather.1 = (bf16[2048,4096]{1,0:T(8,128)(2,1)}, bf16[512,128]{1,0:T(8,128)(2,1)}, bf16[512,2048]{1,0:T(8,128)(2,1)}, bf16[512,2048]{1,0:T(8,128)(2,1)}) custom-call(bf16[128,4096]{1,0:T(8,128)(2,1)} %pad_maximum_fusion.1.refs_0_, bf16[32,128]{1,0:T(8,128)(2,1)} %copy-done.16, bf16[512,2048]{1,0:T(8,128)(2,1)} %x_ref.3), custom_call_target="tpu_custom_call" | custom-call | tf_op jit(solution)/shard_map/ring_gather/pallas_call | solution.py:218
  124.4 2.7 copy.29
  129.1 12.1 %first_norm.1 = (bf16[1536,2048]{1,0:T(8,128)(2,1)}, bf16[2048,1536]{1,0:T(8,128)(2,1)}) custom-call(bf16[512,2048]{1,0:T(8,128)(2,1)} %get-tuple-element.84.far_ref, bf16[512,2048]{1,0:T(8,128)(2,1)} %get-tuple-element.85.near_ref, bf16[512,2048]{1,0:T(8,128)(2,1)} %x_ref.3, f32[1,2048]{1,0:T(1,128)} %bitcast.27), custom_call_target="tpu_custom_call" | custom-call | flops 25165824 | bytes 14680064 | tf_op jit(solution)/shard_map/first_norm/pallas_call | solution.py:996
  141.4 2.8 fusion
  144.2 1.6 pad_maximum_fusion.2
  145.8 24.5 %project.1 = (bf16[512,1024]{1,0:T(8,128)(2,1)}, bf16[1536,2048]{1,0:T(8,128)(2,1)}) custom-call(bf16[1536,2048]{1,0:T(8,128)(2,1)} %get-tuple-element.87.x_ref, bf16[2048,4096]{1,0:T(8,128)(2,1)} %get-tuple-element.88.w_ref, f32[1536,128]{1,0:T(8,128)} %get-tuple-element.147.c_ref.c_hbm, f32[1536,128]{1,0:T(8,128)} %get-tuple-element.148.s_ref.s_hbm), custom_call_target="tpu_custom_call" | custom-call | flops 15032385536 | bytes 28311552 | tf_op jit(solution)/shard_map/project/pallas_call | solution.py:556
  170.3 20.3 %attend.1 = (bf16[512,1024]{1,0:T(8,128)(2,1)}, bf16[8,2,1280,256]{3,2,1,0:T(8,128)(2,1)}) custom-call(bf16[512,1024]{1,0:T(8,128)(2,1)} %get-tuple-element.89.q_ref, bf16[1536,2048]{1,0:T(8,128)(2,1)} %get-tuple-element.90.k_ref.v_ref, bf16[1536,2048]{1,0:T(8,128)(2,1)} %get-tuple-element.90.k_ref.v_ref, s32[1,512]{1,0:T(1,128)} %bitcast.31), custom_call_target="tpu_custom_call" | custom-call | flops 5368709120 | bytes 10485760 | tf_op jit(solution)/shard_map/attend/pallas_call | solution.py:601
  190.7 53.1 %out_norm.1 = (f32[512,2048]{1,0:T(8,128)}, bf16[512,2048]{1,0:T(8,128)(2,1)}, bf16[2048,512]{1,0:T(8,128)(2,1)}) custom-call(bf16[512,1024]{1,0:T(8,128)(2,1)} %get-tuple-element.92.x_ref, bf16[2048,4096]{1,0:T(8,128)(2,1)} %get-tuple-element.88.w_ref, bf16[512,2048]{1,0:T(8,128)(2,1)} %x_ref.3, f32[1,2048]{1,0:T(1,128)} %bitcast.29), custom_call_target="tpu_custom_call" | custom-call | flops 2147483648 | bytes 12582912 | tf_op jit(solution)/shard_map/out_norm/pallas_call | solution.py:1053
  244.6 9.0 %all-gather.2.cloned.1.call-done.g_ref.u_ref.d_ref.wg_ref.wu_ref.w_ref = bf16[2048,6144]{1,0:T(8,128)(2,1)} async-done(((bf16[128,6144]{1,0:T(8,128)(2,1)}), bf16[2048,6144]{1,0:T(8,128)(2,1)}) %all-gather.2.cloned.1.call-update) | async-done | bytes 25165840 | tf_op jit(solution)/shard_map/all_gather | solution.py:1480
  253.6 54.1 %feed.1 = (bf16[512,2048]{1,0:T(8,128)(2,1)}, bf16[2,512,2048]{2,1,0:T(8,128)(2,1)}, bf16[2048,2048]{1,0:T(8,128)(2,1)}, bf16[2048,2304]{1,0:T(8,128)(2,1)}) custom-call(bf16[512,2048]{1,0:T(8,128)(2,1)} %get-tuple-element.94.x_hbm, bf16[512,2048]{1,0:T(8,128)(2,1)} %y_ref.1, bf16[2048,512]{1,0:T(8,128)(2,1)} %bitcast.20, ...), custom_call_target="tpu_custom_call" | custom-call | flops 17179869184 | bytes 41943040 | tf_op jit(solution)/shard_map/feed/pallas_call | solution.py:1262
  307.8 72.6 %ffn_back.1 = (bf16[512,768]{1,0:T(8,128)(2,1)}, bf16[2,2048,2816]{2,1,0:T(8,128)(2,1)}, bf16[512,2048]{1,0:T(8,128)(2,1)}, bf16[512,2048]{1,0:T(8,128)(2,1)}, f32[128,2816]{1,0:T(8,128)}) custom-call(bf16[512,2048]{1,0:T(8,128)(2,1)} %get-tuple-element.94.x_hbm, bf16[2048,512]{1,0:T(8,128)(2,1)} %get-tuple-element.95.xt_hbm, bf16[512,2048]{1,0:T(8,128)(2,1)} %y_ref.1, ...), custom_call_target="tpu_custom_call" | custom-call | flops 30064771072 | bytes 57671680 | tf_op jit(solution)/shard_map/ffn_back/pallas_call | solution.py:1404
  380.3 66.0 %attend_back.1 = (bf16[512,1024]{1,0:T(8,128)(2,1)}, bf16[1536,1024]{1,0:T(8,128)(2,1)}, bf16[1536,1024]{1,0:T(8,128)(2,1)}, bf16[2048,1024]{1,0:T(8,128)(2,1)},...) custom-call(bf16[512,1024]{1,0:T(8,128)(2,1)} %get-tuple-element.89.q_ref, ...), custom_call_target="tpu_custom_call" | custom-call | flops 10737418240 | bytes 10485760 | tf_op jit(solution)/shard_map/attend_back/pallas_call | solution.py:713
  446.4 111.2 %qkv_back.1 = (bf16[2048,3072]{1,0:T(8,128)(2,1)}, bf16[512,2048]{1,0:T(8,128)(2,1)}, bf16[512,2048]{1,0:T(8,128)(2,1)}, bf16[256,2048]{1,0:T(8,128)(2,1)}, f32[128,2752]{1,0:T(8,128)}, /*index=5*/f32[128,1024]{1,0:T(8,128)}) custom-call(bf16[2048,1536]{1,0:T(8,128)(2,1)} %get-tuple-element.86.xt_hbm, bf16[512,1024]{1,0:T(8,128)(2,1)} %get-tuple-element.104.dq_hbm, ...), custom_call_target="tpu_custom_call" | custom-call | flops 30064771072 | bytes 25165824 | tf_op jit(solution)/shard_map/qkv_back/pallas_call | solution.py:896
  557.6 76.9 %last_pass.1 = (f32[512,2048]{1,0:T(8,128)}, bf16[512,2048]{1,0:T(8,128)(2,1)}, f32[1024,128]{1,0:T(8,128)}, f32[128,1024]{1,0:T(8,128)}, f32[128,1024]{1,0:T(8,...) custom-call(bf16[512,2048]{1,0:T(8,128)(2,1)} %x_ref.3, f32[1,2048]{1,0:T(1,128)} %bitcast.28, ...), custom_call_target="tpu_custom_call" | custom-call | flops 20971520 | bytes 25165824 | tf_op jit(solution)/shard_map/last_pass/pallas_call | solution.py:1179
  634.5 1.3 slice_bitcast_fusion
  635.8 1.5 copy.33
  637.4 1.5 copy.32
  639.4 1.3 copy.46
  640.7 1.6 copy-done.3
  642.3 2.0 copy.47
  (62 shorter events, 9.3 us)
Async XLA Ops:
  7.2 2.7 copy-start.8
  7.2 246.5 %all-gather.2.cloned.1.call-start = ((), (), s32[]{:S(2)}) async-start(), calls=%async_computation | async-start | bytes 26738688 | tf_op jit(solution)/shard_map/all_gather | solution.py:1480
  9.8 1.8 copy-start.1
  10.1 1.6 copy-start.18
  11.6 1.4 copy-start.19
  11.6 1.4 copy-start.13
  11.6 1.4 copy-start.14
  11.6 1.4 copy-start.15
  13.0 1.1 copy-start.16
  14.1 109.8 %copy-start.17 = (s32[512]{0:T(512)S(1)}, s32[512]{0:T(512)}, u32[]{:S(2)}) copy-start(s32[512]{0:T(512)} %param.17) | copy-start | bytes 6148
  14.1 110.4 %copy-start = (bf16[512,2048]{1,0:T(8,128)(2,1)S(1)}, bf16[512,2048]{1,0:T(8,128)(2,1)}, u32[]{:S(2)}) copy-start(bf16[512,2048]{1,0:T(8,128)(2,1)} %y_ref.1) | copy-start | bytes 6291460
  129.1 12.2 %copy-start.2 = (bf16[128,2752]{1,0:T(8,128)(2,1)S(1)}, bf16[128,2752]{1,0:T(8,128)(2,1)}, u32[]{:S(2)}) copy-start(bf16[128,2752]{1,0:T(8,128)(2,1)} %copy-done.1) | copy-start | bytes 2113540
  557.6 78.3 %copy-start.6 = (f32[128,2752]{1,0:T(8,128)S(1)}, f32[128,2752]{1,0:T(8,128)}, u32[]{:S(2)}) copy-start(f32[128,2752]{1,0:T(8,128)} %get-tuple-element.136) | copy-start | bytes 4227076
  634.5 2.8 copy-start.5
  637.4 2.0 copy-start.4
  639.4 2.9 copy-start.3
  642.3 2.0 copy-start.12
  642.3 2.8 copy-start.11
  642.3 3.6 copy-start.10
  644.3 2.4 copy-start.9
  644.3 3.2 copy-start.7
Sparse Core Ops, SparseCore 0:
  124.0 129.5 all-gather.1

commit v8 on v7

--- a/solution.py
+++ b/solution.py
@@ -19,6 +19,7 @@
 KB = WINDOW + QB
 TILE = 256
 ROWS = 128
+SOON = 2
 LATE = 3
 VMEM = 59 * 1024 * 1024
 
@@ -49,194 +50,6 @@
     column = lax.rem(chip, 2)
     row = chip // 2
     return (1 - column) * row + column * (chips - 1 - row)
-
-
-def gather_kernel(devices, chunks, count, *refs):
-    ins, tokens = refs[:count], refs[count]
-    outs, near, far = refs[count + 1 : 2 * count + 1], refs[2 * count + 1], refs[2 * count + 2]
-    local_sem, a_send, a_recv, b_send, b_recv, c_send, c_recv, far_send, far_recv, near_send, near_recv = refs[2 * count + 3 :]
-    chips = devices // 2
-    me = lax.axis_index("dp")
-    side = lax.axis_index("tensor")
-    core = lax.rem(me, 2)
-    place = ring_place(me // 2, chips)
-
-    def device(q):
-        return ring_chip(q, chips) * 2 + core
-
-    right = device(place + 1)
-    left = device(place - 1)
-    partner = me + 1 - 2 * core
-    across = lax.rem(side + 1, lax.axis_size("tensor"))
-    later, before = lax.rem(me + 2, devices), lax.rem(me + devices - 2, devices)
-    barrier = pltpu.get_barrier_semaphore()
-    for other in ((right, side), (left, side), (partner, side), (me, across), (later, side), (before, side)):
-        pl.semaphore_signal(barrier, inc=1, device_id=other, device_id_type=MESH)
-    pl.semaphore_wait(barrier, 6)
-
-    pieces = []
-    for index, parts in enumerate(chunks):
-        width = ins[index].shape[1] // parts
-        for part in range(parts):
-            pieces.append((index, part * width, width))
-    hops = chips - 1
-
-    def view(ref, row, half, piece, rows):
-        index, column, width = piece
-        start = row * rows + half * (rows // 2)
-        if not isinstance(start, int):
-            start = pl.multiple_of(start, 16)
-        return ref.at[pl.ds(start, rows // 2), pl.ds(column, width)]
-
-    def described(source, target, send, recv, other):
-        return pltpu.make_async_remote_copy(
-            src_ref=source, dst_ref=target, send_sem=send, recv_sem=recv, device_id=other, device_id_type=MESH
-        )
-
-    def remote(source, target, send, recv, other):
-        copy = described(source, target, send, recv, (other, side))
-        copy.start()
-        return copy
-
-    span = tokens.shape[0] // 2
-
-    def half_rows(ref, which):
-        return ref.at[pl.ds(pl.multiple_of(which * span, span), span)]
-
-    far_copy = described(half_rows(tokens, side), half_rows(far, side), far_send.at[0], far_recv.at[0], (later, side))
-    cross_copy = described(half_rows(far, side), half_rows(far, side), far_send.at[1], far_recv.at[1], (me, across))
-    own_near = [described(half_rows(tokens, which), half_rows(near, which), near_send.at[which], near_recv.at[which], (partner, side)) for which in range(2)]
-    far_near = [described(half_rows(far, which), half_rows(near, which), near_send.at[slot], near_recv.at[slot], (partner, side)) for slot, which in enumerate((side, across))]
-
-    @pl.when(me < devices - 2)
-    def _():
-        far_copy.start()
-
-    @pl.when(core == 0)
-    def _():
-        for copy in own_near:
-            copy.start()
-
-    def pass_on(slot):
-        @pl.when(me >= 2)
-        def _():
-            if slot == 0:
-                far_copy.wait_recv()
-                cross_copy.start()
-            else:
-                cross_copy.wait_recv()
-
-            @pl.when(core == 1)
-            def _():
-                far_near[slot].start()
-
-    local = []
-    for index in range(count):
-        rows = ins[index].shape[0]
-        copy = pltpu.make_async_copy(
-            ins[index], outs[index].at[pl.ds(pl.multiple_of(me * rows, 16), rows)], local_sem.at[index]
-        )
-        copy.start()
-        local.append(copy)
-    forward, partner_copies = {}, []
-    for number, piece in enumerate(pieces):
-        ref, out = ins[piece[0]], outs[piece[0]]
-        rows = ref.shape[0]
-        forward[number, 0] = (
-            remote(view(ref, 0, 0, piece, rows), view(out, me, 0, piece, rows), a_send.at[number, 0], a_recv.at[number, 0], right),
-            remote(view(ref, 0, 1, piece, rows), view(out, me, 1, piece, rows), b_send.at[number, 0], b_recv.at[number, 0], left),
-        )
-    for number, piece in enumerate(pieces):
-        ref, out = ins[piece[0]], outs[piece[0]]
-        rows = ref.shape[0]
-        for half in range(2):
-            partner_copies.append(
-                remote(view(ref, 0, half, piece, rows), view(out, me, half, piece, rows), c_send.at[number, 0, half], c_recv.at[number, 0, half], partner)
-            )
-    for hop in range(hops):
-        for number, piece in enumerate(pieces):
-            out = outs[piece[0]]
-            rows = ins[piece[0]].shape[0]
-            came = forward[number, hop]
-            sent = []
-            for half in range(2):
-                came[half].wait_recv()
-                owner = device(place - 1 - hop if half == 0 else place + 1 + hop)
-                block = view(out, owner, half, piece, rows)
-                send, recv = (a_send, a_recv) if half == 0 else (b_send, b_recv)
-                if hop < hops - 1:
-                    sent.append(
-                        remote(block, block, send.at[number, hop + 1], recv.at[number, hop + 1], right if half == 0 else left)
-                    )
-                partner_copies.append(
-                    remote(block, block, c_send.at[number, hop + 1, half], c_recv.at[number, hop + 1, half], partner)
-                )
-            if sent:
-                forward[number, hop + 1] = tuple(sent)
-        if hop == hops // 2:
-            pass_on(0)
-        if hop == hops - 2:
-            pass_on(1)
-    for copy in local:
-        copy.wait()
-    for pair in forward.values():
-        for copy in pair:
-            copy.wait_send()
-    for copy in partner_copies:
-        copy.wait()
-
-    @pl.when(me < devices - 2)
-    def _():
-        far_copy.wait_send()
-
-    @pl.when(me >= 2)
-    def _():
-        cross_copy.wait_send()
-
-        @pl.when(core == 1)
-        def _():
-            for copy in far_near:
-                copy.wait_send()
-
-    @pl.when(core == 0)
-    def _():
-        for copy in own_near:
-            copy.wait_send()
-
-    @pl.when((core == 1) | (me >= 2))
-    def _():
-        for copy in own_near:
-            copy.wait_recv()
-
-
-def ring_gather(arrays, chunks, tokens, identity):
-    devices = lax.axis_size("dp")
-    hops = devices // 2 - 1
-    pieces = sum(chunks)
-    dma = pltpu.SemaphoreType.DMA
-    any_space = pl.BlockSpec(memory_space=pl.ANY)
-    return pl.pallas_call(
-        functools.partial(gather_kernel, devices, chunks, len(arrays)),
-        out_shape=[jax.ShapeDtypeStruct((a.shape[0] * devices, a.shape[1]), a.dtype) for a in arrays]
-        + [jax.ShapeDtypeStruct(tokens.shape, tokens.dtype)] * 2,
-        in_specs=[any_space] * (len(arrays) + 1),
-        out_specs=[any_space] * (len(arrays) + 2),
-        scratch_shapes=[
-            dma((len(arrays),)),
-            dma((pieces, hops)),
-            dma((pieces, hops)),
-            dma((pieces, hops)),
-            dma((pieces, hops)),
-            dma((pieces, hops + 1, 2)),
-            dma((pieces, hops + 1, 2)),
-            dma((2,)),
-            dma((2,)),
-            dma((2,)),
-            dma((2,)),
-        ],
-        compiler_params=pltpu.CompilerParams(collective_id=identity, has_side_effects=True),
-        name="ring_gather",
-    )(*arrays, tokens)
 
 
 class Spread:
@@ -260,29 +73,30 @@
         chips = devices // 2
         return [dma((count,))] + [dma((count, amount, 2)) for amount in (chips - 1, chips - 1, chips, chips)]
 
-    def barrier(self):
+    def barrier(self, others=()):
         semaphore = pltpu.get_barrier_semaphore()
-        for other in (*self.next, self.partner):
-            pl.semaphore_signal(semaphore, inc=1, device_id=(other, self.side), device_id_type=MESH)
-        pl.semaphore_wait(semaphore, 3)
+        everyone = [(self.next[0], self.side), (self.next[1], self.side), (self.partner, self.side), *others]
+        for other in everyone:
+            pl.semaphore_signal(semaphore, inc=1, device_id=other, device_id_type=MESH)
+        pl.semaphore_wait(semaphore, len(everyone))
 
     def block(self, index, stage, half):
-        source, whole, column, width = self.pieces[index]
+        source, _, whole, column, width = self.pieces[index]
         rows = source.shape[0]
         owner = ring_chip(self.place - stage if half == 0 else self.place + stage, self.chips) * 2 + self.core
         return whole.at[pl.ds(pl.multiple_of(owner * rows + half * (rows // 2), 16), rows // 2), pl.ds(column, width)]
 
     def first(self, index, half):
-        source, _, column, width = self.pieces[index]
+        source, column, _, _, width = self.pieces[index]
         rows = source.shape[0]
         return source.at[pl.ds(half * (rows // 2), rows // 2), pl.ds(column, width)]
 
     def local(self, index):
-        source, whole, column, width = self.pieces[index]
+        source, start, whole, column, width = self.pieces[index]
         rows = source.shape[0]
         span = pl.ds(pl.multiple_of(self.me * rows, 16), rows)
         return pltpu.make_async_copy(
-            source.at[:, pl.ds(column, width)], whole.at[span, pl.ds(column, width)], self.local_sem.at[index]
+            source.at[:, pl.ds(start, width)], whole.at[span, pl.ds(column, width)], self.local_sem.at[index]
         )
 
     def copy(self, index, stage, half, start, across):
@@ -348,6 +162,155 @@
             return carry
 
         lax.fori_loop(1, self.chips, gave, 0)
+
+
+def first_gather(w_query, w_key, w_value, w_out, gains, tokens, w_gate_t, w_up_t, w_down, identity):
+    devices = lax.axis_size("dp")
+    sides = lax.axis_size("tensor")
+    rows, columns = w_query.shape
+    units = w_down.shape[0]
+    tiles = (units + TILE - 1) // TILE
+    padded, late = tiles * TILE, LATE * TILE
+    some = padded - late
+    span = tokens.shape[0] // 2
+
+    def kernel(q_ref, k_ref, v_ref, o_hbm, gains_ref, tokens_ref, gate_hbm, up_hbm, down_hbm, attn_ref, all_ref, near, far, early_hbm, late_hbm, o_in, o_turned, gate_in, up_in, down_in, early_pack, late_pack, load_sem, store_sem, far_send, far_recv, near_send, near_recv, *scratch):
+        pieces = [(ref, 0, attn_ref, number * columns, columns) for number, ref in enumerate((q_ref, k_ref, v_ref, o_turned))]
+        spread = Spread(devices, [*pieces, (gains_ref, 0, all_ref, 0, gains_ref.shape[1])], scratch)
+        me, side, core = spread.me, spread.side, spread.core
+        across = lax.rem(side + 1, sides)
+        later, before = lax.rem(me + 2, devices), lax.rem(me + devices - 2, devices)
+        parts = (gate_in, up_in, down_in)
+        brought = loads(
+            (o_hbm, gate_hbm, up_hbm, down_hbm), (o_in, *[part.at[pl.ds(0, units)] for part in parts]), load_sem
+        )
+        stored = loads((early_pack, late_pack), (early_hbm, late_hbm), store_sem)
+        for copy in brought:
+            copy.start()
+        spread.barrier(((me, across), (later, side), (before, side)))
+
+        def described(source, target, send, recv, other):
+            return pltpu.make_async_remote_copy(
+                src_ref=source, dst_ref=target, send_sem=send, recv_sem=recv, device_id=other, device_id_type=MESH
+            )
+
+        def half_rows(ref, which):
+            return ref.at[pl.ds(pl.multiple_of(which * span, span), span)]
+
+        far_copy = described(half_rows(tokens_ref, side), half_rows(far, side), far_send.at[0], far_recv.at[0], (later, side))
+        cross_copy = described(half_rows(far, side), half_rows(far, side), far_send.at[1], far_recv.at[1], (me, across))
+
+        def near_copy(source, which, slot):
+            return described(half_rows(source, which), half_rows(near, which), near_send.at[slot], near_recv.at[slot], (spread.partner, side))
+
+        own_near = [near_copy(tokens_ref, which, which) for which in range(2)]
+        far_near = [near_copy(far, which, slot) for slot, which in enumerate((side, across))]
+
+        brought[0].wait()
+        o_turned[...] = o_in[...].T
+        spread.begin()
+
+        @pl.when(me < devices - 2)
+        def _():
+            far_copy.start()
+
+        @pl.when(core == 0)
+        def _():
+            for copy in own_near:
+                copy.start()
+
+        for number, part in enumerate(parts):
+            brought[1 + number].wait()
+            part[units:, :] = jnp.zeros((padded - units, rows), BF)
+            made = part[...].T
+            early_pack[:, number * some : (number + 1) * some] = made[:, :some]
+            late_pack[:, number * late : (number + 1) * late] = made[:, some:]
+        for copy in stored:
+            copy.start()
+
+        def one(stage, carry):
+            for index in range(len(pieces) + 1):
+                spread.stage(stage, index)
+
+            @pl.when((stage == spread.chips // 2) & (me >= 2))
+            def _():
+                far_copy.wait_recv()
+                cross_copy.start()
+
+                @pl.when(core == 1)
+                def _():
+                    far_near[0].start()
+
+            @pl.when((stage == spread.chips - 2) & (me >= 2))
+            def _():
+                cross_copy.wait_recv()
+
+                @pl.when(core == 1)
+                def _():
+                    far_near[1].start()
+
+            return carry
+
+        lax.fori_loop(1, spread.chips, one, 0)
+        for copy in stored:
+            copy.wait()
+        spread.finish()
+
+        @pl.when(me < devices - 2)
+        def _():
+            far_copy.wait_send()
+
+        @pl.when(me >= 2)
+        def _():
+            cross_copy.wait_send()
+
+            @pl.when(core == 1)
+            def _():
+                for copy in far_near:
+                    copy.wait_send()
+
+        @pl.when(core == 0)
+        def _():
+            for copy in own_near:
+                copy.wait_send()
+
+        @pl.when((core == 1) | (me >= 2))
+        def _():
+            for copy in own_near:
+                copy.wait_recv()
+
+    dma = pltpu.SemaphoreType.DMA
+    any_space = pl.BlockSpec(memory_space=pl.ANY)
+    low = functools.partial(jax.ShapeDtypeStruct, dtype=BF)
+    return pl.pallas_call(
+        kernel,
+        out_shape=[
+            low((rows * devices, 4 * columns)),
+            low((gains.shape[0] * devices, gains.shape[1])),
+            low(tokens.shape),
+            low(tokens.shape),
+            low((rows, 3 * some)),
+            low((rows, 3 * late)),
+        ],
+        in_specs=[any_space] * 9,
+        out_specs=[any_space] * 6,
+        scratch_shapes=[
+            pltpu.VMEM(w_out.shape, BF),
+            pltpu.VMEM((rows, columns), BF),
+            *[pltpu.VMEM((padded, rows), BF)] * 3,
+            pltpu.VMEM((rows, 3 * some), BF),
+            pltpu.VMEM((rows, 3 * late), BF),
+            dma((4,)),
+            dma((2,)),
+            dma((2,)),
+            dma((2,)),
+            dma((2,)),
+            dma((2,)),
+            *Spread.scratch(devices, 5),
+        ],
+        compiler_params=pltpu.CompilerParams(vmem_limit_bytes=VMEM, collective_id=identity, has_side_effects=True),
+        name="first_gather",
+    )(w_query, w_key, w_value, w_out, gains, tokens, w_gate_t, w_up_t, w_down)
 
 
 class Ring:
@@ -619,7 +582,7 @@
     )(query, kv, kv, places)
 
 
-def attend_back(query, kv, probs, mixed, w_attn, hidden, gain, d_normed, d_normed_other, cotangent, cosine, sine, flip, ring_source, heads, out_width, identity):
+def attend_back(query, kv, probs, mixed, w_attn, hidden, gain, d_normed, d_normed_other, cotangent, cosine, sine, flip, act_early, act_late, w_ffn, rest, ring_source, heads, out_width, identity):
     m, width = hidden.shape
     firsts = m // ROWS
     devices, rows, ring_width = ring_source.shape[1:]
@@ -627,19 +590,29 @@
     factor = E ** (-0.5)
     reach = WINDOW + m
     columns = heads * E
-
-    def kernel(q_ref, k_ref, v_ref, p_ref, x_ref, w_ref, h_ref, gain_ref, dn_ref, do_ref, y_ref, c_hbm, s_hbm, flip_hbm, source, dq_ref, dk_ref, dv_ref, out_ref, sum_ref, flipped_ref, dh_ref, gain_out, c_ref, s_ref, flip_ref, load_sem, g_ref, gt_ref, keys_sum, values_sum, *scratch):
+    some, late = act_early.shape[1], act_late.shape[1]
+    sides = lax.axis_size("tensor")
+
+    def kernel(q_ref, k_ref, v_ref, p_ref, x_ref, w_ref, h_ref, gain_ref, dn_ref, do_ref, y_ref, c_hbm, s_hbm, flip_hbm, ae_hbm, al_hbm, wd_ref, rd_ref, source, dq_ref, dk_ref, dv_ref, out_ref, sum_ref, flipped_ref, dh_ref, gain_out, sent_ref, got, c_ref, s_ref, flip_ref, ae_ref, al_ref, load_sem, sent, y_send, y_recv, g_ref, gt_ref, keys_sum, values_sum, *scratch):
         step = pl.program_id(0)
         half = ring_width // 2
         ring = Ring(devices, [(source.at[0], 0, half), (source.at[0], half, half)], [(sum_ref, 0), (sum_ref, half)], [[0], [1]], scratch)
-        brought = loads((c_hbm, s_hbm, flip_hbm), (c_ref, s_ref, flip_ref), load_sem)
+        brought = loads((c_hbm, s_hbm, flip_hbm, ae_hbm, al_hbm), (c_ref, s_ref, flip_ref, ae_ref, al_ref), load_sem)
+        other = (ring.me, lax.rem(ring.side + 1, sides))
+
+        def across(which):
+            return pltpu.make_async_remote_copy(
+                src_ref=sent.at[which], dst_ref=got.at[:, pl.ds(pl.multiple_of(which * TILE, TILE), TILE)],
+                send_sem=y_send.at[which], recv_sem=y_recv.at[which], device_id=other, device_id_type=MESH,
+            )
+
         turns = [(firsts + 2 * heads, 1)]
 
         @pl.when(step == 0)
         def _():
             for copy in brought:
                 copy.start()
-            ring.barrier()
+            ring.barrier((other,))
             ring.begin()
 
         @pl.when(step == firsts)
@@ -670,6 +643,14 @@
         @pl.when(step >= firsts)
         def _():
             head = step - firsts
+
+            @pl.when(head < SOON)
+            def _():
+                down = (dot_nt(ae_ref[...], wd_ref[...]) + dot_nt(al_ref[...], rd_ref[...])).astype(BF)
+                sent[head] = down
+                sent_ref[...] = down
+                across(head).start()
+
             grad_all = dot_nn(g_ref[...], w_ref[...]).astype(BF)
             out_ref[...] = dot_nn(gt_ref[...], x_ref[...]).astype(BF)
             keys_t = k_ref[...].T
@@ -701,6 +682,8 @@
 
             @pl.when(head == heads - 1)
             def _():
+                for which in range(SOON):
+                    across(which).wait()
                 ring.finish()
 
     def at(i):
@@ -709,6 +692,11 @@
     head_spec = pl.BlockSpec((m, E), lambda i: (0, at(i)))
     long_spec = pl.BlockSpec((reach, E), lambda i: (0, at(i)))
     rows_spec = pl.BlockSpec((ROWS, width), lambda i: (jnp.minimum(i, firsts - 1), 0))
+    dma = pltpu.SemaphoreType.DMA
+
+    def soon(i):
+        return jnp.minimum(at(i), SOON - 1)
+
     any_space = pl.BlockSpec(memory_space=pl.ANY)
     return pl.pallas_call(
         kernel,
@@ -722,6 +710,8 @@
             jax.ShapeDtypeStruct((out_width, rows), F32),
             jax.ShapeDtypeStruct((m, width), F32),
             jax.ShapeDtypeStruct((1, width), F32),
+            jax.ShapeDtypeStruct((m, SOON * TILE), BF),
+            jax.ShapeDtypeStruct((m, SOON * TILE), BF),
         ],
         in_specs=[
             head_spec,
@@ -735,7 +725,10 @@
             rows_spec,
             rows_spec,
             rows_spec,
-            any_space, any_space, any_space, any_space,
+            any_space, any_space, any_space, any_space, any_space,
+            pl.BlockSpec((TILE, some), lambda i: (soon(i), 2)),
+            pl.BlockSpec((TILE, late), lambda i: (soon(i), 2)),
+            any_space,
         ],
         out_specs=[
             head_spec,
@@ -746,9 +739,13 @@
             single((out_width, rows)),
             rows_spec,
             single((1, width)),
+            pl.BlockSpec((m, TILE), lambda i: (0, soon(i))),
+            any_space,
         ],
         scratch_shapes=[
-            pltpu.VMEM((reach, E), F32), pltpu.VMEM((reach, E), F32), pltpu.VMEM(flip.shape, F32), pltpu.SemaphoreType.DMA((3,)),
+            pltpu.VMEM((reach, E), F32), pltpu.VMEM((reach, E), F32), pltpu.VMEM(flip.shape, F32),
+            pltpu.VMEM((m, some), BF), pltpu.VMEM((m, late), BF), dma((5,)),
+            pltpu.VMEM((SOON, m, TILE), BF), dma((SOON,)), dma((SOON,)),
             pltpu.VMEM((m, width), BF), pltpu.VMEM((width, m), BF),
             pltpu.VMEM((reach, E), F32), pltpu.VMEM((reach, E), F32),
             *Ring.scratch(devices, [(rows, ring_width // 2)] * 2),
@@ -756,7 +753,7 @@
         compiler_params=pltpu.CompilerParams(vmem_limit_bytes=VMEM, collective_id=identity, has_side_effects=True),
         cost_estimate=cost(8 * heads * m * KB * E * 2, 2 * heads * m * KB),
         name="attend_back",
-    )(query, kv, kv, probs, mixed, w_attn, hidden, gain, d_normed, d_normed_other, cotangent, cosine, sine, flip, ring_source)
+    )(query, kv, kv, probs, mixed, w_attn, hidden, gain, d_normed, d_normed_other, cotangent, cosine, sine, flip, act_early, act_late, w_ffn, rest, ring_source)
 
 
 def qkv_back(x_t, d_query, d_key, d_value, w_attn, up_part, out_part, out_width, identity):
@@ -1072,14 +1069,15 @@
     )(mixed, w_attn, tokens, gain)
 
 
-def last_pass(tokens, gain, grad, grad_other, grad_add, d_hidden, hidden, act_early, act_late, w_ffn, rest, gain_ffn_grad, flip, qkv_part, lanes, identity):
+def last_pass(tokens, gain, grad, grad_other, grad_add, d_hidden, hidden, ffn_part, ffn_other, act_early, act_late, w_ffn, rest, gain_ffn_grad, flip, qkv_part, lanes, identity):
     m, width = tokens.shape
     devices, rows, all_columns = qkv_part.shape
     columns = all_columns // 3
     chips = devices // 2
     size = ROWS // 2
     steps = m // size
-    total = tiles_of(width) + steps + chips
+    downs = tiles_of(width) - SOON
+    total = downs + steps + chips
     names = 3
     half = m // 2
     tiles = tiles_of(width)
@@ -1087,20 +1085,27 @@
     sides = lax.axis_size("tensor")
     assert chips >= tiles
 
-    def kernel(x_ref, g_ref, dn_ref, do_ref, add_hbm, dh_ref, h_ref, a_hbm, al_hbm, w_ref, rest_ref, gf_ref, flip_hbm, source, grad_ref, layer_ref, flipped_ref, q_ref, k_ref, v_ref, gains_ref, a_ref, al_ref, flip_ref, add, load_sem, add_send, add_recv, gain_sum, gain_source, sent, got, y_send, y_recv, *scratch):
+    def kernel(x_ref, g_ref, dn_ref, do_ref, add_hbm, dh_ref, h_ref, fp_ref, fo_ref, a_hbm, al_hbm, w_ref, rest_ref, gf_ref, flip_hbm, source, grad_ref, layer_ref, flipped_ref, q_ref, k_ref, v_ref, gains_ref, a_ref, al_ref, flip_ref, add, load_sem, add_send, add_recv, gain_sum, gain_source, gain_in, gain_send, gain_recv, sent, got, y_send, y_recv, *scratch):
         step = pl.program_id(0)
         ring = Ring(
             devices, [(source, number * columns, columns) for number in range(names)], [(q_ref, 0), (k_ref, 0), (v_ref, 0)],
-            [[0], [1], [2]], scratch[: 3 * names + 5],
+            [[0], [1], [2]], scratch,
         )
-        gain_ring = Ring(devices, [(gain_source, 0, lanes)], [(gains_ref, 0)], [[0]], scratch[3 * names + 5 :])
+
+        def gain_copy(away):
+            owner = lax.rem(ring.me + away, devices)
+            return pltpu.make_async_remote_copy(
+                src_ref=gain_source.at[owner], dst_ref=gain_in.at[away], send_sem=gain_send.at[away], recv_sem=gain_recv.at[away],
+                device_id=(owner, ring.side), device_id_type=MESH,
+            )
+
         other = (ring.me, lax.rem(ring.side + 1, sides))
         brought = loads((a_hbm, al_hbm, flip_hbm, add_hbm), (a_ref, al_ref, flip_ref, add.at[ring.side]), load_sem)
         add_copy = pltpu.make_async_remote_copy(
             src_ref=add_hbm, dst_ref=add.at[ring.side], send_sem=add_send, recv_sem=add_recv, device_id=other, device_id_type=MESH
         )
-        row_step = step - tiles
-        end_step = step - tiles - steps
+        row_step = step - downs
+        end_step = step - downs - steps
 
         def across(which):
             return pltpu.make_async_remote_copy(
@@ -1112,7 +1117,7 @@
         def _():
             for copy in brought:
                 copy.start()
-            ring.barrier((other,))
+            ring.barrier((other, *[(lax.rem(ring.me + away, devices), ring.side) for away in range(1, devices)]))
             add_copy.start()
             ring.begin()
             for copy in brought:
@@ -1123,7 +1128,7 @@
         def _():
             add_copy.wait()
 
-        @pl.when(step < tiles)
+        @pl.when(step < downs)
         def _():
             sent[step] = (dot_nt(a_ref[...], w_ref[...]) + dot_nt(al_ref[...], rest_ref[...])).astype(BF)
             across(step).start()
@@ -1151,29 +1156,44 @@
                 span = slice(device * rows, (device + 1) * rows)
                 gain_source[device, :16, :rows] = jnp.broadcast_to(gain_sum[:, span], (16, rows)).astype(BF)
                 gain_source[device, 16:, :rows] = jnp.broadcast_to(gf_ref[:, span], (16, rows)).astype(BF)
-            gain_ring.begin()
-
-        ring.pace(step, [(tiles, 4), (steps, 3), (chips, 3)])
-
-        @pl.when(end_step >= 0)
-        def _():
-            gain_ring.run(end_step, jnp.minimum(end_step + 1, gain_ring.events))
-
-        @pl.when((end_step >= 0) & (end_step < tiles))
-        def _():
-            across(end_step).wait()
-            layer_ref[...] = (h_ref[...] + (sent[end_step].astype(F32) + got[end_step].astype(F32))).astype(BF)
+
+            def send(away, carry):
+                gain_copy(away).start()
+                return carry
+
+            lax.fori_loop(1, devices, send, 0)
+
+        ring.pace(step, [(downs, 5), (steps, 3), (chips, 3)])
+
+        @pl.when((end_step >= 0) & (end_step < SOON))
+        def _():
+            layer_ref[...] = (h_ref[...] + (fp_ref[...].astype(F32) + fo_ref[...].astype(F32))).astype(BF)
+
+        @pl.when((end_step >= SOON) & (end_step < tiles))
+        def _():
+            which = end_step - SOON
+            across(which).wait()
+            layer_ref[...] = (h_ref[...] + (sent[which].astype(F32) + got[which].astype(F32))).astype(BF)
 
         @pl.when(step == total - 1)
         def _():
             ring.finish()
-            gain_ring.finish()
+
+            def take(away, total):
+                gain_copy(away).wait()
+                return total + gain_in[away].astype(F32)
+
+            gains_ref[...] = lax.fori_loop(1, devices, take, gain_source[ring.me].astype(F32))
 
     def early(i):
-        return jnp.minimum(i, tiles - 1)
-
-    rows_spec = pl.BlockSpec((size, width), lambda i: (jnp.clip(i - tiles, 0, steps - 1), 0))
-    tile_spec = pl.BlockSpec((m, TILE), lambda i: (0, jnp.clip(i - tiles - steps, 0, tiles - 1)))
+        return jnp.minimum(i, downs - 1) + SOON
+
+    def ending(i):
+        return jnp.clip(i - downs - steps, 0, tiles - 1)
+
+    rows_spec = pl.BlockSpec((size, width), lambda i: (jnp.clip(i - downs, 0, steps - 1), 0))
+    tile_spec = pl.BlockSpec((m, TILE), lambda i: (0, ending(i)))
+    soon_spec = pl.BlockSpec((m, TILE), lambda i: (0, jnp.minimum(ending(i), SOON - 1)))
     dma = pltpu.SemaphoreType.DMA
     sums = jax.ShapeDtypeStruct((rows, columns), F32)
     return pl.pallas_call(
@@ -1187,7 +1207,7 @@
             jax.ShapeDtypeStruct((32, lanes), F32),
         ],
         in_specs=[
-            rows_spec, single((1, width)), rows_spec, rows_spec, pl.BlockSpec(memory_space=pl.ANY), rows_spec, tile_spec, pl.BlockSpec(memory_space=pl.ANY), pl.BlockSpec(memory_space=pl.ANY),
+            rows_spec, single((1, width)), rows_spec, rows_spec, pl.BlockSpec(memory_space=pl.ANY), rows_spec, tile_spec, soon_spec, soon_spec, pl.BlockSpec(memory_space=pl.ANY), pl.BlockSpec(memory_space=pl.ANY),
             pl.BlockSpec((TILE, some), lambda i: (early(i), 2)), pl.BlockSpec((TILE, late), lambda i: (early(i), 2)), single((1, width)),
             pl.BlockSpec(memory_space=pl.ANY), pl.BlockSpec(memory_space=pl.ANY),
         ],
@@ -1205,17 +1225,19 @@
             dma,
             pltpu.VMEM((1, width), F32),
             pltpu.VMEM((devices, 32, lanes), BF),
-            pltpu.VMEM((tiles, m, TILE), BF),
-            pltpu.VMEM((tiles, m, TILE), BF),
-            dma((tiles,)),
-            dma((tiles,)),
+            pltpu.VMEM((devices, 32, lanes), BF),
+            dma((devices,)),
+            dma((devices,)),
+            pltpu.VMEM((downs, m, TILE), BF),
+            pltpu.VMEM((downs, m, TILE), BF),
+            dma((downs,)),
+            dma((downs,)),
             *Ring.scratch(devices, [(rows, columns)] * names),
-            *Ring.scratch(devices, [(32, lanes)]),
         ],
         compiler_params=pltpu.CompilerParams(vmem_limit_bytes=VMEM, collective_id=identity, has_side_effects=True),
         cost_estimate=cost(20 * m * width, 24 * m * width),
         name="last_pass",
-    )(tokens, gain, grad, grad_other, grad_add, d_hidden, hidden, act_early, act_late, w_ffn, rest, gain_ffn_grad, flip, qkv_part)
+    )(tokens, gain, grad, grad_other, grad_add, d_hidden, hidden, ffn_part, ffn_other, act_early, act_late, w_ffn, rest, gain_ffn_grad, flip, qkv_part)
 
 
 def feed_tile(x_ref, dy_ref, dyt_ref, g_ref, u_ref, d_ref, act_ref, both_ref, down_ref):
@@ -1240,7 +1262,7 @@
     def kernel(x_hbm, dy_hbm, dyt_hbm, g_ref, u_ref, d_ref, block_ref, act_ref, both_ref, down_ref, rest_ref, x_ref, dy_ref, dyt_ref, load_sem, *scratch):
         step = pl.program_id(0)
         brought = loads((x_hbm, dy_hbm, dyt_hbm), (x_ref, dy_ref, dyt_ref), load_sem)
-        spread = Spread(devices, [(block_ref, rest_ref, 0, width), (block_ref, rest_ref, width, width)], scratch)
+        spread = Spread(devices, [(block_ref, 0, rest_ref, 0, width), (block_ref, width, rest_ref, width, width)], scratch)
 
         @pl.when(step == 0)
         def _():
@@ -1296,9 +1318,10 @@
     devices, rows, some = down_early.shape
     late = LATE * TILE
     padded = some + late
-    early_tiles = some // TILE
     tiles = width // TILE
-    grads = 2 * (early_tiles + LATE)
+    wide = 2 * TILE
+    early_wide, late_wide = some // wide, (late + wide - 1) // wide
+    grads = 2 * (early_wide + late_wide)
     total = LATE + tiles + grads
     sides = lax.axis_size("tensor")
     pieces = [(rows, some // 2)] * 2
@@ -1354,18 +1377,21 @@
             sent_ref[...] = low
             across(which).start()
 
-        @pl.when((step >= LATE + tiles) & (step < LATE + tiles + 2 * early_tiles))
+        @pl.when((step >= LATE + tiles) & (step < LATE + tiles + 2 * early_wide))
         def _():
             grad_ref[0] = dot_nn(xt_ref[...], tile_ref[0]).astype(BF)
 
-        @pl.when(step >= LATE + tiles + 2 * early_tiles)
-        def _():
-            number = step - (LATE + tiles + 2 * early_tiles)
-            here = pl.ds(pl.multiple_of(lax.rem(number, LATE) * TILE, TILE), TILE)
-            grad_ref[0] = dot_nn(xt_ref[...], d_late[number // LATE, :, here]).astype(BF)
-
-        ring.pace(step, [(LATE, 12), (tiles, 8), (grads, 4)])
-        late_ring.pace(step, [(LATE, 0), (tiles, 8), (grads, 4)])
+        number = step - (LATE + tiles + 2 * early_wide)
+        for part in range(late_wide):
+            several = min(wide, late - part * wide)
+
+            @pl.when((number >= 0) & (lax.rem(number, late_wide) == part))
+            def _():
+                piece = d_late[number // late_wide, :, part * wide : part * wide + several]
+                grad_ref[0, :, :several] = dot_nn(xt_ref[...], piece).astype(BF)
+
+        ring.pace(step, [(LATE, 12), (tiles, 8), (grads, 7)])
+        late_ring.pace(step, [(LATE, 0), (tiles, 8), (grads, 7)])
 
         @pl.when(step == total - 1)
         def _():
@@ -1381,20 +1407,20 @@
         return jnp.clip(i - LATE, 0, tiles - 1)
 
     def third(i):
-        at = jnp.clip(i - LATE - tiles, 0, 2 * early_tiles - 1)
-        return (at // early_tiles, 0, at % early_tiles)
+        at = jnp.clip(i - LATE - tiles, 0, 2 * early_wide - 1)
+        return (at // early_wide, 0, at % early_wide)
 
     def grad_at(i):
         at = jnp.maximum(i - LATE - tiles, 0)
-        more = jnp.maximum(at - 2 * early_tiles, 0)
-        is_late = at // (2 * early_tiles)
+        more = jnp.maximum(at - 2 * early_wide, 0)
+        is_late = at // (2 * early_wide)
         return (
-            (1 - is_late) * (at // early_tiles) + is_late * (more // LATE),
+            (1 - is_late) * (at // early_wide) + is_late * (more // late_wide),
             0,
-            (1 - is_late) * (at % early_tiles) + is_late * (early_tiles + more % LATE),
+            (1 - is_late) * (at % early_wide) + is_late * (early_wide + more % late_wide),
         )
 
-    assert LATE <= early_tiles
+    assert late_wide <= early_wide and some % wide == 0
     any_space = pl.BlockSpec(memory_space=pl.ANY)
     dma = pltpu.SemaphoreType.DMA
 
@@ -1415,7 +1441,7 @@
             any_space, any_space, any_space, any_space,
             rest_tile(0), rest_tile(1), rest_tile(2),
             any_space,
-            pl.BlockSpec((1, m, TILE), third),
+            pl.BlockSpec((1, m, wide), third),
             pl.BlockSpec((TILE, some), lambda i: (second(i), 0)),
             pl.BlockSpec((TILE, some), lambda i: (second(i), 1)),
             pl.BlockSpec((TILE, late), lambda i: (second(i), 0)),
@@ -1424,7 +1450,7 @@
         ],
         out_specs=[
             pl.BlockSpec((m, TILE), lambda i: (0, first(i))),
-            pl.BlockSpec((1, width, TILE), grad_at),
+            pl.BlockSpec((1, width, wide), grad_at),
             pl.BlockSpec((m, TILE), lambda i: (0, second(i))),
             any_space,
             single((rows, padded)),
@@ -1464,19 +1490,12 @@
     tiles = (hidden_units + TILE - 1) // TILE
     padded = tiles * TILE
 
-    attn_pack = jnp.concatenate([w_query, w_key, w_value, w_out.T], axis=1)
+    some = padded - LATE * TILE
     lanes = max(128, own_rows)
     gains = jnp.zeros((32, lanes), BF).at[0, :own_rows].set(attn_gain).at[16, :own_rows].set(ffn_gain)
-    w_attn, all_gains, near, far = ring_gather((attn_pack, gains), (2, 1), tokens, 0)
-
-    def wide(matrix):
-        return jnp.pad(matrix, ((0, 0), (0, padded - hidden_units)))
-
-    ffn_parts = [wide(w_gate), wide(w_up), wide(w_down.T)]
-    some = padded - LATE * TILE
-    ffn_pack = jnp.concatenate([part[:, :some] for part in ffn_parts], axis=1)
-    rest_pack = jnp.concatenate([part[:, some:] for part in ffn_parts], axis=1)
-    w_attn, all_gains, ffn_pack = lax.optimization_barrier((w_attn, all_gains, ffn_pack))
+    w_attn, all_gains, near, far, ffn_pack, rest_pack = first_gather(
+        w_query, w_key, w_value, w_out, gains, tokens, w_gate.T, w_up.T, w_down, 0
+    )
     w_ffn = lax.all_gather(ffn_pack, "dp", axis=0, tiled=True)
     all_gains = all_gains.reshape(devices, 32, lanes)
     gain_attn = all_gains[:, 0, :own_rows].reshape(1, width).astype(F32)
@@ -1501,14 +1520,15 @@
     )
     both_part = both_part.reshape(2, devices, own_rows, padded)
 
-    d_query, d_key, d_value, out_part, gate_grad, w_down_grad, d_hidden, gain_ffn_grad = attend_back(
-        query, kv, probs, mixed, w_attn, hidden, gain_ffn, d_normed_ffn, d_normed_other, cotangent, cosine, sine, down_grad, both_part, heads, hidden_units, 2
+    d_query, d_key, d_value, out_part, gate_grad, w_down_grad, d_hidden, gain_ffn_grad, ffn_part, ffn_other = attend_back(
+        query, kv, probs, mixed, w_attn, hidden, gain_ffn, d_normed_ffn, d_normed_other, cotangent, cosine, sine, down_grad, act_early, act_late, w_ffn, rest,
+        both_part, heads, hidden_units, 2,
     )
     qkv_part, d_normed_attn, d_attn_other, d_attn_add, up_grad, out_grad = qkv_back(
         normed_attn_t, d_query, d_key, d_value, w_attn, both_part, out_part.reshape(devices, own_rows, head_columns), hidden_units, 3
     )
     tokens_grad, layer_out, w_out_grad, query_grad, key_grad, value_grad, gain_grads = last_pass(
-        tokens, gain_attn, d_normed_attn, d_attn_other, d_attn_add, d_hidden, hidden, act_early, act_late, w_ffn, rest, gain_ffn_grad, out_grad,
+        tokens, gain_attn, d_normed_attn, d_attn_other, d_attn_add, d_hidden, hidden, ffn_part, ffn_other, act_early, act_late, w_ffn, rest, gain_ffn_grad, out_grad,
         qkv_part.reshape(devices, own_rows, 3 * head_columns), lanes, 4,
     )
     return (

time: 660 us -> 657 us (level)
    unnamed x54 -> x34, local copies, waits for them, and re-layouts: 19.7 us -> 15.9 us
  transfers between devices with their start and end apart: 1 -> 1, of which waited for: 1 -> 1; matrix products, arithmetic and copies ran while one was open for 2% -> 1% of each run, Pallas kernels for 17% -> 17%
where the time goes in v8:
time: 657 us; the launch traced here: 648 us
  Pallas kernels  598 us (91%)
  local copies, waits for them, and re-layouts  19.8 us (3%)
  between operations  15 us (2%)
  waiting for transfers between devices  9.93 us (2%)
    pallas_call x1, Pallas kernels, first_gather(): pl.pallas_call(kernel, out_shape=[low((rows * devices, 4 * columns)), low...  111 us
    pallas_call x1, Pallas kernels, qkv_back(): pl.pallas_call(kernel, grid=(total,), out_shape=[jax.ShapeDtypeStruct((wi...  110 us
    pallas_call x1, Pallas kernels, last_pass(): pl.pallas_call(kernel, grid=(total,), out_shape=[jax.ShapeDtypeStruct((m,...  73 us
    pallas_call x1, Pallas kernels, ffn_back(): pl.pallas_call(kernel, grid=(total,), out_shape=[jax.ShapeDtypeStruct((m,...  72.9 us
    pallas_call x1, Pallas kernels, attend_back(): pl.pallas_call(kernel, grid=(firsts + heads,), out_shape=[jax.ShapeDtypeS...  66.9 us
    pallas_call x1, Pallas kernels, feed(): pl.pallas_call(kernel, grid=(early,), out_shape=[jax.ShapeDtypeStruct((m,...  54.1 us
    pallas_call x1, Pallas kernels, out_norm(): pl.pallas_call(kernel, grid=(2 * steps,), out_shape=[jax.ShapeDtypeStruct...  52.7 us
    pallas_call x1, Pallas kernels, project(): pl.pallas_call(kernel, grid=(3 * some,), out_shape=[jax.ShapeDtypeStruct(...  24.5 us
  transfers between devices with their start and end apart: 1, of which 1 were waited for; matrix products, arithmetic and copies ran while one was open for 1% of the time, Pallas kernels for 17%

profile of v8, /device:TPU:0, one launch (start us, length us, event | category | flops | bytes accessed | tf_op | source)
XLA Modules:
  0.0 647.9 jit_solution(10806575139531712965)
XLA Ops:
  9.2 111.1 %first_gather.1 = (bf16[2048,4096]{1,0:T(8,128)(2,1)}, bf16[512,128]{1,0:T(8,128)(2,1)}, bf16[512,2048]{1,0:T(8,128)(2,1)}, bf16[512,2048]{1,0:T(8,128)(2,1)}, b...) custom-call(bf16[128,1024]{1,0:T(8,128)(2,1)} %q_ref.1, bf16[128,1024]{1,0:T(8,128)(2,1)} %k_ref.1, ...), custom_call_target="tpu_custom_call" | custom-call | tf_op jit(solution)/shard_map/first_gather/pallas_call | solution.py:285
  120.9 2.5 copy.25
  125.4 12.1 %first_norm.1 = (bf16[1536,2048]{1,0:T(8,128)(2,1)}, bf16[2048,1536]{1,0:T(8,128)(2,1)}) custom-call(bf16[512,2048]{1,0:T(8,128)(2,1)} %get-tuple-element.83.far_ref, bf16[512,2048]{1,0:T(8,128)(2,1)} %get-tuple-element.84.near_ref, bf16[512,2048]{1,0:T(8,128)(2,1)} %x_ref.3, f32[1,2048]{1,0:T(1,128)} %bitcast.26), custom_call_target="tpu_custom_call" | custom-call | flops 25165824 | bytes 14680064 | tf_op jit(solution)/shard_map/first_norm/pallas_call | solution.py:993
  137.5 2.8 fusion
  140.3 1.6 pad_maximum_fusion
  141.9 24.5 %project.1 = (bf16[512,1024]{1,0:T(8,128)(2,1)}, bf16[1536,2048]{1,0:T(8,128)(2,1)}) custom-call(bf16[1536,2048]{1,0:T(8,128)(2,1)} %get-tuple-element.86.x_ref, bf16[2048,4096]{1,0:T(8,128)(2,1)} %get-tuple-element.87.w_ref, f32[1536,128]{1,0:T(8,128)} %get-tuple-element.149.c_ref.c_hbm, f32[1536,128]{1,0:T(8,128)} %get-tuple-element.150.s_ref.s_hbm), custom_call_target="tpu_custom_call" | custom-call | flops 15032385536 | bytes 28311552 | tf_op jit(solution)/shard_map/project/pallas_call | solution.py:519
  166.5 20.6 %attend.1 = (bf16[512,1024]{1,0:T(8,128)(2,1)}, bf16[8,2,1280,256]{3,2,1,0:T(8,128)(2,1)}) custom-call(bf16[512,1024]{1,0:T(8,128)(2,1)} %get-tuple-element.88.q_ref, bf16[1536,2048]{1,0:T(8,128)(2,1)} %get-tuple-element.89.k_ref.v_ref, bf16[1536,2048]{1,0:T(8,128)(2,1)} %get-tuple-element.89.k_ref.v_ref, s32[1,512]{1,0:T(1,128)} %bitcast.30), custom_call_target="tpu_custom_call" | custom-call | flops 5368709120 | bytes 10485760 | tf_op jit(solution)/shard_map/attend/pallas_call | solution.py:564
  187.0 52.7 %out_norm.1 = (f32[512,2048]{1,0:T(8,128)}, bf16[512,2048]{1,0:T(8,128)(2,1)}, bf16[2048,512]{1,0:T(8,128)(2,1)}) custom-call(bf16[512,1024]{1,0:T(8,128)(2,1)} %get-tuple-element.91.x_ref, bf16[2048,4096]{1,0:T(8,128)(2,1)} %get-tuple-element.87.w_ref, bf16[512,2048]{1,0:T(8,128)(2,1)} %x_ref.3, f32[1,2048]{1,0:T(1,128)} %bitcast.28), custom_call_target="tpu_custom_call" | custom-call | flops 2147483648 | bytes 12582912 | tf_op jit(solution)/shard_map/out_norm/pallas_call | solution.py:1050
  239.7 9.9 %all-gather.2.cloned.1.call-done.g_ref.u_ref.d_ref.wg_ref.wu_ref.wd_ref.w_ref = bf16[2048,6144]{1,0:T(8,128)(2,1)} async-done(((bf16[128,6144]{1,0:T(8,128)(2,1)}), bf16[2048,6144]{1,0:T(8,128)(2,1)}) %all-gather.2.cloned.1.call-update) | async-done | bytes 25165840 | tf_op jit(solution)/shard_map/all_gather | solution.py:1499
  249.6 54.1 %feed.1 = (bf16[512,2048]{1,0:T(8,128)(2,1)}, bf16[2,512,2048]{2,1,0:T(8,128)(2,1)}, bf16[2048,2048]{1,0:T(8,128)(2,1)}, bf16[2048,2304]{1,0:T(8,128)(2,1)}) custom-call(bf16[512,2048]{1,0:T(8,128)(2,1)} %get-tuple-element.93.x_hbm, bf16[512,2048]{1,0:T(8,128)(2,1)} %y_ref.1, bf16[2048,512]{1,0:T(8,128)(2,1)} %bitcast.20, ...), custom_call_target="tpu_custom_call" | custom-call | flops 17179869184 | bytes 41943040 | tf_op jit(solution)/shard_map/feed/pallas_call | solution.py:1284
  303.8 72.9 %ffn_back.1 = (bf16[512,768]{1,0:T(8,128)(2,1)}, bf16[2,2048,2816]{2,1,0:T(8,128)(2,1)}, bf16[512,2048]{1,0:T(8,128)(2,1)}, bf16[512,2048]{1,0:T(8,128)(2,1)}, f32[128,2816]{1,0:T(8,128)}) custom-call(bf16[512,2048]{1,0:T(8,128)(2,1)} %get-tuple-element.93.x_hbm, bf16[2048,512]{1,0:T(8,128)(2,1)} %get-tuple-element.94.xt_hbm, bf16[512,2048]{1,0:T(8,128)(2,1)} %y_ref.1, ...), custom_call_target="tpu_custom_call" | custom-call | flops 30064771072 | bytes 57671680 | tf_op jit(solution)/shard_map/ffn_back/pallas_call | solution.py:1430
  376.6 66.9 %attend_back.1 = (bf16[512,1024]{1,0:T(8,128)(2,1)}, bf16[1536,1024]{1,0:T(8,128)(2,1)}, bf16[1536,1024]{1,0:T(8,128)(2,1)}, bf16[2048,1024]{1,0:T(8,128)(2,1)},...) custom-call(bf16[512,1024]{1,0:T(8,128)(2,1)} %get-tuple-element.88., ...), custom_call_target="tpu_custom_call" | custom-call | flops 10737418240 | bytes 10485760 | tf_op jit(solution)/shard_map/attend_back/pallas_call | solution.py:701
  443.5 110.3 %qkv_back.1 = (bf16[2048,3072]{1,0:T(8,128)(2,1)}, bf16[512,2048]{1,0:T(8,128)(2,1)}, bf16[512,2048]{1,0:T(8,128)(2,1)}, bf16[256,2048]{1,0:T(8,128)(2,1)}, f32[128,2752]{1,0:T(8,128)}, /*index=5*/f32[128,1024]{1,0:T(8,128)}) custom-call(bf16[2048,1536]{1,0:T(8,128)(2,1)} %get-tuple-element.85.xt_hbm, bf16[512,1024]{1,0:T(8,128)(2,1)} %get-tuple-element.106.dq_hbm, ...), custom_call_target="tpu_custom_call" | custom-call | flops 30064771072 | bytes 25165824 | tf_op jit(solution)/shard_map/qkv_back/pallas_call | solution.py:893
  553.8 73.0 %last_pass.1 = (f32[512,2048]{1,0:T(8,128)}, bf16[512,2048]{1,0:T(8,128)(2,1)}, f32[1024,128]{1,0:T(8,128)}, f32[128,1024]{1,0:T(8,128)}, f32[128,1024]{1,0:T(8,...) custom-call(bf16[512,2048]{1,0:T(8,128)(2,1)} %x_ref.3, f32[1,2048]{1,0:T(1,128)} %bitcast.27, ...), custom_call_target="tpu_custom_call" | custom-call | flops 20971520 | bytes 25165824 | tf_op jit(solution)/shard_map/last_pass/pallas_call | solution.py:1199
  626.8 1.3 slice_bitcast_fusion
  628.1 1.5 copy.27
  629.6 1.5 copy.26
  631.6 1.3 copy.40
  633.0 1.6 copy-done.1
  634.6 2.0 copy.41
  636.6 0.8 copy.42
  637.4 0.8 copy.43
  638.2 0.8 copy.44
  639.8 1.1 copy.46
  (34 shorter events, 5.2 us)
Async XLA Ops:
  7.2 242.5 %all-gather.2.cloned.1.call-start = ((), (), s32[]{:S(2)}) async-start(), calls=%async_computation | async-start | bytes 26738688 | tf_op jit(solution)/shard_map/all_gather | solution.py:1499
  8.6 0.6 copy-start.10
  9.2 111.2 %copy-start.11 = (s32[512]{0:T(512)S(1)}, s32[512]{0:T(512)}, u32[]{:S(2)}) copy-start(s32[512]{0:T(512)} %param.17) | copy-start | bytes 6148
  9.2 111.7 %copy-start = (bf16[512,2048]{1,0:T(8,128)(2,1)S(1)}, bf16[512,2048]{1,0:T(8,128)(2,1)}, u32[]{:S(2)}) copy-start(bf16[512,2048]{1,0:T(8,128)(2,1)} %y_ref.1) | copy-start | bytes 6291460
  553.8 74.3 %copy-start.4 = (f32[128,2752]{1,0:T(8,128)S(1)}, f32[128,2752]{1,0:T(8,128)}, u32[]{:S(2)}) copy-start(f32[128,2752]{1,0:T(8,128)} %get-tuple-element.138) | copy-start | bytes 4227076
  626.8 2.9 copy-start.3
  629.6 2.0 copy-start.2
  631.6 2.9 copy-start.1
  634.6 2.0 copy-start.9
  634.6 2.8 copy-start.8
  634.6 3.6 copy-start.7
  636.6 2.4 copy-start.6
  636.6 3.2 copy-start.5
Sparse Core Ops, SparseCore 0:
  120.5 129.1 all-gather.1

commit v9 on v8

--- a/solution.py
+++ b/solution.py
@@ -2,6 +2,7 @@
 
 import jax
 import jax.numpy as jnp
+import numpy as np
 from jax import lax
 from jax.experimental import pallas as pl
 from jax.experimental.pallas import tpu as pltpu
@@ -52,6 +53,14 @@
     return (1 - column) * row + column * (chips - 1 - row)
 
 
+def paced(at, costs, events):
+    spent, before = 0, 0
+    for steps, each in costs:
+        spent = spent + jnp.minimum(jnp.maximum(at - before, 0), steps) * each
+        before += steps
+    return spent * events // sum(steps * each for steps, each in costs)
+
+
 class Spread:
     def __init__(self, devices, pieces, scratch):
         self.devices, self.chips, self.pieces = devices, devices // 2, pieces
@@ -132,7 +141,7 @@
 
             self.copy(index, stage, half, False, True).start()
 
-    def pace(self, step, total):
+    def pace(self, step, costs):
         count = len(self.pieces)
 
         def one(event, carry):
@@ -140,7 +149,7 @@
                 pl.when(lax.rem(event, count) == index)(functools.partial(self.stage, event // count + 1, index))
             return carry
 
-        lax.fori_loop(step * self.events // total, (step + 1) * self.events // total, one, 0)
+        lax.fori_loop(paced(step, costs, self.events), paced(step + 1, costs, self.events), one, 0)
 
     def finish(self):
         for index in range(len(self.pieces)):
@@ -164,7 +173,7 @@
         lax.fori_loop(1, self.chips, gave, 0)
 
 
-def first_gather(w_query, w_key, w_value, w_out, gains, tokens, w_gate_t, w_up_t, w_down, identity):
+def first_gather(w_query, w_key, w_value, w_out, gains, tokens, w_gate_t, w_up_t, w_down, cotangent, places, identity):
     devices = lax.axis_size("dp")
     sides = lax.axis_size("tensor")
     rows, columns = w_query.shape
@@ -172,9 +181,13 @@
     tiles = (units + TILE - 1) // TILE
     padded, late = tiles * TILE, LATE * TILE
     some = padded - late
-    span = tokens.shape[0] // 2
-
-    def kernel(q_ref, k_ref, v_ref, o_hbm, gains_ref, tokens_ref, gate_hbm, up_hbm, down_hbm, attn_ref, all_ref, near, far, early_hbm, late_hbm, o_in, o_turned, gate_in, up_in, down_in, early_pack, late_pack, load_sem, store_sem, far_send, far_recv, near_send, near_recv, *scratch):
+    m, width = tokens.shape
+    span = m // 2
+    reach = WINDOW + m
+    rates = THETA ** (-(np.arange(E // 2, dtype=np.float32) * 2.0 / E))
+    rates = jnp.asarray(np.concatenate([rates, rates])[None, :], F32)
+
+    def kernel(q_ref, k_ref, v_ref, o_hbm, gains_ref, tokens_ref, gate_hbm, up_hbm, down_hbm, dy_hbm, places_ref, rates_ref, attn_ref, all_ref, near, far, early_hbm, late_hbm, dyt_hbm, cos_hbm, sin_hbm, o_in, o_turned, gate_in, up_in, down_in, early_pack, late_pack, dy_in, dyt, cosine, sine, load_sem, store_sem, far_send, far_recv, near_send, near_recv, *scratch):
         pieces = [(ref, 0, attn_ref, number * columns, columns) for number, ref in enumerate((q_ref, k_ref, v_ref, o_turned))]
         spread = Spread(devices, [*pieces, (gains_ref, 0, all_ref, 0, gains_ref.shape[1])], scratch)
         me, side, core = spread.me, spread.side, spread.core
@@ -182,9 +195,27 @@
         later, before = lax.rem(me + 2, devices), lax.rem(me + devices - 2, devices)
         parts = (gate_in, up_in, down_in)
         brought = loads(
-            (o_hbm, gate_hbm, up_hbm, down_hbm), (o_in, *[part.at[pl.ds(0, units)] for part in parts]), load_sem
+            (o_hbm, gate_hbm, up_hbm, down_hbm, dy_hbm), (o_in, *[part.at[pl.ds(0, units)] for part in parts], dy_in), load_sem
         )
-        stored = loads((early_pack, late_pack), (early_hbm, late_hbm), store_sem)
+        stored = loads((early_pack, late_pack, dyt, cosine, sine), (early_hbm, late_hbm, dyt_hbm, cos_hbm, sin_hbm), store_sem)
+
+        def tables(first, made):
+            angles = made * rates_ref[...]
+            lane = lax.broadcasted_iota(jnp.int32, (E, E), 1)
+            cosine[first : first + E, :] = jnp.cos(angles)
+            turn = jnp.sin(angles)
+            sine[first : first + E, :] = jnp.where(lane < E // 2, -turn, turn)
+
+        def own_tables():
+            for first in range(0, m, E):
+                row = places_ref[:, first : first + E].astype(F32)
+                tables(WINDOW + first, jnp.broadcast_to(row, (E, E)).T)
+
+        def earlier_tables(begin, end):
+            for first in range(begin, end, E):
+                row = lax.broadcasted_iota(jnp.int32, (E, E), 0) + (first - WINDOW)
+                tables(first, (row + places_ref[:, :1]).astype(F32))
+
         for copy in brought:
             copy.start()
         spread.barrier(((me, across), (later, side), (before, side)))
@@ -225,12 +256,23 @@
             made = part[...].T
             early_pack[:, number * some : (number + 1) * some] = made[:, :some]
             late_pack[:, number * late : (number + 1) * late] = made[:, some:]
-        for copy in stored:
+        for copy in stored[:2]:
             copy.start()
 
         def one(stage, carry):
             for index in range(len(pieces) + 1):
                 spread.stage(stage, index)
+
+            pl.when(stage == 1)(own_tables)
+            pl.when(stage == 2)(functools.partial(earlier_tables, 0, WINDOW // 2))
+            pl.when(stage == 3)(functools.partial(earlier_tables, WINDOW // 2, WINDOW))
+
+            @pl.when(stage == 4)
+            def _():
+                brought[4].wait()
+                dyt[...] = dy_in[...].T
+                for copy in stored[2:]:
+                    copy.start()
 
             @pl.when((stage == spread.chips // 2) & (me >= 2))
             def _():
@@ -291,17 +333,24 @@
             low(tokens.shape),
             low((rows, 3 * some)),
             low((rows, 3 * late)),
-        ],
-        in_specs=[any_space] * 9,
-        out_specs=[any_space] * 6,
+            low((width, m)),
+            jax.ShapeDtypeStruct((reach, E), F32),
+            jax.ShapeDtypeStruct((reach, E), F32),
+        ],
+        in_specs=[any_space] * 10 + [pl.BlockSpec(memory_space=pltpu.VMEM)] * 2,
+        out_specs=[any_space] * 9,
         scratch_shapes=[
             pltpu.VMEM(w_out.shape, BF),
             pltpu.VMEM((rows, columns), BF),
             *[pltpu.VMEM((padded, rows), BF)] * 3,
             pltpu.VMEM((rows, 3 * some), BF),
             pltpu.VMEM((rows, 3 * late), BF),
-            dma((4,)),
-            dma((2,)),
+            pltpu.VMEM((m, width), BF),
+            pltpu.VMEM((width, m), BF),
+            pltpu.VMEM((reach, E), F32),
+            pltpu.VMEM((reach, E), F32),
+            dma((5,)),
+            dma((5,)),
             dma((2,)),
             dma((2,)),
             dma((2,)),
@@ -310,7 +359,7 @@
         ],
         compiler_params=pltpu.CompilerParams(vmem_limit_bytes=VMEM, collective_id=identity, has_side_effects=True),
         name="first_gather",
-    )(w_query, w_key, w_value, w_out, gains, tokens, w_gate_t, w_up_t, w_down)
+    )(w_query, w_key, w_value, w_out, gains, tokens, w_gate_t, w_up_t, w_down, cotangent, places, rates)
 
 
 class Ring:
@@ -445,16 +494,7 @@
         lax.fori_loop(first, stop, one, 0)
 
     def pace(self, step, costs):
-        whole = sum(steps * each for steps, each in costs)
-
-        def done(at):
-            spent, before = 0, 0
-            for steps, each in costs:
-                spent = spent + jnp.minimum(jnp.maximum(at - before, 0), steps) * each
-                before += steps
-            return spent * self.events // whole
-
-        self.run(done(step), done(step + 1))
+        self.run(paced(step, costs, self.events), paced(step + 1, costs, self.events))
 
     def finish(self):
         for index, half in self.each():
@@ -488,98 +528,6 @@
     if back:
         return block * cosine - other * sine
     return block * cosine + other * sine
-
-
-def project(x, w, cosine, sine, own, heads):
-    m, k = x.shape
-    per = TILE // E
-    some = heads // per
-
-    def kernel(x_ref, w_ref, c_ref, s_ref, q_ref, kv_ref):
-        step = pl.program_id(0)
-
-        def rotate_to(ref, made, rows):
-            for part in range(per):
-                piece = slice(part * E, (part + 1) * E)
-                ref[:, piece] = turned(made[:, piece], c_ref[rows, :], s_ref[rows, :], False).astype(BF)
-
-        @pl.when(step < some)
-        def _():
-            rows = slice(m - own, m)
-            rotate_to(q_ref, dot_nn(x_ref[rows, :], w_ref[...]), rows)
-
-        @pl.when((step >= some) & (step < 2 * some))
-        def _():
-            rotate_to(kv_ref, dot_nn(x_ref[...], w_ref[...]), slice(0, m))
-
-        @pl.when(step >= 2 * some)
-        def _():
-            kv_ref[...] = dot_nn(x_ref[...], w_ref[...]).astype(BF)
-
-    return pl.pallas_call(
-        kernel,
-        grid=(3 * some,),
-        out_shape=[jax.ShapeDtypeStruct((own, heads * E), BF), jax.ShapeDtypeStruct((m, 2 * heads * E), BF)],
-        in_specs=[single((m, k)), pl.BlockSpec((k, TILE), lambda i: (0, i)), single((m, E)), single((m, E))],
-        out_specs=[
-            pl.BlockSpec((own, TILE), lambda i: (0, jnp.minimum(i, some - 1))),
-            pl.BlockSpec((m, TILE), lambda i: (0, jnp.maximum(i - some, 0))),
-        ],
-        compiler_params=pltpu.CompilerParams(vmem_limit_bytes=VMEM),
-        cost_estimate=cost(2 * (own + 2 * m) * k * heads * E, 2 * (m * k + 3 * (m + k) * heads * E)),
-        name="project",
-    )(x, w, cosine, sine)
-
-
-def attend(query, kv, places, heads):
-    m = query.shape[0]
-    blocks = m // QB
-    factor = E ** (-0.5) * LOG2E
-
-    def kernel(q_ref, k_ref, v_ref, p_ref, o_ref, probs_ref, bias):
-        @pl.when(pl.program_id(0) == 0)
-        def _():
-            for block in range(blocks):
-                key = lax.broadcasted_iota(jnp.int32, (KB, QB), 0) + block * QB
-                query = lax.broadcasted_iota(jnp.int32, (KB, QB), 1) + block * QB
-                place = p_ref[:, block * QB : (block + 1) * QB]
-                allowed = (key <= query + WINDOW) & (key > query) & (key >= query + WINDOW - place)
-                bias[block] = jnp.where(allowed, 0.0, -1e30)
-
-        values_t = v_ref[...].T
-        for block in range(blocks):
-            span = slice(block * QB, block * QB + KB)
-            scores = dot_nt(k_ref[span, :], q_ref[block * QB : (block + 1) * QB, :]) * factor + bias[block]
-            largest = jnp.max(scores, axis=0, keepdims=True)
-            grown = jnp.exp2(scores - largest)
-            inverse = 1.0 / jnp.sum(grown, axis=0, keepdims=True)
-            probs = (grown * inverse).astype(BF)
-            probs_ref[0, block] = probs
-            mixed_t = dot_nn(values_t[:, span], probs)
-            o_ref[block * QB : (block + 1) * QB, :] = mixed_t.T.astype(BF)
-
-    head = pl.BlockSpec((m, E), lambda i: (0, i))
-    reach = kv.shape[0]
-
-    return pl.pallas_call(
-        kernel,
-        grid=(heads,),
-        out_shape=[
-            jax.ShapeDtypeStruct((m, heads * E), BF),
-            jax.ShapeDtypeStruct((heads, blocks, KB, QB), BF),
-        ],
-        in_specs=[
-            head,
-            pl.BlockSpec((reach, E), lambda i: (0, i)),
-            pl.BlockSpec((reach, E), lambda i: (0, i + heads)),
-            whole_spec((1, m)),
-        ],
-        out_specs=[head, pl.BlockSpec((1, blocks, KB, QB), lambda i: (i, 0, 0, 0))],
-        scratch_shapes=[pltpu.VMEM((blocks, KB, QB), F32)],
-        compiler_params=pltpu.CompilerParams(vmem_limit_bytes=VMEM),
-        cost_estimate=cost(4 * heads * m * KB * E * 2, 2 * heads * m * KB, heads * m * KB),
-        name="attend",
-    )(query, kv, kv, places)
 
 
 def attend_back(query, kv, probs, mixed, w_attn, hidden, gain, d_normed, d_normed_other, cotangent, cosine, sine, flip, act_early, act_late, w_ffn, rest, ring_source, heads, out_width, identity):
@@ -949,124 +897,212 @@
     return root * pushed - rows * (root * root * root * inner), jnp.sum(grad * rows * root, axis=0, keepdims=True)
 
 
-def first_norm(far, near, tokens, gain):
+def forward(far, near, tokens, gain, w_attn, cosine, sine, places, gain_ffn, block, heads, identity):
     m, width = tokens.shape
-    steps = m // ROWS
-
-    def kernel(far_ref, near_ref, x_ref, g_ref, o_ref, t_ref):
+    reach = 3 * m
+    columns = heads * E
+    devices = lax.axis_size("dp")
+    sides = lax.axis_size("tensor")
+    part_steps = m // ROWS
+    per = TILE // E
+    some = heads // per
+    blocks = m // QB
+    factor = E ** (-0.5) * LOG2E
+    counts = (3 * part_steps, some, 2 * some, heads, part_steps, part_steps)
+    starts = [sum(counts[:number]) for number in range(len(counts) + 1)]
+    total = starts[-1]
+    piece = block.shape[1] // 4
+
+    def kernel(far_ref, near_ref, x_ref, again_ref, g_ref, w_ref, c_ref, s_ref, places_ref, gf_ref, w_hbm, block_ref, nt_ref, q_out, kv_out, mixed_out, probs_ref, hidden_ref, normed_ref, turned_ref, whole_ref, normed, q_all, kv_all, mixed_all, w_out, bias, sent, got, load_sem, y_send, y_recv, *scratch):
         step = pl.program_id(0)
-        me = lax.axis_index("dp")
-
-        def normed(ref):
-            rows = ref[...].astype(F32)
-            return (rows * root_of(rows) * g_ref[...]).astype(BF)
-
-        def earlier(ref, there):
-            @pl.when(there)
+        spread = Spread(devices, [(block_ref, number * piece, whole_ref, number * piece, piece) for number in range(4)], scratch)
+        me, side = spread.me, spread.side
+        other = (me, lax.rem(side + 1, sides))
+        brought = loads((w_hbm.at[:, pl.ds(3 * columns, columns)],), (w_out,), load_sem)
+
+        def across(which):
+            return pltpu.make_async_remote_copy(
+                src_ref=sent.at[which], dst_ref=got.at[which], send_sem=y_send.at[which], recv_sem=y_recv.at[which],
+                device_id=other, device_id_type=MESH,
+            )
+
+        def phase(number):
+            return pl.when((step >= starts[number]) & (step < starts[number + 1]))
+
+        @pl.when(step == 0)
+        def _():
+            brought[0].start()
+            spread.barrier((other,))
+            spread.begin()
+
+        @phase(0)
+        def _():
+            here = pl.ds(pl.multiple_of(step * ROWS, ROWS), ROWS)
+
+            def put(ref):
+                rows = ref[...].astype(F32)
+                made = (rows * root_of(rows) * g_ref[...]).astype(BF)
+                normed[here, :] = made
+                nt_ref[...] = made.T
+
+            def earlier(ref, there):
+                pl.when(there)(functools.partial(put, ref))
+
+                @pl.when(jnp.logical_not(there))
+                def _():
+                    normed[here, :] = jnp.zeros((ROWS, width), BF)
+                    nt_ref[...] = jnp.zeros((width, ROWS), BF)
+
+            pl.when(step < part_steps)(functools.partial(earlier, far_ref, me >= 2))
+            pl.when((step >= part_steps) & (step < 2 * part_steps))(functools.partial(earlier, near_ref, me >= 1))
+            pl.when(step >= 2 * part_steps)(functools.partial(put, x_ref))
+
+        def rotated(made, rows):
+            pieces = [turned(made[:, part * E : (part + 1) * E], c_ref[rows, :], s_ref[rows, :], False) for part in range(per)]
+            return jnp.concatenate(pieces, axis=1).astype(BF)
+
+        @phase(1)
+        def _():
+            rows = slice(reach - m, reach)
+            made = rotated(dot_nn(normed[rows, :], w_ref[...]), rows)
+            q_out[...] = made
+            q_all[:, pl.ds(pl.multiple_of((step - starts[1]) * TILE, TILE), TILE)] = made
+
+        @phase(2)
+        def _():
+            number = step - starts[2]
+
+            def put(made):
+                kv_out[...] = made
+                kv_all[:, pl.ds(pl.multiple_of(number * TILE, TILE), TILE)] = made
+
+            @pl.when(number < some)
             def _():
-                made = normed(ref)
-                o_ref[...] = made
-                t_ref[...] = made.T
-
-            @pl.when(jnp.logical_not(there))
+                put(rotated(dot_nn(normed[...], w_ref[...]), slice(0, reach)))
+
+            @pl.when(number >= some)
             def _():
-                o_ref[...] = jnp.zeros_like(o_ref)
-                t_ref[...] = jnp.zeros_like(t_ref)
-
-        @pl.when(step < steps)
-        def _():
-            earlier(far_ref, me >= 2)
-
-        @pl.when((step >= steps) & (step < 2 * steps))
-        def _():
-            earlier(near_ref, me >= 1)
-
-        @pl.when(step >= 2 * steps)
-        def _():
-            made = normed(x_ref)
-            o_ref[...] = made
-            t_ref[...] = made.T
-
-    def part(which):
-        return pl.BlockSpec((ROWS, width), lambda i: (jnp.clip(i - which * steps, 0, steps - 1), 0))
-
+                put(dot_nn(normed[...], w_ref[...]).astype(BF))
+
+        @pl.when(step == starts[3])
+        def _():
+            for number in range(blocks):
+                key = lax.broadcasted_iota(jnp.int32, (KB, QB), 0) + number * QB
+                query = lax.broadcasted_iota(jnp.int32, (KB, QB), 1) + number * QB
+                place = places_ref[:, number * QB : (number + 1) * QB]
+                allowed = (key <= query + WINDOW) & (key > query) & (key >= query + WINDOW - place)
+                bias[number] = jnp.where(allowed, 0.0, -1e30)
+
+        @phase(3)
+        def _():
+            head = step - starts[3]
+            lanes = pl.ds(pl.multiple_of(head * E, E), E)
+            queries = q_all[:, lanes]
+            keys = kv_all[:, lanes]
+            values_t = kv_all[:, pl.ds(pl.multiple_of(columns + head * E, E), E)].T
+            for number in range(blocks):
+                span = slice(number * QB, number * QB + KB)
+                here = slice(number * QB, (number + 1) * QB)
+                scores = dot_nt(keys[span], queries[here]) * factor + bias[number]
+                largest = jnp.max(scores, axis=0, keepdims=True)
+                grown = jnp.exp2(scores - largest)
+                inverse = 1.0 / jnp.sum(grown, axis=0, keepdims=True)
+                probs = (grown * inverse).astype(BF)
+                probs_ref[0, number] = probs
+                made = dot_nn(values_t[:, span], probs).T.astype(BF)
+                mixed_out[here, :] = made
+                mixed_all[here, lanes] = made
+
+        @pl.when(step == starts[4])
+        def _():
+            brought[0].wait()
+
+        @phase(4)
+        def _():
+            which = step - starts[4]
+            here = pl.ds(pl.multiple_of(which * ROWS, ROWS), ROWS)
+            sent[which] = dot_nt(mixed_all[here, :], w_out[...]).astype(BF)
+            across(which).start()
+
+        @phase(5)
+        def _():
+            which = step - starts[5]
+            across(which).wait()
+            hidden = again_ref[...].astype(F32) + (sent[which].astype(F32) + got[which].astype(F32))
+            made = (hidden * root_of(hidden) * gf_ref[...]).astype(BF)
+            hidden_ref[...] = hidden
+            normed_ref[...] = made
+            turned_ref[...] = made.T
+
+        spread.pace(step, list(zip(counts, (2, 2, 5, 5, 5, 20))))
+
+        @pl.when(step == total - 1)
+        def _():
+            spread.finish()
+
+    def within(number, i, length):
+        return jnp.clip(i - starts[number], 0, length - 1)
+
+    def rows_at(first):
+        return pl.BlockSpec((ROWS, width), lambda i: (jnp.clip(i - first, 0, part_steps - 1), 0))
+
+    any_space = pl.BlockSpec(memory_space=pl.ANY)
+    dma = pltpu.SemaphoreType.DMA
+    low = functools.partial(jax.ShapeDtypeStruct, dtype=BF)
     return pl.pallas_call(
         kernel,
-        grid=(3 * steps,),
-        out_shape=[jax.ShapeDtypeStruct((3 * m, width), BF), jax.ShapeDtypeStruct((width, 3 * m), BF)],
-        in_specs=[part(0), part(1), part(2), whole_spec((1, width))],
+        grid=(total,),
+        out_shape=[
+            low((width, reach)),
+            low((m, columns)),
+            low((reach, 2 * columns)),
+            low((m, columns)),
+            low((heads, blocks, KB, QB)),
+            jax.ShapeDtypeStruct((m, width), F32),
+            low((m, width)),
+            low((width, m)),
+            low((block.shape[0] * devices, block.shape[1])),
+        ],
+        in_specs=[
+            rows_at(0), rows_at(part_steps), rows_at(2 * part_steps), rows_at(starts[5]),
+            single((1, width)),
+            pl.BlockSpec((width, TILE), lambda i: (0, within(1, i, 3 * some))),
+            single((reach, E)),
+            single((reach, E)),
+            single((1, m)),
+            single((1, width)),
+            any_space,
+            any_space,
+        ],
         out_specs=[
-            pl.BlockSpec((ROWS, width), lambda i: (i, 0)),
-            pl.BlockSpec((width, ROWS), lambda i: (0, i)),
-        ],
-        compiler_params=pltpu.CompilerParams(vmem_limit_bytes=VMEM),
-        cost_estimate=cost(24 * m * width, 14 * m * width),
-        name="first_norm",
-    )(far, near, tokens, gain)
-
-
-def out_norm(mixed, w_attn, place, tokens, gain, identity):
-    m, columns = mixed.shape
-    width = tokens.shape[1]
-    steps = m // ROWS
-    sides = lax.axis_size("tensor")
-
-    def kernel(x_ref, w_ref, r_ref, g_ref, hidden_ref, normed_ref, turned_ref, sent, got, send, recv):
-        step = pl.program_id(0)
-        other = (lax.axis_index("dp"), lax.rem(lax.axis_index("tensor") + 1, sides))
-
-        @pl.when(step == 0)
-        def _():
-            semaphore = pltpu.get_barrier_semaphore()
-            pl.semaphore_signal(semaphore, inc=1, device_id=other, device_id_type=MESH)
-            pl.semaphore_wait(semaphore, 1)
-
-        def across(which):
-            return pltpu.make_async_remote_copy(
-                src_ref=sent.at[which], dst_ref=got.at[which], send_sem=send.at[which], recv_sem=recv.at[which],
-                device_id=other, device_id_type=MESH,
-            )
-
-        @pl.when(step < steps)
-        def _():
-            sent[step] = dot_nt(x_ref[...], w_ref[...]).astype(BF)
-            across(step).start()
-
-        @pl.when(step >= steps)
-        def _():
-            which = step - steps
-            across(which).wait()
-            hidden = r_ref[...].astype(F32) + (sent[which].astype(F32) + got[which].astype(F32))
-            normed = (hidden * root_of(hidden) * g_ref[...]).astype(BF)
-            hidden_ref[...] = hidden
-            normed_ref[...] = normed
-            turned_ref[...] = normed.T
-
-    def late(i):
-        return jnp.maximum(i - steps, 0)
-
-    late_rows = pl.BlockSpec((ROWS, width), lambda i: (late(i), 0))
-    dma = pltpu.SemaphoreType.DMA
-    return pl.pallas_call(
-        kernel,
-        grid=(2 * steps,),
-        out_shape=[
-            jax.ShapeDtypeStruct((m, width), F32),
-            jax.ShapeDtypeStruct((m, width), BF),
-            jax.ShapeDtypeStruct((width, m), BF),
-        ],
-        in_specs=[
-            pl.BlockSpec((ROWS, columns), lambda i: (jnp.minimum(i, steps - 1), 0)),
-            pl.BlockSpec((width, columns), lambda i: (0, place), pipeline_mode=pl.Buffered(1)),
-            late_rows,
-            single((1, width)),
-        ],
-        out_specs=[late_rows, late_rows, pl.BlockSpec((width, ROWS), lambda i: (0, late(i)))],
-        scratch_shapes=[pltpu.VMEM((steps, ROWS, width), BF), pltpu.VMEM((steps, ROWS, width), BF), dma((steps,)), dma((steps,))],
+            pl.BlockSpec((width, ROWS), lambda i: (0, within(0, i, 3 * part_steps))),
+            pl.BlockSpec((m, TILE), lambda i: (0, within(1, i, some))),
+            pl.BlockSpec((reach, TILE), lambda i: (0, within(2, i, 2 * some))),
+            pl.BlockSpec((m, E), lambda i: (0, within(3, i, heads))),
+            pl.BlockSpec((1, blocks, KB, QB), lambda i: (within(3, i, heads), 0, 0, 0)),
+            rows_at(starts[5]),
+            rows_at(starts[5]),
+            pl.BlockSpec((width, ROWS), lambda i: (0, within(5, i, part_steps))),
+            any_space,
+        ],
+        scratch_shapes=[
+            pltpu.VMEM((reach, width), BF),
+            pltpu.VMEM((m, columns), BF),
+            pltpu.VMEM((reach, 2 * columns), BF),
+            pltpu.VMEM((m, columns), BF),
+            pltpu.VMEM((width, columns), BF),
+            pltpu.VMEM((blocks, KB, QB), F32),
+            pltpu.VMEM((part_steps, ROWS, width), BF),
+            pltpu.VMEM((part_steps, ROWS, width), BF),
+            dma((1,)),
+            dma((part_steps,)),
+            dma((part_steps,)),
+            *Spread.scratch(devices, 4),
+        ],
         compiler_params=pltpu.CompilerParams(vmem_limit_bytes=VMEM, collective_id=identity, has_side_effects=True),
-        cost_estimate=cost(2 * m * width * columns, 12 * m * width),
-        name="out_norm",
-    )(mixed, w_attn, tokens, gain)
+        cost_estimate=cost(2 * (m + 2 * reach) * width * columns, 8 * reach * width, heads * m * KB),
+        name="forward",
+    )(far, near, tokens, tokens, gain, w_attn, cosine, sine, places, gain_ffn, w_attn, block)
 
 
 def last_pass(tokens, gain, grad, grad_other, grad_add, d_hidden, hidden, ffn_part, ffn_other, act_early, act_late, w_ffn, rest, gain_ffn_grad, flip, qkv_part, lanes, identity):
@@ -1274,7 +1310,7 @@
                 copy.wait()
 
         feed_tile(x_ref, dy_ref, dyt_ref, g_ref, u_ref, d_ref, act_ref, both_ref, down_ref)
-        spread.pace(step, early)
+        spread.pace(step, [(early, 1)])
 
         @pl.when(step == early - 1)
         def _():
@@ -1493,27 +1529,18 @@
     some = padded - LATE * TILE
     lanes = max(128, own_rows)
     gains = jnp.zeros((32, lanes), BF).at[0, :own_rows].set(attn_gain).at[16, :own_rows].set(ffn_gain)
-    w_attn, all_gains, near, far, ffn_pack, rest_pack = first_gather(
-        w_query, w_key, w_value, w_out, gains, tokens, w_gate.T, w_up.T, w_down, 0
+    places = positions[None, :]
+    w_attn, all_gains, near, far, ffn_pack, rest_pack, cotangent_t, cosine, sine = first_gather(
+        w_query, w_key, w_value, w_out, gains, tokens, w_gate.T, w_up.T, w_down, cotangent, places, 0
     )
-    w_ffn = lax.all_gather(ffn_pack, "dp", axis=0, tiled=True)
     all_gains = all_gains.reshape(devices, 32, lanes)
     gain_attn = all_gains[:, 0, :own_rows].reshape(1, width).astype(F32)
     gain_ffn = all_gains[:, 16, :own_rows].reshape(1, width).astype(F32)
 
-    frequency = THETA ** (-(jnp.arange(E // 2, dtype=F32) * 2.0 / E))
-    earlier = positions[0] - WINDOW + jnp.arange(WINDOW, dtype=jnp.int32)
-    angles = jnp.concatenate([earlier, positions]).astype(F32)[:, None] * frequency[None, :]
-    cosine_half, sine_half = jnp.cos(angles), jnp.sin(angles)
-    cosine = jnp.concatenate([cosine_half, cosine_half], axis=1)
-    sine = jnp.concatenate([-sine_half, sine_half], axis=1)
-
-    normed_attn, normed_attn_t = first_norm(far, near, tokens, gain_attn)
-    query, kv = project(normed_attn, w_attn, cosine, sine, span, heads)
-    mixed, probs = attend(query, kv, positions[None, :], heads)
-    hidden, normed_ffn, normed_ffn_t = out_norm(mixed, w_attn, 3, tokens, gain_ffn, 5)
-
-    cotangent_t = cotangent.T
+    normed_attn_t, query, kv, mixed, probs, hidden, normed_ffn, normed_ffn_t, w_ffn = forward(
+        far, near, tokens, gain_attn, w_attn, cosine, sine, places, gain_ffn, ffn_pack, heads, 5
+    )
+
     act_early, d_early, down_early, rest = feed(normed_ffn, cotangent, cotangent_t, w_ffn, rest_pack, tiles, 6)
     act_late, both_part, d_normed_ffn, d_normed_other, down_grad = ffn_back(
         normed_ffn, normed_ffn_t, cotangent, cotangent_t, d_early, w_ffn, rest, down_early.reshape(devices, own_rows, some), 1

time: 657 us -> 644 us (0.980)
  Pallas kernels: 598 us -> 621 us
  between operations: 15 us -> 0.92 us
  waiting for transfers between devices: 9.93 us -> 0 us
    pallas_call x4 -> x1, Pallas kernels: 110 us -> 133 us  [forward(): pl.pallas_call(kernel, grid=(total,), out_shape=[low((width, reach)), low...]
    all_gather x1 -> x0, waiting for transfers between devices: 9.91 us -> none  [shards(): w_ffn = lax.all_gather(ffn_pack, 'dp', axis=0, tiled=True)]
    unnamed x34 -> x29, local copies, waits for them, and re-layouts: 15.9 us -> 13.4 us
  transfers between devices with their start and end apart: 1 -> 0, of which waited for: 1 -> 0; matrix products, arithmetic and copies ran while one was open for 1% -> 0% of each run, Pallas kernels for 17% -> 0%
where the time goes in v9:
time: 644 us; the launch traced here: 639 us
  Pallas kernels  621 us (96%)
  local copies, waits for them, and re-layouts  16.8 us (3%)
    pallas_call x1, Pallas kernels, forward(): pl.pallas_call(kernel, grid=(total,), out_shape=[low((width, reach)), low...  133 us
    pallas_call x1, Pallas kernels, first_gather(): pl.pallas_call(kernel, out_shape=[low((rows * devices, 4 * columns)), low...  112 us
    pallas_call x1, Pallas kernels, qkv_back(): pl.pallas_call(kernel, grid=(total,), out_shape=[jax.ShapeDtypeStruct((wi...  110 us
    pallas_call x1, Pallas kernels, last_pass(): pl.pallas_call(kernel, grid=(total,), out_shape=[jax.ShapeDtypeStruct((m,...  73 us
    pallas_call x1, Pallas kernels, ffn_back(): pl.pallas_call(kernel, grid=(total,), out_shape=[jax.ShapeDtypeStruct((m,...  71.6 us
    pallas_call x1, Pallas kernels, attend_back(): pl.pallas_call(kernel, grid=(firsts + heads,), out_shape=[jax.ShapeDtypeS...  66.7 us
    pallas_call x1, Pallas kernels, feed(): pl.pallas_call(kernel, grid=(early,), out_shape=[jax.ShapeDtypeStruct((m,...  53.8 us
    unnamed x29, local copies, waits for them, and re-layouts  13.4 us

profile of v9, /device:TPU:0, one launch (start us, length us, event | category | flops | bytes accessed | tf_op | source)
XLA Modules:
  0.0 639.0 jit_solution(7503573782464469417)
XLA Ops:
  0.6 0.7 scatter.6
  1.3 0.7 scatter.9.gains_ref
  2.0 0.6 copy-done.9
  2.6 111.9 %first_gather.1 = (bf16[2048,4096]{1,0:T(8,128)(2,1)}, bf16[512,128]{1,0:T(8,128)(2,1)}, bf16[512,2048]{1,0:T(8,128)(2,1)}, bf16[512,2048]{1,0:T(8,128)(2,1)}, b...) custom-call(bf16[128,1024]{1,0:T(8,128)(2,1)} %q_ref.1, ...), custom_call_target="tpu_custom_call" | custom-call | tf_op jit(solution)/shard_map/first_gather/pallas_call | solution.py:327
  114.4 0.8 fusion
  115.2 0.6 copy_convert_fusion
  115.8 133.3 %forward.1 = (bf16[2048,1536]{1,0:T(8,128)(2,1)}, bf16[512,1024]{1,0:T(8,128)(2,1)}, bf16[1536,2048]{1,0:T(8,128)(2,1)}, bf16[512,1024]{1,0:T(8,128)(2,1)}, bf16...) custom-call(bf16[512,2048]{1,0:T(8,128)(2,1)} %get-tuple-element.86., ...), custom_call_target="tpu_custom_call" | custom-call | flops 15032385536 | bytes 25165824 | tf_op jit(solution)/shard_map/forward/pallas_call | solution.py:1052
  249.1 53.8 %feed.1 = (bf16[512,2048]{1,0:T(8,128)(2,1)}, bf16[2,512,2048]{2,1,0:T(8,128)(2,1)}, bf16[2048,2048]{1,0:T(8,128)(2,1)}, bf16[2048,2304]{1,0:T(8,128)(2,1)}) custom-call(bf16[512,2048]{1,0:T(8,128)(2,1)} %get-tuple-element.98.x_hbm, bf16[512,2048]{1,0:T(8,128)(2,1)} %y_ref.1, bf16[2048,512]{1,0:T(8,128)(2,1)} %get-tuple-element.100.dyt_hbm, ...), custom_call_target="tpu_custom_call" | custom-call | flops 17179869184 | bytes 41943040 | tf_op jit(solution)/shard_map/feed/pallas_call | solution.py:1320
  302.9 71.6 %ffn_back.1 = (bf16[512,768]{1,0:T(8,128)(2,1)}, bf16[2,2048,2816]{2,1,0:T(8,128)(2,1)}, bf16[512,2048]{1,0:T(8,128)(2,1)}, bf16[512,2048]{1,0:T(8,128)(2,1)}, f32[128,2816]{1,0:T(8,128)}) custom-call(bf16[512,2048]{1,0:T(8,128)(2,1)} %get-tuple-element.98.x_hbm, bf16[2048,512]{1,0:T(8,128)(2,1)} %get-tuple-element.99.xt_hbm, bf16[512,2048]{1,0:T(8,128)(2,1)} %y_ref.1, ...), custom_call_target="tpu_custom_call" | custom-call | flops 30064771072 | bytes 57671680 | tf_op jit(solution)/shard_map/ffn_back/pallas_call | solution.py:1466
  374.6 66.7 %attend_back.1 = (bf16[512,1024]{1,0:T(8,128)(2,1)}, bf16[1536,1024]{1,0:T(8,128)(2,1)}, bf16[1536,1024]{1,0:T(8,128)(2,1)}, bf16[2048,1024]{1,0:T(8,128)(2,1)},...) custom-call(bf16[512,1024]{1,0:T(8,128)(2,1)} %get-tuple-element.93., ...), custom_call_target="tpu_custom_call" | custom-call | flops 10737418240 | bytes 10485760 | tf_op jit(solution)/shard_map/attend_back/pallas_call | solution.py:649
  441.3 110.3 %qkv_back.1 = (bf16[2048,3072]{1,0:T(8,128)(2,1)}, bf16[512,2048]{1,0:T(8,128)(2,1)}, bf16[512,2048]{1,0:T(8,128)(2,1)}, bf16[256,2048]{1,0:T(8,128)(2,1)}, f32[128,2752]{1,0:T(8,128)}, /*index=5*/f32[128,1024]{1,0:T(8,128)}) custom-call(bf16[2048,1536]{1,0:T(8,128)(2,1)} %get-tuple-element.92.xt_hbm, bf16[512,1024]{1,0:T(8,128)(2,1)} %get-tuple-element.112.dq_hbm, ...), custom_call_target="tpu_custom_call" | custom-call | flops 30064771072 | bytes 25165824 | tf_op jit(solution)/shard_map/qkv_back/pallas_call | solution.py:841
  551.6 73.0 %last_pass.1 = (f32[512,2048]{1,0:T(8,128)}, bf16[512,2048]{1,0:T(8,128)(2,1)}, f32[1024,128]{1,0:T(8,128)}, f32[128,1024]{1,0:T(8,128)}, f32[128,1024]{1,0:T(8,...) custom-call(bf16[512,2048]{1,0:T(8,128)(2,1)} %x_ref.3, f32[1,2048]{1,0:T(1,128)} %bitcast.23, ...), custom_call_target="tpu_custom_call" | custom-call | flops 20971520 | bytes 25165824 | tf_op jit(solution)/shard_map/last_pass/pallas_call | solution.py:1235
  624.7 1.3 slice_bitcast_fusion
  626.0 1.5 copy.27
  627.5 1.5 copy.26
  629.0 0.5 copy-done.1
  629.5 1.3 copy.40
  630.8 1.6 copy-done
  632.5 2.0 copy.41
  634.5 0.8 copy.42
  635.3 0.8 copy.43
  636.1 0.8 copy.44
  636.9 0.8 copy.45
  637.7 1.1 copy.46
  (17 shorter events, 0.0 us)
Async XLA Ops:
  2.0 0.6 copy-start.9
  551.6 74.4 %copy-start.3 = (f32[128,2752]{1,0:T(8,128)S(1)}, f32[128,2752]{1,0:T(8,128)}, u32[]{:S(2)}) copy-start(f32[128,2752]{1,0:T(8,128)} %get-tuple-element.144) | copy-start | bytes 4227076
  624.7 2.8 copy-start.2
  627.5 2.0 copy-start.1
  629.5 2.9 copy-start
  632.5 2.0 copy-start.8
  632.5 2.8 copy-start.7
  632.5 3.6 copy-start.6
  634.5 2.4 copy-start.5
  634.5 3.2 copy-start.4

commit v10 on v9

--- a/solution.py
+++ b/solution.py
@@ -173,7 +173,7 @@
         lax.fori_loop(1, self.chips, gave, 0)
 
 
-def first_gather(w_query, w_key, w_value, w_out, gains, tokens, w_gate_t, w_up_t, w_down, cotangent, places, identity):
+def first_gather(w_query, w_key, w_value, w_out, attn_gain, ffn_gain, tokens, w_gate_t, w_up_t, w_down, cotangent, places, identity):
     devices = lax.axis_size("dp")
     sides = lax.axis_size("tensor")
     rows, columns = w_query.shape
@@ -187,9 +187,11 @@
     rates = THETA ** (-(np.arange(E // 2, dtype=np.float32) * 2.0 / E))
     rates = jnp.asarray(np.concatenate([rates, rates])[None, :], F32)
 
-    def kernel(q_ref, k_ref, v_ref, o_hbm, gains_ref, tokens_ref, gate_hbm, up_hbm, down_hbm, dy_hbm, places_ref, rates_ref, attn_ref, all_ref, near, far, early_hbm, late_hbm, dyt_hbm, cos_hbm, sin_hbm, o_in, o_turned, gate_in, up_in, down_in, early_pack, late_pack, dy_in, dyt, cosine, sine, load_sem, store_sem, far_send, far_recv, near_send, near_recv, *scratch):
+    lanes = max(128, rows)
+
+    def kernel(q_ref, k_ref, v_ref, o_hbm, tokens_ref, gate_hbm, up_hbm, down_hbm, dy_hbm, ag_ref, fg_ref, places_ref, rates_ref, attn_ref, all_ref, near, far, early_hbm, late_hbm, dyt_hbm, cos_hbm, sin_hbm, o_in, o_turned, gate_in, up_in, down_in, early_pack, late_pack, dy_in, dyt, cosine, sine, gains_ref, load_sem, store_sem, far_send, far_recv, near_send, near_recv, *scratch):
         pieces = [(ref, 0, attn_ref, number * columns, columns) for number, ref in enumerate((q_ref, k_ref, v_ref, o_turned))]
-        spread = Spread(devices, [*pieces, (gains_ref, 0, all_ref, 0, gains_ref.shape[1])], scratch)
+        spread = Spread(devices, [*pieces, (gains_ref, 0, all_ref, 0, lanes)], scratch)
         me, side, core = spread.me, spread.side, spread.core
         across = lax.rem(side + 1, sides)
         later, before = lax.rem(me + 2, devices), lax.rem(me + devices - 2, devices)
@@ -237,6 +239,9 @@
         own_near = [near_copy(tokens_ref, which, which) for which in range(2)]
         far_near = [near_copy(far, which, slot) for slot, which in enumerate((side, across))]
 
+        gains_ref[...] = jnp.zeros_like(gains_ref)
+        gains_ref[:16, :rows] = jnp.broadcast_to(ag_ref[...], (16, rows))
+        gains_ref[16:, :rows] = jnp.broadcast_to(fg_ref[...], (16, rows))
         brought[0].wait()
         o_turned[...] = o_in[...].T
         spread.begin()
@@ -328,7 +333,7 @@
         kernel,
         out_shape=[
             low((rows * devices, 4 * columns)),
-            low((gains.shape[0] * devices, gains.shape[1])),
+            low((32 * devices, lanes)),
             low(tokens.shape),
             low(tokens.shape),
             low((rows, 3 * some)),
@@ -337,7 +342,7 @@
             jax.ShapeDtypeStruct((reach, E), F32),
             jax.ShapeDtypeStruct((reach, E), F32),
         ],
-        in_specs=[any_space] * 10 + [pl.BlockSpec(memory_space=pltpu.VMEM)] * 2,
+        in_specs=[any_space] * 9 + [pl.BlockSpec(memory_space=pltpu.VMEM)] * 4,
         out_specs=[any_space] * 9,
         scratch_shapes=[
             pltpu.VMEM(w_out.shape, BF),
@@ -349,6 +354,7 @@
             pltpu.VMEM((width, m), BF),
             pltpu.VMEM((reach, E), F32),
             pltpu.VMEM((reach, E), F32),
+            pltpu.VMEM((32, lanes), BF),
             dma((5,)),
             dma((5,)),
             dma((2,)),
@@ -359,7 +365,7 @@
         ],
         compiler_params=pltpu.CompilerParams(vmem_limit_bytes=VMEM, collective_id=identity, has_side_effects=True),
         name="first_gather",
-    )(w_query, w_key, w_value, w_out, gains, tokens, w_gate_t, w_up_t, w_down, cotangent, places, rates)
+    )(w_query, w_key, w_value, w_out, tokens, w_gate_t, w_up_t, w_down, cotangent, attn_gain[None, :], ffn_gain[None, :], places, rates)
 
 
 class Ring:
@@ -897,7 +903,7 @@
     return root * pushed - rows * (root * root * root * inner), jnp.sum(grad * rows * root, axis=0, keepdims=True)
 
 
-def forward(far, near, tokens, gain, w_attn, cosine, sine, places, gain_ffn, block, heads, identity):
+def forward(far, near, tokens, gains, w_attn, cosine, sine, places, block, heads, identity):
     m, width = tokens.shape
     reach = 3 * m
     columns = heads * E
@@ -913,7 +919,9 @@
     total = starts[-1]
     piece = block.shape[1] // 4
 
-    def kernel(far_ref, near_ref, x_ref, again_ref, g_ref, w_ref, c_ref, s_ref, places_ref, gf_ref, w_hbm, block_ref, nt_ref, q_out, kv_out, mixed_out, probs_ref, hidden_ref, normed_ref, turned_ref, whole_ref, normed, q_all, kv_all, mixed_all, w_out, bias, sent, got, load_sem, y_send, y_recv, *scratch):
+    own = width // devices
+
+    def kernel(far_ref, near_ref, x_ref, again_ref, gains_ref, w_ref, c_ref, s_ref, places_ref, w_hbm, block_ref, nt_ref, q_out, kv_out, mixed_out, probs_ref, hidden_ref, normed_ref, turned_ref, whole_ref, g_ref, gf_ref, normed, q_all, kv_all, mixed_all, w_out, bias, sent, got, load_sem, y_send, y_recv, *scratch):
         step = pl.program_id(0)
         spread = Spread(devices, [(block_ref, number * piece, whole_ref, number * piece, piece) for number in range(4)], scratch)
         me, side = spread.me, spread.side
@@ -934,6 +942,10 @@
             brought[0].start()
             spread.barrier((other,))
             spread.begin()
+            for device in range(devices):
+                span = slice(device * own, (device + 1) * own)
+                g_ref[:, span] = gains_ref[device * 32 : device * 32 + 1, :own].astype(F32)
+                gf_ref[:, span] = gains_ref[device * 32 + 16 : device * 32 + 17, :own].astype(F32)
 
         @phase(0)
         def _():
@@ -1062,15 +1074,16 @@
             low((m, width)),
             low((width, m)),
             low((block.shape[0] * devices, block.shape[1])),
+            jax.ShapeDtypeStruct((1, width), F32),
+            jax.ShapeDtypeStruct((1, width), F32),
         ],
         in_specs=[
             rows_at(0), rows_at(part_steps), rows_at(2 * part_steps), rows_at(starts[5]),
-            single((1, width)),
+            single(gains.shape),
             pl.BlockSpec((width, TILE), lambda i: (0, within(1, i, 3 * some))),
             single((reach, E)),
             single((reach, E)),
             single((1, m)),
-            single((1, width)),
             any_space,
             any_space,
         ],
@@ -1084,6 +1097,8 @@
             rows_at(starts[5]),
             pl.BlockSpec((width, ROWS), lambda i: (0, within(5, i, part_steps))),
             any_space,
+            single((1, width)),
+            single((1, width)),
         ],
         scratch_shapes=[
             pltpu.VMEM((reach, width), BF),
@@ -1102,7 +1117,7 @@
         compiler_params=pltpu.CompilerParams(vmem_limit_bytes=VMEM, collective_id=identity, has_side_effects=True),
         cost_estimate=cost(2 * (m + 2 * reach) * width * columns, 8 * reach * width, heads * m * KB),
         name="forward",
-    )(far, near, tokens, tokens, gain, w_attn, cosine, sine, places, gain_ffn, w_attn, block)
+    )(far, near, tokens, tokens, gains, w_attn, cosine, sine, places, w_attn, block)
 
 
 def last_pass(tokens, gain, grad, grad_other, grad_add, d_hidden, hidden, ffn_part, ffn_other, act_early, act_late, w_ffn, rest, gain_ffn_grad, flip, qkv_part, lanes, identity):
@@ -1528,17 +1543,12 @@
 
     some = padded - LATE * TILE
     lanes = max(128, own_rows)
-    gains = jnp.zeros((32, lanes), BF).at[0, :own_rows].set(attn_gain).at[16, :own_rows].set(ffn_gain)
     places = positions[None, :]
     w_attn, all_gains, near, far, ffn_pack, rest_pack, cotangent_t, cosine, sine = first_gather(
-        w_query, w_key, w_value, w_out, gains, tokens, w_gate.T, w_up.T, w_down, cotangent, places, 0
+        w_query, w_key, w_value, w_out, attn_gain, ffn_gain, tokens, w_gate.T, w_up.T, w_down, cotangent, places, 0
     )
-    all_gains = all_gains.reshape(devices, 32, lanes)
-    gain_attn = all_gains[:, 0, :own_rows].reshape(1, width).astype(F32)
-    gain_ffn = all_gains[:, 16, :own_rows].reshape(1, width).astype(F32)
-
-    normed_attn_t, query, kv, mixed, probs, hidden, normed_ffn, normed_ffn_t, w_ffn = forward(
-        far, near, tokens, gain_attn, w_attn, cosine, sine, places, gain_ffn, ffn_pack, heads, 5
+    normed_attn_t, query, kv, mixed, probs, hidden, normed_ffn, normed_ffn_t, w_ffn, gain_attn, gain_ffn = forward(
+        far, near, tokens, all_gains, w_attn, cosine, sine, places, ffn_pack, heads, 5
     )
 
     act_early, d_early, down_early, rest = feed(normed_ffn, cotangent, cotangent_t, w_ffn, rest_pack, tiles, 6)

time: 644 us -> 641 us (level)
    unnamed x29 -> x27, local copies, waits for them, and re-layouts: 13.4 us -> 12.8 us
where the time goes in v10:
time: 641 us; the launch traced here: 636 us
  Pallas kernels  621 us (97%)
  local copies, waits for them, and re-layouts  14.1 us (2%)
    pallas_call x1, Pallas kernels, forward(): pl.pallas_call(kernel, grid=(total,), out_shape=[low((width, reach)), low...  133 us
    pallas_call x1, Pallas kernels, first_gather(): pl.pallas_call(kernel, out_shape=[low((rows * devices, 4 * columns)), low...  112 us
    pallas_call x1, Pallas kernels, qkv_back(): pl.pallas_call(kernel, grid=(total,), out_shape=[jax.ShapeDtypeStruct((wi...  110 us
    pallas_call x1, Pallas kernels, last_pass(): pl.pallas_call(kernel, grid=(total,), out_shape=[jax.ShapeDtypeStruct((m,...  73 us
    pallas_call x1, Pallas kernels, ffn_back(): pl.pallas_call(kernel, grid=(total,), out_shape=[jax.ShapeDtypeStruct((m,...  71.7 us
    pallas_call x1, Pallas kernels, attend_back(): pl.pallas_call(kernel, grid=(firsts + heads,), out_shape=[jax.ShapeDtypeS...  66.8 us
    pallas_call x1, Pallas kernels, feed(): pl.pallas_call(kernel, grid=(early,), out_shape=[jax.ShapeDtypeStruct((m,...  53.8 us

profile of v10, /device:TPU:0, one launch (start us, length us, event | category | flops | bytes accessed | tf_op | source)
XLA Modules:
  0.0 635.8 jit_solution(13828076052975426176)
XLA Ops:
  0.6 111.9 %first_gather.1 = (bf16[2048,4096]{1,0:T(8,128)(2,1)}, bf16[512,128]{1,0:T(8,128)(2,1)}, bf16[512,2048]{1,0:T(8,128)(2,1)}, bf16[512,2048]{1,0:T(8,128)(2,1)}, b...) custom-call(bf16[128,1024]{1,0:T(8,128)(2,1)} %q_ref.1, ...), custom_call_target="tpu_custom_call" | custom-call | tf_op jit(solution)/shard_map/first_gather/pallas_call | solution.py:332
  112.6 133.4 %forward.1 = (bf16[2048,1536]{1,0:T(8,128)(2,1)}, bf16[512,1024]{1,0:T(8,128)(2,1)}, bf16[1536,2048]{1,0:T(8,128)(2,1)}, bf16[512,1024]{1,0:T(8,128)(2,1)}, bf16...) custom-call(bf16[512,2048]{1,0:T(8,128)(2,1)} %get-tuple-element.63., ...), custom_call_target="tpu_custom_call" | custom-call | flops 15032385536 | bytes 25165824 | tf_op jit(solution)/shard_map/forward/pallas_call | solution.py:1064
  246.0 53.8 %feed.1 = (bf16[512,2048]{1,0:T(8,128)(2,1)}, bf16[2,512,2048]{2,1,0:T(8,128)(2,1)}, bf16[2048,2048]{1,0:T(8,128)(2,1)}, bf16[2048,2304]{1,0:T(8,128)(2,1)}) custom-call(bf16[512,2048]{1,0:T(8,128)(2,1)} %get-tuple-element.78.x_hbm, bf16[512,2048]{1,0:T(8,128)(2,1)} %y_ref.1, bf16[2048,512]{1,0:T(8,128)(2,1)} %get-tuple-element.80.dyt_hbm, ...), custom_call_target="tpu_custom_call" | custom-call | flops 17179869184 | bytes 41943040 | tf_op jit(solution)/shard_map/feed/pallas_call | solution.py:1335
  299.8 71.7 %ffn_back.1 = (bf16[512,768]{1,0:T(8,128)(2,1)}, bf16[2,2048,2816]{2,1,0:T(8,128)(2,1)}, bf16[512,2048]{1,0:T(8,128)(2,1)}, bf16[512,2048]{1,0:T(8,128)(2,1)}, f32[128,2816]{1,0:T(8,128)}) custom-call(bf16[512,2048]{1,0:T(8,128)(2,1)} %get-tuple-element.78.x_hbm, bf16[2048,512]{1,0:T(8,128)(2,1)} %get-tuple-element.79.xt_hbm, bf16[512,2048]{1,0:T(8,128)(2,1)} %y_ref.1, ...), custom_call_target="tpu_custom_call" | custom-call | flops 30064771072 | bytes 57671680 | tf_op jit(solution)/shard_map/ffn_back/pallas_call | solution.py:1481
  371.4 66.8 %attend_back.1 = (bf16[512,1024]{1,0:T(8,128)(2,1)}, bf16[1536,1024]{1,0:T(8,128)(2,1)}, bf16[1536,1024]{1,0:T(8,128)(2,1)}, bf16[2048,1024]{1,0:T(8,128)(2,1)},...) custom-call(bf16[512,1024]{1,0:T(8,128)(2,1)} %get-tuple-element.72., ...), custom_call_target="tpu_custom_call" | custom-call | flops 10737418240 | bytes 10485760 | tf_op jit(solution)/shard_map/attend_back/pallas_call | solution.py:655
  438.2 110.2 %qkv_back.1 = (bf16[2048,3072]{1,0:T(8,128)(2,1)}, bf16[512,2048]{1,0:T(8,128)(2,1)}, bf16[512,2048]{1,0:T(8,128)(2,1)}, bf16[256,2048]{1,0:T(8,128)(2,1)}, f32[128,2752]{1,0:T(8,128)}, /*index=5*/f32[128,1024]{1,0:T(8,128)}) custom-call(bf16[2048,1536]{1,0:T(8,128)(2,1)} %get-tuple-element.71.xt_hbm, bf16[512,1024]{1,0:T(8,128)(2,1)} %get-tuple-element.92.dq_hbm, ...), custom_call_target="tpu_custom_call" | custom-call | flops 30064771072 | bytes 25165824 | tf_op jit(solution)/shard_map/qkv_back/pallas_call | solution.py:847
  548.5 0.0 copy-start.3
  548.5 73.0 %last_pass.1 = (f32[512,2048]{1,0:T(8,128)}, bf16[512,2048]{1,0:T(8,128)(2,1)}, f32[1024,128]{1,0:T(8,128)}, f32[128,1024]{1,0:T(8,128)}, f32[128,1024]{1,0:T(8,...) custom-call(bf16[512,2048]{1,0:T(8,128)(2,1)} %x_ref.3, f32[1,2048]{1,0:T(1,128)} %get-tuple-element.70.g_ref, ...), custom_call_target="tpu_custom_call" | custom-call | flops 20971520 | bytes 25165824 | tf_op jit(solution)/shard_map/last_pass/pallas_call | solution.py:1250
  621.5 0.0 copy-start.2
  621.5 1.3 slice_bitcast_fusion
  622.8 0.0 copy-done.3
  622.8 1.5 copy.25
  624.3 1.5 copy.24
  625.9 0.5 copy-done.1
  626.4 1.3 copy.33
  627.7 1.6 copy-done
  629.3 2.0 copy.34
  631.3 0.8 copy.35
  632.1 0.8 copy.36
  632.9 0.8 copy.37
  633.7 0.0 copy-done.5
  633.7 0.8 copy.38
  634.5 0.0 copy-done.4
  634.5 1.1 copy.39
  (11 shorter events, 0.0 us)
Async XLA Ops:
  548.5 74.3 %copy-start.3 = (f32[128,2752]{1,0:T(8,128)S(1)}, f32[128,2752]{1,0:T(8,128)}, u32[]{:S(2)}) copy-start(f32[128,2752]{1,0:T(8,128)} %get-tuple-element.124) | copy-start | bytes 4227076
  621.5 2.8 copy-start.2
  624.3 2.0 copy-start.1
  626.3 2.9 copy-start
  629.3 2.0 copy-start.8
  629.3 2.8 copy-start.7
  629.3 3.6 copy-start.6
  631.3 2.4 copy-start.5
  631.3 3.2 copy-start.4

commit v11 on v10

--- a/solution.py
+++ b/solution.py
@@ -20,7 +20,7 @@
 KB = WINDOW + QB
 TILE = 256
 ROWS = 128
-SOON = 2
+SOON = 3
 LATE = 3
 VMEM = 59 * 1024 * 1024
 

time: 641 us -> 641 us (level)
  no operation moved by 1% of the time
where the time goes in v11:
time: 641 us; the launch traced here: 635 us
  Pallas kernels  620 us (97%)
  local copies, waits for them, and re-layouts  14.1 us (2%)
    pallas_call x1, Pallas kernels, forward(): pl.pallas_call(kernel, grid=(total,), out_shape=[low((width, reach)), low...  133 us
    pallas_call x1, Pallas kernels, first_gather(): pl.pallas_call(kernel, out_shape=[low((rows * devices, 4 * columns)), low...  112 us
    pallas_call x1, Pallas kernels, qkv_back(): pl.pallas_call(kernel, grid=(total,), out_shape=[jax.ShapeDtypeStruct((wi...  110 us
    pallas_call x1, Pallas kernels, last_pass(): pl.pallas_call(kernel, grid=(total,), out_shape=[jax.ShapeDtypeStruct((m,...  72.9 us
    pallas_call x1, Pallas kernels, ffn_back(): pl.pallas_call(kernel, grid=(total,), out_shape=[jax.ShapeDtypeStruct((m,...  71.7 us
    pallas_call x1, Pallas kernels, attend_back(): pl.pallas_call(kernel, grid=(firsts + heads,), out_shape=[jax.ShapeDtypeS...  66.9 us
    pallas_call x1, Pallas kernels, feed(): pl.pallas_call(kernel, grid=(early,), out_shape=[jax.ShapeDtypeStruct((m,...  53.8 us

profile of v11, /device:TPU:0, one launch (start us, length us, event | category | flops | bytes accessed | tf_op | source)
XLA Modules:
  0.0 635.5 jit_solution(8077926599199124409)
XLA Ops:
  0.6 111.9 %first_gather.1 = (bf16[2048,4096]{1,0:T(8,128)(2,1)}, bf16[512,128]{1,0:T(8,128)(2,1)}, bf16[512,2048]{1,0:T(8,128)(2,1)}, bf16[512,2048]{1,0:T(8,128)(2,1)}, b...) custom-call(bf16[128,1024]{1,0:T(8,128)(2,1)} %q_ref.1, ...), custom_call_target="tpu_custom_call" | custom-call | tf_op jit(solution)/shard_map/first_gather/pallas_call | solution.py:332
  112.6 133.4 %forward.1 = (bf16[2048,1536]{1,0:T(8,128)(2,1)}, bf16[512,1024]{1,0:T(8,128)(2,1)}, bf16[1536,2048]{1,0:T(8,128)(2,1)}, bf16[512,1024]{1,0:T(8,128)(2,1)}, bf16...) custom-call(bf16[512,2048]{1,0:T(8,128)(2,1)} %get-tuple-element.63., ...), custom_call_target="tpu_custom_call" | custom-call | flops 15032385536 | bytes 25165824 | tf_op jit(solution)/shard_map/forward/pallas_call | solution.py:1064
  246.0 53.8 %feed.1 = (bf16[512,2048]{1,0:T(8,128)(2,1)}, bf16[2,512,2048]{2,1,0:T(8,128)(2,1)}, bf16[2048,2048]{1,0:T(8,128)(2,1)}, bf16[2048,2304]{1,0:T(8,128)(2,1)}) custom-call(bf16[512,2048]{1,0:T(8,128)(2,1)} %get-tuple-element.78.x_hbm, bf16[512,2048]{1,0:T(8,128)(2,1)} %y_ref.1, bf16[2048,512]{1,0:T(8,128)(2,1)} %get-tuple-element.80.dyt_hbm, ...), custom_call_target="tpu_custom_call" | custom-call | flops 17179869184 | bytes 41943040 | tf_op jit(solution)/shard_map/feed/pallas_call | solution.py:1335
  299.7 71.7 %ffn_back.1 = (bf16[512,768]{1,0:T(8,128)(2,1)}, bf16[2,2048,2816]{2,1,0:T(8,128)(2,1)}, bf16[512,2048]{1,0:T(8,128)(2,1)}, bf16[512,2048]{1,0:T(8,128)(2,1)}, f32[128,2816]{1,0:T(8,128)}) custom-call(bf16[512,2048]{1,0:T(8,128)(2,1)} %get-tuple-element.78.x_hbm, bf16[2048,512]{1,0:T(8,128)(2,1)} %get-tuple-element.79.xt_hbm, bf16[512,2048]{1,0:T(8,128)(2,1)} %y_ref.1, ...), custom_call_target="tpu_custom_call" | custom-call | flops 30064771072 | bytes 57671680 | tf_op jit(solution)/shard_map/ffn_back/pallas_call | solution.py:1481
  371.4 66.9 %attend_back.1 = (bf16[512,1024]{1,0:T(8,128)(2,1)}, bf16[1536,1024]{1,0:T(8,128)(2,1)}, bf16[1536,1024]{1,0:T(8,128)(2,1)}, bf16[2048,1024]{1,0:T(8,128)(2,1)},...) custom-call(bf16[512,1024]{1,0:T(8,128)(2,1)} %get-tuple-element.72., ...), custom_call_target="tpu_custom_call" | custom-call | flops 10737418240 | bytes 10485760 | tf_op jit(solution)/shard_map/attend_back/pallas_call | solution.py:655
  438.3 109.9 %qkv_back.1 = (bf16[2048,3072]{1,0:T(8,128)(2,1)}, bf16[512,2048]{1,0:T(8,128)(2,1)}, bf16[512,2048]{1,0:T(8,128)(2,1)}, bf16[256,2048]{1,0:T(8,128)(2,1)}, f32[128,2752]{1,0:T(8,128)}, /*index=5*/f32[128,1024]{1,0:T(8,128)}) custom-call(bf16[2048,1536]{1,0:T(8,128)(2,1)} %get-tuple-element.71.xt_hbm, bf16[512,1024]{1,0:T(8,128)(2,1)} %get-tuple-element.92.dq_hbm, ...), custom_call_target="tpu_custom_call" | custom-call | flops 30064771072 | bytes 25165824 | tf_op jit(solution)/shard_map/qkv_back/pallas_call | solution.py:847
  548.2 0.0 copy-start.3
  548.2 72.9 %last_pass.1 = (f32[512,2048]{1,0:T(8,128)}, bf16[512,2048]{1,0:T(8,128)(2,1)}, f32[1024,128]{1,0:T(8,128)}, f32[128,1024]{1,0:T(8,128)}, f32[128,1024]{1,0:T(8,...) custom-call(bf16[512,2048]{1,0:T(8,128)(2,1)} %x_ref.3, f32[1,2048]{1,0:T(1,128)} %get-tuple-element.70.g_ref, ...), custom_call_target="tpu_custom_call" | custom-call | flops 20971520 | bytes 25165824 | tf_op jit(solution)/shard_map/last_pass/pallas_call | solution.py:1250
  621.2 0.0 copy-start.2
  621.2 1.3 slice_bitcast_fusion
  622.5 0.0 copy-done.3
  622.5 1.5 copy.25
  624.0 0.0 copy-done.2
  624.0 1.5 copy.24
  625.6 0.5 copy-done.1
  626.0 1.3 copy.33
  627.4 1.6 copy-done
  629.0 2.0 copy.34
  631.0 0.8 copy.35
  631.8 0.8 copy.36
  632.6 0.8 copy.37
  633.4 0.8 copy.38
  634.2 0.0 copy-done.4
  634.2 1.1 copy.39
  (11 shorter events, 0.0 us)
Async XLA Ops:
  548.2 74.3 %copy-start.3 = (f32[128,2752]{1,0:T(8,128)S(1)}, f32[128,2752]{1,0:T(8,128)}, u32[]{:S(2)}) copy-start(f32[128,2752]{1,0:T(8,128)} %get-tuple-element.124) | copy-start | bytes 4227076
  621.2 2.8 copy-start.2
  624.0 2.0 copy-start.1
  626.0 2.9 copy-start
  629.0 2.0 copy-start.8
  629.0 2.8 copy-start.7
  629.0 3.6 copy-start.6
  631.0 2.4 copy-start.5
  631.0 3.2 copy-start.4
